TPU v7x, 32 devices: a whole 2x2x4 slice. The times are simulated.
32 devices in a mesh: batch: 4 (over z), fsdp: 8 (over y, x, core).
Axes of the slice: x: 2, y: 2, z: 4, core: 2. Of those that a mesh axis runs over, the one named last changes fastest.
Arguments:
- tokens: bfloat16 [64, 512, 768], P(('batch', 'fsdp')), may hold values from -6 to 6
- seg_ids: int32 [64, 512], P(('batch', 'fsdp')), may hold values from 0 to 7, never falling along the last dimension, each value on 1 to 128 neighbouring positions
- positive: int32 [512], P(('batch', 'fsdp')), may hold values from 0 to 511, as said below
- out_grad: bfloat16 [64, 512, 768], P(('batch', 'fsdp')), may hold values from -6 to 6
- w_qkv: bfloat16 [768, 2304], P('fsdp'), may hold values from -0.3125 to 0.3125
- b_qv: bfloat16 [1536], P('fsdp'), may hold values from -3 to 3
- w_out: bfloat16 [768, 768], P('fsdp'), may hold values from -0.875 to 0.875
- b_out: bfloat16 [768], P('fsdp'), may hold values from -3 to 3
- norm1_gain: bfloat16 [768], P('fsdp'), may hold values from 0.25 to 1.75
- norm1_shift: bfloat16 [768], P('fsdp'), may hold values from -3 to 3
- w_up: bfloat16 [768, 3072], P('fsdp'), may hold values from -0.21875 to 0.21875
- b_up: bfloat16 [3072], P('fsdp'), may hold values from -3 to 3
- w_down: bfloat16 [3072, 768], P('fsdp'), may hold values from -0.15625 to 0.15625
- b_down: bfloat16 [768], P('fsdp'), may hold values from -3 to 3
- norm2_gain: bfloat16 [768], P('fsdp'), may hold values from 0.25 to 1.75
- norm2_shift: bfloat16 [768], P('fsdp'), may hold values from -3 to 3
Outputs:
- result_out: bfloat16 [64, 512, 768], P(('batch', 'fsdp'))
- pair_loss: float32 [512], P(('batch', 'fsdp'))
- grad_tokens: float32 [64, 512, 768], P(('batch', 'fsdp'))
- grad_wqkv: float32 [768, 2304], P('fsdp')
- grad_bqv: float32 [1536], P('fsdp')
- grad_wout: float32 [768, 768], P('fsdp')
- grad_bout: float32 [768], P('fsdp')
- grad_gain1: float32 [768], P('fsdp')
- grad_shift1: float32 [768], P('fsdp')
- grad_wup: float32 [768, 3072], P('fsdp')
- grad_bup: float32 [3072], P('fsdp')
- grad_wdown: float32 [3072, 768], P('fsdp')
- grad_bdown: float32 [768], P('fsdp')
- grad_gain2: float32 [768], P('fsdp')
- grad_shift2: float32 [768], P('fsdp')
Inputs may be any that keep to these rules, and one draw needn't show every extreme that they name: `positive`: a permutation of the 512 segments in one cycle: no segment is its own partner.
All inputs are finite; a program needn't handle non-finite values.
Results may differ from a plain program's by a relative error of at most 0.013.
Values may be sent and summed in bfloat16 or wider, within the bound.
No kernel may reach another device: no remote copies, remote signals or barrier semaphores. Data moves between devices by JAX's collectives and lax.ppermute only.
A program may use at most 192 MiB of HBM per device.

v0:
```python
import math

import jax
import jax.numpy as jnp
from jax import lax
from jax.sharding import PartitionSpec as P

HEADS = 12
SEGS = 8


norm_eps = 1e-06
pool_eps = 1e-06
score_scale = 50.0
pair_weight = 256.0
masked_value = -1000000000.0


def scale_rows(values):
    row_mean = jnp.mean(values, axis=-1, keepdims=True)
    centred = values - row_mean
    spread = jnp.mean(centred * centred, axis=-1, keepdims=True)
    return centred * lax.rsqrt(spread + norm_eps)


def normalize(pooled):
    return pooled * lax.rsqrt(jnp.mean(pooled * pooled, axis=-1, keepdims=True) + pool_eps)


def gelu_exact(values):
    return jax.nn.gelu(values, approximate=False)


def masked_scores(queries, key_rows, row_ids):
    inv_root = 1.0 / math.sqrt(queries.shape[-1])
    scores = (
        jnp.einsum("qhd,khd->hqk", queries, key_rows, preferred_element_type=jnp.float32) * inv_root
    )
    same_seg = row_ids[:, None] == row_ids[None, :]
    return jnp.where(same_seg[None], scores, masked_value)


def attend_forward(pieces):
    queries, key_rows, values, row_ids = pieces
    scores = masked_scores(queries, key_rows, row_ids)
    row_max = jnp.max(scores, axis=-1, keepdims=True)
    exp_terms = jnp.exp(scores - row_max)
    row_total = jnp.sum(exp_terms, axis=-1, keepdims=True)
    attn_probs = (exp_terms / row_total).astype(jnp.bfloat16)
    context = jnp.einsum("hqk,khd->qhd", attn_probs, values, preferred_element_type=jnp.float32)
    return (context, row_max[..., 0] + jnp.log(row_total[..., 0]))


def attend_backward(pieces):
    queries, key_rows, values, row_ids, log_total, d_context = pieces
    inv_root = 1.0 / math.sqrt(queries.shape[-1])
    scores = masked_scores(queries, key_rows, row_ids)
    attn_probs = jnp.exp(scores - log_total[..., None])
    d_probs = jnp.einsum("qhd,khd->hqk", d_context, values, preferred_element_type=jnp.float32)
    d_values = jnp.einsum(
        "hqk,qhd->khd",
        attn_probs.astype(jnp.bfloat16),
        d_context,
        preferred_element_type=jnp.float32,
    )
    d_scores = (
        attn_probs * (d_probs - jnp.sum(d_probs * attn_probs, axis=-1, keepdims=True))
    ).astype(jnp.bfloat16)
    d_queries = (
        jnp.einsum("hqk,khd->qhd", d_scores, key_rows, preferred_element_type=jnp.float32)
        * inv_root
    )
    d_keys = (
        jnp.einsum("hqk,qhd->khd", d_scores, queries, preferred_element_type=jnp.float32) * inv_root
    )
    row_length = queries.shape[0]
    return jnp.concatenate(
        [
            d_queries.reshape(row_length, -1),
            d_keys.reshape(row_length, -1),
            d_values.reshape(row_length, -1),
        ],
        axis=-1,
    )


def attention_forward(token_rows, seg_ids, param_set):
    w_qkv_full, b_qv_full, w_out_full, b_out_full, gain_one, shift_one = param_set
    model_width = token_rows.shape[1]
    row_count, row_length = seg_ids.shape
    head_count = HEADS
    zero_bias = jnp.zeros((model_width,), jnp.float32)
    bias_full = b_qv_full.astype(jnp.float32)
    qkv_bias = jnp.concatenate([bias_full[:model_width], zero_bias, bias_full[model_width:]])
    qkv_rows = (
        jnp.dot(token_rows, w_qkv_full, preferred_element_type=jnp.float32) + qkv_bias
    ).astype(jnp.bfloat16)
    qkv_split = qkv_rows.reshape(row_count, row_length, 3, head_count, model_width // head_count)
    context, log_total = lax.map(
        attend_forward, (qkv_split[:, :, 0], qkv_split[:, :, 1], qkv_split[:, :, 2], seg_ids)
    )
    context_b = context.reshape(row_count * row_length, model_width).astype(jnp.bfloat16)
    attn_out = jnp.dot(
        context_b, w_out_full, preferred_element_type=jnp.float32
    ) + b_out_full.astype(jnp.float32)
    attn_sum = token_rows.astype(jnp.float32) + attn_out
    hidden = scale_rows(attn_sum) * gain_one.astype(jnp.float32) + shift_one.astype(jnp.float32)
    return (qkv_split, log_total, context_b, attn_sum, hidden)


def ffn_forward(hidden, param_set):
    w_up_full, b_up_full, w_down_full, b_down_full, gain_two, shift_two = param_set
    hidden_b = hidden.astype(jnp.bfloat16)
    up_pre = jnp.dot(hidden_b, w_up_full, preferred_element_type=jnp.float32) + b_up_full.astype(
        jnp.float32
    )
    activated = gelu_exact(up_pre).astype(jnp.bfloat16)
    down_out = jnp.dot(
        activated, w_down_full, preferred_element_type=jnp.float32
    ) + b_down_full.astype(jnp.float32)
    summed = hidden + down_out
    result = scale_rows(summed) * gain_two.astype(jnp.float32) + shift_two.astype(jnp.float32)
    return (hidden_b, up_pre, activated, summed, result)


def norm_backward(values, gain, d_output):
    normed, pull_rows = jax.vjp(scale_rows, values)
    grad_gain = jnp.sum(d_output * normed, axis=0)
    grad_shift = jnp.sum(d_output, axis=0)
    d_values = pull_rows(d_output * gain.astype(jnp.float32))[0]
    return (d_values, grad_gain, grad_shift)


def body(
    tokens,
    seg_ids,
    positive,
    out_grad,
    w_qkv,
    b_qv,
    w_out,
    b_out,
    norm1_gain,
    norm1_shift,
    w_up,
    b_up,
    w_down,
    b_down,
    norm2_gain,
    norm2_shift,
):
    row_count, row_length, model_width = tokens.shape
    token_count = row_count * row_length
    token_rows = tokens.reshape(token_count, model_width)
    full_set = (
        lax.all_gather(w_qkv, "fsdp", axis=0, tiled=True),
        lax.all_gather(b_qv, "fsdp", axis=0, tiled=True),
        lax.all_gather(w_out, "fsdp", axis=0, tiled=True),
        lax.all_gather(b_out, "fsdp", axis=0, tiled=True),
        lax.all_gather(norm1_gain, "fsdp", axis=0, tiled=True),
        lax.all_gather(norm1_shift, "fsdp", axis=0, tiled=True),
        lax.all_gather(w_up, "fsdp", axis=0, tiled=True),
        lax.all_gather(b_up, "fsdp", axis=0, tiled=True),
        lax.all_gather(w_down, "fsdp", axis=0, tiled=True),
        lax.all_gather(b_down, "fsdp", axis=0, tiled=True),
        lax.all_gather(norm2_gain, "fsdp", axis=0, tiled=True),
        lax.all_gather(norm2_shift, "fsdp", axis=0, tiled=True),
    )
    qkv_split, log_total, context_b, attn_sum, hidden = attention_forward(
        token_rows, seg_ids, full_set[:6]
    )
    hidden_b, up_pre, activated, summed, result = ffn_forward(hidden, full_set[6:])
    seg_count = SEGS
    member = (seg_ids[:, None, :] == jnp.arange(seg_count, dtype=jnp.int32)[None, :, None]).astype(
        jnp.float32
    )
    counts = jnp.sum(member, axis=-1, keepdims=True)
    sums = jnp.einsum(
        "rsl,rld->rsd",
        member,
        result.reshape(row_count, row_length, model_width),
        precision=lax.Precision.HIGHEST,
    )
    own_count = row_count * seg_count
    pooled = (sums / counts).reshape(own_count, model_width)
    embedding, pull_embed = jax.vjp(normalize, pooled)
    embedding_b = embedding.astype(jnp.bfloat16)
    everyone = lax.all_gather(embedding_b, ("batch", "fsdp"), axis=0, tiled=True)
    factor = score_scale / model_width
    logits = (
        jnp.einsum("id,jd->ij", embedding_b, everyone, preferred_element_type=jnp.float32) * factor
    )
    own_index = lax.axis_index(("batch", "fsdp")) * own_count + jnp.arange(
        own_count, dtype=jnp.int32
    )
    columns = jnp.arange(everyone.shape[0], dtype=jnp.int32)
    logits = jnp.where(columns[None, :] == own_index[:, None], masked_value, logits)
    row_max = jnp.max(logits, axis=-1, keepdims=True)
    exp_terms = jnp.exp(logits - row_max)
    row_total = jnp.sum(exp_terms, axis=-1, keepdims=True)
    is_positive = columns[None, :] == positive[:, None]
    picked = jnp.sum(jnp.where(is_positive, logits, 0.0), axis=-1)
    pair_total = row_max[:, 0] + jnp.log(row_total[:, 0])
    pair_loss = pair_total - picked
    d_logits = (pair_weight * (exp_terms / row_total - is_positive.astype(jnp.float32))).astype(
        jnp.bfloat16
    )
    d_own = jnp.einsum("ij,jd->id", d_logits, everyone, preferred_element_type=jnp.float32) * factor
    d_terms = (
        jnp.einsum("ij,id->jd", d_logits, embedding_b, preferred_element_type=jnp.float32) * factor
    )
    d_back = lax.psum_scatter(d_terms, ("batch", "fsdp"), scatter_dimension=0, tiled=True)
    d_pooled = pull_embed(d_own + d_back)[0]
    spread_back = jnp.einsum(
        "rsl,rsd->rld",
        member / counts,
        d_pooled.reshape(row_count, seg_count, model_width),
        precision=lax.Precision.HIGHEST,
    )
    d_result = out_grad.reshape(token_count, model_width).astype(jnp.float32) + spread_back.reshape(
        token_count, model_width
    )
    back_set = (
        lax.all_gather(w_qkv, "fsdp", axis=0, tiled=True),
        lax.all_gather(w_out, "fsdp", axis=0, tiled=True),
        lax.all_gather(norm1_gain, "fsdp", axis=0, tiled=True),
        lax.all_gather(w_up, "fsdp", axis=0, tiled=True),
        lax.all_gather(w_down, "fsdp", axis=0, tiled=True),
        lax.all_gather(norm2_gain, "fsdp", axis=0, tiled=True),
    )
    w_qkv_full, w_out_full, gain_one, w_up_full, w_down_full, gain_two = back_set
    d_summed, grad_gain2, grad_shift2 = norm_backward(summed, gain_two, d_result)
    d_down = d_summed.astype(jnp.bfloat16)
    grad_bdown = jnp.sum(d_down, axis=0, dtype=jnp.float32)
    grad_wdown = jnp.einsum("tf,td->fd", activated, d_down, preferred_element_type=jnp.float32)
    d_activated = jnp.einsum("td,fd->tf", d_down, w_down_full, preferred_element_type=jnp.float32)
    _, pull_gelu = jax.vjp(gelu_exact, up_pre)
    d_up = pull_gelu(d_activated)[0].astype(jnp.bfloat16)
    grad_bup = jnp.sum(d_up, axis=0, dtype=jnp.float32)
    grad_wup = jnp.einsum("td,tf->df", hidden_b, d_up, preferred_element_type=jnp.float32)
    d_hidden = d_summed + jnp.einsum(
        "tf,df->td", d_up, w_up_full, preferred_element_type=jnp.float32
    )
    d_attn_sum, grad_gain1, grad_shift1 = norm_backward(attn_sum, gain_one, d_hidden)
    d_attn = d_attn_sum.astype(jnp.bfloat16)
    grad_bout = jnp.sum(d_attn, axis=0, dtype=jnp.float32)
    grad_wout = jnp.einsum("td,te->de", context_b, d_attn, preferred_element_type=jnp.float32)
    d_context = jnp.einsum(
        "te,de->td", d_attn, w_out_full, preferred_element_type=jnp.float32
    ).astype(jnp.bfloat16)
    head_count = HEADS
    d_context_rows = d_context.reshape(row_count, row_length, head_count, model_width // head_count)
    d_qkv = lax.map(
        attend_backward,
        (
            qkv_split[:, :, 0],
            qkv_split[:, :, 1],
            qkv_split[:, :, 2],
            seg_ids,
            log_total,
            d_context_rows,
        ),
    )
    d_qkv_b = d_qkv.reshape(token_count, 3 * model_width).astype(jnp.bfloat16)
    grad_wqkv = jnp.einsum("td,te->de", token_rows, d_qkv_b, preferred_element_type=jnp.float32)
    column_sums = jnp.sum(d_qkv_b, axis=0, dtype=jnp.float32)
    grad_bqv = jnp.concatenate([column_sums[:model_width], column_sums[2 * model_width :]])
    grad_input = d_attn_sum + jnp.einsum(
        "te,de->td", d_qkv_b, w_qkv_full, preferred_element_type=jnp.float32
    )
    shares = (
        lax.psum_scatter(grad_wqkv, "fsdp", scatter_dimension=0, tiled=True),
        lax.psum_scatter(grad_bqv, "fsdp", scatter_dimension=0, tiled=True),
        lax.psum_scatter(grad_wout, "fsdp", scatter_dimension=0, tiled=True),
        lax.psum_scatter(grad_bout, "fsdp", scatter_dimension=0, tiled=True),
        lax.psum_scatter(grad_gain1, "fsdp", scatter_dimension=0, tiled=True),
        lax.psum_scatter(grad_shift1, "fsdp", scatter_dimension=0, tiled=True),
        lax.psum_scatter(grad_wup, "fsdp", scatter_dimension=0, tiled=True),
        lax.psum_scatter(grad_bup, "fsdp", scatter_dimension=0, tiled=True),
        lax.psum_scatter(grad_wdown, "fsdp", scatter_dimension=0, tiled=True),
        lax.psum_scatter(grad_bdown, "fsdp", scatter_dimension=0, tiled=True),
        lax.psum_scatter(grad_gain2, "fsdp", scatter_dimension=0, tiled=True),
        lax.psum_scatter(grad_shift2, "fsdp", scatter_dimension=0, tiled=True),
    )
    totals = lax.psum(
        (
            shares[0],
            shares[1],
            shares[2],
            shares[3],
            shares[4],
            shares[5],
            shares[6],
            shares[7],
            shares[8],
            shares[9],
            shares[10],
            shares[11],
        ),
        "batch",
    )
    result_out = result.reshape(row_count, row_length, model_width).astype(jnp.bfloat16)
    grad_tokens = grad_input.reshape(row_count, row_length, model_width)
    return (
        result_out,
        pair_loss,
        grad_tokens,
        totals[0],
        totals[1],
        totals[2],
        totals[3],
        totals[4],
        totals[5],
        totals[6],
        totals[7],
        totals[8],
        totals[9],
        totals[10],
        totals[11],
    )


def solution(mesh):
    placed = (
        P(("batch", "fsdp"), None, None),
        P(("batch", "fsdp"), None),
        P(("batch", "fsdp")),
        P(("batch", "fsdp"), None, None),
        P("fsdp", None),
        P("fsdp"),
        P("fsdp", None),
        P("fsdp"),
        P("fsdp"),
        P("fsdp"),
        P("fsdp", None),
        P("fsdp"),
        P("fsdp", None),
        P("fsdp"),
        P("fsdp"),
        P("fsdp"),
    )
    return jax.shard_map(
        body,
        mesh=mesh,
        in_specs=placed,
        out_specs=(
            P(("batch", "fsdp"), None, None),
            P(("batch", "fsdp")),
            P(("batch", "fsdp"), None, None),
            P("fsdp", None),
            P("fsdp"),
            P("fsdp", None),
            P("fsdp"),
            P("fsdp"),
            P("fsdp"),
            P("fsdp", None),
            P("fsdp"),
            P("fsdp", None),
            P("fsdp"),
            P("fsdp"),
            P("fsdp"),
        ),
        check_vma=False,
    )
```

profile of v0, /device:TPU:0, one launch (start us, length us, event | category | flops | bytes accessed | tf_op | source)
XLA Modules:
  0.0 874.4 jit_solution(16344255632563367258)
XLA Ops:
  18.6 26.1 %all-reduce.18 = (bf16[1536]{0:T(1024)(128)(2,1)S(1)}, bf16[768]{0:T(1024)(128)(2,1)S(1)}, bf16[768]{0:T(1024)(128)(2,1)S(1)}, bf16[768]{0:T(1024)(128)(2,1)S(1)...) all-reduce(bf16[1536]{0:T(1024)(128)(2,1)S(1)} %dynamic-update-slic, ...), channel_id=1, replica_groups=mesh['batch'=4,'fsdp'=8] {'fsdp'}, use_global_device_ids=true, to_apply=%add | all-reduce | flops 6144 | bytes 24576
  47.1 7.9 all-gather
  57.0 8.4 add_convert_fusion.1
  65.4 6.9 copy.61
  72.3 8.8 %reshape.243 = bf16[2,512,3,12,64]{1,0,4,3,2:T(2,128)(2,1)} reshape(bf16[1024,2304]{0,1:T(8,128)(2,1)} %copy.61) | data formatting | bytes 9437184 | tf_op jit(solution)/shard_map/reshape | solution.py:98
  81.1 5.5 slice_bitcast_fusion
  88.9 21.0 %while.22 = (s32[]{:T(128)}, bf16[2,512,12,64]{1,3,2,0:T(8,128)(2,1)}, f32[2,12,512]{2,1,0:T(8,128)S(1)}, bf16[2,512,12,64]{1,3,2,0:T(8,128)(2,1)}, s32[2,512]{1...) while((s32[]{:T(128)}, ...), condition=%wide.region_3.4_spmd, body=%wide.region_0.3_spmd.sunk | while | flops 843311104 | bytes 42958948 | solution.py:99
  93.7 5.5 bitcast_dynamic-update-slice_fusion.4
  104.1 5.5 bitcast_dynamic-update-slice_fusion.4
  120.2 36.5 %multiply_convert_fusion.1 = (bf16[1024,3072]{1,0:T(8,128)(2,1)}, f32[1024,3072]{1,0:T(8,128)}, f32[1024,3072]{1,0:T(8,128)}) fusion(f32[3072]{0:T(1024)S(1)} %bitcast.194, bf16[768,3072]{1,0:T(8,128)(2,1)} %all-gather.10.cloned.1.call-done, f32[1024,768]{1,0:T(8,128)S(1)} %get-tuple-element.269, f32[768]{0:T(1024)S(1)} %convert_element_type.113, ...), kind=kOutput, calls=%fused_computation.61 | convolution fusion | flops 5043388416 | bytes 39348224 | tf_op jit(solution)/shard_map/dot_general | solution.py:114
  156.7 9.8 %fusion.75 = (f32[1024]{0:T(1024)S(1)}, f32[1024,768]{1,0:T(8,128)S(1)}) fusion(f32[768]{0:T(1024)S(1)} %copy-done.57, bf16[1024,3072]{1,0:T(8,128)(2,1)} %get-tuple-element.253, bf16[3072,768]{1,0:T(8,128)(2,1)} %all-gather.12.cloned.1.call-done, f32[768]{0:T(1024)S(1)} %convert_element_type.113, f32[768]{0:T(1024)S(1)} %convert_element_type.112, ...), kind=kOutput, calls=%fused_computation.157 | convolution fusion | flops 4837342208 | bytes 17323008 | tf_op jit(solution)/shard_map/dot_general | solution.py:118
  169.3 42.9 %all_gather.57 = bf16[512,768]{1,0:T(8,128)(2,1)S(1)} all-gather(bf16[16,768]{1,0:T(8,128)(2,1)S(1)} %fusion.53), channel_id=1, replica_groups=mesh['batch'=4,'fsdp'=8] {'batch','fsdp'}, dimensions={0}, use_global_device_ids=true | all-gather | bytes 811008 | tf_op jit(solution)/shard_map/all_gather | solution.py:188
  216.0 93.3 %reduce-scatter.8.cloned.1.call-done = f32[16,768]{1,0:T(8,128)} async-done(((f32[512,768]{1,0:T(8,128)}), f32[16,768]{1,0:T(8,128)}) %reduce-scatter.8.cloned.1.call-update) | async-done | bytes 49168 | tf_op jit(solution)/shard_map/reduce_scatter | solution.py:212
  321.4 18.9 %convert_reduce_fusion = (f32[3072]{0:T(1024)}, bf16[1024,3072]{1,0:T(8,128)(2,1)}) fusion(f32[1024,3072]{1,0:T(8,128)} %get-tuple-element.254, bf16[1024,768]{1,0:T(8,128)(2,1)} %get-tuple-element.246, bf16[3072,768]{1,0:T(8,128)(2,1)} %all-gather.12.cloned.1.call-done, f32[1024,3072]{1,0:T(8,128)} %get-tuple-element.270, f32[3072]{0:T(1024)S(1)} %bitcast.195), kind=kOutput, calls=%fused_computation.59 | convolution fusion | flops 4885312512 | bytes 37773312 | tf_op jit(solution)/shard_map/td,fd->tf/dot_general | solution.py:236
  340.3 10.2 %multiply_reduce_fusion.1 = (f32[768]{0:T(1024)}, f32[1024]{0:T(1024)S(1)}, f32[768]{0:T(1024)}, f32[1024,768]{1,0:T(8,128)S(1)}) fusion(f32[1024,768]{1,0:T(8,128)S(1)} %copy-done.9, f32[1024]{0:T(1024)S(1)} %fusion.62, f32[1024]{0:T(1024)S(1)} %broadcast_multiply_fusion.1, f32[768]{0:T(1024)S(1)} %convert_element_type.112, ...), kind=kOutput, calls=%fused_computation.84 | convolution fusion | flops 4839699456 | bytes 20472832 | tf_op jit(solution)/shard_map/tf,df->td/dot_general | solution.py:241
  365.8 58.4 %while.23 = (s32[]{:T(128)}, bf16[2,512,2304]{2,1,0:T(8,128)(2,1)}, bf16[2,512,12,64]{1,3,2,0:T(8,128)(2,1)S(1)}, s32[2,512]{1,0:T(2,128)S(1)}, bf16[2,512,12,64...) while((s32[]{:T(128)}, bf16[2,512,2304]{2,1,0:T(8,128)(2,1)}, ...), condition=%wide.region_21.22_spmd, body=%wide.region_19.21_spmd.sunk | while | flops 2069358592 | bytes 145948944 | solution.py:253
  372.0 6.7 multiply_reduce_fusion.8
  378.7 7.0 multiply_convert_fusion.6
  401.0 6.7 multiply_reduce_fusion.8
  407.7 7.0 multiply_convert_fusion.6
  424.2 9.6 %convolution_bitcast_fusion = f32[768,2304]{0,1:T(8,128)} fusion(bf16[2,512,2304]{2,1,0:T(8,128)(2,1)} %get-tuple-element.480, bf16[2,512,768]{2,1,0:T(8,128)(2,1)} %param.20), kind=kOutput, calls=%fused_computation.77 | convolution fusion | flops 3623878656 | bytes 13369344 | tf_op jit(solution)/shard_map/td,te->de/dot_general | solution.py:265
  433.8 8.0 copy.79
  446.9 11.3 %fusion.64 = f32[768,3072]{1,0:T(8,128)} fusion(bf16[1024,3072]{1,0:T(8,128)(2,1)} %get-tuple-element.281, f32[1024,768]{1,0:T(8,128)S(1)} %copy-done.10, f32[768]{0:T(1024)S(1)} %copy-done.39, f32[768]{0:T(1024)S(1)} %copy-done.33, f32[1024]{0:T(1024)S(1)} %copy-done.28, f32[1024]{0:T(1024)S(1)} %copy-done.26), kind=kOutput, calls=%fused_computation.149 | convolution fusion | flops 4835770368 | bytes 18888704 | tf_op jit(solution)/shard_map/td,tf->df/dot_general | solution.py:240
  459.6 10.3 %fusion.79 = f32[3072,768]{1,0:T(8,128)} fusion(bf16[1024,3072]{1,0:T(8,128)(2,1)} %get-tuple-element.253, bf16[1024,768]{1,0:T(8,128)(2,1)S(1)} %copy-done.19), kind=kOutput, calls=%fused_computation.162 | convolution fusion | flops 4831838208 | bytes 17301504 | tf_op jit(solution)/shard_map/tf,td->fd/dot_general | solution.py:235
  470.1 36.4 %reduce-scatter.16.cloned.1.call-done = f32[96,2304]{1,0:T(8,128)} async-done(((f32[768,2304]{1,0:T(8,128)}), f32[96,2304]{1,0:T(8,128)}) %reduce-scatter.16.cloned.1.call-update) | async-done | bytes 884752
  509.0 43.7 %reduce-scatter.10.cloned.1.call-done = f32[96,768]{1,0:T(8,128)} async-done(((f32[768,768]{1,0:T(8,128)}), f32[96,768]{1,0:T(8,128)}) %reduce-scatter.10.cloned.1.call-update) | async-done | bytes 294928 | tf_op jit(solution)/shard_map/reduce_scatter | solution.py:274
  552.7 80.0 %reduce-scatter.12.cloned.1.call-done = f32[96,3072]{1,0:T(8,128)} async-done(((f32[768,3072]{1,0:T(8,128)}), f32[96,3072]{1,0:T(8,128)}) %reduce-scatter.12.cloned.1.call-update) | async-done | bytes 1179664 | tf_op jit(solution)/shard_map/reduce_scatter | solution.py:278
  632.7 80.0 %reduce-scatter.14.cloned.1.call-done = f32[384,768]{1,0:T(8,128)} async-done(((f32[3072,768]{1,0:T(8,128)}), f32[384,768]{1,0:T(8,128)}) %reduce-scatter.14.cloned.1.call-update) | async-done | bytes 1179664 | tf_op jit(solution)/shard_map/reduce_scatter | solution.py:280
  720.5 25.5 %all-reduce.15 = (f32[1536]{0:T(1024)S(1)}, f32[768]{0:T(1024)S(1)}, f32[768]{0:T(1024)S(1)}, f32[768]{0:T(1024)S(1)}, f32[3072]{0:T(1024)S(1)}, /*index=5*/f32[...) all-reduce(f32[1536]{0:T(1024)S(1)} %pad_maximum_fusion.1, ...), channel_id=4, replica_groups=mesh['batch'=4,'fsdp'=8] {'fsdp'}, use_global_device_ids=true, to_apply=%region_25.26.clone | all-reduce | flops 9216 | bytes 73728
  746.6 13.6 %all-reduce.16 = (f32[192]{0:T(256)}, f32[96]{0:T(128)}, f32[96]{0:T(128)}, f32[96]{0:T(128)}, f32[384]{0:T(512)}, /*index=5*/f32[96]{0:T(128)}, f32[96]{0:T(128)}, f32[96]{0:T(128)}) all-reduce(f32[192]{0:T(256)S(1)} %dynamic-slice.8, f32[96]{0:T(128)S(1)} %dynamic-slice.10, ...), channel_id=1, replica_groups=mesh['batch'=4,'fsdp'=8] {'batch'}, use_global_device_ids=true, to_apply=%region_26.27 | all-reduce | flops 1152 | bytes 9216 | tf_op jit(solution)/shard_map/psum | solution.py:285
  760.2 8.9 %add_add_fusion.4 = f32[1024,768]{1,0:T(8,128)} fusion(f32[1024,768]{1,0:T(8,128)S(1)} %copy-done.15, bf16[1024,2304]{1,0:T(8,128)(2,1)} %bitcast.189, bf16[768,2304]{1,0:T(8,128)(2,1)} %all-gather.6.cloned.1.call-done, f32[1024]{0:T(1024)S(1)} %copy-done.45), kind=kOutput, calls=%fused_computation.95 | convolution fusion | flops 3625451520 | bytes 14553088 | tf_op jit(solution)/shard_map/te,de->td/dot_general | solution.py:268
  769.1 91.5 %all-reduce.21.cloned.1.call-done = (f32[96,2304]{0,1:T(8,128)}, f32[96,768]{1,0:T(8,128)}, f32[96,3072]{1,0:T(8,128)}, f32[384,768]{1,0:T(8,128)}) async-done(((f32[96,2304]{0,1:T(8,128)}, f32[96,768]{1,0:T(8,128)}, f32[96,3072]{1,0:T(8,128)}, f32[384,768]{1,0:T(8,128)}), (f32[96,2304]{0,1:T(8,128)}, f32[96,768]{1,0:T(8,128)}, f32[96,3072]{1,0:T(8,128)}, ...) | async-done | bytes 3538960 | tf_op jit(solution)/shard_map/psum | solution.py:285
  (277 shorter events, 122.3 us)
Async XLA Ops:
  7.2 49.8 %all-gather.6.cloned.1.call-start = ((), (), s32[]{:S(2)}) async-start(), calls=%async_computation.5 | async-start | bytes 3981312 | tf_op jit(solution)/shard_map/all_gather | solution.py:156
  7.9 107.8 %all-gather.8.cloned.1.call-start = ((), (), s32[]{:S(2)}) async-start(), calls=%async_computation.6 | async-start | bytes 1327104 | tf_op jit(solution)/shard_map/all_gather | solution.py:158
  8.7 111.5 %all-gather.10.cloned.1.call-start = ((), (), s32[]{:S(2)}) async-start(), calls=%async_computation.7 | async-start | bytes 5308416 | tf_op jit(solution)/shard_map/all_gather | solution.py:162
  9.4 147.3 %all-gather.12.cloned.1.call-start = ((), (), s32[]{:S(2)}) async-start(), calls=%async_computation.8 | async-start | bytes 5308416 | tf_op jit(solution)/shard_map/all_gather | solution.py:164
  10.0 299.3 %reduce-scatter.8.cloned.1.call-start = ((), (), s32[]{:S(2)}) async-start(), calls=%async_computation.9 | async-start | bytes 1622016 | tf_op jit(solution)/shard_map/reduce_scatter | solution.py:212
  55.1 101.6 %copy-start.38 = (f32[768]{0:T(1024)}, f32[768]{0:T(1024)S(1)}, u32[]{:S(2)}) copy-start(f32[768]{0:T(1024)S(1)} %convert_element_type.113) | copy-start | bytes 9220
  55.1 295.4 %copy-start.32 = (f32[768]{0:T(1024)}, f32[768]{0:T(1024)S(1)}, u32[]{:S(2)}) copy-start(f32[768]{0:T(1024)S(1)} %convert_element_type.112) | copy-start | bytes 9220
  119.6 37.1 %copy-start.8 = (f32[1024,768]{1,0:T(8,128)}, f32[1024,768]{1,0:T(8,128)S(1)}, u32[]{:S(2)}) copy-start(f32[1024,768]{1,0:T(8,128)S(1)} %get-tuple-element.269) | copy-start | bytes 9437188
  119.6 230.9 %copy-start.25 = (f32[1024]{0:T(1024)}, f32[1024]{0:T(1024)S(1)}, u32[]{:S(2)}) copy-start(f32[1024]{0:T(1024)S(1)} %broadcast_multiply_fusion.1) | copy-start | bytes 12292
  120.1 36.6 %copy-start.42 = (f32[1024]{0:T(1024)}, f32[1024]{0:T(1024)S(1)}, u32[]{:S(2)}) copy-start(f32[1024]{0:T(1024)S(1)} %multiply_reduce_fusion.5) | copy-start | bytes 12292
  120.1 230.4 %copy-start.27 = (f32[1024]{0:T(1024)}, f32[1024]{0:T(1024)S(1)}, u32[]{:S(2)}) copy-start(f32[1024]{0:T(1024)S(1)} %fusion.62) | copy-start | bytes 12292
  120.1 36.5 %copy-start.57 = (f32[768]{0:T(1024)S(1)}, f32[768]{0:T(1024)}, u32[]{:S(2)}) copy-start(f32[768]{0:T(1024)} %convert_element_type.117) | copy-start | bytes 9220
  166.5 150.8 %copy-start.6 = (f32[1024,768]{1,0:T(8,128)}, f32[1024,768]{1,0:T(8,128)S(1)}, u32[]{:S(2)}) copy-start(f32[1024,768]{1,0:T(8,128)S(1)} %get-tuple-element.272) | copy-start | bytes 9437188
  166.5 150.8 %copy-start.30 = (f32[1024]{0:T(1024)}, f32[1024]{0:T(1024)S(1)}, u32[]{:S(2)}) copy-start(f32[1024]{0:T(1024)S(1)} %broadcast_multiply_fusion) | copy-start | bytes 12292
  167.2 150.1 %copy-start.36 = (f32[1024]{0:T(1024)}, f32[1024]{0:T(1024)S(1)}, u32[]{:S(2)}) copy-start(f32[1024]{0:T(1024)S(1)} %fusion.63) | copy-start | bytes 12292
  167.8 45.4 %copy-start.61 = (s32[16]{0:T(128)S(1)}, s32[16]{0:T(128)}, u32[]{:S(2)}) copy-start(s32[16]{0:T(128)} %iota_add_fusion) | copy-start | bytes 196
  167.8 45.8 %copy-start.56 = (s32[16]{0:T(128)S(1)}, s32[16]{0:T(128)}, u32[]{:S(2)}) copy-start(s32[16]{0:T(128)} %param.22) | copy-start | bytes 196
  213.6 102.1 %copy-start.50 = (f32[16]{0:T(128)}, f32[16]{0:T(128)S(1)}, u32[]{:S(2)}) copy-start(f32[16]{0:T(128)S(1)} %get-tuple-element.275) | copy-start | bytes 196
  214.3 101.4 %copy-start.54 = (f32[16]{0:T(128)}, f32[16]{0:T(128)S(1)}, u32[]{:S(2)}) copy-start(f32[16]{0:T(128)S(1)} %get-tuple-element.186) | copy-start | bytes 196
  215.9 290.5 %reduce-scatter.16.cloned.1.call-start = ((), (), s32[]{:S(2)}) async-start(), calls=%async_computation.13 | async-start | bytes 7962624
  321.4 18.9 %copy-start.17 = (f32[1024,768]{1,0:T(8,128)S(1)}, f32[1024,768]{1,0:T(8,128)}, u32[]{:S(2)}) copy-start(f32[1024,768]{1,0:T(8,128)} %copy-done.16) | copy-start | bytes 9437188
  441.8 110.9 %reduce-scatter.10.cloned.1.call-start = ((), (), s32[]{:S(2)}) async-start(), calls=%async_computation.10 | async-start | bytes 2654208 | tf_op jit(solution)/shard_map/reduce_scatter | solution.py:274
  446.8 185.9 %reduce-scatter.12.cloned.1.call-start = ((), (), s32[]{:S(2)}) async-start(), calls=%async_computation.11 | async-start | bytes 10616832 | tf_op jit(solution)/shard_map/reduce_scatter | solution.py:278
  458.2 254.5 %reduce-scatter.14.cloned.1.call-start = ((), (), s32[]{:S(2)}) async-start(), calls=%async_computation.12 | async-start | bytes 10616832 | tf_op jit(solution)/shard_map/reduce_scatter | solution.py:280
  470.0 244.8 %copy-start.7 = (f32[1024,768]{1,0:T(8,128)S(1)}, f32[1024,768]{1,0:T(8,128)}, u32[]{:S(2)}) copy-start(f32[1024,768]{1,0:T(8,128)} %copy-done.6) | copy-start | bytes 9437188
  470.0 244.8 %copy-start.31 = (f32[1024]{0:T(1024)S(1)}, f32[1024]{0:T(1024)}, u32[]{:S(2)}) copy-start(f32[1024]{0:T(1024)} %copy-done.30) | copy-start | bytes 12292
  470.0 244.8 %copy-start.35 = (f32[768]{0:T(1024)S(1)}, f32[768]{0:T(1024)}, u32[]{:S(2)}) copy-start(f32[768]{0:T(1024)} %convert_element_type.118) | copy-start | bytes 9220
  470.0 244.8 %copy-start.37 = (f32[1024]{0:T(1024)S(1)}, f32[1024]{0:T(1024)}, u32[]{:S(2)}) copy-start(f32[1024]{0:T(1024)} %copy-done.36) | copy-start | bytes 12292
  470.0 244.8 %copy-start.41 = (f32[768]{0:T(1024)S(1)}, f32[768]{0:T(1024)}, u32[]{:S(2)}) copy-start(f32[768]{0:T(1024)} %convert_element_type.119) | copy-start | bytes 9220
  470.0 390.6 %all-reduce.21.cloned.1.call-start = ((), (), s32[]{:S(2)}) async-start(), calls=%async_computation.14 | async-start | bytes 7667712 | tf_op jit(solution)/shard_map/psum | solution.py:285
  716.5 43.7 %copy-start.15 = (f32[1024,768]{1,0:T(8,128)S(1)}, f32[1024,768]{1,0:T(8,128)}, u32[]{:S(2)}) copy-start(f32[1024,768]{1,0:T(8,128)} %copy-done.14) | copy-start | bytes 9437188
  716.5 43.7 %copy-start.45 = (f32[1024]{0:T(1024)S(1)}, f32[1024]{0:T(1024)}, u32[]{:S(2)}) copy-start(f32[1024]{0:T(1024)} %copy-done.44) | copy-start | bytes 12292
  (46 other events, 185.7 us)
Sparse Core Ops, SparseCore 0:
  9.9 36.8 all-gather.5
  48.7 24.0 all-gather.7
  74.7 38.9 all-gather.9
  115.3 38.9 all-gather.11
  216.1 93.1 reduce-scatter.7
  441.9 64.5 reduce-scatter.15
  510.2 42.4 reduce-scatter.9
  556.2 76.4 reduce-scatter.11
  636.2 76.4 reduce-scatter.13
  715.8 144.8 all-reduce.20
where the time goes:
time: 880 us; the launch traced here: 874 us
  waiting for transfers between devices  428 us (49%)
  matrix products  190 us (22%)
  blocking collectives  116 us (13%)
  local copies, waits for them, and re-layouts  80.7 us (9%)
  other arithmetic  39.9 us (5%)
  between operations  18.8 us (2%)
    reduce_scatter x1, waiting for transfers between devices, body(): lax.psum_scatter(d_terms, ('batch', 'fsdp'), scatter_dimension=0, tiled=T...  93.3 us
    psum x1, waiting for transfers between devices, body(): lax.psum((shares[0], shares[1], shares[2], shares[3], shares[4], shares[5...  91.5 us
    reduce_scatter x1, waiting for transfers between devices, body(): lax.psum_scatter(grad_wdown, 'fsdp', scatter_dimension=0, tiled=True)  80 us
    reduce_scatter x1, waiting for transfers between devices, body(): lax.psum_scatter(grad_wup, 'fsdp', scatter_dimension=0, tiled=True)  80 us
    unnamed x2, blocking collectives  51.5 us
    reduce_scatter x1, waiting for transfers between devices, body(): lax.psum_scatter(grad_wout, 'fsdp', scatter_dimension=0, tiled=True)  43.7 us
    all_gather x1, blocking collectives, body(): lax.all_gather(embedding_b, ('batch', 'fsdp'), axis=0, tiled=True)  42.9 us
    unnamed x11, waiting for transfers between devices  39.1 us
  transfers between devices with their start and end apart: 10, of which 6 were waited for; matrix products, arithmetic and copies ran while one was open for 18% of the time, Pallas kernels for 0%

commit v1 on v0

v1 whole, which is shorter than its diff:
```python
import functools
import math

import jax
import jax.numpy as jnp
from jax import lax
from jax.experimental import pallas as pl
from jax.experimental.pallas import tpu as pltpu
from jax.sharding import PartitionSpec as P

HEADS = 12
SEGS = 8

norm_eps = 1e-06
pool_eps = 1e-06
score_scale = 50.0
pair_weight = 256.0
masked_value = -1000000000.0

BLOCKS = 8
TILE = 128
TAIL = 128
BASE = 64

bf16 = jnp.bfloat16
f32 = jnp.float32
ANY = pl.BlockSpec(memory_space=pl.ANY)
VMEM_BYTES = 56 * 1024 * 1024


def dot(left, right):
    return jnp.dot(left, right, preferred_element_type=f32)


def dot_nt(left, right):
    return lax.dot_general(left, right, (((1,), (1,)), ((), ())), preferred_element_type=f32)


def whole(shape):
    return pl.BlockSpec(shape, lambda *_: (0,) * len(shape))


def call(kernel, grid, in_specs, out_specs, out_shape, scratch, flops, moved, special=0):
    return pl.pallas_call(
        kernel,
        out_shape=out_shape,
        grid_spec=pltpu.PrefetchScalarGridSpec(
            num_scalar_prefetch=1,
            grid=grid,
            in_specs=in_specs,
            out_specs=out_specs,
            scratch_shapes=scratch,
        ),
        compiler_params=pltpu.CompilerParams(vmem_limit_bytes=VMEM_BYTES),
        cost_estimate=pl.CostEstimate(
            flops=int(flops), bytes_accessed=int(moved), transcendentals=int(special)
        ),
    )


def shaped(shape, dtype):
    return jax.ShapeDtypeStruct(shape, dtype)


def swap(value, axis, size, bit):
    return lax.ppermute(value, axis, [(i, i ^ bit) for i in range(size)])


def fsdp_swap(value, bit):
    return swap(value, "fsdp", BLOCKS, bit)


def gather_first(shard):
    return fsdp_swap(shard, 2), fsdp_swap(shard, 4)


def gather_second(shard, over_x, over_y):
    rows = shard.shape[0]
    half = rows // 2
    far_top = fsdp_swap(over_y[:half], 2)
    far_low = fsdp_swap(over_x[half:], 4)
    mine = [
        (shard, 0, 0),
        (over_x, 2, 0),
        (over_y, 4, 0),
        (far_top, 6, 0),
        (far_low, 6, half),
    ]
    theirs = [(fsdp_swap(value, 1), place ^ 1, off) for value, place, off in mine]
    return mine + theirs


def gather_whole(shard):
    full = lax.all_gather(shard, "fsdp", axis=0, tiled=True)
    rows = full.shape[0] // BLOCKS
    return [(full[i * rows : (i + 1) * rows], i, 0) for i in range(BLOCKS)]


def meta_of(pieces):
    return tuple((place, off, value.shape[0]) for value, place, off in pieces)


def arrays_of(pieces):
    return [value for value, _, _ in pieces]


def load(meta, rows, refs, target, sems, index):
    copies = []
    for number, ((place, off, count), ref) in enumerate(zip(meta, refs)):
        start = pl.multiple_of((index ^ place) * rows + off, 16)
        copies.append(pltpu.make_async_copy(ref, target.at[pl.ds(start, count)], sems.at[number]))
    for copy in copies:
        copy.start()
    return copies


def fill_mask(seg_row, mask_ref):
    length = seg_row.shape[1]
    keys = jnp.broadcast_to(seg_row, (TILE, length)).T
    for lo, hi, at in bands(length):
        same = keys[lo:hi] == seg_row[:, at : at + TILE]
        mask_ref[lo:hi, at : at + TILE] = jnp.where(same, 0.0, masked_value)


def bands(length):
    out = []
    for at in range(0, length, TILE):
        out.append((max(at - TILE, 0), min(at + 2 * TILE, length), at))
    return out


def two_heads(pair):
    lane = lax.broadcasted_iota(jnp.int32, (1, pair.shape[1]), 1)
    first = (lane < pair.shape[1] // 2).astype(f32).astype(bf16)
    return jnp.concatenate([pair * first, pair * (1.0 - first)], axis=0)


def twice(value):
    return jnp.concatenate([value, value], axis=1)


def attend_kernel(meta, index_ref, tok_ref, bias_ref, seg_ref, *rest):
    pieces, rest = rest[: len(meta)], rest[len(meta) :]
    qkv_ref, ctx_ref, lse_ref, w_ref, vt_ref, ct_ref, mask_ref, sems = rest
    width = tok_ref.shape[1]
    length = tok_ref.shape[0]
    pairs = HEADS // 2
    lanes = width // pairs
    half = lanes // 2

    @pl.when(pl.program_id(0) == 0)
    def _():
        for copy in load(meta, width // BLOCKS, pieces, w_ref, sems, index_ref[0]):
            copy.wait()

    fill_mask(seg_ref[0].astype(f32), mask_ref)
    inv_root = 1.0 / math.sqrt(half)
    for part in range(3):
        cols = slice(part * width, (part + 1) * width)
        value = dot(tok_ref[...], w_ref[:, cols]) + bias_ref[:, cols]
        if part == 0:
            value = value * inv_root
        qkv_ref[:, cols] = value.astype(bf16)
    vt_ref[...] = qkv_ref[:, 2 * width :].T

    def one_pair(pair, carry):
        at_q = pl.multiple_of(pair * lanes, lanes)
        at_k = pl.multiple_of(width + pair * lanes, lanes)
        for lo, hi, at in bands(length):
            queries = two_heads(qkv_ref[at : at + TILE, pl.ds(at_q, lanes)])
            scores = dot_nt(qkv_ref[lo:hi, pl.ds(at_k, lanes)], queries)
            scores = scores + twice(mask_ref[lo:hi, at : at + TILE])
            top = jnp.max(scores, axis=0, keepdims=True)
            terms = jnp.exp(scores - top)
            total = jnp.sum(terms, axis=0, keepdims=True)
            probs = (terms * (1.0 / total)).astype(bf16)
            context = dot(vt_ref[pl.ds(at_q, lanes), lo:hi], probs)
            lse = top + jnp.log(total)
            for head in range(2):
                rows = pl.ds(pl.multiple_of(at_q + head * half, half), half)
                part = context[head * half : (head + 1) * half, head * TILE : (head + 1) * TILE]
                ct_ref[rows, at : at + TILE] = part.astype(bf16)
                lse_ref[0, pair, head : head + 1, at : at + TILE] = lse[
                    :, head * TILE : (head + 1) * TILE
                ]
        return carry

    lax.fori_loop(0, pairs, one_pair, 0)
    ctx_ref[...] = ct_ref[...].T


def attend(index, tokens, bias, seg_rows, pieces):
    count, width = tokens.shape
    rows, _, length = seg_rows.shape
    pairs = HEADS // 2
    meta = meta_of(pieces)
    return call(
        functools.partial(attend_kernel, meta),
        (rows,),
        [
            pl.BlockSpec((length, width), lambda i, s: (i, 0)),
            whole((1, 3 * width)),
            pl.BlockSpec((1, 1, length), lambda i, s: (i, 0, 0)),
        ]
        + [ANY] * len(meta),
        [
            pl.BlockSpec((length, 3 * width), lambda i, s: (i, 0)),
            pl.BlockSpec((length, width), lambda i, s: (i, 0)),
            pl.BlockSpec((1, pairs, 2, length), lambda i, s: (i, 0, 0, 0)),
        ],
        [
            shaped((count, 3 * width), bf16),
            shaped((count, width), bf16),
            shaped((rows, pairs, 2, length), f32),
        ],
        [
            pltpu.VMEM((width, 3 * width), bf16),
            pltpu.VMEM((width, length), bf16),
            pltpu.VMEM((width, length), bf16),
            pltpu.VMEM((length, length), f32),
            pltpu.SemaphoreType.DMA((len(meta),)),
        ],
        count * width * width * 6 + count * length * width * 4,
        count * width * 10 + width * width * 6,
        count * length * HEADS * 5 // 8,
    )(index, tokens, bias, seg_rows, *arrays_of(pieces))


def row_stats(values):
    mean = jnp.mean(values, axis=-1, keepdims=True)
    centred = values - mean
    spread = jnp.mean(centred * centred, axis=-1, keepdims=True)
    return centred, lax.rsqrt(spread + norm_eps)


def project_kernel(meta, index_ref, ctx_ref, tok_ref, vec_ref, *rest):
    pieces, rest = rest[: len(meta)], rest[len(meta) :]
    norm_ref, root_ref, hid_ref, w_ref, sems = rest

    @pl.when(pl.program_id(0) == 0)
    def _():
        rows = w_ref.shape[0] // BLOCKS
        for copy in load(meta, rows, pieces, w_ref, sems, index_ref[0]):
            copy.wait()

    summed = tok_ref[...].astype(f32) + (dot(ctx_ref[...], w_ref[...]) + vec_ref[0:1])
    centred, root = row_stats(summed)
    normed = centred * root
    norm_ref[...] = normed
    root_ref[...] = root
    hid_ref[...] = (normed * vec_ref[1:2] + vec_ref[2:3]).astype(bf16)


def project(index, context, tokens, vectors, pieces, step=256):
    count, width = tokens.shape
    meta = meta_of(pieces)
    rows = pl.BlockSpec((step, width), lambda i, s: (i, 0))
    return call(
        functools.partial(project_kernel, meta),
        (count // step,),
        [rows, rows, whole(vectors.shape)] + [ANY] * len(meta),
        [rows, pl.BlockSpec((step, 1), lambda i, s: (i, 0)), rows],
        [shaped((count, width), f32), shaped((count, 1), f32), shaped((count, width), bf16)],
        [pltpu.VMEM((width, width), bf16), pltpu.SemaphoreType.DMA((len(meta),))],
        count * width * width * 2,
        count * width * 10 + width * width * 2,
    )(index, context, tokens, vectors, *arrays_of(pieces))


def up_kernel(meta, index_ref, hid_ref, bias_ref, *rest):
    pieces, rest = rest[: len(meta)], rest[len(meta) :]
    act_ref, slope_ref, w_ref, sems = rest
    step = act_ref.shape[1]
    col = pl.program_id(1)

    @pl.when((pl.program_id(0) == 0) & (col == 0))
    def _():
        rows = w_ref.shape[0] // BLOCKS
        for copy in load(meta, rows, pieces, w_ref, sems, index_ref[0]):
            copy.wait()

    cols = pl.ds(pl.multiple_of(col * step, step), step)
    value = dot(hid_ref[...], w_ref[:, cols]) + bias_ref[...]
    share = 0.5 * (1.0 + lax.erf(value * math.sqrt(0.5)))
    density = jnp.exp(value * value * -0.5) * (1.0 / math.sqrt(2.0 * math.pi))
    act_ref[...] = (value * share).astype(bf16)
    slope_ref[...] = (share + value * density).astype(bf16)


def up(index, hidden, bias, pieces, step=256, tile=768):
    count, width = hidden.shape
    inner = bias.shape[1]
    meta = meta_of(pieces)
    out = pl.BlockSpec((step, tile), lambda i, j, s: (i, j))
    return call(
        functools.partial(up_kernel, meta),
        (count // step, inner // tile),
        [
            pl.BlockSpec((step, width), lambda i, j, s: (i, 0)),
            pl.BlockSpec((1, tile), lambda i, j, s: (0, j)),
        ]
        + [ANY] * len(meta),
        [out, out],
        [shaped((count, inner), bf16), shaped((count, inner), bf16)],
        [pltpu.VMEM((width, inner), bf16), pltpu.SemaphoreType.DMA((len(meta),))],
        count * width * inner * 2,
        count * (width * 2 + inner * 4) + width * inner * 2,
        count * inner * 4,
    )(index, hidden, bias, *arrays_of(pieces))


def down_kernel(meta, index_ref, act_ref, norm_ref, vec_ref, seg_ref, pos_ref, *rest):
    pieces, rest = rest[: len(meta)], rest[len(meta) :]
    res_ref, norm2_ref, root_ref, pay_ref, pool_ref, stat_ref, w_ref, sum_ref, num_ref, sems = rest
    step = pl.program_id(0)
    steps = pl.num_programs(0)
    width = res_ref.shape[1]

    @pl.when(step == 0)
    def _():
        sum_ref[...] = jnp.zeros_like(sum_ref)
        num_ref[...] = jnp.zeros_like(num_ref)
        rows = w_ref.shape[0] // BLOCKS
        for copy in load(meta, rows, pieces, w_ref, sems, index_ref[0]):
            copy.wait()

    hidden = norm_ref[...] * vec_ref[1:2] + vec_ref[2:3]
    summed = hidden + (dot(act_ref[...], w_ref[...]) + vec_ref[3:4])
    centred, root = row_stats(summed)
    normed = centred * root
    result = normed * vec_ref[4:5] + vec_ref[5:6]
    norm2_ref[...] = normed
    root_ref[...] = root
    high = result.astype(bf16)
    res_ref[...] = high
    low = (result - high.astype(f32)).astype(bf16)
    seg = seg_ref[0]
    wanted = lax.broadcasted_iota(jnp.int32, (SEGS, seg.shape[1]), 0)
    member = (wanted == seg).astype(f32)
    member_b = member.astype(bf16)
    own = pl.ds(pl.multiple_of(step // (steps * SEGS // sum_ref.shape[0]) * SEGS, SEGS), SEGS)
    sum_ref[own] += dot(member_b, high) + dot(member_b, low)
    num_ref[own] += jnp.broadcast_to(jnp.sum(member, axis=1, keepdims=True), (SEGS, TAIL))

    @pl.when(step == steps - 1)
    def _():
        counts = num_ref[:, 0:1]
        pooled = sum_ref[...] / counts
        scale = lax.rsqrt(jnp.mean(pooled * pooled, axis=-1, keepdims=True) + pool_eps)
        pool_ref[...] = pooled
        lane = lax.broadcasted_iota(jnp.int32, (pooled.shape[0], TAIL), 1)
        stat_ref[...] = jnp.where(lane == 0, scale, counts)
        pay_ref[:, :width] = (pooled * scale).astype(bf16)
        partner = pos_ref[...]
        digit = jnp.where(lane == 0, partner // BASE, partner % BASE)
        pay_ref[:, width:] = jnp.where(lane < 2, digit, 0).astype(f32).astype(bf16)


def down(index, activated, normed, vectors, seg_rows, positive, pieces, step=256):
    count, width = normed.shape
    inner = activated.shape[1]
    rows, _, length = seg_rows.shape
    own = rows * SEGS
    per_row = length // step
    meta = meta_of(pieces)
    block = pl.BlockSpec((step, width), lambda i, s: (i, 0))
    return call(
        functools.partial(down_kernel, meta),
        (count // step,),
        [
            pl.BlockSpec((step, inner), lambda i, s: (i, 0)),
            block,
            whole(vectors.shape),
            pl.BlockSpec((1, 1, step), lambda i, s: (i // per_row, 0, i % per_row)),
            whole((own, 1)),
        ]
        + [ANY] * len(meta),
        [
            block,
            block,
            pl.BlockSpec((step, 1), lambda i, s: (i, 0)),
            whole((own, width + TAIL)),
            whole((own, width)),
            whole((own, TAIL)),
        ],
        [
            shaped((count, width), bf16),
            shaped((count, width), f32),
            shaped((count, 1), f32),
            shaped((own, width + TAIL), bf16),
            shaped((own, width), f32),
            shaped((own, TAIL), f32),
        ],
        [
            pltpu.VMEM((inner, width), bf16),
            pltpu.VMEM((own, width), f32),
            pltpu.VMEM((own, TAIL), f32),
            pltpu.SemaphoreType.DMA((len(meta),)),
        ],
        count * width * inner * 2,
        count * (width * 10 + inner * 2) + width * inner * 2,
    )(index, activated, normed, vectors, seg_rows, positive, *arrays_of(pieces))


def contrast_kernel(place_ref, all_ref, own_ref, pos_ref, pool_ref, stat_ref, loss_ref, grad_ref):
    total = all_ref.shape[0]
    own, width = pool_ref.shape
    factor = score_scale / width
    block = min(total, 512)
    flip, first = place_ref[0], place_ref[1]
    mine = own_ref[:, :width]
    mine_id = lax.broadcasted_iota(jnp.int32, (own, total), 0) + first
    other_id = lax.broadcasted_iota(jnp.int32, (own, total), 1) ^ flip
    logits = dot_nt(mine, all_ref[:, :width]) * factor
    logits = jnp.where(mine_id == other_id, masked_value, logits)
    top = jnp.max(logits, axis=1, keepdims=True)
    log_own = top + jnp.log(jnp.sum(jnp.exp(logits - top), axis=1, keepdims=True))
    is_positive = other_id == pos_ref[...]
    picked = jnp.sum(jnp.where(is_positive, logits, 0.0), axis=1, keepdims=True)
    loss_ref[...] = log_own - picked
    d_logits = pair_weight * (jnp.exp(logits - log_own) - is_positive.astype(f32))
    d_emb = dot(d_logits.astype(bf16), all_ref[:, :width])
    lane = lax.broadcasted_iota(jnp.int32, (SEGS, TAIL), 1)
    digits = jnp.where(lane == 0, float(BASE), jnp.where(lane == 1, 1.0, 0.0)).astype(bf16)
    for at in range(0, total, block):
        rows = slice(at, at + block)
        table = dot_nt(all_ref[:, :width], all_ref[rows, :width]) * factor
        left = lax.broadcasted_iota(jnp.int32, (total, block), 0)
        right = lax.broadcasted_iota(jnp.int32, (total, block), 1) + at
        table = jnp.where(left == right, masked_value, table)
        top = jnp.max(table, axis=0, keepdims=True)
        log_all = top + jnp.log(jnp.sum(jnp.exp(table - top), axis=0, keepdims=True))
        partner = dot_nt(digits, all_ref[rows, width:])[0:1].astype(jnp.int32)
        chosen = partner == mine_id[:, rows]
        back = pair_weight * (jnp.exp(logits[:, rows] - log_all) - chosen.astype(f32))
        d_emb += dot(back.astype(bf16), all_ref[rows, :width])
    d_emb = d_emb * factor
    scale, counts = stat_ref[:, 0:1], stat_ref[:, 1:2]
    pooled = pool_ref[...]
    along = jnp.mean(d_emb * pooled, axis=-1, keepdims=True)
    grad_ref[...] = (d_emb * scale - pooled * (scale * scale * scale * along)) / counts


def contrast(place, everyone, payload, positive, pooled, stats):
    own, width = pooled.shape
    total = everyone.shape[0]
    return call(
        contrast_kernel,
        (1,),
        [whole(v.shape) for v in (everyone, payload, positive, pooled, stats)],
        [whole((own, 1)), whole((own, width))],
        [shaped((own, 1), f32), shaped((own, width), f32)],
        [],
        total * total * width * 2,
        total * width * 2,
        total * total,
    )(place, everyone, payload, positive, pooled, stats)


def norm_back(d_out, normed, root, gain):
    scaled = d_out * gain
    mean = jnp.mean(scaled, axis=-1, keepdims=True)
    along = jnp.mean(scaled * normed, axis=-1, keepdims=True)
    return root * (scaled - mean - normed * along)


def column_sum(values):
    return jnp.sum(values, axis=0, keepdims=True)


def rank_of(step):
    return jnp.where(step < 4, 2 * step + 1, 2 * (step - 4))


def norm2_kernel(index_ref, og_ref, norm_ref, root_ref, seg_ref, gain_ref, dp_ref, act_ref, *rest):
    dsum_ref, ddown_ref, vec_ref, keep_ref, send_ref, dt_ref = rest
    step = pl.program_id(0)
    count, width = og_ref.shape
    own = dp_ref.shape[0]
    per_row = count * SEGS // own

    @pl.when(step == 0)
    def _():
        vec_ref[...] = jnp.zeros_like(vec_ref)
        chunk = 256
        pad = jnp.zeros((TILE - 3 * SEGS, width), bf16)
        for at in range(0, count, chunk):
            row = at // per_row
            pool = dp_ref[row * SEGS : (row + 1) * SEGS]
            high = pool.astype(bf16)
            left = pool - high.astype(f32)
            mid = left.astype(bf16)
            low = (left - mid.astype(f32)).astype(bf16)
            table = jnp.concatenate([high, mid, low, pad], axis=0)
            lane = lax.broadcasted_iota(jnp.int32, (chunk, TILE), 1)
            here = slice(at, at + chunk)
            member = (lane % SEGS == seg_ref[here]).astype(f32).astype(bf16)
            d_res = og_ref[here].astype(f32) + dot(member, table)
            normed = norm_ref[here]
            d_sum = norm_back(d_res, normed, root_ref[here], gain_ref[...])
            d_down = d_sum.astype(bf16)
            dsum_ref[here] = d_sum
            ddown_ref[here] = d_down
            dt_ref[:, here] = d_down.T
            vec_ref[0:1] += column_sum(d_res * normed)
            vec_ref[1:2] += column_sum(d_res)
            vec_ref[2:3] += column_sum(d_down.astype(f32))

    grad = dot(dt_ref[...], act_ref[...]).astype(bf16)

    @pl.when(step < 4)
    def _():
        send_ref[0] = grad

    @pl.when(step >= 4)
    def _():
        keep_ref[0] = grad


def norm2(index, out_grad, normed, root, seg_col, gain, d_pool, activated):
    count, width = out_grad.shape
    inner = activated.shape[1]
    tile = inner // BLOCKS
    own = d_pool.shape[0]
    return call(
        norm2_kernel,
        (BLOCKS,),
        [
            whole((count, width)),
            whole((count, width)),
            whole((count, 1)),
            whole((count, 1)),
            whole((1, width)),
            whole((own, width)),
            pl.BlockSpec((count, tile), lambda i, s: (0, s[0] ^ rank_of(i))),
        ],
        [
            whole((count, width)),
            whole((count, width)),
            whole((SEGS, width)),
            pl.BlockSpec((1, width, tile), lambda i, s: (jnp.maximum(i - 4, 0), 0, 0)),
            pl.BlockSpec((1, width, tile), lambda i, s: (jnp.minimum(i, 3), 0, 0)),
        ],
        [
            shaped((count, width), f32),
            shaped((count, width), bf16),
            shaped((SEGS, width), f32),
            shaped((4, width, tile), bf16),
            shaped((4, width, tile), bf16),
        ],
        [pltpu.VMEM((width, count), bf16)],
        count * width * inner * 2,
        count * (width * 12 + inner * 2) + width * inner * 2,
    )(index, out_grad, normed, root, seg_col, gain, d_pool, activated)


def put_turned(source_ref, target_ref, turn_ref, index):
    turn_ref[...] = source_ref[...].T
    rows = turn_ref.shape[0] // BLOCKS
    for place in range(BLOCKS):
        block = index ^ ((place % 4) * 2 + place // 4)
        start = pl.multiple_of(block * rows, 16)
        target_ref[place * rows : (place + 1) * rows] = turn_ref[pl.ds(start, rows)]


def up_back_kernel(
    down_meta, up_meta, index_ref, ddown_ref, slope_ref, hid_ref, *rest
):
    low_pieces, rest = rest[: len(down_meta)], rest[len(down_meta) :]
    up_pieces, rest = rest[: len(up_meta)], rest[len(up_meta) :]
    dhid_ref, bias_ref, keep_ref, send_ref, wd_ref, wu_ref, turn_ref, ht_ref, sems, up_sems = rest
    step = pl.program_id(0)
    tile = slope_ref.shape[1]
    width = ht_ref.shape[0]

    @pl.when(step == 0)
    def _():
        index = index_ref[0]
        first = load(down_meta, tile, low_pieces, wd_ref, sems, 0)
        second = load(up_meta, width // BLOCKS, up_pieces, wu_ref, up_sems, index)
        put_turned(hid_ref, ht_ref, turn_ref, index)
        for copy in first + second:
            copy.wait()
        dhid_ref[...] = jnp.zeros_like(dhid_ref)

    rows = pl.ds(pl.multiple_of(step * tile, tile), tile)
    cols = pl.ds(pl.multiple_of((index_ref[0] ^ step) * tile, tile), tile)
    d_act = dot_nt(ddown_ref[...], wd_ref[rows])
    d_up = (d_act * slope_ref[...].astype(f32)).astype(bf16)
    bias_ref[...] = column_sum(d_up.astype(f32))
    grad = dot(ht_ref[...], d_up).astype(bf16)
    half = width // 2
    keep_ref[...] = grad[:half].reshape(keep_ref.shape)
    send_ref[...] = grad[half:].reshape(send_ref.shape)
    dhid_ref[...] += dot_nt(d_up, wu_ref[:, cols])


def up_back(index, d_down, slope, hidden, down_pieces, up_pieces):
    count, width = d_down.shape
    inner = slope.shape[1]
    tile = inner // BLOCKS
    part = width // BLOCKS
    down_meta, up_meta = meta_of(down_pieces), meta_of(up_pieces)
    grads = pl.BlockSpec((4, part, tile), lambda i, s: (0, 0, s[0] ^ i))
    return call(
        functools.partial(up_back_kernel, down_meta, up_meta),
        (BLOCKS,),
        [
            whole((count, width)),
            pl.BlockSpec((count, tile), lambda i, s: (0, s[0] ^ i)),
            whole((count, width)),
        ]
        + [ANY] * (len(down_meta) + len(up_meta)),
        [
            whole((count, width)),
            pl.BlockSpec((1, tile), lambda i, s: (0, s[0] ^ i)),
            grads,
            grads,
        ],
        [
            shaped((count, width), f32),
            shaped((1, inner), f32),
            shaped((4, part, inner), bf16),
            shaped((4, part, inner), bf16),
        ],
        [
            pltpu.VMEM((inner, width), bf16),
            pltpu.VMEM((width, inner), bf16),
            pltpu.VMEM((width, count), bf16),
            pltpu.VMEM((width, count), bf16),
            pltpu.SemaphoreType.DMA((len(down_meta),)),
            pltpu.SemaphoreType.DMA((len(up_meta),)),
        ],
        count * width * inner * 6,
        count * (width * 8 + inner * 2) + width * inner * 6,
    )(index, d_down, slope, hidden, *arrays_of(down_pieces), *arrays_of(up_pieces))


def norm1_kernel(meta, index_ref, dhid_ref, dsum_ref, norm_ref, root_ref, gain_ref, ctx_ref, *rest):
    pieces, rest = rest[: len(meta)], rest[len(meta) :]
    dattn_ref, dctx_ref, vec_ref, keep_ref, send_ref, w_ref, acc_ref, sems = rest
    step = pl.program_id(0)
    rows = w_ref.shape[0] // BLOCKS

    @pl.when(step == 0)
    def _():
        copies = load(meta, rows, pieces, w_ref, sems, index_ref[0])
        vec_ref[...] = jnp.zeros_like(vec_ref)
        acc_ref[...] = jnp.zeros_like(acc_ref)
        for copy in copies:
            copy.wait()

    d_hid = dsum_ref[...] + dhid_ref[...]
    normed = norm_ref[...]
    d_sum = norm_back(d_hid, normed, root_ref[...], gain_ref[...])
    d_attn = d_sum.astype(bf16)
    dattn_ref[...] = d_sum
    vec_ref[0:1] += column_sum(d_hid * normed)
    vec_ref[1:2] += column_sum(d_hid)
    vec_ref[2:3] += column_sum(d_attn.astype(f32))
    dctx_ref[...] = dot_nt(d_attn, w_ref[...]).astype(bf16)
    acc_ref[...] += dot(ctx_ref[...].T, d_attn)

    @pl.when(step == pl.num_programs(0) - 1)
    def _():
        for place in range(4):
            for target, core in ((keep_ref, 0), (send_ref, 1)):
                start = pl.multiple_of((index_ref[0] ^ (2 * place + core)) * rows, 16)
                target[place] = acc_ref[pl.ds(start, rows)].astype(bf16)


def norm1(index, d_hidden, d_summed, normed, root, gain, context, pieces, step=256):
    count, width = d_hidden.shape
    meta = meta_of(pieces)
    part = width // BLOCKS
    block = pl.BlockSpec((step, width), lambda i, s: (i, 0))
    return call(
        functools.partial(norm1_kernel, meta),
        (count // step,),
        [
            block,
            block,
            block,
            pl.BlockSpec((step, 1), lambda i, s: (i, 0)),
            whole((1, width)),
            block,
        ]
        + [ANY] * len(meta),
        [
            block,
            block,
            whole((SEGS, width)),
            whole((4, part, width)),
            whole((4, part, width)),
        ],
        [
            shaped((count, width), f32),
            shaped((count, width), bf16),
            shaped((SEGS, width), f32),
            shaped((4, part, width), bf16),
            shaped((4, part, width), bf16),
        ],
        [
            pltpu.VMEM((width, width), bf16),
            pltpu.VMEM((width, width), f32),
            pltpu.SemaphoreType.DMA((len(meta),)),
        ],
        count * width * width * 4,
        count * width * 20 + width * width * 4,
    )(index, d_hidden, d_summed, normed, root, gain, context, *arrays_of(pieces))


def attend_back_kernel(index_ref, q_ref, k_ref, v_ref, dctx_ref, lse_ref, seg_ref, tok_ref, *rest):
    dq_ref, dk_ref, dv_ref, bias_ref, keep_ref, send_ref = rest[:6]
    mask_ref, turn_ref, tt_ref, dk_acc, dv_acc, both_ref = rest[6:]
    rows, _, length = seg_ref.shape
    lanes = q_ref.shape[1]
    half = lanes // 2
    inv_root = 1.0 / math.sqrt(half)

    @pl.when(pl.program_id(0) == 0)
    def _():
        put_turned(tok_ref, tt_ref, turn_ref, index_ref[0])
        for row in range(rows):
            fill_mask(seg_ref[row].astype(f32), mask_ref.at[row])

    for row in range(rows):
        base = row * length
        here = slice(base, base + length)
        kt = k_ref[here].T
        dk_acc[...] = jnp.zeros_like(dk_acc)
        dv_acc[...] = jnp.zeros_like(dv_acc)
        for lo, hi, at in bands(length):
            tile = slice(base + at, base + at + TILE)
            keys = k_ref[base + lo : base + hi]
            values = v_ref[base + lo : base + hi]
            queries = two_heads(q_ref[tile])
            d_context = two_heads(dctx_ref[tile])
            lse = jnp.concatenate(
                [lse_ref[row, 0, head : head + 1, at : at + TILE] for head in range(2)], axis=1
            )
            scores = dot_nt(keys, queries) + twice(mask_ref[row, lo:hi, at : at + TILE])
            probs = jnp.exp(scores - lse)
            d_probs = dot_nt(values, d_context)
            inner = jnp.sum(d_probs * probs, axis=0, keepdims=True)
            d_scores = (probs * (d_probs - inner)).astype(bf16)
            dv_acc[lo:hi] += dot(probs.astype(bf16), d_context)
            dk_acc[lo:hi] += dot(d_scores, queries)
            dq = dot(kt[:, lo:hi], d_scores) * inv_root
            dq = jnp.concatenate([dq[:half, :TILE], dq[half:, TILE:]], axis=0)
            both_ref[tile, :lanes] = dq.T.astype(bf16)
        both_ref[here, lanes : 2 * lanes] = dk_acc[...].astype(bf16)
        both_ref[here, 2 * lanes :] = dv_acc[...].astype(bf16)
    both = both_ref[...]
    dq_ref[...] = both[:, :lanes]
    dk_ref[...] = both[:, lanes : 2 * lanes]
    dv_ref[...] = both[:, 2 * lanes :]
    bias_ref[0, 0:1] = column_sum(both.astype(f32))
    grad = dot(tt_ref[...], both).astype(bf16)
    middle = grad.shape[0] // 2
    keep_ref[...] = grad[:middle].reshape(keep_ref.shape)
    send_ref[...] = grad[middle:].reshape(send_ref.shape)


def attend_back(index, qkv, d_context, lse, seg_rows, tokens, first, pairs):
    count, width = tokens.shape
    rows, _, length = seg_rows.shape
    every = HEADS // 2
    lanes = width // every
    part = width // BLOCKS
    column = lambda place: pl.BlockSpec((count, lanes), lambda i, s: (0, place + i))
    out = pl.BlockSpec((count, lanes), lambda i, s: (0, i))
    grads = pl.BlockSpec((4, part, 3 * lanes), lambda i, s: (0, 0, i))
    return call(
        attend_back_kernel,
        (pairs,),
        [
            column(first),
            column(every + first),
            column(2 * every + first),
            column(first),
            pl.BlockSpec((rows, 1, 2, length), lambda i, s: (0, first + i, 0, 0)),
            whole((rows, 1, length)),
            whole((count, width)),
        ],
        [
            out,
            out,
            out,
            pl.BlockSpec((1, SEGS, 3 * lanes), lambda i, s: (i, 0, 0)),
            grads,
            grads,
        ],
        [
            shaped((count, pairs * lanes), bf16),
            shaped((count, pairs * lanes), bf16),
            shaped((count, pairs * lanes), bf16),
            shaped((pairs, SEGS, 3 * lanes), f32),
            shaped((4, part, pairs * 3 * lanes), bf16),
            shaped((4, part, pairs * 3 * lanes), bf16),
        ],
        [
            pltpu.VMEM((rows, length, length), f32),
            pltpu.VMEM((width, count), bf16),
            pltpu.VMEM((width, count), bf16),
            pltpu.VMEM((length, lanes), f32),
            pltpu.VMEM((length, lanes), f32),
            pltpu.VMEM((count, 3 * lanes), bf16),
        ],
        count * pairs * lanes * (width * 6 + length * 6),
        count * pairs * lanes * 14 + count * width * 2,
        count * length * pairs * 5 // 4,
    )(index, qkv, qkv, qkv, d_context, lse, seg_rows, tokens)


def input_kernel(meta, parts, index_ref, dattn_ref, *rest):
    grads, rest = rest[: 3 * parts], rest[3 * parts :]
    pieces, rest = rest[: len(meta)], rest[len(meta) :]
    out_ref, w_ref, sems = rest
    width = out_ref.shape[1]
    step = width // parts

    @pl.when(pl.program_id(0) == 0)
    def _():
        rows = w_ref.shape[0] // BLOCKS
        for copy in load(meta, rows, pieces, w_ref, sems, index_ref[0]):
            copy.wait()

    total = dattn_ref[...]
    for kind in range(3):
        for part in range(parts):
            at = kind * width + part * step
            total += dot_nt(grads[kind * parts + part][...], w_ref[:, at : at + step])
    out_ref[...] = total


def input_grad(index, d_attn, grads, pieces, step=256):
    count, width = d_attn.shape
    meta = meta_of(pieces)
    parts = len(grads) // 3
    block = pl.BlockSpec((step, width), lambda i, s: (i, 0))
    return call(
        functools.partial(input_kernel, meta, parts),
        (count // step,),
        [block]
        + [pl.BlockSpec((step, g.shape[1]), lambda i, s: (i, 0)) for g in grads]
        + [ANY] * len(meta),
        block,
        shaped((count, width), f32),
        [pltpu.VMEM((width, 3 * width), bf16), pltpu.SemaphoreType.DMA((len(meta),))],
        count * width * width * 6,
        count * width * 14 + width * width * 6,
    )(index, d_attn, *grads, *arrays_of(pieces))


def rounded(value):
    return lax.optimization_barrier(value.astype(bf16))


def add(*values):
    total = values[0].astype(f32)
    for value in values[1:]:
        total = total + value.astype(f32)
    return total


def reduce_blocks(blocks):
    mine, over_x, over_y, far = blocks
    half = far.shape[0] // 2
    top = fsdp_swap(far[:half], 2)
    low = fsdp_swap(far[half:], 4)
    over_x = jnp.concatenate([over_x[:half], add(over_x[half:], low).astype(bf16)], axis=0)
    over_y = jnp.concatenate([add(over_y[:half], top).astype(bf16), over_y[half:]], axis=0)
    from_x = fsdp_swap(over_x, 2)
    from_y = fsdp_swap(over_y, 4)
    return rounded(add(mine, from_x, from_y))


def reduce_planes(value, planes):
    value = rounded(add(value, swap(value, "batch", planes, 1)))
    return add(value, swap(value, "batch", planes, 2))


def reduce_shard(keep, send, planes):
    other = fsdp_swap(send, 1)
    blocks = [rounded(add(keep[i], other[i])) for i in range(4)]
    return reduce_planes(reduce_blocks(blocks), planes)


def reduce_general(keep, send):
    full = jnp.stack([keep, send], axis=1)
    total = lax.psum(full, "batch")
    total = total.reshape((BLOCKS,) + keep.shape[1:])
    return total


def layer(
    planes,
    ring,
    tokens,
    seg_ids,
    positive,
    out_grad,
    w_qkv,
    b_qv,
    w_out,
    b_out,
    norm1_gain,
    norm1_shift,
    w_up,
    b_up,
    w_down,
    b_down,
    norm2_gain,
    norm2_shift,
):
    paired = ring == BLOCKS and planes == 4
    row_count, row_length, width = tokens.shape
    count = row_count * row_length
    inner = b_up.shape[0] * ring
    own = row_count * SEGS
    token_rows = tokens.reshape(count, width)
    seg_rows = seg_ids.reshape(row_count, 1, row_length)
    seg_col = seg_ids.reshape(count, 1)
    pos_col = positive.reshape(own, 1)
    fsdp = lax.axis_index("fsdp")
    me = lax.axis_index("batch") * ring + fsdp
    index = (fsdp if paired else jnp.zeros_like(fsdp)).reshape(1).astype(jnp.int32)

    weights = (w_qkv, w_out, w_up, w_down)
    if paired:
        firsts = [gather_first(w) for w in weights]
        qkv_pieces, out_pieces, up_pieces, down_pieces = [
            gather_second(w, *first) for w, first in zip(weights, firsts)
        ]
    else:
        qkv_pieces, out_pieces, up_pieces, down_pieces = [gather_whole(w) for w in weights]

    small = (b_qv, b_out, norm1_gain, norm1_shift, b_up, b_down, norm2_gain, norm2_shift)
    sizes = [value.shape[0] for value in small]
    table = lax.all_gather(jnp.concatenate(small)[None], "fsdp", axis=0, tiled=True).astype(f32)
    vectors, at = [], 0
    for size in sizes:
        vectors.append(table[:, at : at + size].reshape(1, ring * size))
        at += size
    bias_qv, bias_out, gain1, shift1, bias_up, bias_down, gain2, shift2 = vectors
    bias_qkv = jnp.concatenate(
        [bias_qv[:, :width], jnp.zeros((1, width), f32), bias_qv[:, width:]], axis=1
    )
    rows = jnp.concatenate(
        [bias_out, gain1, shift1, bias_down, gain2, shift2, jnp.zeros((2, width), f32)], axis=0
    )

    qkv, context, lse = attend(index, token_rows, bias_qkv, seg_rows, qkv_pieces)
    normed1, root1, hidden = project(index, context, token_rows, rows, out_pieces)
    activated, slope = up(index, hidden, bias_up, up_pieces)
    result, normed2, root2, payload, pooled, stats = down(
        index, activated, normed1, rows, seg_rows, pos_col, down_pieces
    )

    if paired:
        everyone = payload
        for bit in (1, 2, 4):
            everyone = jnp.concatenate([everyone, fsdp_swap(everyone, bit)], axis=0)
        for bit in (1, 2):
            everyone = jnp.concatenate([everyone, swap(everyone, "batch", planes, bit)], axis=0)
        flip = me * own
    else:
        everyone = lax.all_gather(payload, ("batch", "fsdp"), axis=0, tiled=True)
        flip = jnp.zeros_like(me)
    place = jnp.stack([flip, me * own]).astype(jnp.int32)
    pair_loss, d_pool = contrast(place, everyone, payload, pos_col, pooled, stats)

    d_summed, d_down, sums2, keep_down, send_down = norm2(
        index, out_grad.reshape(count, width), normed2, root2, seg_col, gain2, d_pool, activated
    )
    d_hidden, sums_up, keep_up, send_up = up_back(
        index, d_down, slope, hidden, down_pieces, up_pieces
    )
    d_attn, d_context, sums1, keep_out, send_out = norm1(
        index, d_hidden, d_summed, normed1, root1, gain1, context, out_pieces
    )
    pairs = HEADS // 2
    cuts = 2
    backs = [
        attend_back(
            index, qkv, d_context, lse, seg_rows, token_rows, i * pairs // cuts, pairs // cuts
        )
        for i in range(cuts)
    ]
    grads = [backs[cut][kind] for kind in range(3) for cut in range(cuts)]
    grad_tokens = input_grad(index, d_attn, grads, qkv_pieces)

    lanes = width // pairs
    sums_qkv = jnp.concatenate([back[3][:, 0] for back in backs], axis=0).reshape(pairs, 3, lanes)
    sums_qv = jnp.concatenate([sums_qkv[:, 0].reshape(-1), sums_qkv[:, 2].reshape(-1)])
    sums = (sums_qv, sums1[2], sums1[0], sums1[1], sums_up[0], sums2[2], sums2[0], sums2[1])

    if paired:
        vector = jnp.concatenate([v.reshape(ring, -1) for v in sums], axis=1)
        order = [2 * (i % 4) + i // 4 for i in range(BLOCKS)]
        vector = vector[jnp.array(order, jnp.int32) ^ fsdp].astype(bf16)
        vector = jnp.pad(vector[:, None], ((0, 0), (0, 15), (0, 0)))
        grad_down = reduce_shard(keep_down, send_down, planes).T
        grad_up = reduce_shard(keep_up, send_up, planes)
        grad_out = reduce_shard(keep_out, send_out, planes)
        shards = []
        for cut, back in enumerate(backs):
            keep, send = back[4], back[5]
            if cut == cuts - 1:
                keep = jnp.concatenate([keep, vector[:4]], axis=1)
                send = jnp.concatenate([send, vector[4:]], axis=1)
            shards.append(reduce_shard(keep, send, planes))
        part = width // BLOCKS
        line = shards[-1][part]
        shards = [shard[:part] for shard in shards]
        own_vectors, at = [], 0
        for size in sizes:
            own_vectors.append(line[at : at + size])
            at += size
    else:
        scatter = lambda value: lax.psum_scatter(value, "fsdp", scatter_dimension=0, tiled=True)
        joined = lambda value: value.reshape((-1,) + value.shape[2:])
        grad_down = scatter(joined(reduce_general(keep_down, send_down).transpose(0, 2, 1)))
        grad_up = scatter(joined(reduce_general(keep_up, send_up)))
        grad_out = scatter(joined(reduce_general(keep_out, send_out)))
        grad_down, grad_up, grad_out = [add(g) for g in (grad_down, grad_up, grad_out)]
        shards = [add(scatter(joined(reduce_general(back[4], back[5])))) for back in backs]
        own_vectors = [
            lax.psum_scatter(lax.psum(v, "batch"), "fsdp", scatter_dimension=0, tiled=True)
            for v in sums
        ]

    grad_qkv = jnp.concatenate(shards, axis=1)
    depth = grad_qkv.shape[0]
    grad_qkv = grad_qkv.reshape(depth, pairs, 3, lanes).transpose(0, 2, 1, 3)
    grad_qkv = grad_qkv.reshape(depth, 3 * width)
    return (
        result.reshape(tokens.shape),
        pair_loss.reshape(own),
        grad_tokens.reshape(tokens.shape),
        grad_qkv,
        own_vectors[0],
        grad_out,
        own_vectors[1],
        own_vectors[2],
        own_vectors[3],
        grad_up,
        own_vectors[4],
        grad_down,
        own_vectors[5],
        own_vectors[6],
        own_vectors[7],
    )


def solution(mesh):
    rows = P(("batch", "fsdp"), None, None)
    matrix = P("fsdp", None)
    vector = P("fsdp")
    placed = (
        rows,
        P(("batch", "fsdp"), None),
        P(("batch", "fsdp")),
        rows,
        matrix,
        vector,
        matrix,
        vector,
        vector,
        vector,
        matrix,
        vector,
        matrix,
        vector,
        vector,
        vector,
    )
    given = (
        rows,
        P(("batch", "fsdp")),
        rows,
        matrix,
        vector,
        matrix,
        vector,
        vector,
        vector,
        matrix,
        vector,
        matrix,
        vector,
        vector,
        vector,
    )
    return jax.shard_map(
        functools.partial(layer, mesh.shape["batch"], mesh.shape["fsdp"]),
        mesh=mesh,
        in_specs=placed,
        out_specs=given,
        check_vma=False,
    )
```

time: 880 us -> 479 us (0.54)
  waiting for transfers between devices: 428 us -> 171 us
  matrix products: 190 us -> 0 us
  Pallas kernels: 0 us -> 174 us
  blocking collectives: 116 us -> 23.1 us
  starting transfers between devices: 0.4 us -> 62.3 us
  local copies, waits for them, and re-layouts: 80.7 us -> 28.5 us
  other arithmetic: 39.9 us -> 13.2 us
  between operations: 18.8 us -> 1.99 us
    reduce_scatter x4 -> x0, waiting for transfers between devices: 297 us -> none  [the longest x1 93.3 us: body(): lax.psum_scatter(d_terms, ('batch', 'fsdp'), scatter_dimension=0, tiled=T...]
    dot_general x31 -> x0, matrix products: 190 us -> none  [the longest x1 36.5 us: ffn_forward(): jnp.dot(hidden_b, w_up_full, preferred_element_type=jnp.float32)]
    pallas_call x0 -> x11, Pallas kernels: none -> 174 us  [the longest x2 30.5 us: attend_back(): call(attend_back_kernel, (pairs,), [column(first), column(every + first),...]
    ppermute x0 -> x76, waiting for transfers between devices: none -> 171 us  [swap(): return lax.ppermute(value, axis, [(i, i ^ bit) for i in range(size)])]
    psum x1 -> x0, waiting for transfers between devices: 91.5 us -> none  [body(): lax.psum((shares[0], shares[1], shares[2], shares[3], shares[4], shares[5...]
    ppermute x0 -> x76, starting transfers between devices: none -> 62.3 us  [swap(): return lax.ppermute(value, axis, [(i, i ^ bit) for i in range(size)])]
    unnamed x2 -> x0, blocking collectives: 51.5 us -> none
    unnamed x11 -> x0, waiting for transfers between devices: 39.1 us -> none
  transfers between devices with their start and end apart: 10 -> 76, of which waited for: 6 -> 32; matrix products, arithmetic and copies ran while one was open for 18% -> 7% of each run, Pallas kernels for 0% -> 14%
where the time goes in v1:
time: 479 us; the launch traced here: 474 us
  Pallas kernels  174 us (36%)
  waiting for transfers between devices  171 us (36%)
  starting transfers between devices  62.3 us (13%)
  local copies, waits for them, and re-layouts  28.5 us (6%)
  blocking collectives  23.1 us (5%)
  other arithmetic  13.2 us (3%)
    ppermute x76, waiting for transfers between devices, swap(): return lax.ppermute(value, axis, [(i, i ^ bit) for i in range(size)])  171 us
    ppermute x76, starting transfers between devices, swap(): return lax.ppermute(value, axis, [(i, i ^ bit) for i in range(size)])  62.3 us
    pallas_call x2, Pallas kernels, attend_back(): call(attend_back_kernel, (pairs,), [column(first), column(every + first),...  30.5 us
    pallas_call x1, Pallas kernels, attend(): call(functools.partial(attend_kernel, meta), (rows,), [pl.BlockSpec((leng...  29.9 us
    pallas_call x1, Pallas kernels, up_back(): call(functools.partial(up_back_kernel, down_meta, up_meta), (BLOCKS,), [w...  29.6 us
    all_gather x1, blocking collectives, layer(): lax.all_gather(jnp.concatenate(small)[None], 'fsdp', axis=0, tiled=True)  23.1 us
    pallas_call x1, Pallas kernels, up(): call(functools.partial(up_kernel, meta), (count // step, inner // tile),...  18.6 us
    pallas_call x1, Pallas kernels, norm2(): call(norm2_kernel, (BLOCKS,), [whole((count, width)), whole((count, width...  17.8 us
  transfers between devices with their start and end apart: 76, of which 32 were waited for; matrix products, arithmetic and copies ran while one was open for 7% of the time, Pallas kernels for 14%

profile of v1, /device:TPU:0, one launch (start us, length us, event | category | flops | bytes accessed | tf_op | source)
XLA Modules:
  0.0 473.6 jit_solution(18309219980833044891)
XLA Ops:
  10.7 8.8 %collective-permute-done.9.rest_1_ = bf16[96,768]{1,0:T(8,128)(2,1)S(1)} collective-permute-done((bf16[96,768]{1,0:T(8,128)(2,1)}, bf16[96,768]{1,0:T(8,128)(2,1)S(1)}, u32[]{:S(2)}, u32[]{:S(2)}) %collective-permute-start.9) | collective-permute-done | bytes 147488 | tf_op jit(solution)/shard_map/ppermute | solution.py:66
  20.4 3.5 collective-permute-done.12.rest_4_
  30.0 5.4 %concatenate.86 = bf16[1152]{0:T(1024)(128)(2,1)S(1)} concatenate(bf16[192]{0:T(256)(128)(2,1)} %param.22, bf16[96]{0:T(256)(128)(2,1)} %param.24, bf16[96]{0:T(256)(128)(2,1)} %param.25, bf16[96]{0:T(256)(128)(2,1)} %param.26, bf16[384]{0:T(512)(128)(2,1)} %param.28, bf16[96]{0:T(256)(128)(2,1)} %param.30, bf16[96]{0:T(256)(128)(2,1)} %param.31, bf16[96]{0:T(256)(128)(2,1)} %param.32), dimensions={0} | concatenate | bytes 4608 | tf_op jit(solution)/shard_map/concatenate | solution.py:941
  35.4 23.1 %all-gather.1 = bf16[8,1,1152]{2,1,0:T(2,128)(2,1)S(1)} all-gather(bf16[1,1,1152]{2,1,0:T(2,128)(2,1)S(1)} %reshape.223), channel_id=2, replica_groups=mesh['batch'=4,'fsdp'=8] {'fsdp'}, dimensions={0}, use_global_device_ids=true | all-gather | bytes 20736 | tf_op jit(solution)/shard_map/all_gather | solution.py:941
  78.4 6.0 %collective-permute-done.21.rest_4_.rest_14_ = bf16[48,3072]{1,0:T(8,128)(2,1)S(1)} collective-permute-done((bf16[48,3072]{1,0:T(8,128)(2,1)S(1)}, bf16[48,3072]{1,0:T(8,128)(2,1)S(1)}, u32[]{:S(2)}, u32[]{:S(2)}) %collective-permute-start.21) | collective-permute-done | bytes 294944 | tf_op jit(solution)/shard_map/ppermute | solution.py:66
  84.9 5.2 %collective-permute-done.30.rest_4_ = bf16[192,768]{1,0:T(8,128)(2,1)S(1)} collective-permute-done((bf16[192,768]{1,0:T(8,128)(2,1)S(1)}, bf16[192,768]{1,0:T(8,128)(2,1)S(1)}, u32[]{:S(2)}, u32[]{:S(2)}) %collective-permute-start.30) | collective-permute-done | bytes 294944 | tf_op jit(solution)/shard_map/ppermute | solution.py:66
  90.8 29.9 %shard_map.280 = (bf16[1024,2304]{1,0:T(8,128)(2,1)}, bf16[1024,768]{1,0:T(8,128)(2,1)}, f32[2,6,2,512]{3,2,1,0:T(2,128)}) custom-call(s32[1]{0:T(128)} %bitcast.index_ref, bf16[1024,768]{1,0:T(8,128)(2,1)} %bitcast.77, f32[1,2304]{1,0:T(1,128)} %fusion.23.bias_ref, s32[2,1,512]{2,1,0:T(1,128)} %reshape.196.seg_ref, bf16[96,2304]{1,0:T(8,128)(2,1)} %rest_6_.1, ...), custom_call_target="tpu_custom_call" | custom-call | flops 5234491392 | bytes 11403264 | tf_op jit(solution)/shard_map/pallas_call | solution.py:197
  120.7 7.4 %shard_map.281 = (f32[1024,768]{1,0:T(8,128)}, f32[1024,1]{1,0:T(8,128)}, bf16[1024,768]{1,0:T(8,128)(2,1)}) custom-call(s32[1]{0:T(128)} %bitcast.index_ref, bf16[1024,768]{1,0:T(8,128)(2,1)} %get-tuple-element.57.ctx_ref, bf16[1024,768]{1,0:T(8,128)(2,1)} %bitcast.78, f32[8,768]{1,0:T(8,128)} %concatenate.88.vec_ref, bf16[96,768]{1,0:T(8,128)(2,1)} %rest_0_.11, ...), custom_call_target="tpu_custom_call" | custom-call | flops 1207959552 | bytes 9043968 | tf_op jit(solution)/shard_map/pallas_call | solution.py:258
  129.3 18.6 %shard_map.282 = (bf16[1024,3072]{1,0:T(8,128)(2,1)}, bf16[1024,3072]{1,0:T(8,128)(2,1)}) custom-call(s32[1]{0:T(128)} %bitcast.index_ref, bf16[1024,768]{1,0:T(8,128)(2,1)} %get-tuple-element.58.hid_ref, f32[1,3072]{1,0:T(1,128)} %bitcast.90, bf16[96,3072]{1,0:T(8,128)(2,1)} %rest_10_.1, bf16[96,3072]{1,0:T(8,128)(2,1)} %copy-done.19, ...), custom_call_target="tpu_custom_call" | custom-call | flops 4831838208 | bytes 18874368 | tf_op jit(solution)/shard_map/pallas_call | solution.py:295
  149.3 13.8 %shard_map.283 = (bf16[1024,768]{1,0:T(8,128)(2,1)}, f32[1024,768]{1,0:T(8,128)}, f32[1024,1]{1,0:T(8,128)}, bf16[16,896]{1,0:T(8,128)(2,1)}, f32[16,768]{1,0:T(8,128)}, /*index=5*/f32[16,128]{1,0:T(8,128)}) custom-call(s32[1]{0:T(128)} %bitcast.index_ref, bf16[1024,3072]{1,0:T(8,128)(2,1)} %get-tuple-element.59.act_ref, ...), custom_call_target="tpu_custom_call" | custom-call | flops 4831838208 | bytes 18874368 | tf_op jit(solution)/shard_map/pallas_call | solution.py:367
  177.7 4.4 collective-permute-done.39
  182.1 3.3 collective-permute-start.40
  187.0 15.0 %collective-permute-done.40 = bf16[256,896]{1,0:T(8,128)(2,1)S(1)} collective-permute-done((bf16[256,896]{1,0:T(8,128)(2,1)S(1)}, bf16[256,896]{1,0:T(8,128)(2,1)S(1)}, u32[]{:S(2)}, u32[]{:S(2)}) %collective-permute-start.40) | collective-permute-done | bytes 458784 | tf_op jit(solution)/shard_map/ppermute | solution.py:66
  203.0 4.0 shard_map.284
  207.1 17.8 %shard_map.285 = (f32[1024,768]{1,0:T(8,128)}, bf16[1024,768]{1,0:T(8,128)(2,1)}, f32[8,768]{1,0:T(8,128)}, bf16[4,768,384]{2,1,0:T(8,128)(2,1)}, bf16[4,768,384]{2,1,0:T(8,128)(2,1)}) custom-call(s32[1]{0:T(128)} %bitcast.index_ref, bf16[1024,768]{1,0:T(8,128)(2,1)} %bitcast.93, f32[1024,768]{1,0:T(8,128)} %get-tuple-element.66.norm_ref, ...), custom_call_target="tpu_custom_call" | custom-call | flops 4831838208 | bytes 20447232 | tf_op jit(solution)/shard_map/pallas_call | solution.py:525
  224.8 29.6 %shard_map.286 = (f32[1024,768]{1,0:T(8,128)}, f32[1,3072]{1,0:T(1,128)}, bf16[4,96,3072]{2,1,0:T(8,128)(2,1)}, bf16[4,96,3072]{2,1,0:T(8,128)(2,1)}) custom-call(s32[1]{0:T(128)} %bitcast.index_ref, bf16[1024,768]{1,0:T(8,128)(2,1)} %get-tuple-element.69.ddown_ref, bf16[1024,3072]{1,0:T(8,128)(2,1)} %get-tuple-element.70.slope_ref, ...), custom_call_target="tpu_custom_call" | custom-call | flops 14495514624 | bytes 26738688 | tf_op jit(solution)/shard_map/pallas_call | solution.py:605
  254.4 11.1 %shard_map.287 = (f32[1024,768]{1,0:T(8,128)}, bf16[1024,768]{1,0:T(8,128)(2,1)}, f32[8,768]{1,0:T(8,128)}, bf16[4,96,768]{2,1,0:T(8,128)(2,1)}, bf16[4,96,768]{2,1,0:T(8,128)(2,1)}) custom-call(s32[1]{0:T(128)} %bitcast.index_ref, f32[1024,768]{1,0:T(8,128)} %get-tuple-element.71.dhid_ref, f32[1024,768]{1,0:T(8,128)} %get-tuple-element.72.dsum_ref, ...), custom_call_target="tpu_custom_call" | custom-call | flops 2415919104 | bytes 18087936 | tf_op jit(solution)/shard_map/pallas_call | solution.py:677
  265.5 15.2 %shard_map.288 = (bf16[1024,384]{1,0:T(8,128)(2,1)}, bf16[1024,384]{1,0:T(8,128)(2,1)}, bf16[1024,384]{1,0:T(8,128)(2,1)}, f32[3,8,384]{2,1,0:T(8,128)}, bf16[4,...) custom-call(s32[1]{0:T(128)} %bitcast.index_ref, bf16[1024,2304]{1,0:T(8,128)(2,1)} %get-tuple-element.75.q_ref.k_ref.v_ref, ...), custom_call_target="tpu_custom_call" | custom-call | flops 3019898880 | bytes 7077888 | tf_op jit(solution)/shard_map/pallas_call | solution.py:774
  280.8 15.3 %shard_map.289 = (bf16[1024,384]{1,0:T(8,128)(2,1)}, bf16[1024,384]{1,0:T(8,128)(2,1)}, bf16[1024,384]{1,0:T(8,128)(2,1)}, f32[3,8,384]{2,1,0:T(8,128)}, bf16[4,...) custom-call(s32[1]{0:T(128)} %bitcast.index_ref, bf16[1024,2304]{1,0:T(8,128)(2,1)} %get-tuple-element.75.q_ref.k_ref.v_ref, ...), custom_call_target="tpu_custom_call" | custom-call | flops 3019898880 | bytes 7077888 | tf_op jit(solution)/shard_map/pallas_call | solution.py:774
  310.8 11.0 %shard_map.290 = f32[1024,768]{1,0:T(8,128)} custom-call(s32[1]{0:T(128)} %bitcast.index_ref, f32[1024,768]{1,0:T(8,128)} %get-tuple-element.74.dattn_ref, bf16[1024,384]{1,0:T(8,128)(2,1)} %get-tuple-element.78.rest_0_, bf16[1024,384]{1,0:T(8,128)(2,1)} %get-tuple-element.79.rest_1_, bf16[1024,384]{1,0:T(8,128)(2,1)} %get-tuple-element.80.rest_2_, ...), custom_call_target="tpu_custom_call" | custom-call | flops 3623878656 | bytes 14548992 | tf_op jit(solution)/shard_map/pallas_call | solution.py:842
  324.1 4.2 collective-permute-done.60
  340.3 3.2 collective-permute-done.51
  344.6 4.4 collective-permute-done.49
  351.9 4.4 collective-permute-done.46
  360.4 5.5 %collective-permute-done.47 = bf16[96,1152]{1,0:T(8,128)(2,1)S(1)} collective-permute-done((bf16[96,1152]{1,0:T(8,128)(2,1)S(1)}, bf16[96,1152]{1,0:T(8,128)(2,1)S(1)}, u32[]{:S(2)}, u32[]{:S(2)}) %collective-permute-start.47) | collective-permute-done | bytes 221216 | tf_op jit(solution)/shard_map/ppermute | solution.py:66
  379.4 3.8 collective-permute-done.72
  384.1 3.9 collective-permute-done.70
  391.1 16.3 %collective-permute-done.73 = bf16[768,384]{1,0:T(8,128)(2,1)S(1)} collective-permute-done((bf16[768,384]{1,0:T(8,128)(2,1)S(1)}, bf16[768,384]{1,0:T(8,128)(2,1)S(1)}, u32[]{:S(2)}, u32[]{:S(2)}) %collective-permute-start.73) | collective-permute-done | bytes 589856 | tf_op jit(solution)/shard_map/ppermute | solution.py:66
  411.9 18.1 %collective-permute-done.74 = bf16[768,384]{1,0:T(8,128)(2,1)} collective-permute-done((bf16[768,384]{1,0:T(8,128)(2,1)S(1)}, bf16[768,384]{1,0:T(8,128)(2,1)}, u32[]{:S(2)}, u32[]{:S(2)}) %collective-permute-start.74) | collective-permute-done | bytes 589856 | tf_op jit(solution)/shard_map/ppermute | solution.py:66
  431.3 6.1 %collective-permute-done.67 = bf16[96,3072]{1,0:T(8,128)(2,1)} collective-permute-done((bf16[96,3072]{1,0:T(8,128)(2,1)S(1)}, bf16[96,3072]{1,0:T(8,128)(2,1)}, u32[]{:S(2)}, u32[]{:S(2)}) %collective-permute-start.67) | collective-permute-done | bytes 589856 | tf_op jit(solution)/shard_map/ppermute | solution.py:66
  440.0 25.9 %collective-permute-done.75 = bf16[768,384]{1,0:T(8,128)(2,1)S(1)} collective-permute-done((bf16[768,384]{1,0:T(8,128)(2,1)S(1)}, bf16[768,384]{1,0:T(8,128)(2,1)S(1)}, u32[]{:S(2)}, u32[]{:S(2)}) %collective-permute-start.75) | collective-permute-done | bytes 589856 | tf_op jit(solution)/shard_map/ppermute | solution.py:66
  467.3 4.8 %collective-permute-done.68 = bf16[96,3072]{1,0:T(8,128)(2,1)S(1)} collective-permute-done((bf16[96,3072]{1,0:T(8,128)(2,1)S(1)}, bf16[96,3072]{1,0:T(8,128)(2,1)S(1)}, u32[]{:S(2)}, u32[]{:S(2)}) %collective-permute-start.68) | collective-permute-done | bytes 589856 | tf_op jit(solution)/shard_map/ppermute | solution.py:66
  (362 shorter events, 122.5 us)
Async XLA Ops:
  3.7 24.1 %collective-permute-start = (bf16[96,2304]{1,0:T(8,128)(2,1)}, bf16[96,2304]{1,0:T(8,128)(2,1)S(1)}, u32[]{:S(2)}, u32[]{:S(2)}) collective-permute-start(bf16[96,2304]{1,0:T(8,128)(2,1)} %rest_6_.1), channel_id=1, source_target_pairs={{0,2},{1,3},{2,0},{3,1},{4,6},{5,7},{6,4},{7,5},{8,10},{9,11},{10,... | collective-permute-start | bytes 1327112 | tf_op jit(solution)/shard_map/ppermute | solution.py:66
  5.2 22.6 %collective-permute-start.1 = (bf16[96,2304]{1,0:T(8,128)(2,1)}, bf16[96,2304]{1,0:T(8,128)(2,1)S(1)}, u32[]{:S(2)}, u32[]{:S(2)}) collective-permute-start(bf16[96,2304]{1,0:T(8,128)(2,1)} %rest_6_.1), channel_id=1, source_target_pairs={{0,4},{1,5},{2,6},{3,7},{4,0},{5,1},{6,2},{7,3},{8,12},{9,13},{10,... | collective-permute-start | bytes 1327112 | tf_op jit(solution)/shard_map/ppermute | solution.py:66
  25.8 32.8 %collective-permute-start.18 = (bf16[96,3072]{1,0:T(8,128)(2,1)}, bf16[96,3072]{1,0:T(8,128)(2,1)S(1)}, u32[]{:S(2)}, u32[]{:S(2)}) collective-permute-start(bf16[96,3072]{1,0:T(8,128)(2,1)} %rest_10_.1), channel_id=1, source_target_pairs={{0,2},{1,3},{2,0},{3,1},{4,6},{5,7},{6,4},{7,5},{8,10},{9,11},{10,... | collective-permute-start | bytes 1769480 | tf_op jit(solution)/shard_map/ppermute | solution.py:66
  27.3 32.9 %collective-permute-start.19 = (bf16[96,3072]{1,0:T(8,128)(2,1)}, bf16[96,3072]{1,0:T(8,128)(2,1)}, u32[]{:S(2)}, u32[]{:S(2)}) collective-permute-start(bf16[96,3072]{1,0:T(8,128)(2,1)} %rest_10_.1), channel_id=1, source_target_pairs={{0,4},{1,5},{2,6},{3,7},{4,0},{5,1},{6,2},{7,3},{8,12},{9,13},{10,... | collective-permute-start | bytes 1769480 | tf_op jit(solution)/shard_map/ppermute | solution.py:66
  27.8 32.9 %collective-permute-start.22 = (bf16[96,3072]{1,0:T(8,128)(2,1)}, bf16[96,3072]{1,0:T(8,128)(2,1)}, u32[]{:S(2)}, u32[]{:S(2)}) collective-permute-start(bf16[96,3072]{1,0:T(8,128)(2,1)} %rest_10_.1), channel_id=1, source_target_pairs={{0,1},{1,0},{2,3},{3,2},{4,5},{5,4},{6,7},{7,6},{8,9},{9,8},{10,11... | collective-permute-start | bytes 1769480 | tf_op jit(solution)/shard_map/ppermute | solution.py:66
  27.9 32.9 %collective-permute-start.27 = (bf16[384,768]{1,0:T(8,128)(2,1)}, bf16[384,768]{1,0:T(8,128)(2,1)}, u32[]{:S(2)}, u32[]{:S(2)}) collective-permute-start(bf16[384,768]{1,0:T(8,128)(2,1)} %rest_0_.10), channel_id=1, source_target_pairs={{0,2},{1,3},{2,0},{3,1},{4,6},{5,7},{6,4},{7,5},{8,10},{9,11},{10,... | collective-permute-start | bytes 1769480 | tf_op jit(solution)/shard_map/ppermute | solution.py:66
  28.3 34.1 %collective-permute-start.28 = (bf16[384,768]{1,0:T(8,128)(2,1)}, bf16[384,768]{1,0:T(8,128)(2,1)}, u32[]{:S(2)}, u32[]{:S(2)}) collective-permute-start(bf16[384,768]{1,0:T(8,128)(2,1)} %rest_0_.10), channel_id=1, source_target_pairs={{0,4},{1,5},{2,6},{3,7},{4,0},{5,1},{6,2},{7,3},{8,12},{9,13},{10,... | collective-permute-start | bytes 1769480 | tf_op jit(solution)/shard_map/ppermute | solution.py:66
  67.0 23.7 %collective-permute-start.24 = (bf16[96,3072]{1,0:T(8,128)(2,1)}, bf16[96,3072]{1,0:T(8,128)(2,1)}, u32[]{:S(2)}, u32[]{:S(2)}) collective-permute-start(bf16[96,3072]{1,0:T(8,128)(2,1)} %collective-permute-done.19.rest_2_.rest_12_), channel_id=1, source_target_pairs={{0,1},{1,0},{2,3},{3,2},{4,5},{5,4},{6,7},{7,6},{8,9},{9,8},{10,11... | collective-permute-start | bytes 1769480 | tf_op jit(solution)/shard_map/ppermute | solution.py:66
  67.6 22.6 %collective-permute-start.23 = (bf16[96,3072]{1,0:T(8,128)(2,1)}, bf16[96,3072]{1,0:T(8,128)(2,1)}, u32[]{:S(2)}, u32[]{:S(2)}) collective-permute-start(bf16[96,3072]{1,0:T(8,128)(2,1)} %copy-done.19), channel_id=1, source_target_pairs={{0,1},{1,0},{2,3},{3,2},{4,5},{5,4},{6,7},{7,6},{8,9},{9,8},{10,11... | collective-permute-start | bytes 1769480 | tf_op jit(solution)/shard_map/ppermute | solution.py:66
  84.4 63.5 %collective-permute-start.31 = (bf16[384,768]{1,0:T(8,128)(2,1)S(1)}, bf16[384,768]{1,0:T(8,128)(2,1)S(1)}, u32[]{:S(2)}, u32[]{:S(2)}) collective-permute-start(bf16[384,768]{1,0:T(8,128)(2,1)S(1)} %copy-done.34), channel_id=1, source_target_pairs={{0,1},{1,0},{2,3},{3,2},{4,5},{5,4},{6,7},{7,6},{8,9},{9,8},{10,11... | collective-permute-start | bytes 1769480 | tf_op jit(solution)/shard_map/ppermute | solution.py:66
  84.5 63.5 %collective-permute-start.32 = (bf16[384,768]{1,0:T(8,128)(2,1)}, bf16[384,768]{1,0:T(8,128)(2,1)S(1)}, u32[]{:S(2)}, u32[]{:S(2)}) collective-permute-start(bf16[384,768]{1,0:T(8,128)(2,1)} %collective-permute-done.27.rest_1_), channel_id=1, source_target_pairs={{0,1},{1,0},{2,3},{3,2},{4,5},{5,4},{6,7},{7,6},{8,9},{9,8},{10,11... | collective-permute-start | bytes 1769480 | tf_op jit(solution)/shard_map/ppermute | solution.py:66
  90.1 57.8 %collective-permute-start.33 = (bf16[384,768]{1,0:T(8,128)(2,1)}, bf16[384,768]{1,0:T(8,128)(2,1)S(1)}, u32[]{:S(2)}, u32[]{:S(2)}) collective-permute-start(bf16[384,768]{1,0:T(8,128)(2,1)} %collective-permute-done.28.rest_2_), channel_id=1, source_target_pairs={{0,1},{1,0},{2,3},{3,2},{4,5},{5,4},{6,7},{7,6},{8,9},{9,8},{10,11... | collective-permute-start | bytes 1769480 | tf_op jit(solution)/shard_map/ppermute | solution.py:66
  90.2 37.9 %collective-permute-start.25 = (bf16[48,3072]{1,0:T(8,128)(2,1)}, bf16[48,3072]{1,0:T(8,128)(2,1)S(1)}, u32[]{:S(2)}, u32[]{:S(2)}) collective-permute-start(bf16[48,3072]{1,0:T(8,128)(2,1)} %collective-permute-done.20.rest_3_.rest_13_), channel_id=1, source_target_pairs={{0,1},{1,0},{2,3},{3,2},{4,5},{5,4},{6,7},{7,6},{8,9},{9,8},{10,11... | collective-permute-start | bytes 884744 | tf_op jit(solution)/shard_map/ppermute | solution.py:66
  90.7 38.0 %collective-permute-start.26 = (bf16[48,3072]{1,0:T(8,128)(2,1)S(1)}, bf16[48,3072]{1,0:T(8,128)(2,1)S(1)}, u32[]{:S(2)}, u32[]{:S(2)}) collective-permute-start(bf16[48,3072]{1,0:T(8,128)(2,1)S(1)} %collective-permute-done.21.rest_4_.rest_14_), channel_id=1, source_target_pairs={{0,1},{1,0},{2,3},{3,2},{4,5},{5,4},{6,7},{7,6},{8,9},{9,8},{10,11... | collective-permute-start | bytes 884744 | tf_op jit(solution)/shard_map/ppermute | solution.py:66
  128.1 19.9 %collective-permute-start.34 = (bf16[192,768]{1,0:T(8,128)(2,1)S(1)}, bf16[192,768]{1,0:T(8,128)(2,1)S(1)}, u32[]{:S(2)}, u32[]{:S(2)}) collective-permute-start(bf16[192,768]{1,0:T(8,128)(2,1)S(1)} %collective-permute-done.29.rest_3_), channel_id=1, source_target_pairs={{0,1},{1,0},{2,3},{3,2},{4,5},{5,4},{6,7},{7,6},{8,9},{9,8},{10,11... | collective-permute-start | bytes 884744 | tf_op jit(solution)/shard_map/ppermute | solution.py:66
  128.6 19.4 %collective-permute-start.35 = (bf16[192,768]{1,0:T(8,128)(2,1)S(1)}, bf16[192,768]{1,0:T(8,128)(2,1)S(1)}, u32[]{:S(2)}, u32[]{:S(2)}) collective-permute-start(bf16[192,768]{1,0:T(8,128)(2,1)S(1)} %collective-permute-done.30.rest_4_), channel_id=1, source_target_pairs={{0,1},{1,0},{2,3},{3,2},{4,5},{5,4},{6,7},{7,6},{8,9},{9,8},{10,11... | collective-permute-start | bytes 884744 | tf_op jit(solution)/shard_map/ppermute | solution.py:66
  182.1 19.9 %collective-permute-start.40 = (bf16[256,896]{1,0:T(8,128)(2,1)S(1)}, bf16[256,896]{1,0:T(8,128)(2,1)S(1)}, u32[]{:S(2)}, u32[]{:S(2)}) collective-permute-start(bf16[256,896]{1,0:T(8,128)(2,1)S(1)} %get-tuple-element.184), channel_id=1, source_target_pairs={{0,16},{8,24},{16,0},{24,8},{1,17},{9,25},{17,1},{25,9},{2,18},{10... | collective-permute-start | bytes 1376264 | tf_op jit(solution)/shard_map/ppermute | solution.py:66
  304.4 29.6 %collective-permute-start.48 = (bf16[4,112,1152]{2,1,0:T(8,128)(2,1)S(1)}, bf16[4,112,1152]{2,1,0:T(8,128)(2,1)S(1)}, u32[]{:S(2)}, u32[]{:S(2)}) collective-permute-start(bf16[4,112,1152]{2,1,0:T(8,128)(2,1)S(1)} %pad_maximum_fusion), channel_id=1, source_target_pairs={{0,1},{1,0},{2,3},{3,2},{4,5},{5,4},{6,7},{7,6},{8,9},{9,8},{10,11... | collective-permute-start | bytes 3096584 | tf_op jit(solution)/shard_map/ppermute | solution.py:66
  304.7 18.0 %collective-permute-start.41 = (bf16[4,96,1152]{2,1,0:T(8,128)(2,1)}, bf16[4,96,1152]{2,1,0:T(8,128)(2,1)S(1)}, u32[]{:S(2)}, u32[]{:S(2)}) collective-permute-start(bf16[4,96,1152]{2,1,0:T(8,128)(2,1)} %get-tuple-element.85), channel_id=1, source_target_pairs={{0,1},{1,0},{2,3},{3,2},{4,5},{5,4},{6,7},{7,6},{8,9},{9,8},{10,11... | collective-permute-start | bytes 2654216 | tf_op jit(solution)/shard_map/ppermute | solution.py:66
  304.9 64.7 %collective-permute-start.62 = (bf16[4,96,3072]{2,1,0:T(8,128)(2,1)}, bf16[4,96,3072]{2,1,0:T(8,128)(2,1)S(1)}, u32[]{:S(2)}, u32[]{:S(2)}) collective-permute-start(bf16[4,96,3072]{2,1,0:T(8,128)(2,1)} %get-tuple-element.96), channel_id=1, source_target_pairs={{0,1},{1,0},{2,3},{3,2},{4,5},{5,4},{6,7},{7,6},{8,9},{9,8},{10,11... | collective-permute-start | bytes 7077896 | tf_op jit(solution)/shard_map/ppermute | solution.py:66
  321.8 50.9 %collective-permute-start.69 = (bf16[4,768,384]{2,1,0:T(8,128)(2,1)}, bf16[4,768,384]{2,1,0:T(8,128)(2,1)S(1)}, u32[]{:S(2)}, u32[]{:S(2)}) collective-permute-start(bf16[4,768,384]{2,1,0:T(8,128)(2,1)} %get-tuple-element.98), channel_id=1, source_target_pairs={{0,1},{1,0},{2,3},{3,2},{4,5},{5,4},{6,7},{7,6},{8,9},{9,8},{10,11... | collective-permute-start | bytes 7077896 | tf_op jit(solution)/shard_map/ppermute | solution.py:66
  333.0 17.2 %collective-permute-start.45 = (bf16[96,1152]{1,0:T(8,128)(2,1)S(1)}, bf16[96,1152]{1,0:T(8,128)(2,1)S(1)}, u32[]{:S(2)}, u32[]{:S(2)}) collective-permute-start(bf16[96,1152]{1,0:T(8,128)(2,1)S(1)} %pad_maximum_fusion.11), channel_id=1, source_target_pairs={{0,4},{1,5},{2,6},{3,7},{4,0},{5,1},{6,2},{7,3},{8,12},{9,13},{10,... | collective-permute-start | bytes 663560 | tf_op jit(solution)/shard_map/ppermute | solution.py:66
  368.2 22.2 %collective-permute-start.54 = (bf16[112,1152]{1,0:T(8,128)(2,1)S(1)}, bf16[112,1152]{1,0:T(8,128)(2,1)S(1)}, u32[]{:S(2)}, u32[]{:S(2)}) collective-permute-start(bf16[112,1152]{1,0:T(8,128)(2,1)S(1)} %add_convert_fusion.16), channel_id=1, source_target_pairs={{0,16},{8,24},{16,0},{24,8},{1,17},{9,25},{17,1},{25,9},{2,18},{10... | collective-permute-start | bytes 774152 | tf_op jit(solution)/shard_map/ppermute | solution.py:66
  371.7 17.5 %collective-permute-start.63 = (bf16[48,3072]{1,0:T(8,128)(2,1)S(1)}, bf16[48,3072]{1,0:T(8,128)(2,1)S(1)}, u32[]{:S(2)}, u32[]{:S(2)}) collective-permute-start(bf16[48,3072]{1,0:T(8,128)(2,1)S(1)} %get-tuple-element.174), channel_id=1, source_target_pairs={{0,4},{1,5},{2,6},{3,7},{4,0},{5,1},{6,2},{7,3},{8,12},{9,13},{10,... | collective-permute-start | bytes 884744 | tf_op jit(solution)/shard_map/ppermute | solution.py:66
  378.3 30.5 %collective-permute-start.66 = (bf16[96,3072]{1,0:T(8,128)(2,1)S(1)}, bf16[96,3072]{1,0:T(8,128)(2,1)S(1)}, u32[]{:S(2)}, u32[]{:S(2)}) collective-permute-start(bf16[96,3072]{1,0:T(8,128)(2,1)S(1)} %pad_maximum_fusion.3), channel_id=1, source_target_pairs={{0,4},{1,5},{2,6},{3,7},{4,0},{5,1},{6,2},{7,3},{8,12},{9,13},{10,... | collective-permute-start | bytes 1769480 | tf_op jit(solution)/shard_map/ppermute | solution.py:66
  383.3 24.2 %collective-permute-start.73 = (bf16[768,384]{1,0:T(8,128)(2,1)S(1)}, bf16[768,384]{1,0:T(8,128)(2,1)S(1)}, u32[]{:S(2)}, u32[]{:S(2)}) collective-permute-start(bf16[768,384]{1,0:T(8,128)(2,1)S(1)} %pad_maximum_fusion.5), channel_id=1, source_target_pairs={{0,4},{1,5},{2,6},{3,7},{4,0},{5,1},{6,2},{7,3},{8,12},{9,13},{10,... | collective-permute-start | bytes 1769480 | tf_op jit(solution)/shard_map/ppermute | solution.py:66
  388.1 19.3 %collective-permute-start.71 = (bf16[768,384]{1,0:T(8,128)(2,1)S(1)}, bf16[768,384]{1,0:T(8,128)(2,1)S(1)}, u32[]{:S(2)}, u32[]{:S(2)}) collective-permute-start(bf16[768,384]{1,0:T(8,128)(2,1)S(1)} %pad_maximum_fusion.4), channel_id=1, source_target_pairs={{0,2},{1,3},{2,0},{3,1},{4,6},{5,7},{6,4},{7,5},{8,10},{9,11},{10,... | collective-permute-start | bytes 1769480 | tf_op jit(solution)/shard_map/ppermute | solution.py:66
  389.3 19.5 %collective-permute-start.64 = (bf16[96,3072]{1,0:T(8,128)(2,1)S(1)}, bf16[96,3072]{1,0:T(8,128)(2,1)S(1)}, u32[]{:S(2)}, u32[]{:S(2)}) collective-permute-start(bf16[96,3072]{1,0:T(8,128)(2,1)S(1)} %pad_maximum_fusion.2), channel_id=1, source_target_pairs={{0,2},{1,3},{2,0},{3,1},{4,6},{5,7},{6,4},{7,5},{8,10},{9,11},{10,... | collective-permute-start | bytes 1769480 | tf_op jit(solution)/shard_map/ppermute | solution.py:66
  407.7 22.3 %collective-permute-start.74 = (bf16[768,384]{1,0:T(8,128)(2,1)S(1)}, bf16[768,384]{1,0:T(8,128)(2,1)}, u32[]{:S(2)}, u32[]{:S(2)}) collective-permute-start(bf16[768,384]{1,0:T(8,128)(2,1)S(1)} %add_convert_fusion.1), channel_id=1, source_target_pairs={{0,8},{8,0},{16,24},{24,16},{1,9},{9,1},{17,25},{25,17},{2,10},{10... | collective-permute-start | bytes 1769480 | tf_op jit(solution)/shard_map/ppermute | solution.py:66
  409.1 28.3 %collective-permute-start.67 = (bf16[96,3072]{1,0:T(8,128)(2,1)S(1)}, bf16[96,3072]{1,0:T(8,128)(2,1)}, u32[]{:S(2)}, u32[]{:S(2)}) collective-permute-start(bf16[96,3072]{1,0:T(8,128)(2,1)S(1)} %add_convert_fusion.7), channel_id=1, source_target_pairs={{0,8},{8,0},{16,24},{24,16},{1,9},{9,1},{17,25},{25,17},{2,10},{10... | collective-permute-start | bytes 1769480 | tf_op jit(solution)/shard_map/ppermute | solution.py:66
  431.2 34.7 %collective-permute-start.75 = (bf16[768,384]{1,0:T(8,128)(2,1)S(1)}, bf16[768,384]{1,0:T(8,128)(2,1)S(1)}, u32[]{:S(2)}, u32[]{:S(2)}) collective-permute-start(bf16[768,384]{1,0:T(8,128)(2,1)S(1)} %add_convert_fusion), channel_id=1, source_target_pairs={{0,16},{8,24},{16,0},{24,8},{1,17},{9,25},{17,1},{25,9},{2,18},{10... | collective-permute-start | bytes 1769480 | tf_op jit(solution)/shard_map/ppermute | solution.py:66
  438.6 33.6 %collective-permute-start.68 = (bf16[96,3072]{1,0:T(8,128)(2,1)S(1)}, bf16[96,3072]{1,0:T(8,128)(2,1)S(1)}, u32[]{:S(2)}, u32[]{:S(2)}) collective-permute-start(bf16[96,3072]{1,0:T(8,128)(2,1)S(1)} %add_convert_fusion.6), channel_id=1, source_target_pairs={{0,16},{8,24},{16,0},{24,8},{1,17},{9,25},{17,1},{25,9},{2,18},{10... | collective-permute-start | bytes 1769480 | tf_op jit(solution)/shard_map/ppermute | solution.py:66
  (92 other events, 1480.9 us)

commit v2 on v1

v2 whole, which is shorter than its diff:
```python
import functools
import math

import jax
import jax.numpy as jnp
from jax import lax
from jax.experimental import pallas as pl
from jax.experimental.pallas import tpu as pltpu
from jax.sharding import PartitionSpec as P

HEADS = 12
SEGS = 8

norm_eps = 1e-06
pool_eps = 1e-06
score_scale = 50.0
pair_weight = 256.0
masked_value = -1000000000.0

BLOCKS = 8
TILE = 128
TAIL = 128
BASE = 64

bf16 = jnp.bfloat16
f32 = jnp.float32
ANY = pl.BlockSpec(memory_space=pl.ANY)
VMEM_BYTES = 32 * 1024 * 1024


def dot(left, right):
    return jnp.dot(left, right, preferred_element_type=f32)


def dot_nt(left, right):
    return lax.dot_general(left, right, (((1,), (1,)), ((), ())), preferred_element_type=f32)


def whole(shape):
    return pl.BlockSpec(shape, lambda *_: (0,) * len(shape))


def call(
    kernel,
    grid,
    in_specs,
    out_specs,
    out_shape,
    scratch,
    flops,
    moved,
    special=0,
    after=(),
    alias=None,
    near=(),
    room=VMEM_BYTES,
):
    given, extra = len(in_specs) + 1, len(after)

    def body(*refs):
        kernel(*refs[:given], *refs[given + extra :])

    single = not isinstance(out_shape, list)
    shapes = [out_shape] if single else out_shape
    shapes = [
        shape if -1 - number in near else pltpu.HBM(shape.shape, shape.dtype)
        for number, shape in enumerate(shapes)
    ]
    run = pl.pallas_call(
        body,
        out_shape=shapes[0] if single else shapes,
        grid_spec=pltpu.PrefetchScalarGridSpec(
            num_scalar_prefetch=1,
            grid=grid,
            in_specs=in_specs + [ANY] * extra,
            out_specs=out_specs,
            scratch_shapes=scratch,
        ),
        input_output_aliases=alias or {},
        compiler_params=pltpu.CompilerParams(vmem_limit_bytes=room),
        cost_estimate=pl.CostEstimate(
            flops=int(flops), bytes_accessed=int(moved), transcendentals=int(special)
        ),
    )

    def apply(index, *operands):
        placed = [
            value if 1 + number in near else pltpu.with_memory_space_constraint(value, pltpu.HBM)
            for number, value in enumerate(operands)
        ]
        return run(index, *placed, *after)

    return apply


def shaped(shape, dtype):
    return jax.ShapeDtypeStruct(shape, dtype)


def swap(value, axis, size, bit):
    return lax.ppermute(value, axis, [(i, i ^ bit) for i in range(size)])


def fsdp_swap(value, bit):
    return swap(value, "fsdp", BLOCKS, bit)


def middle(shard):
    return shard.shape[0] // 32 * 16


def first_stage(shard):
    return fsdp_swap(shard, 2), fsdp_swap(shard, 4)


def second_stage(shard, over_x, over_y):
    half = middle(shard)
    return fsdp_swap(over_y[:half], 2), fsdp_swap(over_x[half:], 4)


def all_pieces(shard, over_x, over_y, far_top, far_low):
    half = middle(shard)
    mine = [
        (shard, 0, 0),
        (over_x, 2, 0),
        (over_y, 4, 0),
        (far_top, 6, 0),
        (far_low, 6, half),
    ]
    return mine + [(fsdp_swap(value, 1), place ^ 1, off) for value, place, off in mine]


def gather_whole(shard):
    full = lax.all_gather(shard, "fsdp", axis=0, tiled=True)
    rows = full.shape[0] // BLOCKS
    return [full[i * rows : (i + 1) * rows] for i in range(BLOCKS)]


def meta_of(pieces):
    return tuple((place, off, value.shape[0]) for value, place, off in pieces)


def arrays_of(pieces):
    return [value for value, _, _ in pieces]


def copies_of(meta, rows, refs, target, sems, index, source=None, place=None):
    copies = []
    for number, ((block, off, count), ref) in enumerate(zip(meta, refs)):
        start = pl.multiple_of((index ^ block) * rows + off, 16)
        here = pl.ds(start, count)
        copies.append(
            pltpu.make_async_copy(
                ref if source is None else ref.at[:, source],
                target.at[here] if place is None else target.at[here, place],
                sems.at[number],
            )
        )
    return copies


def start_all(copies):
    for copy in copies:
        copy.start()


def wait_all(copies):
    for copy in copies:
        copy.wait()


def columns(number, size, base=0):
    return pl.ds(pl.multiple_of(base + number * size, TILE), size)


def fill_mask(seg_row, mask_ref):
    length = seg_row.shape[1]
    keys = jnp.broadcast_to(seg_row, (TILE, length)).T
    for lo, hi, at in bands(length):
        same = keys[lo:hi] == seg_row[:, at : at + TILE]
        mask_ref[lo:hi, at : at + TILE] = jnp.where(same, 0.0, masked_value)


def bands(length):
    out = []
    for at in range(0, length, TILE):
        out.append((max(at - TILE, 0), min(at + 2 * TILE, length), at))
    return out


def two_heads(pair):
    lane = lax.broadcasted_iota(jnp.int32, (1, pair.shape[1]), 1)
    first = (lane < pair.shape[1] // 2).astype(f32).astype(bf16)
    return jnp.concatenate([pair * first, pair * (1.0 - first)], axis=0)


def twice(value):
    return jnp.concatenate([value, value], axis=1)


def pack_small(small):
    line = jnp.concatenate([jnp.pad(v, (0, -v.shape[0] % TILE)) for v in small])
    return jnp.pad(line[None], ((0, 15), (0, 0)))


def spread(table, at, size):
    count = table.shape[0]
    padded = size + -size % TILE
    block = table[:, at : at + padded].astype(bf16)
    col = lax.broadcasted_iota(jnp.int32, (1, count * size), 1)
    owner = col // size
    place = lax.broadcasted_iota(jnp.int32, (padded, count * size), 0) == col - owner * size
    value = dot(block, place.astype(f32).astype(bf16))
    keep = lax.broadcasted_iota(jnp.int32, value.shape, 0) == owner
    return jnp.sum(jnp.where(keep, value, 0.0), axis=0, keepdims=True), at + padded


def qkv_kernel(meta, small_meta, size, index_ref, tok_ref, *rest):
    pieces, rest = rest[: len(meta)], rest[len(meta) :]
    lines, rest = rest[: len(small_meta)], rest[len(small_meta) :]
    qkv_ref, table_ref, w_ref, small_ref, bias_ref, sems, small_sems = rest
    width = tok_ref.shape[1]
    part = pl.program_id(0)

    def weights(number):
        cols = columns(number, width)
        rows = width // BLOCKS
        return copies_of(meta, rows, pieces, w_ref, sems.at[number], index_ref[0], cols, cols)

    @pl.when(part == 0)
    def _():
        small = copies_of(small_meta, 16, lines, small_ref, small_sems, index_ref[0])
        start_all(small)
        for number in range(3):
            start_all(weights(number))
        wait_all(small)
        line = lax.broadcasted_iota(jnp.int32, (BLOCKS, 16 * BLOCKS), 0) * 16
        pick = line == lax.broadcasted_iota(jnp.int32, (BLOCKS, 16 * BLOCKS), 1)
        table_ref[...] = dot(pick.astype(f32).astype(bf16), small_ref[...])
        bias, _ = spread(table_ref[...], 0, size)
        bias_ref[0] = bias[:, :width]
        bias_ref[1] = jnp.zeros((1, width), f32)
        bias_ref[2] = bias[:, width:]

    wait_all(weights(part))
    scale = jnp.where(part == 0, 1.0 / math.sqrt(width // HEADS), 1.0)
    value = dot(tok_ref[...], w_ref[:, columns(part, width)]) + bias_ref[part]
    qkv_ref[...] = (value * scale).astype(bf16)


def project_qkv(index, tokens, pieces, lines, size):
    count, width = tokens.shape
    meta, small_meta = meta_of(pieces), meta_of(lines)
    used = lines[0][0].shape[1]
    return call(
        functools.partial(qkv_kernel, meta, small_meta, size),
        (3,),
        [whole((count, width))] + [ANY] * len(meta + small_meta),
        [pl.BlockSpec((count, width), lambda i, s: (0, i)), whole((BLOCKS, used))],
        [shaped((count, 3 * width), bf16), shaped((BLOCKS, used), f32)],
        [
            pltpu.VMEM((width, 3 * width), bf16),
            pltpu.VMEM((16 * BLOCKS, used), bf16),
            pltpu.VMEM((3, 1, width), f32),
            pltpu.SemaphoreType.DMA((3, len(meta))),
            pltpu.SemaphoreType.DMA((len(small_meta),)),
        ],
        count * width * width * 6,
        count * width * 8 + width * width * 6,
    )(index, tokens, *arrays_of(pieces), *arrays_of(lines))


def attend_kernel(index_ref, qkv_ref, seg_ref, *rest):
    ctx_ref, lse_ref, vt_ref, ct_ref, mask_ref = rest[-5:]
    length, width = ctx_ref.shape
    pairs = HEADS // 2
    lanes = width // pairs
    half = lanes // 2
    fill_mask(seg_ref[0].astype(f32), mask_ref)
    vt_ref[...] = qkv_ref[:, 2 * width :].T

    tiles = [(pair, band) for pair in range(pairs) for band in bands(length)]

    def scores_of(tile):
        pair, (lo, hi, at) = tile
        queries = two_heads(qkv_ref[at : at + TILE, pair * lanes : (pair + 1) * lanes])
        keys = qkv_ref[lo:hi, width + pair * lanes : width + (pair + 1) * lanes]
        return dot_nt(keys, queries)

    def probs_of(tile, scores):
        pair, (lo, hi, at) = tile
        scores = scores + twice(mask_ref[lo:hi, at : at + TILE])
        top = jnp.max(scores, axis=0, keepdims=True)
        terms = jnp.exp(scores - top)
        total = jnp.sum(terms, axis=0, keepdims=True)
        lse = top + jnp.log(total)
        for head in range(2):
            lse_ref[0, pair, head : head + 1, at : at + TILE] = lse[:, head * TILE : (head + 1) * TILE]
        return (terms * (1.0 / total)).astype(bf16)

    def put_context(tile, probs):
        pair, (lo, hi, at) = tile
        context = dot(vt_ref[pair * lanes : (pair + 1) * lanes, lo:hi], probs)
        for head in range(2):
            rows = slice(pair * lanes + head * half, pair * lanes + (head + 1) * half)
            part = context[head * half : (head + 1) * half, head * TILE : (head + 1) * TILE]
            ct_ref[rows, at : at + TILE] = part.astype(bf16)

    ready = {}
    probs = {}
    for step in range(len(tiles) + 2):
        if step < len(tiles):
            ready[step] = scores_of(tiles[step])
        if 0 <= step - 1 < len(tiles):
            probs[step - 1] = probs_of(tiles[step - 1], ready.pop(step - 1))
        if 0 <= step - 2:
            put_context(tiles[step - 2], probs.pop(step - 2))
    ctx_ref[...] = ct_ref[...].T


def attend(index, qkv, seg_rows, row, before=(), after=()):
    count, width = qkv.shape[0], qkv.shape[1] // 3
    rows, _, length = seg_rows.shape
    pairs = HEADS // 2
    return call(
        attend_kernel,
        (1,),
        [
            pl.BlockSpec((length, 3 * width), lambda i, s: (row, 0)),
            pl.BlockSpec((1, 1, length), lambda i, s: (row, 0, 0)),
        ]
        + [ANY] * len(before),
        [
            pl.BlockSpec((length, width), lambda i, s: (row, 0)),
            pl.BlockSpec((1, pairs, 2, length), lambda i, s: (row, 0, 0, 0)),
        ],
        [shaped((count, width), bf16), shaped((rows, pairs, 2, length), f32)],
        [
            pltpu.VMEM((width, length), bf16),
            pltpu.VMEM((width, length), bf16),
            pltpu.VMEM((length, length), f32),
        ],
        length * length * width * 4,
        length * width * 8,
        length * length * HEADS * 5 // 8,
        after,
        {3 + i: i for i in range(len(before))},
    )(index, qkv, seg_rows, *before)


def row_stats(values):
    mean = jnp.mean(values, axis=-1, keepdims=True)
    centred = values - mean
    spread = jnp.mean(centred * centred, axis=-1, keepdims=True)
    return centred, lax.rsqrt(spread + norm_eps)


def project_kernel(meta, sizes, index_ref, ctx_ref, tok_ref, table_ref, *rest):
    pieces, rest = rest[: len(meta)], rest[len(meta) :]
    norm_ref, root_ref, hid_ref, vec_ref, up_ref, w_ref, sems = rest
    width = w_ref.shape[0]

    @pl.when(pl.program_id(0) == 0)
    def _():
        rows = width // BLOCKS
        here = slice(0, width)
        copies = copies_of(meta, rows, pieces, w_ref, sems, index_ref[0], here, here)
        start_all(copies)
        at = sizes[0] + -sizes[0] % TILE
        line = 0
        vec_ref[...] = jnp.zeros_like(vec_ref)
        for size in sizes[1:]:
            value, at = spread(table_ref[...], at, size)
            if value.shape[1] == width:
                vec_ref[line : line + 1] = value
                line += 1
            else:
                up_ref[...] = value
        wait_all(copies)

    def finish(here, product):
        summed = tok_ref[here].astype(f32) + (product + vec_ref[0:1])
        centred, root = row_stats(summed)
        normed = centred * root
        norm_ref[here] = normed
        root_ref[here] = root
        hid_ref[here] = (normed * vec_ref[1:2] + vec_ref[2:3]).astype(bf16)

    in_turn(ctx_ref.shape[0], lambda here: dot(ctx_ref[here], w_ref[...]), finish)


def in_turn(count, begin, finish, size=2 * TILE):
    last = None
    for at in range(0, count, size):
        here = slice(at, at + size)
        value = begin(here)
        if last is not None:
            finish(*last)
        last = (here, value)
    finish(*last)


def project(index, context, tokens, table, pieces, sizes, step=512):
    count, width = tokens.shape
    inner = 4 * width
    meta = meta_of(pieces)
    rows = pl.BlockSpec((step, width), lambda i, s: (i, 0))
    return call(
        functools.partial(project_kernel, meta, sizes),
        (count // step,),
        [rows, rows, whole(table.shape)] + [ANY] * len(meta),
        [
            rows,
            pl.BlockSpec((step, 1), lambda i, s: (i, 0)),
            rows,
            whole((SEGS, width)),
            whole((1, inner)),
        ],
        [
            shaped((count, width), f32),
            shaped((count, 1), f32),
            shaped((count, width), bf16),
            shaped((SEGS, width), f32),
            shaped((1, inner), f32),
        ],
        [pltpu.VMEM((width, width), bf16), pltpu.SemaphoreType.DMA((len(meta),))],
        count * width * width * 2,
        count * width * 10 + width * width * 2,
    )(index, context, tokens, table, *arrays_of(pieces))


def gelu_parts(value):
    share = 0.5 * lax.erf(value * math.sqrt(0.5)) + 0.5
    bell = jnp.exp2(value * value * (-0.5 / math.log(2.0)))
    return value * share, share + value * bell * (1.0 / math.sqrt(2.0 * math.pi))


def up_kernel(meta, index_ref, hid_ref, bias_ref, *rest):
    pieces, rest = rest[: len(meta)], rest[len(meta) :]
    act_ref, slope_ref, w_ref, sems = rest
    tile = act_ref.shape[1]
    width = w_ref.shape[0]
    step = pl.program_id(0)

    def weights(number):
        source, place = columns(number, tile, width), columns(number, tile)
        rows = width // BLOCKS
        return copies_of(meta, rows, pieces, w_ref, sems.at[number], index_ref[0], source, place)

    @pl.when(step == 0)
    def _():
        for number in range(sems.shape[0]):
            start_all(weights(number))

    wait_all(weights(step))
    wide = 256

    def begin(cols):
        w = w_ref[:, columns(step, tile)] if wide == tile else w_ref[:, pl.ds(
            pl.multiple_of(step * tile + cols.start, wide), wide
        )]
        return dot(hid_ref[...], w) + bias_ref[:, cols]

    def finish(cols, value):
        act, slope = gelu_parts(value)
        act_ref[:, cols] = act.astype(bf16)
        slope_ref[:, cols] = slope.astype(bf16)

    in_turn(tile, begin, finish, wide)


def up(index, hidden, bias, pieces, after=(), tile=768):
    count, width = hidden.shape
    inner = bias.shape[1]
    meta = meta_of(pieces)
    out = pl.BlockSpec((count, tile), lambda i, s: (0, i))
    return call(
        functools.partial(up_kernel, meta),
        (inner // tile,),
        [whole((count, width)), pl.BlockSpec((1, tile), lambda i, s: (0, i))] + [ANY] * len(meta),
        [out, out],
        [shaped((count, inner), bf16), shaped((count, inner), bf16)],
        [
            pltpu.VMEM((width, inner), bf16),
            pltpu.SemaphoreType.DMA((inner // tile, len(meta))),
        ],
        count * width * inner * 2,
        count * (width * 2 + inner * 4) + width * inner * 2,
        count * inner * 4,
        after,
    )(index, hidden, bias, *arrays_of(pieces))


def down_kernel(meta, index_ref, act_ref, norm_ref, vec_ref, seg_ref, pos_ref, *rest):
    pieces, rest = rest[: len(meta)], rest[len(meta) :]
    res_ref, norm2_ref, root_ref, pay_ref, pool_ref, stat_ref, w_ref, sum_ref, num_ref, sems = rest
    step = pl.program_id(0)
    steps = pl.num_programs(0)
    width = res_ref.shape[1]
    inner = w_ref.shape[0]
    copies = copies_of(meta, inner // BLOCKS, pieces, w_ref, sems, index_ref[0])

    @pl.when(step == 0)
    def _():
        start_all(copies)
        sum_ref[...] = jnp.zeros_like(sum_ref)
        num_ref[...] = jnp.zeros_like(num_ref)
        wait_all(copies)

    seg = seg_ref[0]
    wanted = lax.broadcasted_iota(jnp.int32, (SEGS, seg.shape[1]), 0)
    member = (wanted == seg).astype(f32)
    member_b = member.astype(bf16)
    own = pl.ds(pl.multiple_of(step // (steps * SEGS // sum_ref.shape[0]) * SEGS, SEGS), SEGS)
    num_ref[own] += jnp.broadcast_to(jnp.sum(member, axis=1, keepdims=True), (SEGS, TAIL))

    def finish(here, product):
        hidden = norm_ref[here] * vec_ref[1:2] + vec_ref[2:3]
        summed = hidden + (product + vec_ref[3:4])
        centred, root = row_stats(summed)
        normed = centred * root
        result = normed * vec_ref[4:5] + vec_ref[5:6]
        norm2_ref[here] = normed
        root_ref[here] = root
        high = result.astype(bf16)
        res_ref[here] = high
        low = (result - high.astype(f32)).astype(bf16)
        sum_ref[own] += dot(member_b[:, here], high) + dot(member_b[:, here], low)

    in_turn(act_ref.shape[0], lambda here: dot(act_ref[here], w_ref[...]), finish)

    @pl.when(step == steps - 1)
    def _():
        counts = num_ref[:, 0:1]
        pooled = sum_ref[...] / counts
        scale = lax.rsqrt(jnp.mean(pooled * pooled, axis=-1, keepdims=True) + pool_eps)
        pool_ref[...] = pooled
        lane = lax.broadcasted_iota(jnp.int32, (pooled.shape[0], TAIL), 1)
        stat_ref[...] = jnp.where(lane == 0, scale, counts)
        pay_ref[:, :width] = (pooled * scale).astype(bf16)
        partner = pos_ref[...]
        digit = jnp.where(lane == 0, partner // BASE, partner % BASE)
        pay_ref[:, width:] = jnp.where(lane < 2, digit, 0).astype(f32).astype(bf16)


def down(index, activated, normed, vectors, seg_rows, positive, pieces, step=512):
    count, width = normed.shape
    inner = activated.shape[1]
    rows, _, length = seg_rows.shape
    own = rows * SEGS
    per_row = length // step
    meta = meta_of(pieces)
    block = pl.BlockSpec((step, width), lambda i, s: (i, 0))
    return call(
        functools.partial(down_kernel, meta),
        (count // step,),
        [
            pl.BlockSpec((step, inner), lambda i, s: (i, 0)),
            block,
            whole(vectors.shape),
            pl.BlockSpec((1, 1, step), lambda i, s: (i // per_row, 0, i % per_row)),
            whole((own, 1)),
        ]
        + [ANY] * len(meta),
        [
            block,
            block,
            pl.BlockSpec((step, 1), lambda i, s: (i, 0)),
            whole((own, width + TAIL)),
            whole((own, width)),
            whole((own, TAIL)),
        ],
        [
            shaped((count, width), bf16),
            shaped((count, width), f32),
            shaped((count, 1), f32),
            shaped((own, width + TAIL), bf16),
            shaped((own, width), f32),
            shaped((own, TAIL), f32),
        ],
        [
            pltpu.VMEM((inner, width), bf16),
            pltpu.VMEM((own, width), f32),
            pltpu.VMEM((own, TAIL), f32),
            pltpu.SemaphoreType.DMA((len(meta),)),
        ],
        count * width * inner * 2,
        count * (width * 10 + inner * 2) + width * inner * 2,
        near=(3, 5, -4, -5, -6),
    )(index, activated, normed, vectors, seg_rows, positive, *arrays_of(pieces))


def segment_of(row, own, cores, chips, planes):
    block = row // own
    plane, chip, core = block % planes, block // planes % chips, block // (planes * chips)
    return ((plane * chips + chip) * cores + core) * own + row % own


def contrast_kernel(layout, place_ref, own_ref, pos_ref, pool_ref, stat_ref, *rest):
    pieces, (loss_ref, grad_ref, all_ref, sems) = rest[:-4], rest[-4:]
    copies, at = [], 0
    for number, piece in enumerate(pieces):
        here = all_ref.at[at : at + piece.shape[0]]
        copies.append(pltpu.make_async_copy(piece, here, sems.at[number]))
        at += piece.shape[0]
    for copy in copies:
        copy.start()
    for copy in copies:
        copy.wait()
    total = all_ref.shape[0]
    own, width = pool_ref.shape
    factor = score_scale / width
    block = min(total, 512)
    flip, first = place_ref[0], place_ref[1]
    mine = own_ref[:, :width]
    mine_id = lax.broadcasted_iota(jnp.int32, (own, total), 0) + first
    other_id = segment_of(lax.broadcasted_iota(jnp.int32, (1, total), 1), own, *layout) ^ flip
    logits = dot_nt(mine, all_ref[:, :width]) * factor
    logits = jnp.where(mine_id == other_id, masked_value, logits)
    top = jnp.max(logits, axis=1, keepdims=True)
    log_own = top + jnp.log(jnp.sum(jnp.exp(logits - top), axis=1, keepdims=True))
    is_positive = other_id == pos_ref[...]
    picked = jnp.sum(jnp.where(is_positive, logits, 0.0), axis=1, keepdims=True)
    loss_ref[...] = log_own - picked
    d_logits = pair_weight * (jnp.exp(logits - log_own) - is_positive.astype(f32))
    d_emb = dot(d_logits.astype(bf16), all_ref[:, :width])
    lane = lax.broadcasted_iota(jnp.int32, (SEGS, TAIL), 1)
    digits = jnp.where(lane == 0, float(BASE), jnp.where(lane == 1, 1.0, 0.0)).astype(bf16)
    for at in range(0, total, block):
        rows = slice(at, at + block)
        table = dot_nt(all_ref[:, :width], all_ref[rows, :width]) * factor
        left = lax.broadcasted_iota(jnp.int32, (total, block), 0)
        right = lax.broadcasted_iota(jnp.int32, (total, block), 1) + at
        table = jnp.where(left == right, masked_value, table)
        top = jnp.max(table, axis=0, keepdims=True)
        log_all = top + jnp.log(jnp.sum(jnp.exp(table - top), axis=0, keepdims=True))
        partner = dot_nt(digits, all_ref[rows, width:])[0:1].astype(jnp.int32)
        chosen = partner == mine_id[:, rows]
        back = pair_weight * (jnp.exp(logits[:, rows] - log_all) - chosen.astype(f32))
        d_emb += dot(back.astype(bf16), all_ref[rows, :width])
    d_emb = d_emb * factor
    scale, counts = stat_ref[:, 0:1], stat_ref[:, 1:2]
    pooled = pool_ref[...]
    along = jnp.mean(d_emb * pooled, axis=-1, keepdims=True)
    grad_ref[...] = (d_emb * scale - pooled * (scale * scale * scale * along)) / counts


def contrast(place, layout, everyone, payload, positive, pooled, stats):
    own, width = pooled.shape
    total = sum(v.shape[0] for v in everyone)
    return call(
        functools.partial(contrast_kernel, layout),
        (1,),
        [whole(v.shape) for v in (payload, positive, pooled, stats)] + [ANY] * len(everyone),
        [whole((own, 1)), whole((own, width))],
        [shaped((own, 1), f32), shaped((own, width), f32)],
        [
            pltpu.VMEM((total, width + TAIL), bf16),
            pltpu.SemaphoreType.DMA((len(everyone),)),
        ],
        total * total * width * 2,
        total * width * 2,
        total * total,
        near=(1, 2, 3, 4, -1, -2),
    )(place, payload, positive, pooled, stats, *everyone)


def norm_back(d_out, normed, root, gain):
    scaled = d_out * gain
    mean = jnp.mean(scaled, axis=-1, keepdims=True)
    along = jnp.mean(scaled * normed, axis=-1, keepdims=True)
    return root * (scaled - mean - normed * along)


def column_sum(values):
    return jnp.sum(values, axis=0, keepdims=True)


def norm2_kernel(turns, index_ref, og_ref, norm_ref, root_ref, seg_ref, gain_ref, dp_ref, *rest):
    act_ref, dsum_ref, ddown_ref, vec_ref, keep_ref, send_ref, dt_ref = rest
    step = pl.program_id(0)
    chunk, width = og_ref.shape
    own = dp_ref.shape[0]

    @pl.when(step == 0)
    def _():
        vec_ref[...] = jnp.zeros_like(vec_ref)

    @pl.when(step < turns)
    def _():
        row = step // (turns * SEGS // own)
        pool = dp_ref[pl.ds(pl.multiple_of(row * SEGS, SEGS), SEGS)]
        high = pool.astype(bf16)
        left = pool - high.astype(f32)
        mid = left.astype(bf16)
        low = (left - mid.astype(f32)).astype(bf16)
        pad = jnp.zeros((TILE - 3 * SEGS, width), bf16)
        table = jnp.concatenate([high, mid, low, pad], axis=0)
        lane = lax.broadcasted_iota(jnp.int32, (TILE, TILE), 1)

        def begin(here):
            member = (lane % SEGS == seg_ref[here]).astype(f32).astype(bf16)
            return dot(member, table)

        def finish(here, shared):
            d_res = og_ref[here].astype(f32) + shared
            normed = norm_ref[here]
            d_sum = norm_back(d_res, normed, root_ref[here], gain_ref[...])
            d_down = d_sum.astype(bf16)
            dsum_ref[here] = d_sum
            ddown_ref[here] = d_down
            dt_ref[:, columns(step, chunk) if chunk == TILE else pl.ds(
                pl.multiple_of(step * chunk + here.start, TILE), TILE
            )] = d_down.T
            vec_ref[0:1] += column_sum(d_down.astype(f32))
            vec_ref[1:2] += column_sum(d_res * normed)
            vec_ref[2:3] += column_sum(d_res)

        in_turn(chunk, begin, finish, TILE)

    @pl.when(step >= turns)
    def _():
        grad = dot(dt_ref[...], act_ref[...]).astype(bf16)
        half = grad.shape[1] // 2
        odd = index_ref[0] % 2 == 1
        keep_ref[0] = jnp.where(odd, grad[:, half:], grad[:, :half])
        send_ref[0] = jnp.where(odd, grad[:, :half], grad[:, half:])


def norm2(index, out_grad, normed, root, seg_col, gain, d_pool, activated, turns=4):
    count, width = out_grad.shape
    inner = activated.shape[1]
    tile = inner // 4
    own = d_pool.shape[0]
    first = lambda i: jnp.minimum(i, turns - 1)
    then = lambda i: jnp.maximum(i - turns, 0)
    block = pl.BlockSpec((count // turns, width), lambda i, s: (first(i), 0))
    column = pl.BlockSpec((count // turns, 1), lambda i, s: (first(i), 0))
    grads = pl.BlockSpec((1, width, tile // 2), lambda i, s: (then(i), 0, 0))
    return call(
        functools.partial(norm2_kernel, turns),
        (turns + 4,),
        [
            block,
            block,
            column,
            column,
            whole((1, width)),
            whole((own, width)),
            pl.BlockSpec((count, tile), lambda i, s: (0, (s[0] // 2) ^ then(i))),
        ],
        [block, block, whole((SEGS, width)), grads, grads],
        [
            shaped((count, width), f32),
            shaped((count, width), bf16),
            shaped((SEGS, width), f32),
            shaped((4, width, tile // 2), bf16),
            shaped((4, width, tile // 2), bf16),
        ],
        [pltpu.VMEM((width, count), bf16)],
        count * width * inner * 2,
        count * (width * 12 + inner * 2) + width * inner * 2,
        near=(5, 6, -1, -2, -3, -4, -5),
    )(index, out_grad, normed, root, seg_col, gain, d_pool, activated)


def put_turned(source_ref, target_ref, turn_ref, index):
    turn_ref[...] = source_ref[...].T
    rows = turn_ref.shape[0] // BLOCKS
    for place in range(BLOCKS):
        block = index ^ ((place % 4) * 2 + place // 4)
        start = pl.multiple_of(block * rows, 16)
        target_ref[place * rows : (place + 1) * rows] = turn_ref[pl.ds(start, rows)]


def up_back_kernel(
    down_meta, up_meta, first, before, index_ref, ddown_ref, slope_ref, hid_ref, *rest
):
    low_pieces, rest = rest[: len(down_meta)], rest[len(down_meta) :]
    up_pieces, rest = rest[: len(up_meta)], rest[len(up_meta) + before :]
    dhid_ref, bias_ref, keep_ref, send_ref, wd_ref, wu_ref, turn_ref, ht_ref, sems, up_sems = rest
    step = pl.program_id(0)
    tile = slope_ref.shape[1]
    width = ht_ref.shape[0]
    index = index_ref[0]
    steps = sems.shape[0]

    def weights(number):
        copies = []
        here = wd_ref.at[pl.ds(pl.multiple_of(number * tile, tile), tile)]
        for piece, ((place, off, size), ref) in enumerate(zip(down_meta, low_pieces)):
            start = pl.multiple_of(((index ^ place) % 2) * (tile // 2) + off, 16)
            copies.append((place // 2 - first, ref, here.at[pl.ds(start, size)], sems.at[number, piece]))
        cols = columns((index // 2) ^ (number + first), tile, width)
        high = copies_of(
            up_meta, width // BLOCKS, up_pieces, wu_ref.at[number], up_sems.at[number], index, cols
        )
        return copies, high

    def rows_of(number):
        low, _ = weights(number)
        return [
            pltpu.make_async_copy(ref, here, sem) for place, ref, here, sem in low if place == number
        ]

    @pl.when(step == 0)
    def _():
        for number in range(steps):
            start_all(rows_of(number))
            start_all(weights(number)[1])
        put_turned(hid_ref, ht_ref, turn_ref, index)

    for number in range(steps):

        @pl.when(step == number)
        def _():
            wait_all(rows_of(number))

    wide = 256
    parts = []

    def begin(cols):
        rows = pl.ds(pl.multiple_of(step * tile + cols.start, wide), wide)
        return dot_nt(ddown_ref[...], wd_ref[rows])

    def finish(cols, d_act):
        d_up = (d_act * slope_ref[:, cols].astype(f32)).astype(bf16)
        bias_ref[:, cols] = column_sum(d_up.astype(f32))
        parts.append(d_up)

    in_turn(tile, begin, finish, wide)
    d_up = jnp.concatenate(parts, axis=1)
    grad = dot(ht_ref[...], d_up).astype(bf16)
    half = width // 2
    keep_ref[...] = grad[:half].reshape(keep_ref.shape)
    send_ref[...] = grad[half:].reshape(send_ref.shape)
    wait_all(weights(step)[1])
    share = dot_nt(d_up, wu_ref[step])

    @pl.when(step == 0)
    def _():
        dhid_ref[...] = share

    @pl.when(step > 0)
    def _():
        dhid_ref[...] += share


def up_back(index, d_down, slope, hidden, down_pieces, up_pieces, first, steps, before=(), after=()):
    count, width = d_down.shape
    inner = slope.shape[1]
    tile = inner // 4
    part = width // BLOCKS
    down_meta, up_meta = meta_of(down_pieces), meta_of(up_pieces)
    place = lambda i, s: (s[0] // 2) ^ (i + first)
    grads = pl.BlockSpec((4, part, tile), lambda i, s: (0, 0, place(i, s)))
    given = 4 + len(down_meta) + len(up_meta)
    return call(
        functools.partial(up_back_kernel, down_meta, up_meta, first, len(before)),
        (steps,),
        [
            whole((count, width)),
            pl.BlockSpec((count, tile), lambda i, s: (0, place(i, s))),
            whole((count, width)),
        ]
        + [ANY] * (len(down_meta) + len(up_meta) + len(before)),
        [
            whole((count, width)),
            pl.BlockSpec((1, tile), lambda i, s: (0, place(i, s))),
            grads,
            grads,
        ],
        [
            shaped((count, width), f32),
            shaped((1, inner), f32),
            shaped((4, part, inner), bf16),
            shaped((4, part, inner), bf16),
        ],
        [
            pltpu.VMEM((steps * tile, width), bf16),
            pltpu.VMEM((steps, width, tile), bf16),
            pltpu.VMEM((width, count), bf16),
            pltpu.VMEM((width, count), bf16),
            pltpu.SemaphoreType.DMA((steps, len(down_meta))),
            pltpu.SemaphoreType.DMA((steps, len(up_meta))),
        ],
        count * width * tile * 6 * steps,
        count * (width * 8 + inner) + width * inner * 6,
        0,
        after,
        {given + i: 1 + i for i in range(len(before))},
        (1, -1, -2, -3, -4) + tuple(range(given, given + len(before))),
        40 * 1024 * 1024,
    )(index, d_down, slope, hidden, *arrays_of(down_pieces), *arrays_of(up_pieces), *before)


def cut_vector(vector, size, index):
    width = vector.shape[1]
    owner = lax.broadcasted_iota(jnp.int32, (BLOCKS, width), 1) // size
    wanted = lax.broadcasted_iota(jnp.int32, (BLOCKS, width), 0) ^ index
    rows = jnp.where(owner == wanted, vector, 0.0).astype(bf16)
    source = lax.broadcasted_iota(jnp.int32, (width, 1), 0)
    place = source - source // size * size == lax.broadcasted_iota(jnp.int32, (width, TILE), 1)
    return dot(rows, place.astype(f32).astype(bf16))


def norm1_kernel(meta, parts, index_ref, *rest):
    dhids, rest = rest[:parts], rest[parts:]
    dsum_ref, norm_ref, root_ref, gain_ref, ctx_ref, other_ref, up_ref, *rest = rest
    pieces, rest = rest[: len(meta)], rest[len(meta) :]
    dattn_ref, dctx_ref, keep_ref, send_ref, w_ref, acc_ref, vec_ref, sems = rest
    step = pl.program_id(0)
    width = w_ref.shape[0]
    rows = width // BLOCKS

    @pl.when(step == 0)
    def _():
        here = slice(0, width)
        copies = copies_of(meta, rows, pieces, w_ref, sems, index_ref[0], here, here)
        start_all(copies)
        vec_ref[...] = jnp.zeros_like(vec_ref)
        acc_ref[...] = jnp.zeros_like(acc_ref)
        wait_all(copies)

    parts = []

    def begin(here):
        d_hid = dsum_ref[here]
        for dhid_ref in dhids:
            d_hid = d_hid + dhid_ref[here]
        normed = norm_ref[here]
        d_sum = norm_back(d_hid, normed, root_ref[here], gain_ref[...])
        d_attn = d_sum.astype(bf16)
        dattn_ref[here] = d_sum
        vec_ref[0:1] += column_sum(d_attn.astype(f32))
        vec_ref[1:2] += column_sum(d_hid * normed)
        vec_ref[2:3] += column_sum(d_hid)
        parts.append(d_attn)
        return d_attn

    def finish(here, d_attn):
        dctx_ref[here] = dot_nt(d_attn, w_ref[...]).astype(bf16)

    in_turn(dsum_ref.shape[0], begin, finish)
    acc_ref[...] += dot(ctx_ref[...].T, jnp.concatenate(parts, axis=0))

    @pl.when(step == pl.num_programs(0) - 1)
    def _():
        index = index_ref[0]
        vectors = [vec_ref[i : i + 1] for i in range(3)] + [other_ref[i : i + 1] for i in range(3)]
        top = [cut_vector(vector, rows, index) for vector in vectors]
        top = jnp.concatenate(top, axis=1)
        size = up_ref.shape[1] // BLOCKS
        line = lax.broadcasted_iota(jnp.int32, (16, width), 0)
        pad = jnp.zeros((1, width - size), f32)
        for place in range(4):
            for target, core in ((keep_ref, 0), (send_ref, 1)):
                number = 2 * place + core
                block = index ^ number
                start = pl.multiple_of(block * rows, 16)
                target[place, :rows] = acc_ref[pl.ds(start, rows)].astype(bf16)
                low = up_ref[:, pl.ds(pl.multiple_of(block * size, size), size)]
                low = jnp.concatenate([low, pad], axis=1)
                extra = jnp.where(line == 0, top[number : number + 1], 0.0)
                extra = jnp.where(line == 1, low, extra)
                target[place, rows:] = extra.astype(bf16)


def norm1(
    index, d_hiddens, d_summed, normed, root, gain, context, sums, sums_up, pieces, after=(), step=512
):
    count, width = d_summed.shape
    meta = meta_of(pieces)
    part = width // BLOCKS + 16
    block = pl.BlockSpec((step, width), lambda i, s: (i, 0))
    return call(
        functools.partial(norm1_kernel, meta, len(d_hiddens)),
        (count // step,),
        [block] * len(d_hiddens)
        + [
            block,
            block,
            pl.BlockSpec((step, 1), lambda i, s: (i, 0)),
            whole((1, width)),
            block,
            whole(sums.shape),
            whole(sums_up.shape),
        ]
        + [ANY] * len(meta),
        [block, block, whole((4, part, width)), whole((4, part, width))],
        [
            shaped((count, width), f32),
            shaped((count, width), bf16),
            shaped((4, part, width), bf16),
            shaped((4, part, width), bf16),
        ],
        [
            pltpu.VMEM((width, width), bf16),
            pltpu.VMEM((width, width), f32),
            pltpu.VMEM((SEGS, width), f32),
            pltpu.SemaphoreType.DMA((len(meta),)),
        ],
        count * width * width * 4,
        count * width * 20 + width * width * 4,
        0,
        after,
        near=tuple(range(1, 2 + len(d_hiddens))) + (-1, -2, -3, -4),
    )(
        index, *d_hiddens, d_summed, normed, root, gain, context, sums, sums_up, *arrays_of(pieces)
    )


def attend_back_kernel(
    first, index_ref, q_ref, k_ref, v_ref, dctx_ref, lse_ref, seg_ref, tok_ref, *rest
):
    dq_ref, dk_ref, dv_ref, keep_ref, send_ref = rest[:5]
    mask_ref, turn_ref, tt_ref, kt_ref, two_ref, pt_ref, both_ref = rest[5:]
    rows, _, length = seg_ref.shape
    lanes = 2 * tok_ref.shape[1] // HEADS
    half = lanes // 2
    group = q_ref.shape[1] // lanes
    inv_root = 1.0 / math.sqrt(half)

    @pl.when(pl.program_id(0) == 0)
    def _():
        put_turned(tok_ref, tt_ref, turn_ref, index_ref[0])
        for row in range(rows):
            fill_mask(seg_ref[row].astype(f32), mask_ref.at[row])

    tiles = [
        (pair, row, band) for pair in range(group) for row in range(rows) for band in bands(length)
    ]
    for pair in range(group):
        for row in range(rows):
            here = slice(row * length, (row + 1) * length)
            kt_ref[pair, row] = k_ref[here, pair * lanes : (pair + 1) * lanes].T

    def begin(tile):
        pair, row, (lo, hi, at) = tile
        cols = slice(pair * lanes, (pair + 1) * lanes)
        base = row * length
        queries = two_heads(q_ref[base + at : base + at + TILE, cols])
        d_context = two_heads(dctx_ref[base + at : base + at + TILE, cols])
        two_ref[0, pair, row, 2 * at : 2 * at + 2 * TILE] = queries
        two_ref[1, pair, row, 2 * at : 2 * at + 2 * TILE] = d_context
        scores = dot_nt(k_ref[base + lo : base + hi, cols], queries)
        return scores, dot_nt(v_ref[base + lo : base + hi, cols], d_context)

    def middle_part(tile, scores, d_probs):
        pair, row, (lo, hi, at) = tile
        lse = jnp.concatenate(
            [lse_ref[row, pair, head : head + 1, at : at + TILE] for head in range(2)], axis=1
        )
        probs = jnp.exp(scores + twice(mask_ref[row, lo:hi, at : at + TILE]) - lse)
        inner = jnp.sum(d_probs * probs, axis=0, keepdims=True)
        d_scores = (probs * (d_probs - inner)).astype(bf16)
        pt_ref[0, pair, row, lo:hi, 2 * at : 2 * at + 2 * TILE] = d_scores
        pt_ref[1, pair, row, lo:hi, 2 * at : 2 * at + 2 * TILE] = probs.astype(bf16)
        return d_scores

    def put(tile, kind, value):
        pair, row, (_, _, at) = tile
        here = slice(row * length + at, row * length + at + TILE)
        cols = slice((3 * pair + kind) * lanes, (3 * pair + kind + 1) * lanes)
        both_ref[here, cols] = value.astype(bf16)

    def end(tile, d_scores):
        pair, row, (lo, hi, at) = tile
        dq = dot(kt_ref[pair, row, :, lo:hi], d_scores) * inv_root
        dq = jnp.concatenate([dq[:half, :TILE], dq[half:, TILE:]], axis=0)
        put(tile, 0, dq.T)

    def end_keys(tile):
        pair, row, (lo, hi, at) = tile
        cols = slice(2 * lo, 2 * hi)
        for kind in range(2):
            value = dot(
                pt_ref[kind, pair, row, at : at + TILE, cols], two_ref[kind, pair, row, cols]
            )
            put(tile, 1 + kind, value)

    ready = {}
    done = {}
    for step in range(len(tiles) + 3):
        if step < len(tiles):
            ready[step] = begin(tiles[step])
        if 0 <= step - 1 < len(tiles):
            done[step - 1] = middle_part(tiles[step - 1], *ready.pop(step - 1))
        if 0 <= step - 2 < len(tiles):
            end(tiles[step - 2], done.pop(step - 2))
        if 0 <= step - 3 < len(tiles):
            end_keys(tiles[step - 3])
    both = both_ref[...]
    for pair in range(group):
        for kind, target in enumerate((dq_ref, dk_ref, dv_ref)):
            cols = slice((3 * pair + kind) * lanes, (3 * pair + kind + 1) * lanes)
            target[:, pair * lanes : (pair + 1) * lanes] = both[:, cols]
    grad = dot(tt_ref[...], both).astype(bf16)
    width = grad.shape[0]
    part = width // BLOCKS
    span = both.shape[1]
    col = lax.broadcasted_iota(jnp.int32, (1, span), 1)
    kind = col // lanes % 3
    place = (pl.program_id(0) * group + first + col // (3 * lanes)) * lanes + col % lanes
    owner = jnp.where(kind == 1, -1, (place + jnp.where(kind == 2, width, 0)) // (2 * part))
    sums = column_sum(both.astype(f32))
    line = lax.broadcasted_iota(jnp.int32, (16, span), 0)
    for block in range(BLOCKS):
        target, core = (keep_ref, 0) if block < 4 else (send_ref, 1)
        target[block % 4, :part] = grad[block * part : (block + 1) * part]
        here = owner == (index_ref[0] ^ (2 * (block % 4) + core))
        extra = jnp.where(line == 0, jnp.where(here, sums, 0.0), 0.0)
        target[block % 4, part:] = extra.astype(bf16)


def attend_back(
    index, qkv, d_context, lse, seg_rows, tokens, first, pairs, after=(), group=2
):
    count, width = tokens.shape
    rows, _, length = seg_rows.shape
    every = HEADS // 2
    lanes = width // every
    part = width // BLOCKS + 16
    wide = group * lanes
    column = lambda place: pl.BlockSpec((count, wide), lambda i, s: (0, place // group + i))
    out = pl.BlockSpec((count, wide), lambda i, s: (0, i))
    grads = pl.BlockSpec((4, part, 3 * wide), lambda i, s: (0, 0, i))
    return call(
        functools.partial(attend_back_kernel, first),
        (pairs // group,),
        [
            column(first),
            column(every + first),
            column(2 * every + first),
            column(first),
            pl.BlockSpec((rows, group, 2, length), lambda i, s: (0, first // group + i, 0, 0)),
            whole((rows, 1, length)),
            whole((count, width)),
        ],
        [out, out, out, grads, grads],
        [
            shaped((count, pairs * lanes), bf16),
            shaped((count, pairs * lanes), bf16),
            shaped((count, pairs * lanes), bf16),
            shaped((4, part, pairs * 3 * lanes), bf16),
            shaped((4, part, pairs * 3 * lanes), bf16),
        ],
        [
            pltpu.VMEM((rows, length, length), f32),
            pltpu.VMEM((width, count), bf16),
            pltpu.VMEM((width, count), bf16),
            pltpu.VMEM((group, rows, lanes, length), bf16),
            pltpu.VMEM((2, group, rows, 2 * length, lanes), bf16),
            pltpu.VMEM((2, group, rows, length, 2 * length), bf16),
            pltpu.VMEM((count, 3 * wide), bf16),
        ],
        count * pairs * lanes * (width * 6 + length * 6),
        count * pairs * lanes * 14 + count * width * 2,
        count * length * pairs * 5 // 4,
        after,
        near=(4, -1, -2, -3, -4, -5),
    )(index, qkv, qkv, qkv, d_context, lse, seg_rows, tokens)


def input_kernel(meta, parts, index_ref, dattn_ref, *rest):
    grads, rest = rest[: 3 * parts], rest[3 * parts :]
    pieces, rest = rest[: len(meta)], rest[len(meta) :]
    out_ref, w_ref, sems = rest
    width = out_ref.shape[1]
    step = width // parts
    first = pl.program_id(0) == 0

    def weights(kind):
        cols = columns(kind, width)
        rows = width // BLOCKS
        return copies_of(meta, rows, pieces, w_ref, sems.at[kind], index_ref[0], cols, cols)

    @pl.when(first)
    def _():
        for kind in range(3):
            start_all(weights(kind))

    total = dattn_ref[...]
    for kind in range(3):

        @pl.when(first)
        def _():
            wait_all(weights(kind))

        for part in range(parts):
            at = kind * width + part * step
            total += dot_nt(grads[kind * parts + part][...], w_ref[:, at : at + step])
    out_ref[...] = total


def input_grad(index, d_attn, grads, pieces, after=(), step=512):
    count, width = d_attn.shape
    meta = meta_of(pieces)
    parts = len(grads) // 3
    block = pl.BlockSpec((step, width), lambda i, s: (i, 0))
    return call(
        functools.partial(input_kernel, meta, parts),
        (count // step,),
        [block]
        + [pl.BlockSpec((step, g.shape[1]), lambda i, s: (i, 0)) for g in grads]
        + [ANY] * len(meta),
        block,
        shaped((count, width), f32),
        [pltpu.VMEM((width, 3 * width), bf16), pltpu.SemaphoreType.DMA((3, len(meta)))],
        count * width * width * 6,
        count * width * 14 + width * width * 6,
        0,
        after,
        near=tuple(range(1, 2 + len(grads))),
    )(index, d_attn, *grads, *arrays_of(pieces))


def rounded(value):
    return lax.optimization_barrier(value.astype(bf16))


def add(*values):
    total = values[0].astype(f32)
    for value in values[1:]:
        total = total + value.astype(f32)
    return total


def along_z(value, pairs):
    return lax.ppermute(value, "batch", pairs)


class Sum:
    def __init__(self, planes, keeps, sends, line):
        self.planes, self.keeps, self.line = planes, keeps, line
        self.arrived = [fsdp_swap(send, 1) for send in sends]
        self.stages = [self.over_core, self.over_far, self.over_chips, self.over_z, self.over_middle]

    def next(self, clock):
        if clock is not None:
            *self.arrived, _ = lax.optimization_barrier((*self.arrived, clock))
        return self.stages.pop(0)(*self.arrived)

    def over_core(self, *others):
        rows = self.keeps[0].shape[1]
        half = rows // 32 * 16
        cuts = [(0, 0, rows), (1, 0, rows), (2, 0, rows), (3, 0, half), (3, half, rows)]
        self.blocks = []
        for place, lo, hi in cuts:
            sums = [
                add(keep[place, lo:hi], other[place, lo:hi]).astype(bf16)
                for keep, other in zip(self.keeps, others)
            ]
            self.blocks.append(rounded(jnp.concatenate(sums, axis=1)))
        self.half = half
        self.arrived = [fsdp_swap(self.blocks[3], 2), fsdp_swap(self.blocks[4], 4)]
        return self.blocks[3:]

    def over_far(self, top, low):
        _, over_x, over_y, _, _ = self.blocks
        half = self.half
        over_x = over_x.at[half:].set(add(over_x[half:], low).astype(bf16))
        over_y = over_y.at[:half].set(add(over_y[:half], top).astype(bf16))
        self.arrived = [fsdp_swap(over_x, 2), fsdp_swap(over_y, 4)]
        return [over_x, over_y]

    def over_chips(self, from_x, from_y):
        self.total = rounded(add(self.blocks[0], from_x, from_y))
        pairs = [(0, 1), (3, 2)] if self.line else [(0, 1), (1, 0), (2, 3), (3, 2)]
        self.arrived = [along_z(self.total, pairs)]
        return [self.total]

    def over_z(self, other):
        self.total = rounded(add(self.total, other))
        pairs = [(1, 2), (2, 1)] if self.line else [(0, 2), (2, 0), (1, 3), (3, 1)]
        self.arrived = [along_z(self.total, pairs)]
        return [self.total]

    def over_middle(self, other):
        if self.line:
            self.total = rounded(add(self.total, other))
            self.arrived = [along_z(self.total, [(1, 0), (2, 3)])]
        return [self.total]

    def result(self):
        other = self.arrived[0]
        if not self.line:
            return add(self.total, other)
        plane = lax.axis_index("batch")
        inside = (plane == 1) | (plane == 2)
        return jnp.where(inside, self.total, other).astype(f32)


def layer(
    planes,
    ring,
    tokens,
    seg_ids,
    positive,
    out_grad,
    w_qkv,
    b_qv,
    w_out,
    b_out,
    norm1_gain,
    norm1_shift,
    w_up,
    b_up,
    w_down,
    b_down,
    norm2_gain,
    norm2_shift,
):
    paired = ring == BLOCKS and planes == 4
    row_count, row_length, width = tokens.shape
    count = row_count * row_length
    own = row_count * SEGS
    token_rows = tokens.reshape(count, width)
    seg_rows = seg_ids.reshape(row_count, 1, row_length)
    seg_col = seg_ids.reshape(count, 1)
    pos_col = positive.reshape(own, 1)
    fsdp = lax.axis_index("fsdp")
    me = lax.axis_index("batch") * ring + fsdp
    index = (fsdp if paired else jnp.zeros_like(fsdp)).reshape(1).astype(jnp.int32)
    tie = lax.optimization_barrier

    small = (b_qv, b_out, norm1_gain, norm1_shift, b_down, norm2_gain, norm2_shift, b_up)
    sizes = [value.shape[0] * ring // BLOCKS for value in small]
    join = lambda left, right: jnp.concatenate([left, right], axis=1)
    if paired:
        first_xy = first_stage(w_qkv)
        line = tie(pack_small(small))
        lines = [(line, 0, 0)] + [(fsdp_swap(line, bit), bit, 0) for bit in (2, 4, 6)]
        lines = lines + [(fsdp_swap(value, 1), bit ^ 1, 0) for value, bit, _ in lines]
        first_xy = list(first_xy)
        *first_xy, line, second = tie((*first_xy, line, join(w_out, w_up)))
        first_far = second_stage(w_qkv, *first_xy)
        second, *_ = tie((second, *first_far))
        second_xy = first_stage(second)
        qkv_pieces = all_pieces(w_qkv, *first_xy, *first_far)
    else:
        blocks = [gather_whole(value) for value in (w_qkv, w_out, w_up, w_down, *small)]
        lines = [(pack_small(b[4:]), i, 0) for i, b in enumerate(zip(*blocks))]
        qkv_pieces = [(b[0], i, 0) for i, b in enumerate(zip(*blocks))]
        mid_pieces = [(join(b[1], b[2]), i, 0) for i, b in enumerate(zip(*blocks))]
        down_pieces = [(b[3], i, 0) for i, b in enumerate(zip(*blocks))]

    qkv, table = project_qkv(index, token_rows, qkv_pieces, lines, sizes[0])
    attended = ()
    for row in range(row_count):
        late = ()
        if paired and row == row_count - 1:
            *attended, over_x, over_y, third = tie((*attended, *second_xy, w_down))
            second_far = second_stage(second, over_x, over_y)
            third_xy = first_stage(third)
            late = (over_x, over_y)
        attended = attend(index, qkv, seg_rows, row, attended, late)
    context, lse = attended
    if paired:
        mid_pieces = all_pieces(second, over_x, over_y, *second_far)
    normed1, root1, hidden, rows, bias_up = project(
        index, context, token_rows, table, mid_pieces, sizes
    )
    late = ()
    if paired:
        hidden, *third_xy = tie((hidden, *third_xy))
        third_far = second_stage(w_down, *third_xy)
        down_pieces = all_pieces(w_down, *third_xy, *third_far)
        late = tuple(third_xy)
    activated, slope = up(index, hidden, bias_up, mid_pieces, late)
    result, normed2, root2, payload, pooled, stats = down(
        index, activated, normed1, rows, seg_rows, pos_col, down_pieces
    )

    if paired:
        line = [payload] + [swap(payload, "batch", planes, bit) for bit in (1, 2, 3)]
        line = jnp.concatenate(line, axis=0)
        plane = [line] + [fsdp_swap(line, bit) for bit in (2, 4, 6)]
        plane = jnp.concatenate(plane, axis=0)
        everyone = [plane, fsdp_swap(plane, 1)]
        layout = (2, ring // 2, planes)
        flip = me * own
    else:
        everyone = [lax.all_gather(payload, ("batch", "fsdp"), axis=0, tiled=True)]
        layout = (1, planes * ring, 1)
        flip = jnp.zeros_like(me)
    place = jnp.stack([flip, me * own]).astype(jnp.int32)
    pair_loss, d_pool = contrast(place, layout, everyone, payload, pos_col, pooled, stats)

    def start(keeps, sends, line):
        return Sum(planes, keeps, sends, line) if paired else None

    def go(clock, *sums):
        sent = []
        for one in sums:
            if one is not None:
                sent += one.next(clock)
        return tuple(sent)

    gain1, gain2 = rows[1:2], rows[4:5]
    d_summed, d_down, sums2, keep_down, send_down = norm2(
        index, out_grad.reshape(count, width), normed2, root2, seg_col, gain2, d_pool, activated
    )
    sum_down = start([keep_down], [send_down], True)
    halves = [up_back(index, d_down, slope, hidden, down_pieces, mid_pieces, 0, 2)]
    sent = go(halves[0][0], sum_down)
    before = tuple(halves[0][1:])
    halves.append(
        up_back(index, d_down, slope, hidden, down_pieces, mid_pieces, 2, 2, before, sent)
    )
    _, sums_up, keep_up, send_up = halves[1]
    sum_up = start([keep_up], [send_up], True)
    sent = go(halves[1][0], sum_down)
    d_attn, d_context, keep_out, send_out = norm1(
        index,
        [half[0] for half in halves],
        d_summed,
        normed1,
        root1,
        gain1,
        context,
        sums2,
        sums_up,
        mid_pieces,
        sent,
    )
    sent = go(d_context, sum_up)
    pairs = HEADS // 2
    cuts = 3
    backs = []
    for cut in range(cuts):
        backs.append(
            attend_back(
                index,
                qkv,
                d_context,
                lse,
                seg_rows,
                token_rows,
                cut * pairs // cuts,
                pairs // cuts,
                sent,
            )
        )
        if cut == 0:
            sum_left = start([keep_out, backs[0][3]], [send_out, backs[0][4]], True)
            sent = go(backs[0][0], sum_down, sum_up)
        if cut == 1:
            sent = go(backs[1][0], sum_down, sum_left)
    sum_right = start([backs[1][3], backs[2][3]], [backs[1][4], backs[2][4]], False)
    sent = go(backs[2][0], sum_down, sum_up, sum_left)
    grads = [backs[cut][kind] for kind in range(3) for cut in range(cuts)]
    grad_tokens = input_grad(index, d_attn, grads, qkv_pieces, sent)
    lanes = width // pairs

    part = width // BLOCKS
    if paired:
        go(None, sum_right)
        go(None, sum_left, sum_up)
        go(None, sum_right)
        go(None, sum_left, sum_up)
        go(None, sum_right)
        go(None, sum_left)
        go(None, sum_right)
        go(None, sum_right)
        grad_down, grad_up = sum_down.result().T, sum_up.result()
        left, right = sum_left.result(), sum_right.result()
        grad_out = left[:part, :width]
        grad_qkv = jnp.concatenate([left[:part, width:], right[:part]], axis=1)
        vector = jnp.concatenate([left[part, width:], right[part]])
        own_vectors = [left[part, i * TILE : i * TILE + part] for i in range(6)]
        own_vectors.append(left[part + 1, : sizes[-1]])
    else:

        def scatter(keep, send):
            full = lax.psum(jnp.stack([keep, send], axis=1).astype(f32), "batch")
            return full.reshape((BLOCKS,) + full.shape[2:])

        def own_rows(full):
            full = full.reshape((-1,) + full.shape[2:])
            return lax.psum_scatter(full, "fsdp", scatter_dimension=0, tiled=True)

        def own_values(full):
            return lax.psum_scatter(full.reshape(-1), "fsdp", scatter_dimension=0, tiled=True)

        grad_down = own_rows(scatter(keep_down, send_down).transpose(0, 2, 1))
        grad_up = own_rows(scatter(keep_up, send_up))
        left = scatter(keep_out, send_out)
        grad_out = own_rows(left[:, :part])
        own_vectors = [own_values(left[:, part, i * TILE : i * TILE + part]) for i in range(6)]
        own_vectors.append(own_values(left[:, part + 1, : sizes[-1]]))
        wide = jnp.concatenate([scatter(back[3], back[4]) for back in backs], axis=2)
        grad_qkv = own_rows(wide[:, :part])
        vector = lax.psum(jnp.sum(wide[:, part], axis=0), "fsdp")

    depth = grad_qkv.shape[0]
    grad_qkv = grad_qkv.reshape(depth, pairs, 3, lanes).transpose(0, 2, 1, 3)
    grad_qkv = grad_qkv.reshape(depth, 3 * width)
    vector = vector.reshape(pairs, 3, lanes)
    vector = jnp.concatenate([vector[:, 0].reshape(-1), vector[:, 2].reshape(-1)])
    shard = vector.shape[0] // ring
    grad_bqv = lax.dynamic_slice(vector, (fsdp * shard,), (shard,))
    grad_bout, grad_g1, grad_s1, grad_bdown, grad_g2, grad_s2, grad_bup = own_vectors
    return (
        result.reshape(tokens.shape),
        pair_loss.reshape(own),
        grad_tokens.reshape(tokens.shape),
        grad_qkv,
        grad_bqv,
        grad_out,
        grad_bout,
        grad_g1,
        grad_s1,
        grad_up,
        grad_bup,
        grad_down,
        grad_bdown,
        grad_g2,
        grad_s2,
    )


def solution(mesh):
    rows = P(("batch", "fsdp"), None, None)
    matrix = P("fsdp", None)
    vector = P("fsdp")
    placed = (
        rows,
        P(("batch", "fsdp"), None),
        P(("batch", "fsdp")),
        rows,
        matrix,
        vector,
        matrix,
        vector,
        vector,
        vector,
        matrix,
        vector,
        matrix,
        vector,
        vector,
        vector,
    )
    given = (
        rows,
        P(("batch", "fsdp")),
        rows,
        matrix,
        vector,
        matrix,
        vector,
        vector,
        vector,
        matrix,
        vector,
        matrix,
        vector,
        vector,
        vector,
    )
    return jax.shard_map(
        functools.partial(layer, mesh.shape["batch"], mesh.shape["fsdp"]),
        mesh=mesh,
        in_specs=placed,
        out_specs=given,
        check_vma=False,
    )
```

time: 479 us -> 355 us (0.74)
  waiting for transfers between devices: 171 us -> 74.5 us
  Pallas kernels: 174 us -> 147 us
  starting transfers between devices: 62.3 us -> 87.8 us
  blocking collectives: 23.1 us -> 0 us
  local copies, waits for them, and re-layouts: 28.5 us -> 23.1 us
    ppermute x76 -> x63, waiting for transfers between devices: 171 us -> 48.3 us  [swap(): return lax.ppermute(value, axis, [(i, i ^ bit) for i in range(size)])]
    ppermute x0 -> x11, starting transfers between devices: none -> 40.2 us  [along_z(): return lax.ppermute(value, 'batch', pairs)]
    pallas_call x11 -> x15, Pallas kernels: 174 us -> 147 us  [apply(): return run(index, *placed, *after)]
    ppermute x0 -> x11, waiting for transfers between devices: none -> 26.3 us  [along_z(): return lax.ppermute(value, 'batch', pairs)]
    all_gather x1 -> x0, blocking collectives: 23.1 us -> none  [layer(): lax.all_gather(jnp.concatenate(small)[None], 'fsdp', axis=0, tiled=True)]
    ppermute x76 -> x63, starting transfers between devices: 62.3 us -> 47.6 us  [swap(): return lax.ppermute(value, axis, [(i, i ^ bit) for i in range(size)])]
    slice x37 -> x13, local copies, waits for them, and re-layouts: 9.82 us -> 2.16 us  [the longest x1 0.75 us: layer(): grad_out = left[:part, :width]]
    convert_element_type x10 -> x18, other arithmetic: 0.46 us -> 7.8 us  [the longest x16 6.65 us: over_core(): add(keep[place, lo:hi], other[place, lo:hi]).astype(bf16)]
  transfers between devices with their start and end apart: 76 -> 74, of which waited for: 32 -> 28; matrix products, arithmetic and copies ran while one was open for 7% -> 8% of each run, Pallas kernels for 14% -> 28%
where the time goes in v2:
time: 355 us; the launch traced here: 350 us
  Pallas kernels  147 us (41%)
  starting transfers between devices  87.8 us (25%)
  waiting for transfers between devices  74.5 us (21%)
  local copies, waits for them, and re-layouts  23.1 us (7%)
  other arithmetic  16.3 us (5%)
    pallas_call x15, Pallas kernels, apply(): return run(index, *placed, *after)  147 us
    ppermute x63, waiting for transfers between devices, swap(): return lax.ppermute(value, axis, [(i, i ^ bit) for i in range(size)])  48.3 us
    ppermute x63, starting transfers between devices, swap(): return lax.ppermute(value, axis, [(i, i ^ bit) for i in range(size)])  47.6 us
    ppermute x11, starting transfers between devices, along_z(): return lax.ppermute(value, 'batch', pairs)  40.2 us
    ppermute x11, waiting for transfers between devices, along_z(): return lax.ppermute(value, 'batch', pairs)  26.3 us
    unnamed x107, local copies, waits for them, and re-layouts  13.3 us
  transfers between devices with their start and end apart: 74, of which 28 were waited for; matrix products, arithmetic and copies ran while one was open for 8% of the time, Pallas kernels for 28%

profile of v2, /device:TPU:0, one launch (start us, length us, event | category | flops | bytes accessed | tf_op | source)
XLA Modules:
  0.0 350.4 jit_solution(17469573185768478413)
XLA Ops:
  1.2 2.6 collective-permute-start.1
  21.1 3.0 collective-permute-done.11.refs_15_
  37.0 10.0 %shard_map.271 = (bf16[1024,2304]{1,0:T(8,128)(2,1)}, f32[8,1408]{1,0:T(8,128)}) custom-call(s32[1]{0:T(128)} %bitcast.refs_0_, bf16[1024,768]{1,0:T(8,128)(2,1)} %bitcast.88, bf16[96,2304]{1,0:T(8,128)(2,1)} %refs_11_.1, bf16[96,2304]{1,0:T(8,128)(2,1)} %copy-done.25, bf16[96,2304]{1,0:T(8,128)(2,1)} %copy-done.24, bf16[48,2304]{1,0:T(8,128)(2,1)} %copy-done.27, ...), custom_call_target="tpu_custom_call" | custom-call | flops 3623878656 | bytes 9830400 | tf_op jit(solution)/shard_map/pallas_call | solution.py:91
  47.1 6.8 %shard_map.272 = (bf16[1024,768]{1,0:T(8,128)(2,1)}, f32[2,6,2,512]{3,2,1,0:T(2,128)}) custom-call(s32[1]{0:T(128)} %bitcast.refs_0_, bf16[1024,2304]{1,0:T(8,128)(2,1)} %get-tuple-element.194.refs_1_.refs_2_.refs_3_, s32[2,1,512]{2,1,0:T(1,128)} %reshape.375.refs_2_.refs_4_.refs_6_), custom_call_target="tpu_custom_call" | custom-call | flops 805306368 | bytes 3145728 | tf_op jit(solution)/shard_map/pallas_call | solution.py:91
  55.3 9.6 %collective-permute-done.18.refs_7_.refs_6_.refs_17_.refs_13_ = bf16[48,3840]{1,0:T(8,128)(2,1)S(1)} collective-permute-done((bf16[48,3840]{1,0:T(8,128)(2,1)S(1)}, bf16[48,3840]{1,0:T(8,128)(2,1)S(1)}, u32[]{:S(2)}, u32[]{:S(2)}) %collective-permute-start.18) | collective-permute-done | bytes 368672 | tf_op jit(solution)/shard_map/ppermute | solution.py:101
  66.8 7.0 %shard_map.273 = (bf16[1024,768]{1,0:T(8,128)(2,1)}, f32[2,6,2,512]{3,2,1,0:T(2,128)}) custom-call(s32[1]{0:T(128)} %bitcast.refs_0_, bf16[1024,2304]{1,0:T(8,128)(2,1)} %get-tuple-element.194.refs_1_.refs_2_.refs_3_, s32[2,1,512]{2,1,0:T(1,128)} %reshape.375.refs_2_.refs_4_.refs_6_, ...), custom_call_target="tpu_custom_call", output_to_operand_aliasing={{0}: (3, {}), {1}: (4, {})} | custom-call | flops 805306368 | bytes 3145728 | tf_op jit(solution)/shard_map/pallas_call | solution.py:91
  75.0 6.6 %shard_map.274 = (f32[1024,768]{1,0:T(8,128)}, f32[1024,1]{1,0:T(8,128)}, bf16[1024,768]{1,0:T(8,128)(2,1)}, f32[8,768]{1,0:T(8,128)}, f32[1,3072]{1,0:T(1,128)}) custom-call(s32[1]{0:T(128)} %bitcast.refs_0_, bf16[1024,768]{1,0:T(8,128)(2,1)} %get-tuple-element.203.refs_1_.refs_7_, bf16[1024,768]{1,0:T(8,128)(2,1)} %bitcast.89, ...), custom_call_target="tpu_custom_call" | custom-call | flops 1207959552 | bytes 9043968 | tf_op jit(solution)/shard_map/pallas_call | solution.py:91
  85.3 5.8 %collective-permute-done.27.refs_9_.refs_7_ = bf16[192,768]{1,0:T(8,128)(2,1)S(1)} collective-permute-done((bf16[192,768]{1,0:T(8,128)(2,1)S(1)}, bf16[192,768]{1,0:T(8,128)(2,1)S(1)}, u32[]{:S(2)}, u32[]{:S(2)}) %collective-permute-start.27) | collective-permute-done | bytes 294944 | tf_op jit(solution)/shard_map/ppermute | solution.py:101
  92.4 14.2 %shard_map.275 = (bf16[1024,3072]{1,0:T(8,128)(2,1)}, bf16[1024,3072]{1,0:T(8,128)(2,1)}) custom-call(s32[1]{0:T(128)} %bitcast.refs_0_, bf16[1024,768]{1,0:T(8,128)(2,1)} %get-tuple-element.207.refs_1_.refs_3_, f32[1,3072]{1,0:T(1,128)} %get-tuple-element.208.refs_2_, bf16[96,3840]{1,0:T(8,128)(2,1)} %copy-done.15, bf16[96,3840]{1,0:T(8,128)(2,1)} %copy-done.1, ...), custom_call_target="tpu_custom_call" | custom-call | flops 4831838208 | bytes 18874368 | tf_op jit(solution)/shard_map/pallas_call | solution.py:91
  107.9 16.3 %shard_map.276 = (bf16[1024,768]{1,0:T(8,128)(2,1)}, f32[1024,768]{1,0:T(8,128)}, f32[1024,1]{1,0:T(8,128)}, bf16[16,896]{1,0:T(8,128)(2,1)S(1)}, f32[16,768]{1,0:T(8,128)S(1)}, /*index=5*/f32[16,128]{1,0:T(8,128)S(1)}) custom-call(s32[1]{0:T(128)} %bitcast.refs_0_, bf16[1024,3072]{1,0:T(8,128)(2,1)} %get-tuple-element.211.refs_1_.refs_7_, ...), custom_call_target="tpu_custom_call" | custom-call | flops 4831838208 | bytes 18874368 | tf_op jit(solution)/shard_map/pallas_call | solution.py:91
  124.2 3.7 %collective-permute-start.36 = (bf16[16,896]{1,0:T(8,128)(2,1)S(1)}, bf16[16,896]{1,0:T(8,128)(2,1)S(1)}, u32[]{:S(2)}, u32[]{:S(2)}) collective-permute-start(bf16[16,896]{1,0:T(8,128)(2,1)S(1)} %get-tuple-element.215.refs_1_), channel_id=1, source_target_pairs={{0,24},{8,16},{16,8},{24,0},{1,25},{9,17},{17,9},{25,1},{2,26},{10... | collective-permute-start | bytes 86024 | tf_op jit(solution)/shard_map/ppermute | solution.py:101
  128.6 3.4 collective-permute-done.34
  138.2 3.3 collective-permute-done.38
  144.3 3.2 shard_map.277
  147.5 11.5 %shard_map.278 = (f32[1024,768]{1,0:T(8,128)S(1)}, bf16[1024,768]{1,0:T(8,128)(2,1)S(1)}, f32[8,768]{1,0:T(8,128)S(1)}, bf16[4,768,384]{2,1,0:T(8,128)(2,1)S(1)}, bf16[4,768,384]{2,1,0:T(8,128)(2,1)S(1)}) custom-call(s32[1]{0:T(128)} %bitcast.refs_0_, bf16[1024,768]{1,0:T(8,128)(2,1)} %bitcast.101, f32[1024,768]{1,0:T(8,128)} %get-tuple-element.219.refs_2_, ...), custom_call_target="tpu_custom_call" | custom-call | flops 4831838208 | bytes 20447232 | tf_op jit(solution)/shard_map/pallas_call | solution.py:91
  160.0 15.7 %shard_map.279 = (f32[1024,768]{1,0:T(8,128)S(1)}, f32[1,3072]{1,0:T(1,128)S(1)}, bf16[4,96,3072]{2,1,0:T(8,128)(2,1)S(1)}, bf16[4,96,3072]{2,1,0:T(8,128)(2,1)}) custom-call(s32[1]{0:T(128)} %bitcast.refs_0_, bf16[1024,768]{1,0:T(8,128)(2,1)S(1)} %get-tuple-element.222.refs_1_, bf16[1024,3072]{1,0:T(8,128)(2,1)} %get-tuple-element.223.refs_2_, ...), custom_call_target="tpu_custom_call" | custom-call | flops 7247757312 | bytes 23592960 | tf_op jit(solution)/shard_map/pallas_call | solution.py:91
  177.5 16.2 %shard_map.280 = (f32[1024,768]{1,0:T(8,128)S(1)}, f32[1,3072]{1,0:T(1,128)S(1)}, bf16[4,96,3072]{2,1,0:T(8,128)(2,1)S(1)}, bf16[4,96,3072]{2,1,0:T(8,128)(2,1)}) custom-call(s32[1]{0:T(128)} %bitcast.refs_0_, bf16[1024,768]{1,0:T(8,128)(2,1)S(1)} %get-tuple-element.222.refs_1_, ...), custom_call_target="tpu_custom_call", output_to_operand_aliasing={{1}: (24, {}), {2}: (25, {}), {3}: (26, {})} | custom-call | flops 7247757312 | bytes 23592960 | tf_op jit(solution)/shard_map/pallas_call | solution.py:91
  199.6 2.5 fusion.2
  202.2 5.0 %collective-permute-done.42 = bf16[384,384]{1,0:T(8,128)(2,1)S(1)} collective-permute-done((bf16[384,384]{1,0:T(8,128)(2,1)}, bf16[384,384]{1,0:T(8,128)(2,1)S(1)}, u32[]{:S(2)}, u32[]{:S(2)}) %collective-permute-start.42) | collective-permute-done | bytes 294944 | tf_op jit(solution)/shard_map/ppermute | solution.py:101
  209.8 8.3 %shard_map.281 = (f32[1024,768]{1,0:T(8,128)S(1)}, bf16[1024,768]{1,0:T(8,128)(2,1)S(1)}, bf16[4,112,768]{2,1,0:T(8,128)(2,1)S(1)}, bf16[4,112,768]{2,1,0:T(8,128)(2,1)S(1)}) custom-call(s32[1]{0:T(128)} %bitcast.refs_0_, f32[1024,768]{1,0:T(8,128)S(1)} %copy-done.3, f32[1024,768]{1,0:T(8,128)S(1)} %copy-done.5, f32[1024,768]{1,0:T(8,128)S(1)} %get-tuple-element.232.refs_3_, ...), custom_call_target="tpu_custom_call" | custom-call | flops 2415919104 | bytes 18087936 | tf_op jit(solution)/shard_map/pallas_call | solution.py:91
  223.6 7.3 %shard_map.282 = (bf16[1024,256]{1,0:T(8,128)(2,1)S(1)}, bf16[1024,256]{1,0:T(8,128)(2,1)S(1)}, bf16[1024,256]{1,0:T(8,128)(2,1)S(1)}, bf16[4,112,768]{2,1,0:T(8,128)(2,1)S(1)}, bf16[4,112,768]{2,1,0:T(8,128)(2,1)S(1)}) custom-call(s32[1]{0:T(128)} %bitcast.refs_0_, bf16[1024,2304]{1,0:T(8,128)(2,1)} %get-tuple-element.194.refs_1_.refs_2_.refs_3_, ...), custom_call_target="tpu_custom_call" | custom-call | flops 2013265920 | bytes 5242880 | tf_op jit(solution)/shard_map/pallas_call | solution.py:91
  231.2 2.8 collective-permute-start.49
  236.5 7.3 %shard_map.283 = (bf16[1024,256]{1,0:T(8,128)(2,1)S(1)}, bf16[1024,256]{1,0:T(8,128)(2,1)S(1)}, bf16[1024,256]{1,0:T(8,128)(2,1)S(1)}, bf16[4,112,768]{2,1,0:T(8,128)(2,1)S(1)}, bf16[4,112,768]{2,1,0:T(8,128)(2,1)S(1)}) custom-call(s32[1]{0:T(128)} %bitcast.refs_0_, bf16[1024,2304]{1,0:T(8,128)(2,1)} %get-tuple-element.194.refs_1_.refs_2_.refs_3_, ...), custom_call_target="tpu_custom_call" | custom-call | flops 2013265920 | bytes 5242880 | tf_op jit(solution)/shard_map/pallas_call | solution.py:91
  243.8 2.4 collective-permute-done.49
  249.0 7.3 %shard_map.284 = (bf16[1024,256]{1,0:T(8,128)(2,1)S(1)}, bf16[1024,256]{1,0:T(8,128)(2,1)S(1)}, bf16[1024,256]{1,0:T(8,128)(2,1)S(1)}, bf16[4,112,768]{2,1,0:T(8,128)(2,1)S(1)}, bf16[4,112,768]{2,1,0:T(8,128)(2,1)S(1)}) custom-call(s32[1]{0:T(128)} %bitcast.refs_0_, bf16[1024,2304]{1,0:T(8,128)(2,1)} %get-tuple-element.194.refs_1_.refs_2_.refs_3_, ...), custom_call_target="tpu_custom_call" | custom-call | flops 2013265920 | bytes 5242880 | tf_op jit(solution)/shard_map/pallas_call | solution.py:91
  259.9 7.4 %collective-permute-start.70 = (bf16[96,3072]{1,0:T(8,128)(2,1)S(1)}, bf16[96,3072]{1,0:T(8,128)(2,1)S(1)}, u32[]{:S(2)}, u32[]{:S(2)}) collective-permute-start(bf16[96,3072]{1,0:T(8,128)(2,1)S(1)} %add_convert_fusion.2.refs_22_), channel_id=1, source_target_pairs={{0,8},{24,16},{1,9},{25,17},{2,10},{26,18},{3,11},{27,19},{4,12},{... | collective-permute-start | bytes 1769480 | tf_op jit(solution)/shard_map/ppermute | solution.py:1230
  268.9 8.9 %shard_map.285 = f32[1024,768]{1,0:T(8,128)} custom-call(s32[1]{0:T(128)} %bitcast.refs_0_, f32[1024,768]{1,0:T(8,128)S(1)} %get-tuple-element.238.refs_1_, bf16[1024,256]{1,0:T(8,128)(2,1)S(1)} %get-tuple-element.244.refs_2_, bf16[1024,256]{1,0:T(8,128)(2,1)S(1)} %get-tuple-element.249.refs_3_, bf16[1024,256]{1,0:T(8,128)(2,1)S(1)} %get-tuple-element.257.refs_4_, ...), custom_call_target="tpu_custom_call" | custom-call | flops 3623878656 | bytes 14548992 | tf_op jit(solution)/shard_map/pallas_call | solution.py:91
  278.0 10.5 %collective-permute-start.59 = (bf16[112,1536]{1,0:T(8,128)(2,1)S(1)}, bf16[112,1536]{1,0:T(8,128)(2,1)S(1)}, u32[]{:S(2)}, u32[]{:S(2)}) collective-permute-start(bf16[112,1536]{1,0:T(8,128)(2,1)S(1)} %add_convert_fusion.16), channel_id=1, source_target_pairs={{0,8},{24,16},{1,9},{25,17},{2,10},{26,18},{3,11},{27,19},{4,12},{... | collective-permute-start | bytes 1032200 | tf_op jit(solution)/shard_map/ppermute | solution.py:1230
  306.2 11.1 %collective-permute-start.68 = (bf16[112,1536]{1,0:T(8,128)(2,1)S(1)}, bf16[112,1536]{1,0:T(8,128)(2,1)S(1)}, u32[]{:S(2)}, u32[]{:S(2)}) collective-permute-start(bf16[112,1536]{1,0:T(8,128)(2,1)S(1)} %add_convert_fusion.13), channel_id=1, source_target_pairs={{0,8},{8,0},{16,24},{24,16},{1,9},{9,1},{17,25},{25,17},{2,10},{10... | collective-permute-start | bytes 1032200 | tf_op jit(solution)/shard_map/ppermute | solution.py:1230
  319.8 5.1 %collective-permute-done.61 = bf16[112,1536]{1,0:T(8,128)(2,1)S(1)} collective-permute-done((bf16[112,1536]{1,0:T(8,128)(2,1)S(1)}, bf16[112,1536]{1,0:T(8,128)(2,1)S(1)}, u32[]{:S(2)}, u32[]{:S(2)}) %collective-permute-start.61) | collective-permute-done | bytes 344096 | tf_op jit(solution)/shard_map/ppermute | solution.py:1230
  325.5 6.9 %collective-permute-done.68 = bf16[112,1536]{1,0:T(8,128)(2,1)S(1)} collective-permute-done((bf16[112,1536]{1,0:T(8,128)(2,1)S(1)}, bf16[112,1536]{1,0:T(8,128)(2,1)S(1)}, u32[]{:S(2)}, u32[]{:S(2)}) %collective-permute-start.68) | collective-permute-done | bytes 344096 | tf_op jit(solution)/shard_map/ppermute | solution.py:1230
  334.6 10.0 %collective-permute-done.69 = bf16[112,1536]{1,0:T(8,128)(2,1)S(1)} collective-permute-done((bf16[112,1536]{1,0:T(8,128)(2,1)S(1)}, bf16[112,1536]{1,0:T(8,128)(2,1)S(1)}, u32[]{:S(2)}, u32[]{:S(2)}) %collective-permute-start.69) | collective-permute-done | bytes 344096 | tf_op jit(solution)/shard_map/ppermute | solution.py:1230
  (325 shorter events, 106.8 us)
Async XLA Ops:
  0.7 32.1 %collective-permute-start.4 = (bf16[96,2304]{1,0:T(8,128)(2,1)}, bf16[96,2304]{1,0:T(8,128)(2,1)S(1)}, u32[]{:S(2)}, u32[]{:S(2)}) collective-permute-start(bf16[96,2304]{1,0:T(8,128)(2,1)} %refs_11_.1), channel_id=1, source_target_pairs={{0,1},{1,0},{2,3},{3,2},{4,5},{5,4},{6,7},{7,6},{8,9},{9,8},{10,11... | collective-permute-start | bytes 1327112 | tf_op jit(solution)/shard_map/ppermute | solution.py:101
  1.2 13.6 %collective-permute-start.1 = (bf16[96,2304]{1,0:T(8,128)(2,1)}, bf16[96,2304]{1,0:T(8,128)(2,1)S(1)}, u32[]{:S(2)}, u32[]{:S(2)}) collective-permute-start(bf16[96,2304]{1,0:T(8,128)(2,1)} %refs_11_.1), channel_id=1, source_target_pairs={{0,4},{1,5},{2,6},{3,7},{4,0},{5,1},{6,2},{7,3},{8,12},{9,13},{10,... | collective-permute-start | bytes 1327112 | tf_op jit(solution)/shard_map/ppermute | solution.py:101
  31.4 22.6 %collective-permute-start.17 = (bf16[96,3840]{1,0:T(8,128)(2,1)S(1)}, bf16[96,3840]{1,0:T(8,128)(2,1)S(1)}, u32[]{:S(2)}, u32[]{:S(2)}) collective-permute-start(bf16[96,3840]{1,0:T(8,128)(2,1)S(1)} %pad_maximum_fusion.1.refs_4_.refs_3_.refs_14_.refs_10_), channel_id=1, source_target_pairs={{0,4},{1,5},{2,6},{3,7},{4,0},{5,1},{6,2},{7,3},{8,12},{9,13},{10,... | collective-permute-start | bytes 2211848 | tf_op jit(solution)/shard_map/ppermute | solution.py:101
  32.8 21.1 %collective-permute-start.16 = (bf16[96,3840]{1,0:T(8,128)(2,1)S(1)}, bf16[96,3840]{1,0:T(8,128)(2,1)S(1)}, u32[]{:S(2)}, u32[]{:S(2)}) collective-permute-start(bf16[96,3840]{1,0:T(8,128)(2,1)S(1)} %pad_maximum_fusion.1.refs_4_.refs_3_.refs_14_.refs_10_), channel_id=1, source_target_pairs={{0,2},{1,3},{2,0},{3,1},{4,6},{5,7},{6,4},{7,5},{8,10},{9,11},{10,... | collective-permute-start | bytes 2211848 | tf_op jit(solution)/shard_map/ppermute | solution.py:101
  36.9 28.6 %collective-permute-start.20 = (bf16[96,3840]{1,0:T(8,128)(2,1)S(1)}, bf16[96,3840]{1,0:T(8,128)(2,1)S(1)}, u32[]{:S(2)}, u32[]{:S(2)}) collective-permute-start(bf16[96,3840]{1,0:T(8,128)(2,1)S(1)} %pad_maximum_fusion.1.refs_4_.refs_3_.refs_14_.refs_10_), channel_id=1, source_target_pairs={{0,1},{1,0},{2,3},{3,2},{4,5},{5,4},{6,7},{7,6},{8,9},{9,8},{10,11... | collective-permute-start | bytes 2211848 | tf_op jit(solution)/shard_map/ppermute | solution.py:101
  65.4 16.2 %collective-permute-start.26 = (bf16[384,768]{1,0:T(8,128)(2,1)}, bf16[384,768]{1,0:T(8,128)(2,1)S(1)}, u32[]{:S(2)}, u32[]{:S(2)}) collective-permute-start(bf16[384,768]{1,0:T(8,128)(2,1)} %refs_4_.3), channel_id=1, source_target_pairs={{0,4},{1,5},{2,6},{3,7},{4,0},{5,1},{6,2},{7,3},{8,12},{9,13},{10,... | collective-permute-start | bytes 1769480 | tf_op jit(solution)/shard_map/ppermute | solution.py:101
  66.1 15.6 %collective-permute-start.25 = (bf16[384,768]{1,0:T(8,128)(2,1)}, bf16[384,768]{1,0:T(8,128)(2,1)S(1)}, u32[]{:S(2)}, u32[]{:S(2)}) collective-permute-start(bf16[384,768]{1,0:T(8,128)(2,1)} %refs_4_.3), channel_id=1, source_target_pairs={{0,2},{1,3},{2,0},{3,1},{4,6},{5,7},{6,4},{7,5},{8,10},{9,11},{10,... | collective-permute-start | bytes 1769480 | tf_op jit(solution)/shard_map/ppermute | solution.py:101
  84.7 21.9 %collective-permute-start.29 = (bf16[384,768]{1,0:T(8,128)(2,1)}, bf16[384,768]{1,0:T(8,128)(2,1)S(1)}, u32[]{:S(2)}, u32[]{:S(2)}) collective-permute-start(bf16[384,768]{1,0:T(8,128)(2,1)} %refs_4_.3), channel_id=1, source_target_pairs={{0,1},{1,0},{2,3},{3,2},{4,5},{5,4},{6,7},{7,6},{8,9},{9,8},{10,11... | collective-permute-start | bytes 1769480 | tf_op jit(solution)/shard_map/ppermute | solution.py:101
  84.7 22.0 %collective-permute-start.30 = (bf16[384,768]{1,0:T(8,128)(2,1)S(1)}, bf16[384,768]{1,0:T(8,128)(2,1)S(1)}, u32[]{:S(2)}, u32[]{:S(2)}) collective-permute-start(bf16[384,768]{1,0:T(8,128)(2,1)S(1)} %collective-permute-done.25.refs_13_.refs_7_.refs_5_), channel_id=1, source_target_pairs={{0,1},{1,0},{2,3},{3,2},{4,5},{5,4},{6,7},{7,6},{8,9},{9,8},{10,11... | collective-permute-start | bytes 1769480 | tf_op jit(solution)/shard_map/ppermute | solution.py:101
  85.2 21.5 %collective-permute-start.31 = (bf16[384,768]{1,0:T(8,128)(2,1)S(1)}, bf16[384,768]{1,0:T(8,128)(2,1)}, u32[]{:S(2)}, u32[]{:S(2)}) collective-permute-start(bf16[384,768]{1,0:T(8,128)(2,1)S(1)} %collective-permute-done.26.refs_14_.refs_8_.refs_6_), channel_id=1, source_target_pairs={{0,1},{1,0},{2,3},{3,2},{4,5},{5,4},{6,7},{7,6},{8,9},{9,8},{10,11... | collective-permute-start | bytes 1769480 | tf_op jit(solution)/shard_map/ppermute | solution.py:101
  91.1 15.6 %collective-permute-start.32 = (bf16[192,768]{1,0:T(8,128)(2,1)S(1)}, bf16[192,768]{1,0:T(8,128)(2,1)S(1)}, u32[]{:S(2)}, u32[]{:S(2)}) collective-permute-start(bf16[192,768]{1,0:T(8,128)(2,1)S(1)} %collective-permute-done.27.refs_9_.refs_7_), channel_id=1, source_target_pairs={{0,1},{1,0},{2,3},{3,2},{4,5},{5,4},{6,7},{7,6},{8,9},{9,8},{10,11... | collective-permute-start | bytes 884744 | tf_op jit(solution)/shard_map/ppermute | solution.py:101
  92.4 14.3 %collective-permute-start.33 = (bf16[192,768]{1,0:T(8,128)(2,1)}, bf16[192,768]{1,0:T(8,128)(2,1)S(1)}, u32[]{:S(2)}, u32[]{:S(2)}) collective-permute-start(bf16[192,768]{1,0:T(8,128)(2,1)} %collective-permute-done.28.refs_10_.refs_8_), channel_id=1, source_target_pairs={{0,1},{1,0},{2,3},{3,2},{4,5},{5,4},{6,7},{7,6},{8,9},{9,8},{10,11... | collective-permute-start | bytes 884744 | tf_op jit(solution)/shard_map/ppermute | solution.py:101
  159.6 17.8 %collective-permute-start.41 = (bf16[4,768,384]{2,1,0:T(8,128)(2,1)S(1)}, bf16[4,768,384]{2,1,0:T(8,128)(2,1)S(1)}, u32[]{:S(2)}, u32[]{:S(2)}) collective-permute-start(bf16[4,768,384]{2,1,0:T(8,128)(2,1)S(1)} %get-tuple-element.229), channel_id=1, source_target_pairs={{0,1},{1,0},{2,3},{3,2},{4,5},{5,4},{6,7},{7,6},{8,9},{9,8},{10,11... | collective-permute-start | bytes 7077896 | tf_op jit(solution)/shard_map/ppermute | solution.py:101
  196.9 21.4 %collective-permute-start.44 = (bf16[4,96,3072]{2,1,0:T(8,128)(2,1)}, bf16[4,96,3072]{2,1,0:T(8,128)(2,1)}, u32[]{:S(2)}, u32[]{:S(2)}) collective-permute-start(bf16[4,96,3072]{2,1,0:T(8,128)(2,1)} %get-tuple-element.242), channel_id=1, source_target_pairs={{0,1},{1,0},{2,3},{3,2},{4,5},{5,4},{6,7},{7,6},{8,9},{9,8},{10,11... | collective-permute-start | bytes 7077896 | tf_op jit(solution)/shard_map/ppermute | solution.py:101
  207.4 23.5 %collective-permute-start.46 = (bf16[768,384]{1,0:T(8,128)(2,1)S(1)}, bf16[768,384]{1,0:T(8,128)(2,1)S(1)}, u32[]{:S(2)}, u32[]{:S(2)}) collective-permute-start(bf16[768,384]{1,0:T(8,128)(2,1)S(1)} %fusion.9.refs_21_), channel_id=1, source_target_pairs={{0,4},{1,5},{2,6},{3,7},{4,0},{5,1},{6,2},{7,3},{8,12},{9,13},{10,... | collective-permute-start | bytes 1769480 | tf_op jit(solution)/shard_map/ppermute | solution.py:101
  208.8 22.1 %collective-permute-start.45 = (bf16[768,384]{1,0:T(8,128)(2,1)S(1)}, bf16[768,384]{1,0:T(8,128)(2,1)S(1)}, u32[]{:S(2)}, u32[]{:S(2)}) collective-permute-start(bf16[768,384]{1,0:T(8,128)(2,1)S(1)} %fusion.8.refs_20_), channel_id=1, source_target_pairs={{0,2},{1,3},{2,0},{3,1},{4,6},{5,7},{6,4},{7,5},{8,10},{9,11},{10,... | collective-permute-start | bytes 1769480 | tf_op jit(solution)/shard_map/ppermute | solution.py:101
  218.1 28.2 %collective-permute-start.50 = (bf16[4,112,768]{2,1,0:T(8,128)(2,1)S(1)}, bf16[4,112,768]{2,1,0:T(8,128)(2,1)S(1)}, u32[]{:S(2)}, u32[]{:S(2)}) collective-permute-start(bf16[4,112,768]{2,1,0:T(8,128)(2,1)S(1)} %get-tuple-element.252), channel_id=1, source_target_pairs={{0,1},{1,0},{2,3},{3,2},{4,5},{5,4},{6,7},{7,6},{8,9},{9,8},{10,11... | collective-permute-start | bytes 2064392 | tf_op jit(solution)/shard_map/ppermute | solution.py:101
  219.4 14.6 %collective-permute-start.47 = (bf16[48,3072]{1,0:T(8,128)(2,1)S(1)}, bf16[48,3072]{1,0:T(8,128)(2,1)S(1)}, u32[]{:S(2)}, u32[]{:S(2)}) collective-permute-start(bf16[48,3072]{1,0:T(8,128)(2,1)S(1)} %get-tuple-element.312.refs_8_), channel_id=1, source_target_pairs={{0,2},{1,3},{2,0},{3,1},{4,6},{5,7},{6,4},{7,5},{8,10},{9,11},{10,... | collective-permute-start | bytes 884744 | tf_op jit(solution)/shard_map/ppermute | solution.py:101
  231.2 15.0 %collective-permute-start.49 = (bf16[768,384]{1,0:T(8,128)(2,1)S(1)}, bf16[768,384]{1,0:T(8,128)(2,1)S(1)}, u32[]{:S(2)}, u32[]{:S(2)}) collective-permute-start(bf16[768,384]{1,0:T(8,128)(2,1)S(1)} %add_convert_fusion.8.refs_8_), channel_id=1, source_target_pairs={{0,8},{24,16},{1,9},{25,17},{2,10},{26,18},{3,11},{27,19},{4,12},{... | collective-permute-start | bytes 1769480 | tf_op jit(solution)/shard_map/ppermute | solution.py:1230
  234.2 22.2 %collective-permute-start.54 = (bf16[96,3072]{1,0:T(8,128)(2,1)S(1)}, bf16[96,3072]{1,0:T(8,128)(2,1)S(1)}, u32[]{:S(2)}, u32[]{:S(2)}) collective-permute-start(bf16[96,3072]{1,0:T(8,128)(2,1)S(1)} %fusion.13.refs_10_), channel_id=1, source_target_pairs={{0,4},{1,5},{2,6},{3,7},{4,0},{5,1},{6,2},{7,3},{8,12},{9,13},{10,... | collective-permute-start | bytes 1769480 | tf_op jit(solution)/shard_map/ppermute | solution.py:101
  235.3 22.0 %collective-permute-start.53 = (bf16[96,3072]{1,0:T(8,128)(2,1)S(1)}, bf16[96,3072]{1,0:T(8,128)(2,1)S(1)}, u32[]{:S(2)}, u32[]{:S(2)}) collective-permute-start(bf16[96,3072]{1,0:T(8,128)(2,1)S(1)} %fusion.12.refs_9_), channel_id=1, source_target_pairs={{0,2},{1,3},{2,0},{3,1},{4,6},{5,7},{6,4},{7,5},{8,10},{9,11},{10,... | collective-permute-start | bytes 1769480 | tf_op jit(solution)/shard_map/ppermute | solution.py:101
  246.2 13.6 %collective-permute-start.62 = (bf16[4,112,768]{2,1,0:T(8,128)(2,1)S(1)}, bf16[4,112,768]{2,1,0:T(8,128)(2,1)S(1)}, u32[]{:S(2)}, u32[]{:S(2)}) collective-permute-start(bf16[4,112,768]{2,1,0:T(8,128)(2,1)S(1)} %get-tuple-element.270), channel_id=1, source_target_pairs={{0,1},{1,0},{2,3},{3,2},{4,5},{5,4},{6,7},{7,6},{8,9},{9,8},{10,11... | collective-permute-start | bytes 2064392 | tf_op jit(solution)/shard_map/ppermute | solution.py:101
  257.3 31.2 %collective-permute-start.63 = (bf16[4,112,768]{2,1,0:T(8,128)(2,1)S(1)}, bf16[4,112,768]{2,1,0:T(8,128)(2,1)S(1)}, u32[]{:S(2)}, u32[]{:S(2)}) collective-permute-start(bf16[4,112,768]{2,1,0:T(8,128)(2,1)S(1)} %get-tuple-element.272), channel_id=1, source_target_pairs={{0,1},{1,0},{2,3},{3,2},{4,5},{5,4},{6,7},{7,6},{8,9},{9,8},{10,11... | collective-permute-start | bytes 2064392 | tf_op jit(solution)/shard_map/ppermute | solution.py:101
  257.6 20.2 %collective-permute-start.58 = (bf16[112,1536]{1,0:T(8,128)(2,1)S(1)}, bf16[112,1536]{1,0:T(8,128)(2,1)S(1)}, u32[]{:S(2)}, u32[]{:S(2)}) collective-permute-start(bf16[112,1536]{1,0:T(8,128)(2,1)S(1)} %fusion.28.refs_24_), channel_id=1, source_target_pairs={{0,4},{1,5},{2,6},{3,7},{4,0},{5,1},{6,2},{7,3},{8,12},{9,13},{10,... | collective-permute-start | bytes 1032200 | tf_op jit(solution)/shard_map/ppermute | solution.py:101
  259.2 18.6 %collective-permute-start.57 = (bf16[112,1536]{1,0:T(8,128)(2,1)S(1)}, bf16[112,1536]{1,0:T(8,128)(2,1)S(1)}, u32[]{:S(2)}, u32[]{:S(2)}) collective-permute-start(bf16[112,1536]{1,0:T(8,128)(2,1)S(1)} %fusion.14.refs_23_), channel_id=1, source_target_pairs={{0,2},{1,3},{2,0},{3,1},{4,6},{5,7},{6,4},{7,5},{8,10},{9,11},{10,... | collective-permute-start | bytes 1032200 | tf_op jit(solution)/shard_map/ppermute | solution.py:101
  259.9 31.1 %collective-permute-start.70 = (bf16[96,3072]{1,0:T(8,128)(2,1)S(1)}, bf16[96,3072]{1,0:T(8,128)(2,1)S(1)}, u32[]{:S(2)}, u32[]{:S(2)}) collective-permute-start(bf16[96,3072]{1,0:T(8,128)(2,1)S(1)} %add_convert_fusion.2.refs_22_), channel_id=1, source_target_pairs={{0,8},{24,16},{1,9},{25,17},{2,10},{26,18},{3,11},{27,19},{4,12},{... | collective-permute-start | bytes 1769480 | tf_op jit(solution)/shard_map/ppermute | solution.py:1230
  267.6 30.5 %collective-permute-start.73 = (bf16[768,384]{1,0:T(8,128)(2,1)S(1)}, bf16[768,384]{1,0:T(8,128)(2,1)S(1)}, u32[]{:S(2)}, u32[]{:S(2)}) collective-permute-start(bf16[768,384]{1,0:T(8,128)(2,1)S(1)} %add_convert_fusion.4.refs_21_), channel_id=1, source_target_pairs={{8,0},{16,24},{9,1},{17,25},{10,2},{18,26},{11,3},{19,27},{12,4},{... | collective-permute-start | bytes 1769480 | tf_op jit(solution)/shard_map/ppermute | solution.py:1230
  278.0 17.5 %collective-permute-start.59 = (bf16[112,1536]{1,0:T(8,128)(2,1)S(1)}, bf16[112,1536]{1,0:T(8,128)(2,1)S(1)}, u32[]{:S(2)}, u32[]{:S(2)}) collective-permute-start(bf16[112,1536]{1,0:T(8,128)(2,1)S(1)} %add_convert_fusion.16), channel_id=1, source_target_pairs={{0,8},{24,16},{1,9},{25,17},{2,10},{26,18},{3,11},{27,19},{4,12},{... | collective-permute-start | bytes 1032200 | tf_op jit(solution)/shard_map/ppermute | solution.py:1230
  291.1 26.2 %collective-permute-start.71 = (bf16[96,3072]{1,0:T(8,128)(2,1)S(1)}, bf16[96,3072]{1,0:T(8,128)(2,1)}, u32[]{:S(2)}, u32[]{:S(2)}) collective-permute-start(bf16[96,3072]{1,0:T(8,128)(2,1)S(1)} %add_convert_fusion.1), channel_id=1, source_target_pairs={{8,16},{16,8},{9,17},{17,9},{10,18},{18,10},{11,19},{19,11},{12,20... | collective-permute-start | bytes 1769480 | tf_op jit(solution)/shard_map/ppermute | solution.py:1230
  300.7 24.2 %collective-permute-start.61 = (bf16[112,1536]{1,0:T(8,128)(2,1)S(1)}, bf16[112,1536]{1,0:T(8,128)(2,1)S(1)}, u32[]{:S(2)}, u32[]{:S(2)}) collective-permute-start(bf16[112,1536]{1,0:T(8,128)(2,1)S(1)} %add_convert_fusion.14), channel_id=1, source_target_pairs={{8,0},{16,24},{9,1},{17,25},{10,2},{18,26},{11,3},{19,27},{12,4},{... | collective-permute-start | bytes 1032200 | tf_op jit(solution)/shard_map/ppermute | solution.py:1230
  306.2 26.2 %collective-permute-start.68 = (bf16[112,1536]{1,0:T(8,128)(2,1)S(1)}, bf16[112,1536]{1,0:T(8,128)(2,1)S(1)}, u32[]{:S(2)}, u32[]{:S(2)}) collective-permute-start(bf16[112,1536]{1,0:T(8,128)(2,1)S(1)} %add_convert_fusion.13), channel_id=1, source_target_pairs={{0,8},{8,0},{16,24},{24,16},{1,9},{9,1},{17,25},{25,17},{2,10},{10... | collective-permute-start | bytes 1032200 | tf_op jit(solution)/shard_map/ppermute | solution.py:1230
  318.5 30.7 %collective-permute-start.72 = (bf16[96,3072]{1,0:T(8,128)(2,1)S(1)}, bf16[96,3072]{1,0:T(8,128)(2,1)S(1)}, u32[]{:S(2)}, u32[]{:S(2)}) collective-permute-start(bf16[96,3072]{1,0:T(8,128)(2,1)S(1)} %add_convert_fusion), channel_id=1, source_target_pairs={{8,0},{16,24},{9,1},{17,25},{10,2},{18,26},{11,3},{19,27},{12,4},{... | collective-permute-start | bytes 1769480 | tf_op jit(solution)/shard_map/ppermute | solution.py:1230
  (88 other events, 727.5 us)

commit v3 on v2

--- a/solution.py
+++ b/solution.py
@@ -25,7 +25,8 @@
 bf16 = jnp.bfloat16
 f32 = jnp.float32
 ANY = pl.BlockSpec(memory_space=pl.ANY)
-VMEM_BYTES = 32 * 1024 * 1024
+HELD = pl.BlockSpec(memory_space=pltpu.VMEM)
+VMEM_BYTES = 24 * 1024 * 1024
 
 
 def dot(left, right):
@@ -56,24 +57,25 @@
     room=VMEM_BYTES,
 ):
     given, extra = len(in_specs) + 1, len(after)
+    last = given + extra + len(out_shape)
 
     def body(*refs):
-        kernel(*refs[:given], *refs[given + extra :])
-
-    single = not isinstance(out_shape, list)
-    shapes = [out_shape] if single else out_shape
+        refs[last][...] = jnp.zeros_like(refs[last])
+        kernel(*refs[:given], *refs[given + extra : last], *refs[last + 1 :])
+
     shapes = [
         shape if -1 - number in near else pltpu.HBM(shape.shape, shape.dtype)
-        for number, shape in enumerate(shapes)
+        for number, shape in enumerate(out_shape)
     ]
+    shapes.append(shaped((8, TILE), f32))
     run = pl.pallas_call(
         body,
-        out_shape=shapes[0] if single else shapes,
+        out_shape=shapes,
         grid_spec=pltpu.PrefetchScalarGridSpec(
             num_scalar_prefetch=1,
             grid=grid,
             in_specs=in_specs + [ANY] * extra,
-            out_specs=out_specs,
+            out_specs=out_specs + [whole((8, TILE))],
             scratch_shapes=scratch,
         ),
         input_output_aliases=alias or {},
@@ -118,16 +120,16 @@
     return fsdp_swap(over_y[:half], 2), fsdp_swap(over_x[half:], 4)
 
 
-def all_pieces(shard, over_x, over_y, far_top, far_low):
-    half = middle(shard)
-    mine = [
-        (shard, 0, 0),
-        (over_x, 2, 0),
-        (over_y, 4, 0),
-        (far_top, 6, 0),
-        (far_low, 6, half),
-    ]
-    return mine + [(fsdp_swap(value, 1), place ^ 1, off) for value, place, off in mine]
+def own_pieces(shard, over_x, over_y):
+    return [(shard, 0, 0), (over_x, 2, 0), (over_y, 4, 0)]
+
+
+def far_pieces(shard, far_top, far_low):
+    return [(far_top, 6, 0), (far_low, 6, middle(shard))]
+
+
+def both_cores(pieces):
+    return pieces + [(fsdp_swap(value, 1), place ^ 1, off) for value, place, off in pieces]
 
 
 def gather_whole(shard):
@@ -144,18 +146,34 @@
     return [value for value, _, _ in pieces]
 
 
-def copies_of(meta, rows, refs, target, sems, index, source=None, place=None):
+def copies_of(
+    meta, rows, refs, target, sems, index, source=None, place=None, first=0
+):
     copies = []
     for number, ((block, off, count), ref) in enumerate(zip(meta, refs)):
-        start = pl.multiple_of((index ^ block) * rows + off, 16)
-        here = pl.ds(start, count)
+        low, high = max(off, first), min(off + count, first + rows)
+        if low >= high:
+            continue
+        here = pl.ds(pl.multiple_of((index ^ block) * rows + low - first, 16), high - low)
+        part = ref.at[low - off : high - off]
         copies.append(
             pltpu.make_async_copy(
-                ref if source is None else ref.at[:, source],
+                part if source is None else part.at[:, source],
                 target.at[here] if place is None else target.at[here, place],
                 sems.at[number],
             )
         )
+    return copies
+
+
+def pair_copies(meta, size, refs, target, sems, index, chip):
+    copies = []
+    for number, ((block, off, count), ref) in enumerate(zip(meta, refs)):
+        if block // 2 == chip:
+            start = pl.multiple_of((index ^ block) * size + off, 16)
+            copies.append(
+                pltpu.make_async_copy(ref, target.at[pl.ds(start, count)], sems.at[number])
+            )
     return copies
 
 
@@ -198,9 +216,24 @@
     return jnp.concatenate([value, value], axis=1)
 
 
-def pack_small(small):
-    line = jnp.concatenate([jnp.pad(v, (0, -v.shape[0] % TILE)) for v in small])
-    return jnp.pad(line[None], ((0, 15), (0, 0)))
+def pack_line(vectors, width):
+    line = jnp.concatenate([jnp.pad(v, (0, -v.shape[0] % TILE)) for v in vectors])
+    return jnp.pad(line[None], ((0, 15), (0, width - line.shape[0])))
+
+
+def pack_first(w_qkv, b_qv):
+    return jnp.concatenate([w_qkv, pack_line([b_qv], w_qkv.shape[1])], axis=0)
+
+
+def pack_second(w_out, w_up, *vectors):
+    both = jnp.concatenate([w_out, w_up], axis=1)
+    return jnp.concatenate([both, pack_line(vectors, both.shape[1])], axis=0)
+
+
+def table_of(lines):
+    line = lax.broadcasted_iota(jnp.int32, (BLOCKS, 16 * BLOCKS), 0) * 16
+    pick = line == lax.broadcasted_iota(jnp.int32, (BLOCKS, 16 * BLOCKS), 1)
+    return dot(pick.astype(f32).astype(bf16), lines)
 
 
 def spread(table, at, size):
@@ -215,29 +248,27 @@
     return jnp.sum(jnp.where(keep, value, 0.0), axis=0, keepdims=True), at + padded
 
 
-def qkv_kernel(meta, small_meta, size, index_ref, tok_ref, *rest):
+def qkv_kernel(meta, size, index_ref, tok_ref, *rest):
     pieces, rest = rest[: len(meta)], rest[len(meta) :]
-    lines, rest = rest[: len(small_meta)], rest[len(small_meta) :]
-    qkv_ref, table_ref, w_ref, small_ref, bias_ref, sems, small_sems = rest
+    qkv_ref, w_ref, small_ref, bias_ref, sems, small_sems = rest
     width = tok_ref.shape[1]
+    rows = width // BLOCKS
     part = pl.program_id(0)
+    index = index_ref[0]
 
     def weights(number):
         cols = columns(number, width)
-        rows = width // BLOCKS
-        return copies_of(meta, rows, pieces, w_ref, sems.at[number], index_ref[0], cols, cols)
+        return copies_of(meta, rows, pieces, w_ref, sems.at[number], index, cols, cols)
 
     @pl.when(part == 0)
     def _():
-        small = copies_of(small_meta, 16, lines, small_ref, small_sems, index_ref[0])
+        here = slice(0, small_ref.shape[1])
+        small = copies_of(meta, 16, pieces, small_ref, small_sems, index, here, None, rows)
         start_all(small)
         for number in range(3):
             start_all(weights(number))
         wait_all(small)
-        line = lax.broadcasted_iota(jnp.int32, (BLOCKS, 16 * BLOCKS), 0) * 16
-        pick = line == lax.broadcasted_iota(jnp.int32, (BLOCKS, 16 * BLOCKS), 1)
-        table_ref[...] = dot(pick.astype(f32).astype(bf16), small_ref[...])
-        bias, _ = spread(table_ref[...], 0, size)
+        bias, _ = spread(table_of(small_ref[...]), 0, size)
         bias_ref[0] = bias[:, :width]
         bias_ref[1] = jnp.zeros((1, width), f32)
         bias_ref[2] = bias[:, width:]
@@ -248,26 +279,27 @@
     qkv_ref[...] = (value * scale).astype(bf16)
 
 
-def project_qkv(index, tokens, pieces, lines, size):
+def project_qkv(index, tokens, pieces, size):
     count, width = tokens.shape
-    meta, small_meta = meta_of(pieces), meta_of(lines)
-    used = lines[0][0].shape[1]
+    meta = meta_of(pieces)
+    out = pl.BlockSpec((count, width), lambda i, s: (0, i))
     return call(
-        functools.partial(qkv_kernel, meta, small_meta, size),
+        functools.partial(qkv_kernel, meta, size),
         (3,),
-        [whole((count, width))] + [ANY] * len(meta + small_meta),
-        [pl.BlockSpec((count, width), lambda i, s: (0, i)), whole((BLOCKS, used))],
-        [shaped((count, 3 * width), bf16), shaped((BLOCKS, used), f32)],
+        [whole((count, width))] + [ANY] * len(meta),
+        [out],
+        [shaped((count, 3 * width), bf16)],
         [
             pltpu.VMEM((width, 3 * width), bf16),
-            pltpu.VMEM((16 * BLOCKS, used), bf16),
+            pltpu.VMEM((16 * BLOCKS, size + -size % TILE), bf16),
             pltpu.VMEM((3, 1, width), f32),
             pltpu.SemaphoreType.DMA((3, len(meta))),
-            pltpu.SemaphoreType.DMA((len(small_meta),)),
+            pltpu.SemaphoreType.DMA((len(meta),)),
         ],
         count * width * width * 6,
         count * width * 8 + width * width * 6,
-    )(index, tokens, *arrays_of(pieces), *arrays_of(lines))
+        near=(-1,),
+    )(index, tokens, *arrays_of(pieces))
 
 
 def attend_kernel(index_ref, qkv_ref, seg_ref, *rest):
@@ -334,7 +366,10 @@
             pl.BlockSpec((length, width), lambda i, s: (row, 0)),
             pl.BlockSpec((1, pairs, 2, length), lambda i, s: (row, 0, 0, 0)),
         ],
-        [shaped((count, width), bf16), shaped((rows, pairs, 2, length), f32)],
+        [
+            shaped((count, width), bf16),
+            shaped((rows, pairs, 2, length), f32),
+        ],
         [
             pltpu.VMEM((width, length), bf16),
             pltpu.VMEM((width, length), bf16),
@@ -345,6 +380,7 @@
         length * length * HEADS * 5 // 8,
         after,
         {3 + i: i for i in range(len(before))},
+        (1, -1, -2) + ((3, 4) if before else ()),
     )(index, qkv, seg_rows, *before)
 
 
@@ -355,9 +391,9 @@
     return centred, lax.rsqrt(spread + norm_eps)
 
 
-def project_kernel(meta, sizes, index_ref, ctx_ref, tok_ref, table_ref, *rest):
+def project_kernel(meta, sizes, index_ref, ctx_ref, tok_ref, *rest):
     pieces, rest = rest[: len(meta)], rest[len(meta) :]
-    norm_ref, root_ref, hid_ref, vec_ref, up_ref, w_ref, sems = rest
+    norm_ref, root_ref, hid_ref, vec_ref, up_ref, w_ref, small_ref, sems, small_sems = rest
     width = w_ref.shape[0]
 
     @pl.when(pl.program_id(0) == 0)
@@ -365,12 +401,16 @@
         rows = width // BLOCKS
         here = slice(0, width)
         copies = copies_of(meta, rows, pieces, w_ref, sems, index_ref[0], here, here)
+        line = slice(0, small_ref.shape[1])
+        small = copies_of(meta, 16, pieces, small_ref, small_sems, index_ref[0], line, None, rows)
+        start_all(small)
         start_all(copies)
-        at = sizes[0] + -sizes[0] % TILE
-        line = 0
         vec_ref[...] = jnp.zeros_like(vec_ref)
-        for size in sizes[1:]:
-            value, at = spread(table_ref[...], at, size)
+        wait_all(small)
+        table = table_of(small_ref[...])
+        line, at = 0, 0
+        for size in sizes:
+            value, at = spread(table, at, size)
             if value.shape[1] == width:
                 vec_ref[line : line + 1] = value
                 line += 1
@@ -400,15 +440,16 @@
     finish(*last)
 
 
-def project(index, context, tokens, table, pieces, sizes, step=512):
+def project(index, context, tokens, pieces, sizes, after=(), step=512):
     count, width = tokens.shape
     inner = 4 * width
+    used = sum(size + -size % TILE for size in sizes)
     meta = meta_of(pieces)
     rows = pl.BlockSpec((step, width), lambda i, s: (i, 0))
     return call(
         functools.partial(project_kernel, meta, sizes),
         (count // step,),
-        [rows, rows, whole(table.shape)] + [ANY] * len(meta),
+        [rows, rows] + [ANY] * len(meta),
         [
             rows,
             pl.BlockSpec((step, 1), lambda i, s: (i, 0)),
@@ -423,10 +464,18 @@
             shaped((SEGS, width), f32),
             shaped((1, inner), f32),
         ],
-        [pltpu.VMEM((width, width), bf16), pltpu.SemaphoreType.DMA((len(meta),))],
+        [
+            pltpu.VMEM((width, width), bf16),
+            pltpu.VMEM((16 * BLOCKS, used), bf16),
+            pltpu.SemaphoreType.DMA((len(meta),)),
+            pltpu.SemaphoreType.DMA((len(meta),)),
+        ],
         count * width * width * 2,
         count * width * 10 + width * width * 2,
-    )(index, context, tokens, table, *arrays_of(pieces))
+        0,
+        after,
+        near=(1, -3, -4, -5),
+    )(index, context, tokens, *arrays_of(pieces))
 
 
 def gelu_parts(value):
@@ -456,10 +505,8 @@
     wide = 256
 
     def begin(cols):
-        w = w_ref[:, columns(step, tile)] if wide == tile else w_ref[:, pl.ds(
-            pl.multiple_of(step * tile + cols.start, wide), wide
-        )]
-        return dot(hid_ref[...], w) + bias_ref[:, cols]
+        here = pl.ds(pl.multiple_of(step * tile + cols.start, wide), wide)
+        return dot(hid_ref[...], w_ref[:, here]) + bias_ref[:, cols]
 
     def finish(cols, value):
         act, slope = gelu_parts(value)
@@ -477,9 +524,9 @@
     return call(
         functools.partial(up_kernel, meta),
         (inner // tile,),
-        [whole((count, width)), pl.BlockSpec((1, tile), lambda i, s: (0, i))] + [ANY] * len(meta),
+        [HELD, pl.BlockSpec((1, tile), lambda i, s: (0, i))] + [ANY] * len(meta),
         [out, out],
-        [shaped((count, inner), bf16), shaped((count, inner), bf16)],
+        [shaped((count, inner), bf16)] * 2,
         [
             pltpu.VMEM((width, inner), bf16),
             pltpu.SemaphoreType.DMA((inner // tile, len(meta))),
@@ -488,46 +535,64 @@
         count * (width * 2 + inner * 4) + width * inner * 2,
         count * inner * 4,
         after,
+        near=(1, 2),
     )(index, hidden, bias, *arrays_of(pieces))
 
 
 def down_kernel(meta, index_ref, act_ref, norm_ref, vec_ref, seg_ref, pos_ref, *rest):
     pieces, rest = rest[: len(meta)], rest[len(meta) :]
-    res_ref, norm2_ref, root_ref, pay_ref, pool_ref, stat_ref, w_ref, sum_ref, num_ref, sems = rest
-    step = pl.program_id(0)
-    steps = pl.num_programs(0)
-    width = res_ref.shape[1]
-    inner = w_ref.shape[0]
-    copies = copies_of(meta, inner // BLOCKS, pieces, w_ref, sems, index_ref[0])
+    res_ref, norm2_ref, root_ref, pay_ref, pool_ref, stat_ref, *rest = rest
+    w_ref, held_ref, sum_ref, num_ref, sems, act_sems = rest
+    step, steps = pl.program_id(0), pl.num_programs(0)
+    length, width = res_ref.shape
+    tile = w_ref.shape[0] // 4
+    index = index_ref[0]
+
+    def weights(chip):
+        return pair_copies(meta, tile // 2, pieces, w_ref, sems, index, chip)
+
+    def inputs(row, chip):
+        rows = pl.ds(pl.multiple_of(row * length, length), length)
+        source = act_ref.at[rows, columns((index // 2) ^ chip, tile)]
+        return pltpu.make_async_copy(source, held_ref.at[row, chip], act_sems.at[row, chip])
 
     @pl.when(step == 0)
     def _():
-        start_all(copies)
-        sum_ref[...] = jnp.zeros_like(sum_ref)
-        num_ref[...] = jnp.zeros_like(num_ref)
-        wait_all(copies)
-
-    seg = seg_ref[0]
-    wanted = lax.broadcasted_iota(jnp.int32, (SEGS, seg.shape[1]), 0)
-    member = (wanted == seg).astype(f32)
+        inputs(0, 0).start()
+        start_all(weights(0))
+
+    wanted = lax.broadcasted_iota(jnp.int32, (SEGS, length), 0)
+    member = (wanted == seg_ref[0]).astype(f32)
+    product = None
+    for chip in range(4):
+        inputs(step, chip).wait()
+
+        @pl.when(step == 0)
+        def _():
+            wait_all(weights(chip))
+            if chip < 3:
+                inputs(0, chip + 1).start()
+                start_all(weights(chip + 1))
+            else:
+                for other in range(4):
+                    inputs(1, other).start()
+
+        value = dot(held_ref[step, chip], w_ref[columns((index // 2) ^ chip, tile)])
+        product = value if product is None else product + value
+    hidden = norm_ref[...] * vec_ref[1:2] + vec_ref[2:3]
+    summed = hidden + (product + vec_ref[3:4])
+    centred, root = row_stats(summed)
+    normed = centred * root
+    result = normed * vec_ref[4:5] + vec_ref[5:6]
+    norm2_ref[...] = normed
+    root_ref[...] = root
+    high = result.astype(bf16)
+    res_ref[...] = high
+    low = (result - high.astype(f32)).astype(bf16)
+    own = pl.ds(pl.multiple_of(step * SEGS, SEGS), SEGS)
     member_b = member.astype(bf16)
-    own = pl.ds(pl.multiple_of(step // (steps * SEGS // sum_ref.shape[0]) * SEGS, SEGS), SEGS)
-    num_ref[own] += jnp.broadcast_to(jnp.sum(member, axis=1, keepdims=True), (SEGS, TAIL))
-
-    def finish(here, product):
-        hidden = norm_ref[here] * vec_ref[1:2] + vec_ref[2:3]
-        summed = hidden + (product + vec_ref[3:4])
-        centred, root = row_stats(summed)
-        normed = centred * root
-        result = normed * vec_ref[4:5] + vec_ref[5:6]
-        norm2_ref[here] = normed
-        root_ref[here] = root
-        high = result.astype(bf16)
-        res_ref[here] = high
-        low = (result - high.astype(f32)).astype(bf16)
-        sum_ref[own] += dot(member_b[:, here], high) + dot(member_b[:, here], low)
-
-    in_turn(act_ref.shape[0], lambda here: dot(act_ref[here], w_ref[...]), finish)
+    sum_ref[own] = dot(member_b, high) + dot(member_b, low)
+    num_ref[own] = jnp.broadcast_to(jnp.sum(member, axis=1, keepdims=True), (SEGS, TAIL))
 
     @pl.when(step == steps - 1)
     def _():
@@ -543,22 +608,21 @@
         pay_ref[:, width:] = jnp.where(lane < 2, digit, 0).astype(f32).astype(bf16)
 
 
-def down(index, activated, normed, vectors, seg_rows, positive, pieces, step=512):
+def down(index, activated, normed, vectors, seg_rows, positive, pieces, after=()):
     count, width = normed.shape
     inner = activated.shape[1]
-    rows, _, length = seg_rows.shape
+    rows, _, step = seg_rows.shape
     own = rows * SEGS
-    per_row = length // step
     meta = meta_of(pieces)
     block = pl.BlockSpec((step, width), lambda i, s: (i, 0))
     return call(
         functools.partial(down_kernel, meta),
         (count // step,),
         [
-            pl.BlockSpec((step, inner), lambda i, s: (i, 0)),
+            ANY,
             block,
             whole(vectors.shape),
-            pl.BlockSpec((1, 1, step), lambda i, s: (i // per_row, 0, i % per_row)),
+            pl.BlockSpec((1, 1, step), lambda i, s: (i, 0, 0)),
             whole((own, 1)),
         ]
         + [ANY] * len(meta),
@@ -580,12 +644,15 @@
         ],
         [
             pltpu.VMEM((inner, width), bf16),
+            pltpu.VMEM((rows, 4, step, inner // 4), bf16),
             pltpu.VMEM((own, width), f32),
             pltpu.VMEM((own, TAIL), f32),
             pltpu.SemaphoreType.DMA((len(meta),)),
+            pltpu.SemaphoreType.DMA((rows, 4)),
         ],
         count * width * inner * 2,
         count * (width * 10 + inner * 2) + width * inner * 2,
+        after=after,
         near=(3, 5, -4, -5, -6),
     )(index, activated, normed, vectors, seg_rows, positive, *arrays_of(pieces))
 
@@ -645,7 +712,7 @@
     grad_ref[...] = (d_emb * scale - pooled * (scale * scale * scale * along)) / counts
 
 
-def contrast(place, layout, everyone, payload, positive, pooled, stats):
+def contrast(place, layout, everyone, payload, positive, pooled, stats, after=()):
     own, width = pooled.shape
     total = sum(v.shape[0] for v in everyone)
     return call(
@@ -661,6 +728,7 @@
         total * total * width * 2,
         total * width * 2,
         total * total,
+        after=after,
         near=(1, 2, 3, 4, -1, -2),
     )(place, payload, positive, pooled, stats, *everyone)
 
@@ -676,7 +744,7 @@
     return jnp.sum(values, axis=0, keepdims=True)
 
 
-def norm2_kernel(turns, index_ref, og_ref, norm_ref, root_ref, seg_ref, gain_ref, dp_ref, *rest):
+def norm2_kernel(turns, index_ref, og_ref, norm_ref, root_ref, seg_ref, vec_in_ref, dp_ref, *rest):
     act_ref, dsum_ref, ddown_ref, vec_ref, keep_ref, send_ref, dt_ref = rest
     step = pl.program_id(0)
     chunk, width = og_ref.shape
@@ -696,22 +764,22 @@
         low = (left - mid.astype(f32)).astype(bf16)
         pad = jnp.zeros((TILE - 3 * SEGS, width), bf16)
         table = jnp.concatenate([high, mid, low, pad], axis=0)
-        lane = lax.broadcasted_iota(jnp.int32, (TILE, TILE), 1)
+        lane = lax.broadcasted_iota(jnp.int32, (chunk, TILE), 1) % SEGS
+        keys = jnp.broadcast_to(seg_ref[0].astype(f32), (TILE, chunk)).T
+        member = (lane.astype(f32) == keys).astype(f32).astype(bf16)
 
         def begin(here):
-            member = (lane % SEGS == seg_ref[here]).astype(f32).astype(bf16)
-            return dot(member, table)
+            return dot(member[here], table)
 
         def finish(here, shared):
             d_res = og_ref[here].astype(f32) + shared
             normed = norm_ref[here]
-            d_sum = norm_back(d_res, normed, root_ref[here], gain_ref[...])
+            d_sum = norm_back(d_res, normed, root_ref[here], vec_in_ref[4:5])
             d_down = d_sum.astype(bf16)
             dsum_ref[here] = d_sum
             ddown_ref[here] = d_down
-            dt_ref[:, columns(step, chunk) if chunk == TILE else pl.ds(
-                pl.multiple_of(step * chunk + here.start, TILE), TILE
-            )] = d_down.T
+            cols = pl.ds(pl.multiple_of(step * chunk + here.start, TILE), TILE)
+            dt_ref[:, cols] = d_down.T
             vec_ref[0:1] += column_sum(d_down.astype(f32))
             vec_ref[1:2] += column_sum(d_res * normed)
             vec_ref[2:3] += column_sum(d_res)
@@ -727,13 +795,14 @@
         send_ref[0] = jnp.where(odd, grad[:, :half], grad[:, half:])
 
 
-def norm2(index, out_grad, normed, root, seg_col, gain, d_pool, activated, turns=4):
+def norm2(index, out_grad, normed, root, seg_rows, vectors, d_pool, activated, turns=4):
     count, width = out_grad.shape
     inner = activated.shape[1]
     tile = inner // 4
     own = d_pool.shape[0]
     first = lambda i: jnp.minimum(i, turns - 1)
     then = lambda i: jnp.maximum(i - turns, 0)
+    split = turns // seg_rows.shape[0]
     block = pl.BlockSpec((count // turns, width), lambda i, s: (first(i), 0))
     column = pl.BlockSpec((count // turns, 1), lambda i, s: (first(i), 0))
     grads = pl.BlockSpec((1, width, tile // 2), lambda i, s: (then(i), 0, 0))
@@ -744,8 +813,8 @@
             block,
             block,
             column,
-            column,
-            whole((1, width)),
+            pl.BlockSpec((1, 1, count // turns), lambda i, s: (first(i) // split, 0, first(i) % split)),
+            whole(vectors.shape),
             whole((own, width)),
             pl.BlockSpec((count, tile), lambda i, s: (0, (s[0] // 2) ^ then(i))),
         ],
@@ -761,7 +830,7 @@
         count * width * inner * 2,
         count * (width * 12 + inner * 2) + width * inner * 2,
         near=(5, 6, -1, -2, -3, -4, -5),
-    )(index, out_grad, normed, root, seg_col, gain, d_pool, activated)
+    )(index, out_grad, normed, root, seg_rows, vectors, d_pool, activated)
 
 
 def put_turned(source_ref, target_ref, turn_ref, index):
@@ -773,54 +842,71 @@
         target_ref[place * rows : (place + 1) * rows] = turn_ref[pl.ds(start, rows)]
 
 
-def up_back_kernel(
-    down_meta, up_meta, first, before, index_ref, ddown_ref, slope_ref, hid_ref, *rest
-):
-    low_pieces, rest = rest[: len(down_meta)], rest[len(down_meta) :]
-    up_pieces, rest = rest[: len(up_meta)], rest[len(up_meta) + before :]
-    dhid_ref, bias_ref, keep_ref, send_ref, wd_ref, wu_ref, turn_ref, ht_ref, sems, up_sems = rest
+def weights_kernel(down_meta, up_meta, index_ref, *refs):
+    pieces, (wd_ref, wu_ref, sems, up_sems) = refs[:-4], refs[-4:]
+    low, high = pieces[: len(down_meta)], pieces[len(down_meta) :]
+    width, inner = wu_ref.shape
+    here = slice(width, width + inner)
+    copies = copies_of(down_meta, inner // BLOCKS, low, wd_ref, sems, index_ref[0])
+    copies += copies_of(up_meta, width // BLOCKS, high, wu_ref, up_sems, index_ref[0], here)
+    start_all(copies)
+    wait_all(copies)
+
+
+def hold_weights(index, down_pieces, up_pieces, width, inner, after=()):
+    down_meta, up_meta = meta_of(down_pieces), meta_of(up_pieces)
+    return call(
+        functools.partial(weights_kernel, down_meta, up_meta),
+        (1,),
+        [ANY] * (len(down_meta) + len(up_meta)),
+        [HELD, HELD],
+        [shaped((inner, width), bf16), shaped((width, inner), bf16)],
+        [
+            pltpu.SemaphoreType.DMA((len(down_meta),)),
+            pltpu.SemaphoreType.DMA((len(up_meta),)),
+        ],
+        0,
+        width * inner * 8,
+        0,
+        after,
+        near=(-1, -2),
+    )(index, *arrays_of(down_pieces), *arrays_of(up_pieces))
+
+
+def turned_kernel(index_ref, one_ref, two_ref, out_one_ref, out_two_ref, turn_ref):
+    put_turned(one_ref, out_one_ref, turn_ref, index_ref[0])
+    put_turned(two_ref, out_two_ref, turn_ref, index_ref[0])
+
+
+def hold_turned(index, one, two, after=()):
+    count, width = one.shape
+    return call(
+        turned_kernel,
+        (1,),
+        [whole((count, width))] * 2,
+        [HELD, HELD],
+        [shaped((width, count), bf16)] * 2,
+        [pltpu.VMEM((width, count), bf16)],
+        0,
+        count * width * 8,
+        0,
+        after,
+        near=(-1, -2),
+    )(index, one, two)
+
+
+def up_back_kernel(first, before, index_ref, ddown_ref, slope_ref, ht_ref, wd_ref, wu_ref, *rest):
+    earlier, rest = rest[:before], rest[before:]
+    dhid_ref, bias_ref, keep_ref, send_ref = rest
     step = pl.program_id(0)
     tile = slope_ref.shape[1]
     width = ht_ref.shape[0]
-    index = index_ref[0]
-    steps = sems.shape[0]
-
-    def weights(number):
-        copies = []
-        here = wd_ref.at[pl.ds(pl.multiple_of(number * tile, tile), tile)]
-        for piece, ((place, off, size), ref) in enumerate(zip(down_meta, low_pieces)):
-            start = pl.multiple_of(((index ^ place) % 2) * (tile // 2) + off, 16)
-            copies.append((place // 2 - first, ref, here.at[pl.ds(start, size)], sems.at[number, piece]))
-        cols = columns((index // 2) ^ (number + first), tile, width)
-        high = copies_of(
-            up_meta, width // BLOCKS, up_pieces, wu_ref.at[number], up_sems.at[number], index, cols
-        )
-        return copies, high
-
-    def rows_of(number):
-        low, _ = weights(number)
-        return [
-            pltpu.make_async_copy(ref, here, sem) for place, ref, here, sem in low if place == number
-        ]
-
-    @pl.when(step == 0)
-    def _():
-        for number in range(steps):
-            start_all(rows_of(number))
-            start_all(weights(number)[1])
-        put_turned(hid_ref, ht_ref, turn_ref, index)
-
-    for number in range(steps):
-
-        @pl.when(step == number)
-        def _():
-            wait_all(rows_of(number))
-
+    here = columns((index_ref[0] // 2) ^ (step + first), tile)
     wide = 256
     parts = []
 
     def begin(cols):
-        rows = pl.ds(pl.multiple_of(step * tile + cols.start, wide), wide)
+        rows = pl.ds(pl.multiple_of(here.start + cols.start, wide), wide)
         return dot_nt(ddown_ref[...], wd_ref[rows])
 
     def finish(cols, d_act):
@@ -834,64 +920,44 @@
     half = width // 2
     keep_ref[...] = grad[:half].reshape(keep_ref.shape)
     send_ref[...] = grad[half:].reshape(send_ref.shape)
-    wait_all(weights(step)[1])
-    share = dot_nt(d_up, wu_ref[step])
+    share = dot_nt(d_up, wu_ref[:, here])
 
     @pl.when(step == 0)
     def _():
-        dhid_ref[...] = share
+        dhid_ref[...] = earlier[0][...] + share if earlier else share
 
     @pl.when(step > 0)
     def _():
         dhid_ref[...] += share
 
 
-def up_back(index, d_down, slope, hidden, down_pieces, up_pieces, first, steps, before=(), after=()):
+def up_back(index, d_down, slope, turned, w_down, w_up, first, steps, before=(), after=()):
     count, width = d_down.shape
     inner = slope.shape[1]
     tile = inner // 4
     part = width // BLOCKS
-    down_meta, up_meta = meta_of(down_pieces), meta_of(up_pieces)
     place = lambda i, s: (s[0] // 2) ^ (i + first)
     grads = pl.BlockSpec((4, part, tile), lambda i, s: (0, 0, place(i, s)))
-    given = 4 + len(down_meta) + len(up_meta)
     return call(
-        functools.partial(up_back_kernel, down_meta, up_meta, first, len(before)),
+        functools.partial(up_back_kernel, first, len(before)),
         (steps,),
-        [
-            whole((count, width)),
-            pl.BlockSpec((count, tile), lambda i, s: (0, place(i, s))),
-            whole((count, width)),
-        ]
-        + [ANY] * (len(down_meta) + len(up_meta) + len(before)),
-        [
-            whole((count, width)),
-            pl.BlockSpec((1, tile), lambda i, s: (0, place(i, s))),
-            grads,
-            grads,
-        ],
+        [HELD, pl.BlockSpec((count, tile), lambda i, s: (0, place(i, s))), HELD, HELD, HELD]
+        + ([HELD] + [ANY] * 3 if before else []),
+        [HELD, pl.BlockSpec((1, tile), lambda i, s: (0, place(i, s))), grads, grads],
         [
             shaped((count, width), f32),
             shaped((1, inner), f32),
             shaped((4, part, inner), bf16),
             shaped((4, part, inner), bf16),
         ],
-        [
-            pltpu.VMEM((steps * tile, width), bf16),
-            pltpu.VMEM((steps, width, tile), bf16),
-            pltpu.VMEM((width, count), bf16),
-            pltpu.VMEM((width, count), bf16),
-            pltpu.SemaphoreType.DMA((steps, len(down_meta))),
-            pltpu.SemaphoreType.DMA((steps, len(up_meta))),
-        ],
+        [],
         count * width * tile * 6 * steps,
         count * (width * 8 + inner) + width * inner * 6,
         0,
         after,
-        {given + i: 1 + i for i in range(len(before))},
-        (1, -1, -2, -3, -4) + tuple(range(given, given + len(before))),
-        40 * 1024 * 1024,
-    )(index, d_down, slope, hidden, *arrays_of(down_pieces), *arrays_of(up_pieces), *before)
+        {6 + i: i for i in range(len(before))},
+        (1, 3, 4, 5, 6, 7, 8, 9, -1, -2, -3, -4),
+    )(index, d_down, slope, turned, w_down, w_up, *before)
 
 
 def cut_vector(vector, size, index):
@@ -929,7 +995,7 @@
         for dhid_ref in dhids:
             d_hid = d_hid + dhid_ref[here]
         normed = norm_ref[here]
-        d_sum = norm_back(d_hid, normed, root_ref[here], gain_ref[...])
+        d_sum = norm_back(d_hid, normed, root_ref[here], gain_ref[1:2])
         d_attn = d_sum.astype(bf16)
         dattn_ref[here] = d_sum
         vec_ref[0:1] += column_sum(d_attn.astype(f32))
@@ -981,7 +1047,7 @@
             block,
             block,
             pl.BlockSpec((step, 1), lambda i, s: (i, 0)),
-            whole((1, width)),
+            whole(gain.shape),
             block,
             whole(sums.shape),
             whole(sums_up.shape),
@@ -1004,26 +1070,25 @@
         count * width * 20 + width * width * 4,
         0,
         after,
-        near=tuple(range(1, 2 + len(d_hiddens))) + (-1, -2, -3, -4),
+        near=tuple(range(1, 2 + len(d_hiddens))) + (6, 7, 8, -1, -2, -3, -4),
     )(
         index, *d_hiddens, d_summed, normed, root, gain, context, sums, sums_up, *arrays_of(pieces)
     )
 
 
 def attend_back_kernel(
-    first, index_ref, q_ref, k_ref, v_ref, dctx_ref, lse_ref, seg_ref, tok_ref, *rest
+    first, index_ref, q_ref, k_ref, v_ref, dctx_ref, lse_ref, seg_ref, tt_ref, *rest
 ):
     dq_ref, dk_ref, dv_ref, keep_ref, send_ref = rest[:5]
-    mask_ref, turn_ref, tt_ref, kt_ref, two_ref, pt_ref, both_ref = rest[5:]
+    mask_ref, kt_ref, two_ref, pt_ref, both_ref = rest[5:]
     rows, _, length = seg_ref.shape
-    lanes = 2 * tok_ref.shape[1] // HEADS
+    lanes = 2 * tt_ref.shape[0] // HEADS
     half = lanes // 2
     group = q_ref.shape[1] // lanes
     inv_root = 1.0 / math.sqrt(half)
 
     @pl.when(pl.program_id(0) == 0)
     def _():
-        put_turned(tok_ref, tt_ref, turn_ref, index_ref[0])
         for row in range(rows):
             fill_mask(seg_ref[row].astype(f32), mask_ref.at[row])
 
@@ -1114,9 +1179,9 @@
 
 
 def attend_back(
-    index, qkv, d_context, lse, seg_rows, tokens, first, pairs, after=(), group=2
+    index, qkv, d_context, lse, seg_rows, turned, first, pairs, after=(), group=2
 ):
-    count, width = tokens.shape
+    width, count = turned.shape
     rows, _, length = seg_rows.shape
     every = HEADS // 2
     lanes = width // every
@@ -1135,7 +1200,7 @@
             column(first),
             pl.BlockSpec((rows, group, 2, length), lambda i, s: (0, first // group + i, 0, 0)),
             whole((rows, 1, length)),
-            whole((count, width)),
+            HELD,
         ],
         [out, out, out, grads, grads],
         [
@@ -1147,8 +1212,6 @@
         ],
         [
             pltpu.VMEM((rows, length, length), f32),
-            pltpu.VMEM((width, count), bf16),
-            pltpu.VMEM((width, count), bf16),
             pltpu.VMEM((group, rows, lanes, length), bf16),
             pltpu.VMEM((2, group, rows, 2 * length, lanes), bf16),
             pltpu.VMEM((2, group, rows, length, 2 * length), bf16),
@@ -1158,8 +1221,8 @@
         count * pairs * lanes * 14 + count * width * 2,
         count * length * pairs * 5 // 4,
         after,
-        near=(4, -1, -2, -3, -4, -5),
-    )(index, qkv, qkv, qkv, d_context, lse, seg_rows, tokens)
+        near=(4, 5, 7, -1, -2, -3, -4, -5),
+    )(index, qkv, qkv, qkv, d_context, lse, seg_rows, turned)
 
 
 def input_kernel(meta, parts, index_ref, dattn_ref, *rest):
@@ -1204,8 +1267,8 @@
         [block]
         + [pl.BlockSpec((step, g.shape[1]), lambda i, s: (i, 0)) for g in grads]
         + [ANY] * len(meta),
-        block,
-        shaped((count, width), f32),
+        [block],
+        [shaped((count, width), f32)],
         [pltpu.VMEM((width, 3 * width), bf16), pltpu.SemaphoreType.DMA((3, len(meta)))],
         count * width * width * 6,
         count * width * 14 + width * width * 6,
@@ -1230,29 +1293,53 @@
     return lax.ppermute(value, "batch", pairs)
 
 
+def core_kernel(parts, index_ref, *refs):
+    keeps, others = refs[:parts], refs[parts : 2 * parts]
+    mine_ref, x_ref, y_ref, top_ref, low_ref = refs[2 * parts :]
+    half = top_ref.shape[0]
+    at = 0
+    for keep, other in zip(keeps, others):
+        cols = slice(at, at + keep.shape[2])
+        at = cols.stop
+        for place, target in enumerate((mine_ref, x_ref, y_ref)):
+            target[:, cols] = add(keep[place], other[place]).astype(bf16)
+        far = add(keep[3], other[3]).astype(bf16)
+        top_ref[:, cols] = far[:half]
+        low_ref[:, cols] = far[half:]
+
+
+def add_cores(index, keeps, others):
+    rows = keeps[0].shape[1]
+    width = sum(keep.shape[2] for keep in keeps)
+    half = rows // 32 * 16
+    heights = (rows, rows, rows, half, rows - half)
+    count = 2 * len(keeps)
+    return call(
+        functools.partial(core_kernel, len(keeps)),
+        (1,),
+        [HELD] * count,
+        [HELD] * 5,
+        [shaped((height, width), bf16) for height in heights],
+        [],
+        rows * width * 4,
+        rows * width * 24,
+        near=tuple(range(1, 1 + count)) + (-1, -2, -3, -4, -5),
+    )(index, *keeps, *others)
+
+
 class Sum:
-    def __init__(self, planes, keeps, sends, line):
-        self.planes, self.keeps, self.line = planes, keeps, line
+    def __init__(self, index, planes, keeps, sends, line):
+        self.index, self.planes, self.keeps, self.line = index, planes, keeps, line
         self.arrived = [fsdp_swap(send, 1) for send in sends]
         self.stages = [self.over_core, self.over_far, self.over_chips, self.over_z, self.over_middle]
 
     def next(self, clock):
-        if clock is not None:
-            *self.arrived, _ = lax.optimization_barrier((*self.arrived, clock))
-        return self.stages.pop(0)(*self.arrived)
+        *self.arrived, _ = lax.optimization_barrier((*self.arrived, clock))
+        return list(self.stages.pop(0)(*self.arrived))
 
     def over_core(self, *others):
-        rows = self.keeps[0].shape[1]
-        half = rows // 32 * 16
-        cuts = [(0, 0, rows), (1, 0, rows), (2, 0, rows), (3, 0, half), (3, half, rows)]
-        self.blocks = []
-        for place, lo, hi in cuts:
-            sums = [
-                add(keep[place, lo:hi], other[place, lo:hi]).astype(bf16)
-                for keep, other in zip(self.keeps, others)
-            ]
-            self.blocks.append(rounded(jnp.concatenate(sums, axis=1)))
-        self.half = half
+        *self.blocks, _ = add_cores(self.index, self.keeps, others)
+        self.half = self.blocks[3].shape[0]
         self.arrived = [fsdp_swap(self.blocks[3], 2), fsdp_swap(self.blocks[4], 4)]
         return self.blocks[3:]
 
@@ -1317,152 +1404,171 @@
     own = row_count * SEGS
     token_rows = tokens.reshape(count, width)
     seg_rows = seg_ids.reshape(row_count, 1, row_length)
-    seg_col = seg_ids.reshape(count, 1)
     pos_col = positive.reshape(own, 1)
     fsdp = lax.axis_index("fsdp")
     me = lax.axis_index("batch") * ring + fsdp
     index = (fsdp if paired else jnp.zeros_like(fsdp)).reshape(1).astype(jnp.int32)
     tie = lax.optimization_barrier
 
-    small = (b_qv, b_out, norm1_gain, norm1_shift, b_down, norm2_gain, norm2_shift, b_up)
+    small = (b_out, norm1_gain, norm1_shift, b_down, norm2_gain, norm2_shift, b_up)
     sizes = [value.shape[0] * ring // BLOCKS for value in small]
-    join = lambda left, right: jnp.concatenate([left, right], axis=1)
+    inner = sizes[-1] * BLOCKS
     if paired:
-        first_xy = first_stage(w_qkv)
-        line = tie(pack_small(small))
-        lines = [(line, 0, 0)] + [(fsdp_swap(line, bit), bit, 0) for bit in (2, 4, 6)]
-        lines = lines + [(fsdp_swap(value, 1), bit ^ 1, 0) for value, bit, _ in lines]
-        first_xy = list(first_xy)
-        *first_xy, line, second = tie((*first_xy, line, join(w_out, w_up)))
-        first_far = second_stage(w_qkv, *first_xy)
-        second, *_ = tie((second, *first_far))
+        first = pack_first(w_qkv, b_qv)
+        first_xy = first_stage(first)
+        *first_xy, second = tie((*first_xy, pack_second(w_out, w_up, *small)))
+        first_far = second_stage(first, *first_xy)
+        second, *first_far = tie((second, *first_far))
         second_xy = first_stage(second)
-        qkv_pieces = all_pieces(w_qkv, *first_xy, *first_far)
+        qkv_pieces = both_cores(own_pieces(first, *first_xy))
+        qkv_pieces += both_cores(far_pieces(first, *first_far))
     else:
-        blocks = [gather_whole(value) for value in (w_qkv, w_out, w_up, w_down, *small)]
-        lines = [(pack_small(b[4:]), i, 0) for i, b in enumerate(zip(*blocks))]
-        qkv_pieces = [(b[0], i, 0) for i, b in enumerate(zip(*blocks))]
-        mid_pieces = [(join(b[1], b[2]), i, 0) for i, b in enumerate(zip(*blocks))]
-        down_pieces = [(b[3], i, 0) for i, b in enumerate(zip(*blocks))]
-
-    qkv, table = project_qkv(index, token_rows, qkv_pieces, lines, sizes[0])
+        blocks = [gather_whole(value) for value in (w_qkv, b_qv, w_down, w_out, w_up, *small)]
+        blocks = list(enumerate(zip(*blocks)))
+        qkv_pieces = [(pack_first(*b[:2]), i, 0) for i, b in blocks]
+        down_pieces = [(b[2], i, 0) for i, b in blocks]
+        mid_pieces = [(pack_second(*b[3:]), i, 0) for i, b in blocks]
+
+    qkv, clock = project_qkv(index, token_rows, qkv_pieces, 2 * width // BLOCKS)
     attended = ()
     for row in range(row_count):
         late = ()
         if paired and row == row_count - 1:
-            *attended, over_x, over_y, third = tie((*attended, *second_xy, w_down))
-            second_far = second_stage(second, over_x, over_y)
+            *second_xy, third, clock = tie((*second_xy, w_down, clock))
+            second_far = second_stage(second, *second_xy)
             third_xy = first_stage(third)
-            late = (over_x, over_y)
-        attended = attend(index, qkv, seg_rows, row, attended, late)
+            late = (*second_xy, clock)
+        *attended, clock = attend(index, qkv, seg_rows, row, attended, late)
     context, lse = attended
     if paired:
-        mid_pieces = all_pieces(second, over_x, over_y, *second_far)
-    normed1, root1, hidden, rows, bias_up = project(
-        index, context, token_rows, table, mid_pieces, sizes
+        mid_pieces = both_cores(own_pieces(second, *second_xy))
+        *second_far, clock = tie((*second_far, clock))
+        mid_pieces += both_cores(far_pieces(second, *second_far))
+    normed1, root1, hidden, rows, bias_up, clock = project(
+        index, context, token_rows, mid_pieces, sizes, (clock,)
     )
     late = ()
     if paired:
-        hidden, *third_xy = tie((hidden, *third_xy))
+        *third_xy, clock = tie((*third_xy, clock))
         third_far = second_stage(w_down, *third_xy)
-        down_pieces = all_pieces(w_down, *third_xy, *third_far)
-        late = tuple(third_xy)
-    activated, slope = up(index, hidden, bias_up, mid_pieces, late)
-    result, normed2, root2, payload, pooled, stats = down(
-        index, activated, normed1, rows, seg_rows, pos_col, down_pieces
+        late = (*third_xy, clock)
+    activated, slope, clock = up(index, hidden, bias_up, mid_pieces, late)
+    if paired:
+        down_pieces = both_cores(own_pieces(w_down, *third_xy))
+        *third_far, clock = tie((*third_far, clock))
+        down_pieces += both_cores(far_pieces(w_down, *third_far))
+    result, normed2, root2, payload, pooled, stats, _ = down(
+        index, activated, normed1, rows, seg_rows, pos_col, down_pieces, (clock,)
     )
 
+    hidden_turned, tokens_turned, clock = hold_turned(index, hidden, token_rows, (payload,))
     if paired:
         line = [payload] + [swap(payload, "batch", planes, bit) for bit in (1, 2, 3)]
+        *line, clock = tie((*line, clock))
         line = jnp.concatenate(line, axis=0)
         plane = [line] + [fsdp_swap(line, bit) for bit in (2, 4, 6)]
+        wd_full, wu_full, clock = hold_weights(
+            index, down_pieces, mid_pieces, width, inner, (line, clock)
+        )
+        *plane, clock = tie((*plane, clock))
         plane = jnp.concatenate(plane, axis=0)
         everyone = [plane, fsdp_swap(plane, 1)]
         layout = (2, ring // 2, planes)
         flip = me * own
     else:
+        wd_full, wu_full, clock = hold_weights(index, down_pieces, mid_pieces, width, inner)
         everyone = [lax.all_gather(payload, ("batch", "fsdp"), axis=0, tiled=True)]
         layout = (1, planes * ring, 1)
         flip = jnp.zeros_like(me)
     place = jnp.stack([flip, me * own]).astype(jnp.int32)
-    pair_loss, d_pool = contrast(place, layout, everyone, payload, pos_col, pooled, stats)
+    pair_loss, d_pool, _ = contrast(
+        place, layout, everyone, payload, pos_col, pooled, stats, (clock,)
+    )
 
     def start(keeps, sends, line):
-        return Sum(planes, keeps, sends, line) if paired else None
-
-    def go(clock, *sums):
-        sent = []
+        return Sum(index, planes, keeps, sends, line) if paired else None
+
+    def go(results, *sums):
+        sent, clock = [], results[0]
         for one in sums:
             if one is not None:
-                sent += one.next(clock)
-        return tuple(sent)
-
-    gain1, gain2 = rows[1:2], rows[4:5]
-    d_summed, d_down, sums2, keep_down, send_down = norm2(
-        index, out_grad.reshape(count, width), normed2, root2, seg_col, gain2, d_pool, activated
+                stage = one.next(clock)
+                clock = stage[0]
+                sent += stage
+        if sent:
+            results = tie((*results, *sent))[: len(results)]
+        return results, tuple(sent)
+
+    d_summed, d_down, sums2, keep_down, send_down, _ = norm2(
+        index,
+        out_grad.reshape(count, width),
+        normed2,
+        root2,
+        seg_rows,
+        rows,
+        d_pool,
+        activated,
     )
     sum_down = start([keep_down], [send_down], True)
-    halves = [up_back(index, d_down, slope, hidden, down_pieces, mid_pieces, 0, 2)]
-    sent = go(halves[0][0], sum_down)
-    before = tuple(halves[0][1:])
-    halves.append(
-        up_back(index, d_down, slope, hidden, down_pieces, mid_pieces, 2, 2, before, sent)
-    )
-    _, sums_up, keep_up, send_up = halves[1]
+    half, sent = (), ()
+    for first in (0, 2):
+        half = up_back(
+            index, d_down, slope, hidden_turned, wd_full, wu_full, first, 2, tuple(half), sent
+        )[:4]
+        half, sent = go(half, sum_down)
+    d_hidden, sums_up, keep_up, send_up = half
     sum_up = start([keep_up], [send_up], True)
-    sent = go(halves[1][0], sum_down)
-    d_attn, d_context, keep_out, send_out = norm1(
+    *first_norm, _ = norm1(
         index,
-        [half[0] for half in halves],
+        [d_hidden],
         d_summed,
         normed1,
         root1,
-        gain1,
+        rows,
         context,
         sums2,
         sums_up,
         mid_pieces,
         sent,
     )
-    sent = go(d_context, sum_up)
+    (d_attn, d_context, keep_out, send_out), sent = go(first_norm, sum_up)
     pairs = HEADS // 2
     cuts = 3
     backs = []
     for cut in range(cuts):
-        backs.append(
-            attend_back(
-                index,
-                qkv,
-                d_context,
-                lse,
-                seg_rows,
-                token_rows,
-                cut * pairs // cuts,
-                pairs // cuts,
-                sent,
-            )
+        *back, _ = attend_back(
+            index,
+            qkv,
+            d_context,
+            lse,
+            seg_rows,
+            tokens_turned,
+            cut * pairs // cuts,
+            pairs // cuts,
+            sent,
         )
         if cut == 0:
-            sum_left = start([keep_out, backs[0][3]], [send_out, backs[0][4]], True)
-            sent = go(backs[0][0], sum_down, sum_up)
+            back, sent = go(back, sum_down, sum_up)
+            sum_left = start([keep_out, back[3]], [send_out, back[4]], True)
         if cut == 1:
-            sent = go(backs[1][0], sum_down, sum_left)
-    sum_right = start([backs[1][3], backs[2][3]], [backs[1][4], backs[2][4]], False)
-    sent = go(backs[2][0], sum_down, sum_up, sum_left)
+            back, sent = go(back, sum_left)
+        if cut == 2:
+            sum_right = start([backs[1][3], back[3]], [backs[1][4], back[4]], False)
+            back, sent = go(back, sum_down, sum_up, sum_left, sum_right)
+        backs.append(back)
     grads = [backs[cut][kind] for kind in range(3) for cut in range(cuts)]
-    grad_tokens = input_grad(index, d_attn, grads, qkv_pieces, sent)
+    grad_tokens, _ = input_grad(index, d_attn, grads, qkv_pieces, sent)
+
     lanes = width // pairs
 
     part = width // BLOCKS
     if paired:
-        go(None, sum_right)
-        go(None, sum_left, sum_up)
-        go(None, sum_right)
-        go(None, sum_left, sum_up)
-        go(None, sum_right)
-        go(None, sum_left)
-        go(None, sum_right)
-        go(None, sum_right)
+        (grad_tokens,), sent = go((grad_tokens,), sum_right, sum_down, sum_up)
+        _, sent = go(sent, sum_left)
+        _, sent = go(sent, sum_right)
+        _, sent = go(sent, sum_up, sum_left)
+        _, sent = go(sent, sum_right, sum_left)
+        go(sent, sum_right)
         grad_down, grad_up = sum_down.result().T, sum_up.result()
         left, right = sum_left.result(), sum_right.result()
         grad_out = left[:part, :width]

time: 355 us -> 316 us (0.89)
  starting transfers between devices: 87.8 us -> 59.9 us
  waiting for transfers between devices: 74.5 us -> 65.7 us
  Pallas kernels: 147 us -> 142 us
    ppermute x11, starting transfers between devices: 40.2 us -> 19.4 us  [along_z(): return lax.ppermute(value, 'batch', pairs)]
    ppermute x63 -> x56, starting transfers between devices: 47.6 us -> 40.5 us  [swap(): return lax.ppermute(value, axis, [(i, i ^ bit) for i in range(size)])]
    convert_element_type x16 -> x0, other arithmetic: 6.65 us -> none  [over_core(): add(keep[place, lo:hi], other[place, lo:hi]).astype(bf16)]
    ppermute x63 -> x56, waiting for transfers between devices: 48.3 us -> 41.7 us  [swap(): return lax.ppermute(value, axis, [(i, i ^ bit) for i in range(size)])]
    pallas_call x15 -> x21, Pallas kernels: 147 us -> 142 us  [apply(): return run(index, *placed, *after)]
  transfers between devices with their start and end apart: 74 -> 67, of which waited for: 28 -> 22; matrix products, arithmetic and copies ran while one was open for 8% -> 7% of each run, Pallas kernels for 28% -> 35%
where the time goes in v3:
time: 316 us; the launch traced here: 311 us
  Pallas kernels  142 us (45%)
  waiting for transfers between devices  65.7 us (21%)
  starting transfers between devices  59.9 us (19%)
  local copies, waits for them, and re-layouts  26.1 us (8%)
  other arithmetic  15.2 us (5%)
    pallas_call x21, Pallas kernels, apply(): return run(index, *placed, *after)  142 us
    ppermute x56, waiting for transfers between devices, swap(): return lax.ppermute(value, axis, [(i, i ^ bit) for i in range(size)])  41.7 us
    ppermute x56, starting transfers between devices, swap(): return lax.ppermute(value, axis, [(i, i ^ bit) for i in range(size)])  40.5 us
    ppermute x11, waiting for transfers between devices, along_z(): return lax.ppermute(value, 'batch', pairs)  24 us
    ppermute x11, starting transfers between devices, along_z(): return lax.ppermute(value, 'batch', pairs)  19.4 us
    unnamed x107, local copies, waits for them, and re-layouts  13.6 us
  transfers between devices with their start and end apart: 67, of which 22 were waited for; matrix products, arithmetic and copies ran while one was open for 7% of the time, Pallas kernels for 35%

profile of v3, /device:TPU:0, one launch (start us, length us, event | category | flops | bytes accessed | tf_op | source)
XLA Modules:
  0.0 311.4 jit_solution(16538485999453284521)
XLA Ops:
  2.4 3.0 collective-permute-start
  21.1 7.1 %collective-permute-done.5.refs_8_.refs_17_ = bf16[48,2304]{1,0:T(8,128)(2,1)S(1)} collective-permute-done((bf16[48,2304]{1,0:T(8,128)(2,1)S(1)}, bf16[48,2304]{1,0:T(8,128)(2,1)S(1)}, u32[]{:S(2)}, u32[]{:S(2)}) %collective-permute-start.5) | collective-permute-done | bytes 221216 | tf_op jit(solution)/shard_map/ppermute | solution.py:103
  31.6 9.4 %shard_map.271 = (bf16[1024,2304]{1,0:T(8,128)(2,1)S(1)}, f32[8,128]{1,0:T(8,128)}) custom-call(s32[1]{0:T(128)} %bitcast.refs_0_, bf16[1024,768]{1,0:T(8,128)(2,1)} %bitcast.28, bf16[112,2304]{1,0:T(8,128)(2,1)} %copy-done.33, bf16[112,2304]{1,0:T(8,128)(2,1)} %copy-done.34, bf16[112,2304]{1,0:T(8,128)(2,1)} %copy-done.35, ...), custom_call_target="tpu_custom_call" | custom-call | flops 3623878656 | bytes 9830400 | tf_op jit(solution)/shard_map/pallas_call | solution.py:93
  41.0 5.0 %shard_map.272 = (bf16[1024,768]{1,0:T(8,128)(2,1)S(1)}, f32[2,6,2,512]{3,2,1,0:T(2,128)S(1)}, f32[8,128]{1,0:T(8,128)S(1)}) custom-call(s32[1]{0:T(128)} %bitcast.refs_0_, bf16[1024,2304]{1,0:T(8,128)(2,1)S(1)} %get-tuple-element.284.refs_1_.refs_2_.refs_3_, s32[2,1,512]{2,1,0:T(1,128)} %reshape.252.refs_2_.refs_4_.refs_6_), custom_call_target="tpu_custom_call" | custom-call | flops 805306368 | bytes 3145728 | tf_op jit(solution)/shard_map/pallas_call | solution.py:93
  46.0 3.1 collective-permute-done.9.refs_5_.refs_4_.refs_12_.refs_10_
  51.6 5.0 %shard_map.273 = (bf16[1024,768]{1,0:T(8,128)(2,1)S(1)}, f32[2,6,2,512]{3,2,1,0:T(2,128)S(1)}, f32[8,128]{1,0:T(8,128)S(1)}) custom-call(s32[1]{0:T(128)} %bitcast.refs_0_, bf16[1024,2304]{1,0:T(8,128)(2,1)S(1)} %get-tuple-element.284.refs_1_.refs_2_.refs_3_, ...), custom_call_target="tpu_custom_call", output_to_operand_aliasing={{0}: (3, {}), {1}: (4, {})} | custom-call | flops 805306368 | bytes 3145728 | tf_op jit(solution)/shard_map/pallas_call | solution.py:93
  56.6 4.1 %collective-permute-done.14.refs_9_.refs_17_.refs_15_ = bf16[48,3840]{1,0:T(8,128)(2,1)S(1)} collective-permute-done((bf16[48,3840]{1,0:T(8,128)(2,1)S(1)}, bf16[48,3840]{1,0:T(8,128)(2,1)S(1)}, u32[]{:S(2)}, u32[]{:S(2)}) %collective-permute-start.14) | collective-permute-done | bytes 368672 | tf_op jit(solution)/shard_map/ppermute | solution.py:103
  60.6 2.5 collective-permute-done.15.refs_10_.refs_18_.refs_16_
  67.7 6.9 %shard_map.274 = (f32[1024,768]{1,0:T(8,128)}, f32[1024,1]{1,0:T(8,128)}, bf16[1024,768]{1,0:T(8,128)(2,1)S(1)}, f32[8,768]{1,0:T(8,128)S(1)}, f32[1,3072]{1,0:T(1,128)S(1)}, /*index=5*/f32[8,128]{1,0:T(8,128)S(1)}) custom-call(s32[1]{0:T(128)} %bitcast.refs_0_, bf16[1024,768]{1,0:T(8,128)(2,1)S(1)} %get-tuple-element.292.refs_1_.refs_6_, ...), custom_call_target="tpu_custom_call" | custom-call | flops 1207959552 | bytes 9043968 | tf_op jit(solution)/shard_map/pallas_call | solution.py:93
  74.7 4.5 %collective-permute-done.18.refs_13_.refs_7_.refs_2_ = bf16[384,768]{1,0:T(8,128)(2,1)} collective-permute-done((bf16[384,768]{1,0:T(8,128)(2,1)}, bf16[384,768]{1,0:T(8,128)(2,1)}, u32[]{:S(2)}, u32[]{:S(2)}) %collective-permute-start.18) | collective-permute-done | bytes 589856 | tf_op jit(solution)/shard_map/ppermute | solution.py:103
  83.9 12.7 %shard_map.275 = (bf16[1024,3072]{1,0:T(8,128)(2,1)}, bf16[1024,3072]{1,0:T(8,128)(2,1)}, f32[8,128]{1,0:T(8,128)S(1)}) custom-call(s32[1]{0:T(128)} %bitcast.refs_0_, bf16[1024,768]{1,0:T(8,128)(2,1)S(1)} %get-tuple-element.297.refs_1_, f32[1,3072]{1,0:T(1,128)S(1)} %get-tuple-element.298.refs_2_, bf16[112,3840]{1,0:T(8,128)(2,1)} %fusion.2.refs_3_.refs_11_.refs_9_, ...), custom_call_target="tpu_custom_call" | custom-call | flops 4831838208 | bytes 18874368 | tf_op jit(solution)/shard_map/pallas_call | solution.py:93
  99.0 15.6 %shard_map.276 = (bf16[1024,768]{1,0:T(8,128)(2,1)}, f32[1024,768]{1,0:T(8,128)}, f32[1024,1]{1,0:T(8,128)}, bf16[16,896]{1,0:T(8,128)(2,1)S(1)}, f32[16,768]{1,...) custom-call(s32[1]{0:T(128)} %bitcast.refs_0_, bf16[1024,3072]{1,0:T(8,128)(2,1)} %get-tuple-element.304.refs_1_.refs_7_, ...), custom_call_target="tpu_custom_call" | custom-call | flops 4831838208 | bytes 18874368 | tf_op jit(solution)/shard_map/pallas_call | solution.py:93
  116.4 2.6 collective-permute-start.28
  119.1 3.0 shard_map.277
  128.3 3.8 %shard_map.278 = (bf16[3072,768]{1,0:T(8,128)(2,1)S(1)}, bf16[768,3072]{1,0:T(8,128)(2,1)S(1)}, f32[8,128]{1,0:T(8,128)S(1)}) custom-call(s32[1]{0:T(128)} %bitcast.refs_0_, bf16[384,768]{1,0:T(8,128)(2,1)} %refs_1_.1, bf16[384,768]{1,0:T(8,128)(2,1)} %collective-permute-done.18.refs_13_.refs_7_.refs_2_, ...), custom_call_target="tpu_custom_call" | custom-call | bytes 18874368 | tf_op jit(solution)/shard_map/pallas_call | solution.py:93
  141.3 3.5 %shard_map.279 = (f32[16,1]{1,0:T(8,128)S(1)}, f32[16,768]{1,0:T(8,128)S(1)}, f32[8,128]{1,0:T(8,128)}) custom-call(s32[2]{0:T(128)S(1)} %pad_add_fusion.refs_0_, bf16[16,896]{1,0:T(8,128)(2,1)S(1)} %get-tuple-element.316.refs_3_.refs_1_, s32[16,1]{1,0:T(8,128)S(1)} %copy.41.refs_5_.refs_2_, f32[16,768]{1,0:T(8,128)S(1)} %get-tuple-element.313.refs_3_, ...), custom_call_target="tpu_custom_call" | custom-call | flops 402653184 | bytes 786432 | tf_op jit(solution)/shard_map/pallas_call | solution.py:93
  144.8 12.3 %shard_map.280 = (f32[1024,768]{1,0:T(8,128)S(1)}, bf16[1024,768]{1,0:T(8,128)(2,1)S(1)}, f32[8,768]{1,0:T(8,128)S(1)}, bf16[4,768,384]{2,1,0:T(8,128)(2,1)S(1)}...) custom-call(s32[1]{0:T(128)} %bitcast.refs_0_, bf16[1024,768]{1,0:T(8,128)(2,1)} %bitcast.36, ...), custom_call_target="tpu_custom_call" | custom-call | flops 4831838208 | bytes 20447232 | tf_op jit(solution)/shard_map/pallas_call | solution.py:93
  157.3 10.9 %shard_map.281 = (f32[1024,768]{1,0:T(8,128)S(1)}, f32[1,3072]{1,0:T(1,128)S(1)}, bf16[4,96,3072]{2,1,0:T(8,128)(2,1)S(1)}, bf16[4,96,3072]{2,1,0:T(8,128)(2,1)S(1)}, f32[8,128]{1,0:T(8,128)}) custom-call(s32[1]{0:T(128)} %bitcast.refs_0_, bf16[1024,768]{1,0:T(8,128)(2,1)S(1)} %get-tuple-element.331.refs_1_, bf16[1024,3072]{1,0:T(8,128)(2,1)} %get-tuple-element.332.refs_2_, ...), custom_call_target="tpu_custom_call" | custom-call | flops 7247757312 | bytes 23592960 | tf_op jit(solution)/shard_map/pallas_call | solution.py:93
  171.9 10.9 %shard_map.283 = (f32[1024,768]{1,0:T(8,128)S(1)}, f32[1,3072]{1,0:T(1,128)S(1)}, bf16[4,96,3072]{2,1,0:T(8,128)(2,1)S(1)}, bf16[4,96,3072]{2,1,0:T(8,128)(2,1)S(1)}, f32[8,128]{1,0:T(8,128)}) custom-call(s32[1]{0:T(128)} %bitcast.refs_0_, ...), custom_call_target="tpu_custom_call", output_to_operand_aliasing={{0}: (6, {}), {1}: (7, {}), {2}: (8, {}), {3}: (9, {})} | custom-call | flops 7247757312 | bytes 23592960 | tf_op jit(solution)/shard_map/pallas_call | solution.py:93
  184.5 8.7 %shard_map.284 = (f32[1024,768]{1,0:T(8,128)S(1)}, bf16[1024,768]{1,0:T(8,128)(2,1)S(1)}, bf16[4,112,768]{2,1,0:T(8,128)(2,1)S(1)}, bf16[4,112,768]{2,1,0:T(8,128)(2,1)}, f32[8,128]{1,0:T(8,128)}) custom-call(s32[1]{0:T(128)} %bitcast.refs_0_, f32[1024,768]{1,0:T(8,128)S(1)} %get-tuple-element.357.refs_1_, f32[1024,768]{1,0:T(8,128)S(1)} %get-tuple-element.358.refs_2_, ...), custom_call_target="tpu_custom_call" | custom-call | flops 2415919104 | bytes 18087936 | tf_op jit(solution)/shard_map/pallas_call | solution.py:93
  199.6 7.5 %shard_map.286 = (bf16[1024,256]{1,0:T(8,128)(2,1)S(1)}, bf16[1024,256]{1,0:T(8,128)(2,1)S(1)}, bf16[1024,256]{1,0:T(8,128)(2,1)S(1)}, bf16[4,112,768]{2,1,0:T(8...) custom-call(s32[1]{0:T(128)} %bitcast.refs_0_, bf16[1024,2304]{1,0:T(8,128)(2,1)} %copy-done, ...), custom_call_target="tpu_custom_call" | custom-call | flops 2013265920 | bytes 5242880 | tf_op jit(solution)/shard_map/pallas_call | solution.py:93
  212.2 2.5 collective-permute-start.44
  216.4 6.6 %shard_map.287 = (bf16[1024,256]{1,0:T(8,128)(2,1)S(1)}, bf16[1024,256]{1,0:T(8,128)(2,1)S(1)}, bf16[1024,256]{1,0:T(8,128)(2,1)S(1)}, bf16[4,112,768]{2,1,0:T(8...) custom-call(s32[1]{0:T(128)} %bitcast.refs_0_, bf16[1024,2304]{1,0:T(8,128)(2,1)} %copy-done, ...), custom_call_target="tpu_custom_call" | custom-call | flops 2013265920 | bytes 5242880 | tf_op jit(solution)/shard_map/pallas_call | solution.py:93
  228.0 6.6 %shard_map.289 = (bf16[1024,256]{1,0:T(8,128)(2,1)S(1)}, bf16[1024,256]{1,0:T(8,128)(2,1)S(1)}, bf16[1024,256]{1,0:T(8,128)(2,1)S(1)}, bf16[4,112,768]{2,1,0:T(8...) custom-call(s32[1]{0:T(128)} %bitcast.refs_0_, bf16[1024,2304]{1,0:T(8,128)(2,1)} %copy-done, ...), custom_call_target="tpu_custom_call" | custom-call | flops 2013265920 | bytes 5242880 | tf_op jit(solution)/shard_map/pallas_call | solution.py:93
  237.6 3.5 %collective-permute-start.54 = (bf16[96,3072]{1,0:T(8,128)(2,1)S(1)}, bf16[96,3072]{1,0:T(8,128)(2,1)S(1)}, u32[]{:S(2)}, u32[]{:S(2)}) collective-permute-start(bf16[96,3072]{1,0:T(8,128)(2,1)S(1)} %add_convert_fusion.3.refs_22_), channel_id=1, source_target_pairs={{0,8},{24,16},{1,9},{25,17},{2,10},{26,18},{3,11},{27,19},{4,12},{... | collective-permute-start | bytes 1769480 | tf_op jit(solution)/shard_map/ppermute | solution.py:1293
  244.7 9.0 %shard_map.291 = (f32[1024,768]{1,0:T(8,128)}, f32[8,128]{1,0:T(8,128)}) custom-call(s32[1]{0:T(128)} %bitcast.refs_0_, f32[1024,768]{1,0:T(8,128)S(1)} %copy-done.8, bf16[1024,256]{1,0:T(8,128)(2,1)S(1)} %copy-done.19, bf16[1024,256]{1,0:T(8,128)(2,1)S(1)} %get-tuple-element.401.refs_3_, bf16[1024,256]{1,0:T(8,128)(2,1)S(1)} %get-tuple-element.421.refs_4_, ...), custom_call_target="tpu_custom_call" | custom-call | flops 3623878656 | bytes 14548992 | tf_op jit(solution)/shard_map/pallas_call | solution.py:93
  258.8 6.5 %collective-permute-done.56 = bf16[112,1536]{1,0:T(8,128)(2,1)S(1)} collective-permute-done((bf16[112,1536]{1,0:T(8,128)(2,1)S(1)}, bf16[112,1536]{1,0:T(8,128)(2,1)S(1)}, u32[]{:S(2)}, u32[]{:S(2)}) %collective-permute-start.56) | collective-permute-done | bytes 344096 | tf_op jit(solution)/shard_map/ppermute | solution.py:103
  266.1 3.2 %collective-permute-start.57 = (bf16[112,1536]{1,0:T(8,128)(2,1)S(1)}, bf16[112,1536]{1,0:T(8,128)(2,1)S(1)}, u32[]{:S(2)}, u32[]{:S(2)}) collective-permute-start(bf16[112,1536]{1,0:T(8,128)(2,1)S(1)} %add_convert_fusion.10), channel_id=1, source_target_pairs={{0,8},{24,16},{1,9},{25,17},{2,10},{26,18},{3,11},{27,19},{4,12},{... | collective-permute-start | bytes 1032200 | tf_op jit(solution)/shard_map/ppermute | solution.py:1293
  272.2 4.5 %collective-permute-done.57 = bf16[112,1536]{1,0:T(8,128)(2,1)S(1)} collective-permute-done((bf16[112,1536]{1,0:T(8,128)(2,1)S(1)}, bf16[112,1536]{1,0:T(8,128)(2,1)S(1)}, u32[]{:S(2)}, u32[]{:S(2)}) %collective-permute-start.57) | collective-permute-done | bytes 344096 | tf_op jit(solution)/shard_map/ppermute | solution.py:1293
  281.7 3.5 %collective-permute-start.64 = (bf16[112,1536]{1,0:T(8,128)(2,1)S(1)}, bf16[112,1536]{1,0:T(8,128)(2,1)S(1)}, u32[]{:S(2)}, u32[]{:S(2)}) collective-permute-start(bf16[112,1536]{1,0:T(8,128)(2,1)S(1)} %add_convert_fusion.7), channel_id=1, source_target_pairs={{0,16},{16,0},{8,24},{24,8},{1,17},{17,1},{9,25},{25,9},{2,18},{18... | collective-permute-start | bytes 1032200 | tf_op jit(solution)/shard_map/ppermute | solution.py:1293
  287.5 14.4 %collective-permute-done.64 = bf16[112,1536]{1,0:T(8,128)(2,1)S(1)} collective-permute-done((bf16[112,1536]{1,0:T(8,128)(2,1)S(1)}, bf16[112,1536]{1,0:T(8,128)(2,1)S(1)}, u32[]{:S(2)}, u32[]{:S(2)}) %collective-permute-start.64) | collective-permute-done | bytes 344096 | tf_op jit(solution)/shard_map/ppermute | solution.py:1293
  303.2 3.2 %collective-permute-done.63 = bf16[112,1536]{1,0:T(8,128)(2,1)S(1)} collective-permute-done((bf16[112,1536]{1,0:T(8,128)(2,1)S(1)}, bf16[112,1536]{1,0:T(8,128)(2,1)S(1)}, u32[]{:S(2)}, u32[]{:S(2)}) %collective-permute-start.63) | collective-permute-done | bytes 344096 | tf_op jit(solution)/shard_map/ppermute | solution.py:1293
  (295 shorter events, 103.8 us)
Async XLA Ops:
  2.4 14.8 %collective-permute-start = (bf16[112,2304]{1,0:T(8,128)(2,1)S(1)}, bf16[112,2304]{1,0:T(8,128)(2,1)S(1)}, u32[]{:S(2)}, u32[]{:S(2)}) collective-permute-start(bf16[112,2304]{1,0:T(8,128)(2,1)S(1)} %fusion.3.refs_2_.refs_11_), channel_id=1, source_target_pairs={{0,2},{1,3},{2,0},{3,1},{4,6},{5,7},{6,4},{7,5},{8,10},{9,11},{10,... | collective-permute-start | bytes 1548296 | tf_op jit(solution)/shard_map/ppermute | solution.py:103
  5.4 13.2 %collective-permute-start.1 = (bf16[112,2304]{1,0:T(8,128)(2,1)S(1)}, bf16[112,2304]{1,0:T(8,128)(2,1)S(1)}, u32[]{:S(2)}, u32[]{:S(2)}) collective-permute-start(bf16[112,2304]{1,0:T(8,128)(2,1)S(1)} %fusion.3.refs_2_.refs_11_), channel_id=1, source_target_pairs={{0,4},{1,5},{2,6},{3,7},{4,0},{5,1},{6,2},{7,3},{8,12},{9,13},{10,... | collective-permute-start | bytes 1548296 | tf_op jit(solution)/shard_map/ppermute | solution.py:103
  6.9 22.1 %collective-permute-start.2 = (bf16[112,2304]{1,0:T(8,128)(2,1)S(1)}, bf16[112,2304]{1,0:T(8,128)(2,1)}, u32[]{:S(2)}, u32[]{:S(2)}) collective-permute-start(bf16[112,2304]{1,0:T(8,128)(2,1)S(1)} %fusion.3.refs_2_.refs_11_), channel_id=1, source_target_pairs={{0,1},{1,0},{2,3},{3,2},{4,5},{5,4},{6,7},{7,6},{8,9},{9,8},{10,11... | collective-permute-start | bytes 1548296 | tf_op jit(solution)/shard_map/ppermute | solution.py:103
  28.1 21.0 %collective-permute-start.9 = (bf16[112,3840]{1,0:T(8,128)(2,1)}, bf16[112,3840]{1,0:T(8,128)(2,1)S(1)}, u32[]{:S(2)}, u32[]{:S(2)}) collective-permute-start(bf16[112,3840]{1,0:T(8,128)(2,1)} %fusion.2.refs_3_.refs_11_.refs_9_), channel_id=1, source_target_pairs={{0,2},{1,3},{2,0},{3,1},{4,6},{5,7},{6,4},{7,5},{8,10},{9,11},{10,... | collective-permute-start | bytes 2580488 | tf_op jit(solution)/shard_map/ppermute | solution.py:103
  28.7 20.7 %collective-permute-start.10 = (bf16[112,3840]{1,0:T(8,128)(2,1)}, bf16[112,3840]{1,0:T(8,128)(2,1)S(1)}, u32[]{:S(2)}, u32[]{:S(2)}) collective-permute-start(bf16[112,3840]{1,0:T(8,128)(2,1)} %fusion.2.refs_3_.refs_11_.refs_9_), channel_id=1, source_target_pairs={{0,4},{1,5},{2,6},{3,7},{4,0},{5,1},{6,2},{7,3},{8,12},{9,13},{10,... | collective-permute-start | bytes 2580488 | tf_op jit(solution)/shard_map/ppermute | solution.py:103
  30.9 33.7 %collective-permute-start.11 = (bf16[112,3840]{1,0:T(8,128)(2,1)}, bf16[112,3840]{1,0:T(8,128)(2,1)S(1)}, u32[]{:S(2)}, u32[]{:S(2)}) collective-permute-start(bf16[112,3840]{1,0:T(8,128)(2,1)} %fusion.2.refs_3_.refs_11_.refs_9_), channel_id=1, source_target_pairs={{0,1},{1,0},{2,3},{3,2},{4,5},{5,4},{6,7},{7,6},{8,9},{9,8},{10,11... | collective-permute-start | bytes 2580488 | tf_op jit(solution)/shard_map/ppermute | solution.py:103
  49.4 15.8 %collective-permute-start.12 = (bf16[112,3840]{1,0:T(8,128)(2,1)S(1)}, bf16[112,3840]{1,0:T(8,128)(2,1)S(1)}, u32[]{:S(2)}, u32[]{:S(2)}) collective-permute-start(bf16[112,3840]{1,0:T(8,128)(2,1)S(1)} %collective-permute-done.9.refs_5_.refs_4_.refs_12_.refs_10_), channel_id=1, source_target_pairs={{0,1},{1,0},{2,3},{3,2},{4,5},{5,4},{6,7},{7,6},{8,9},{9,8},{10,11... | collective-permute-start | bytes 2580488 | tf_op jit(solution)/shard_map/ppermute | solution.py:103
  49.4 13.7 %collective-permute-start.15 = (bf16[64,3840]{1,0:T(8,128)(2,1)S(1)}, bf16[64,3840]{1,0:T(8,128)(2,1)S(1)}, u32[]{:S(2)}, u32[]{:S(2)}) collective-permute-start(bf16[64,3840]{1,0:T(8,128)(2,1)S(1)} %slice.223), channel_id=1, source_target_pairs={{0,4},{1,5},{2,6},{3,7},{4,0},{5,1},{6,2},{7,3},{8,12},{9,13},{10,... | collective-permute-start | bytes 1474568 | tf_op jit(solution)/shard_map/ppermute | solution.py:103
  51.6 13.6 %collective-permute-start.13 = (bf16[112,3840]{1,0:T(8,128)(2,1)S(1)}, bf16[112,3840]{1,0:T(8,128)(2,1)S(1)}, u32[]{:S(2)}, u32[]{:S(2)}) collective-permute-start(bf16[112,3840]{1,0:T(8,128)(2,1)S(1)} %collective-permute-done.10.refs_6_.refs_5_.refs_13_.refs_11_), channel_id=1, source_target_pairs={{0,1},{1,0},{2,3},{3,2},{4,5},{5,4},{6,7},{7,6},{8,9},{9,8},{10,11... | collective-permute-start | bytes 2580488 | tf_op jit(solution)/shard_map/ppermute | solution.py:103
  63.1 16.1 %collective-permute-start.18 = (bf16[384,768]{1,0:T(8,128)(2,1)}, bf16[384,768]{1,0:T(8,128)(2,1)}, u32[]{:S(2)}, u32[]{:S(2)}) collective-permute-start(bf16[384,768]{1,0:T(8,128)(2,1)} %refs_1_.1), channel_id=1, source_target_pairs={{0,2},{1,3},{2,0},{3,1},{4,6},{5,7},{6,4},{7,5},{8,10},{9,11},{10,... | collective-permute-start | bytes 1769480 | tf_op jit(solution)/shard_map/ppermute | solution.py:103
  64.6 15.8 %collective-permute-start.19 = (bf16[384,768]{1,0:T(8,128)(2,1)}, bf16[384,768]{1,0:T(8,128)(2,1)}, u32[]{:S(2)}, u32[]{:S(2)}) collective-permute-start(bf16[384,768]{1,0:T(8,128)(2,1)} %refs_1_.1), channel_id=1, source_target_pairs={{0,4},{1,5},{2,6},{3,7},{4,0},{5,1},{6,2},{7,3},{8,12},{9,13},{10,... | collective-permute-start | bytes 1769480 | tf_op jit(solution)/shard_map/ppermute | solution.py:103
  65.1 32.1 %collective-permute-start.20 = (bf16[384,768]{1,0:T(8,128)(2,1)}, bf16[384,768]{1,0:T(8,128)(2,1)S(1)}, u32[]{:S(2)}, u32[]{:S(2)}) collective-permute-start(bf16[384,768]{1,0:T(8,128)(2,1)} %refs_1_.1), channel_id=1, source_target_pairs={{0,1},{1,0},{2,3},{3,2},{4,5},{5,4},{6,7},{7,6},{8,9},{9,8},{10,11... | collective-permute-start | bytes 1769480 | tf_op jit(solution)/shard_map/ppermute | solution.py:103
  80.4 16.9 %collective-permute-start.22 = (bf16[384,768]{1,0:T(8,128)(2,1)}, bf16[384,768]{1,0:T(8,128)(2,1)S(1)}, u32[]{:S(2)}, u32[]{:S(2)}) collective-permute-start(bf16[384,768]{1,0:T(8,128)(2,1)} %collective-permute-done.19.refs_14_.refs_8_.refs_3_), channel_id=1, source_target_pairs={{0,1},{1,0},{2,3},{3,2},{4,5},{5,4},{6,7},{7,6},{8,9},{9,8},{10,11... | collective-permute-start | bytes 1769480 | tf_op jit(solution)/shard_map/ppermute | solution.py:103
  81.4 15.9 %collective-permute-start.21 = (bf16[384,768]{1,0:T(8,128)(2,1)}, bf16[384,768]{1,0:T(8,128)(2,1)}, u32[]{:S(2)}, u32[]{:S(2)}) collective-permute-start(bf16[384,768]{1,0:T(8,128)(2,1)} %collective-permute-done.18.refs_13_.refs_7_.refs_2_), channel_id=1, source_target_pairs={{0,1},{1,0},{2,3},{3,2},{4,5},{5,4},{6,7},{7,6},{8,9},{9,8},{10,11... | collective-permute-start | bytes 1769480 | tf_op jit(solution)/shard_map/ppermute | solution.py:103
  82.9 13.6 %collective-permute-start.23 = (bf16[192,768]{1,0:T(8,128)(2,1)S(1)}, bf16[192,768]{1,0:T(8,128)(2,1)S(1)}, u32[]{:S(2)}, u32[]{:S(2)}) collective-permute-start(bf16[192,768]{1,0:T(8,128)(2,1)S(1)} %slice.224), channel_id=1, source_target_pairs={{0,2},{1,3},{2,0},{3,1},{4,6},{5,7},{6,4},{7,5},{8,10},{9,11},{10,... | collective-permute-start | bytes 884744 | tf_op jit(solution)/shard_map/ppermute | solution.py:103
  83.5 13.1 %collective-permute-start.24 = (bf16[192,768]{1,0:T(8,128)(2,1)S(1)}, bf16[192,768]{1,0:T(8,128)(2,1)}, u32[]{:S(2)}, u32[]{:S(2)}) collective-permute-start(bf16[192,768]{1,0:T(8,128)(2,1)S(1)} %slice.225), channel_id=1, source_target_pairs={{0,4},{1,5},{2,6},{3,7},{4,0},{5,1},{6,2},{7,3},{8,12},{9,13},{10,... | collective-permute-start | bytes 884744 | tf_op jit(solution)/shard_map/ppermute | solution.py:103
  168.8 14.0 %collective-permute-start.35 = (bf16[384,384]{1,0:T(8,128)(2,1)S(1)}, bf16[384,384]{1,0:T(8,128)(2,1)S(1)}, u32[]{:S(2)}, u32[]{:S(2)}) collective-permute-start(bf16[384,384]{1,0:T(8,128)(2,1)S(1)} %get-tuple-element.343.refs_10_), channel_id=1, source_target_pairs={{0,2},{1,3},{2,0},{3,1},{4,6},{5,7},{6,4},{7,5},{8,10},{9,11},{10,... | collective-permute-start | bytes 884744 | tf_op jit(solution)/shard_map/ppermute | solution.py:103
  183.3 23.7 %collective-permute-start.38 = (bf16[768,384]{1,0:T(8,128)(2,1)S(1)}, bf16[768,384]{1,0:T(8,128)(2,1)S(1)}, u32[]{:S(2)}, u32[]{:S(2)}) collective-permute-start(bf16[768,384]{1,0:T(8,128)(2,1)S(1)} %fusion.4.refs_19_), channel_id=1, source_target_pairs={{0,2},{1,3},{2,0},{3,1},{4,6},{5,7},{6,4},{7,5},{8,10},{9,11},{10,... | collective-permute-start | bytes 1769480 | tf_op jit(solution)/shard_map/ppermute | solution.py:103
  184.0 23.1 %collective-permute-start.39 = (bf16[768,384]{1,0:T(8,128)(2,1)S(1)}, bf16[768,384]{1,0:T(8,128)(2,1)S(1)}, u32[]{:S(2)}, u32[]{:S(2)}) collective-permute-start(bf16[768,384]{1,0:T(8,128)(2,1)S(1)} %fusion.5.refs_20_), channel_id=1, source_target_pairs={{0,4},{1,5},{2,6},{3,7},{4,0},{5,1},{6,2},{7,3},{8,12},{9,13},{10,... | collective-permute-start | bytes 1769480 | tf_op jit(solution)/shard_map/ppermute | solution.py:103
  208.2 14.8 %collective-permute-start.42 = (bf16[4,112,768]{2,1,0:T(8,128)(2,1)}, bf16[4,112,768]{2,1,0:T(8,128)(2,1)}, u32[]{:S(2)}, u32[]{:S(2)}) collective-permute-start(bf16[4,112,768]{2,1,0:T(8,128)(2,1)} %get-tuple-element.395), channel_id=1, source_target_pairs={{0,1},{1,0},{2,3},{3,2},{4,5},{5,4},{6,7},{7,6},{8,9},{9,8},{10,11... | collective-permute-start | bytes 2064392 | tf_op jit(solution)/shard_map/ppermute | solution.py:103
  212.2 22.4 %collective-permute-start.44 = (bf16[768,384]{1,0:T(8,128)(2,1)}, bf16[768,384]{1,0:T(8,128)(2,1)}, u32[]{:S(2)}, u32[]{:S(2)}) collective-permute-start(bf16[768,384]{1,0:T(8,128)(2,1)} %add_convert_fusion.5.refs_8_), channel_id=1, source_target_pairs={{0,8},{24,16},{1,9},{25,17},{2,10},{26,18},{3,11},{27,19},{4,12},{... | collective-permute-start | bytes 1769480 | tf_op jit(solution)/shard_map/ppermute | solution.py:1293
  215.3 21.5 %collective-permute-start.45 = (bf16[96,3072]{1,0:T(8,128)(2,1)}, bf16[96,3072]{1,0:T(8,128)(2,1)S(1)}, u32[]{:S(2)}, u32[]{:S(2)}) collective-permute-start(bf16[96,3072]{1,0:T(8,128)(2,1)} %fusion.6.refs_9_), channel_id=1, source_target_pairs={{0,2},{1,3},{2,0},{3,1},{4,6},{5,7},{6,4},{7,5},{8,10},{9,11},{10,... | collective-permute-start | bytes 1769480 | tf_op jit(solution)/shard_map/ppermute | solution.py:103
  215.9 20.9 %collective-permute-start.46 = (bf16[96,3072]{1,0:T(8,128)(2,1)}, bf16[96,3072]{1,0:T(8,128)(2,1)S(1)}, u32[]{:S(2)}, u32[]{:S(2)}) collective-permute-start(bf16[96,3072]{1,0:T(8,128)(2,1)} %fusion.7.refs_10_), channel_id=1, source_target_pairs={{0,4},{1,5},{2,6},{3,7},{4,0},{5,1},{6,2},{7,3},{8,12},{9,13},{10,... | collective-permute-start | bytes 1769480 | tf_op jit(solution)/shard_map/ppermute | solution.py:103
  226.5 14.7 %collective-permute-start.48 = (bf16[64,1536]{1,0:T(8,128)(2,1)S(1)}, bf16[64,1536]{1,0:T(8,128)(2,1)S(1)}, u32[]{:S(2)}, u32[]{:S(2)}) collective-permute-start(bf16[64,1536]{1,0:T(8,128)(2,1)S(1)} %get-tuple-element.400.refs_9_), channel_id=1, source_target_pairs={{0,4},{1,5},{2,6},{3,7},{4,0},{5,1},{6,2},{7,3},{8,12},{9,13},{10,... | collective-permute-start | bytes 589832 | tf_op jit(solution)/shard_map/ppermute | solution.py:103
  236.1 19.9 %collective-permute-start.53 = (bf16[768,384]{1,0:T(8,128)(2,1)S(1)}, bf16[768,384]{1,0:T(8,128)(2,1)S(1)}, u32[]{:S(2)}, u32[]{:S(2)}) collective-permute-start(bf16[768,384]{1,0:T(8,128)(2,1)S(1)} %add_convert_fusion.4.refs_21_), channel_id=1, source_target_pairs={{8,16},{16,8},{9,17},{17,9},{10,18},{18,10},{11,19},{19,11},{12,20... | collective-permute-start | bytes 1769480 | tf_op jit(solution)/shard_map/ppermute | solution.py:1293
  237.6 19.8 %collective-permute-start.54 = (bf16[96,3072]{1,0:T(8,128)(2,1)S(1)}, bf16[96,3072]{1,0:T(8,128)(2,1)S(1)}, u32[]{:S(2)}, u32[]{:S(2)}) collective-permute-start(bf16[96,3072]{1,0:T(8,128)(2,1)S(1)} %add_convert_fusion.3.refs_22_), channel_id=1, source_target_pairs={{0,8},{24,16},{1,9},{25,17},{2,10},{26,18},{3,11},{27,19},{4,12},{... | collective-permute-start | bytes 1769480 | tf_op jit(solution)/shard_map/ppermute | solution.py:1293
  241.3 17.5 %collective-permute-start.55 = (bf16[112,1536]{1,0:T(8,128)(2,1)S(1)}, bf16[112,1536]{1,0:T(8,128)(2,1)S(1)}, u32[]{:S(2)}, u32[]{:S(2)}) collective-permute-start(bf16[112,1536]{1,0:T(8,128)(2,1)S(1)} %fusion.8.refs_23_), channel_id=1, source_target_pairs={{0,2},{1,3},{2,0},{3,1},{4,6},{5,7},{6,4},{7,5},{8,10},{9,11},{10,... | collective-permute-start | bytes 1032200 | tf_op jit(solution)/shard_map/ppermute | solution.py:103
  255.4 13.9 %collective-permute-start.59 = (bf16[112,1536]{1,0:T(8,128)(2,1)S(1)}, bf16[112,1536]{1,0:T(8,128)(2,1)S(1)}, u32[]{:S(2)}, u32[]{:S(2)}) collective-permute-start(bf16[112,1536]{1,0:T(8,128)(2,1)S(1)} %fusion.9), channel_id=1, source_target_pairs={{0,2},{1,3},{2,0},{3,1},{4,6},{5,7},{6,4},{7,5},{8,10},{9,11},{10,... | collective-permute-start | bytes 1032200 | tf_op jit(solution)/shard_map/ppermute | solution.py:103
  256.2 22.1 %collective-permute-start.66 = (bf16[768,384]{1,0:T(8,128)(2,1)S(1)}, bf16[768,384]{1,0:T(8,128)(2,1)S(1)}, u32[]{:S(2)}, u32[]{:S(2)}) collective-permute-start(bf16[768,384]{1,0:T(8,128)(2,1)S(1)} %add_convert_fusion.2), channel_id=1, source_target_pairs={{8,0},{16,24},{9,1},{17,25},{10,2},{18,26},{11,3},{19,27},{12,4},{... | collective-permute-start | bytes 1769480 | tf_op jit(solution)/shard_map/ppermute | solution.py:1293
  270.9 31.1 %collective-permute-start.65 = (bf16[96,3072]{1,0:T(8,128)(2,1)S(1)}, bf16[96,3072]{1,0:T(8,128)(2,1)S(1)}, u32[]{:S(2)}, u32[]{:S(2)}) collective-permute-start(bf16[96,3072]{1,0:T(8,128)(2,1)S(1)} %add_convert_fusion), channel_id=1, source_target_pairs={{8,0},{16,24},{9,1},{17,25},{10,2},{18,26},{11,3},{19,27},{12,4},{... | collective-permute-start | bytes 1769480 | tf_op jit(solution)/shard_map/ppermute | solution.py:1293
  281.7 20.2 %collective-permute-start.64 = (bf16[112,1536]{1,0:T(8,128)(2,1)S(1)}, bf16[112,1536]{1,0:T(8,128)(2,1)S(1)}, u32[]{:S(2)}, u32[]{:S(2)}) collective-permute-start(bf16[112,1536]{1,0:T(8,128)(2,1)S(1)} %add_convert_fusion.7), channel_id=1, source_target_pairs={{0,16},{16,0},{8,24},{24,8},{1,17},{17,1},{9,25},{25,9},{2,18},{18... | collective-permute-start | bytes 1032200 | tf_op jit(solution)/shard_map/ppermute | solution.py:1293
  286.2 20.2 %collective-permute-start.63 = (bf16[112,1536]{1,0:T(8,128)(2,1)S(1)}, bf16[112,1536]{1,0:T(8,128)(2,1)S(1)}, u32[]{:S(2)}, u32[]{:S(2)}) collective-permute-start(bf16[112,1536]{1,0:T(8,128)(2,1)S(1)} %add_convert_fusion.6), channel_id=1, source_target_pairs={{8,0},{16,24},{9,1},{17,25},{10,2},{18,26},{11,3},{19,27},{12,4},{... | collective-permute-start | bytes 1032200 | tf_op jit(solution)/shard_map/ppermute | solution.py:1293
  (83 other events, 688.3 us)

commit v4 on v3

--- a/solution.py
+++ b/solution.py
@@ -1126,7 +1126,7 @@
     def put(tile, kind, value):
         pair, row, (_, _, at) = tile
         here = slice(row * length + at, row * length + at + TILE)
-        cols = slice((3 * pair + kind) * lanes, (3 * pair + kind + 1) * lanes)
+        cols = slice((kind * group + pair) * lanes, (kind * group + pair + 1) * lanes)
         both_ref[here, cols] = value.astype(bf16)
 
     def end(tile, d_scores):
@@ -1156,17 +1156,16 @@
         if 0 <= step - 3 < len(tiles):
             end_keys(tiles[step - 3])
     both = both_ref[...]
-    for pair in range(group):
-        for kind, target in enumerate((dq_ref, dk_ref, dv_ref)):
-            cols = slice((3 * pair + kind) * lanes, (3 * pair + kind + 1) * lanes)
-            target[:, pair * lanes : (pair + 1) * lanes] = both[:, cols]
+    wide = group * lanes
+    for kind, target in enumerate((dq_ref, dk_ref, dv_ref)):
+        target[...] = both[:, kind * wide : (kind + 1) * wide]
     grad = dot(tt_ref[...], both).astype(bf16)
     width = grad.shape[0]
     part = width // BLOCKS
     span = both.shape[1]
     col = lax.broadcasted_iota(jnp.int32, (1, span), 1)
-    kind = col // lanes % 3
-    place = (pl.program_id(0) * group + first + col // (3 * lanes)) * lanes + col % lanes
+    kind = col // wide
+    place = (pl.program_id(0) * group + first) * lanes + col - kind * wide
     owner = jnp.where(kind == 1, -1, (place + jnp.where(kind == 2, width, 0)) // (2 * part))
     sums = column_sum(both.astype(f32))
     line = lax.broadcasted_iota(jnp.int32, (16, span), 0)
@@ -1353,9 +1352,16 @@
 
     def over_chips(self, from_x, from_y):
         self.total = rounded(add(self.blocks[0], from_x, from_y))
-        pairs = [(0, 1), (3, 2)] if self.line else [(0, 1), (1, 0), (2, 3), (3, 2)]
-        self.arrived = [along_z(self.total, pairs)]
-        return [self.total]
+        sent = self.total
+        if self.line:
+            self.arrived = [along_z(sent, [(0, 1), (3, 2)])]
+            return [sent]
+        half = sent.shape[0] // 2
+        self.odd = lax.axis_index("batch") % 2 == 1
+        self.total = jnp.where(self.odd, sent[half:], sent[:half])
+        sent = jnp.where(self.odd, sent[:half], sent[half:])
+        self.arrived = [swap(sent, "batch", self.planes, 1)]
+        return [sent]
 
     def over_z(self, other):
         self.total = rounded(add(self.total, other))
@@ -1364,18 +1370,20 @@
         return [self.total]
 
     def over_middle(self, other):
-        if self.line:
-            self.total = rounded(add(self.total, other))
-            self.arrived = [along_z(self.total, [(1, 0), (2, 3)])]
+        self.total = rounded(add(self.total, other))
+        pairs = [(1, 0), (2, 3)] if self.line else [(0, 1), (1, 0), (2, 3), (3, 2)]
+        self.arrived = [along_z(self.total, pairs)]
         return [self.total]
 
     def result(self):
         other = self.arrived[0]
-        if not self.line:
-            return add(self.total, other)
-        plane = lax.axis_index("batch")
-        inside = (plane == 1) | (plane == 2)
-        return jnp.where(inside, self.total, other).astype(f32)
+        if self.line:
+            plane = lax.axis_index("batch")
+            inside = (plane == 1) | (plane == 2)
+            return jnp.where(inside, self.total, other).astype(f32)
+        upper = jnp.where(self.odd, other, self.total)
+        lower = jnp.where(self.odd, self.total, other)
+        return jnp.concatenate([upper, lower], axis=0).astype(f32)
 
 
 def layer(
@@ -1450,13 +1458,13 @@
     late = ()
     if paired:
         *third_xy, clock = tie((*third_xy, clock))
-        third_far = second_stage(w_down, *third_xy)
+        third_far = fsdp_swap(third_xy[0], 4)
         late = (*third_xy, clock)
     activated, slope, clock = up(index, hidden, bias_up, mid_pieces, late)
     if paired:
         down_pieces = both_cores(own_pieces(w_down, *third_xy))
-        *third_far, clock = tie((*third_far, clock))
-        down_pieces += both_cores(far_pieces(w_down, *third_far))
+        third_far, clock = tie((third_far, clock))
+        down_pieces += both_cores([(third_far, 6, 0)])
     result, normed2, root2, payload, pooled, stats, _ = down(
         index, activated, normed1, rows, seg_rows, pos_col, down_pieces, (clock,)
     )
@@ -1517,7 +1525,7 @@
         )[:4]
         half, sent = go(half, sum_down)
     d_hidden, sums_up, keep_up, send_up = half
-    sum_up = start([keep_up], [send_up], True)
+    sum_up = start([keep_up], [send_up], False)
     *first_norm, _ = norm1(
         index,
         [d_hidden],
@@ -1572,8 +1580,7 @@
         grad_down, grad_up = sum_down.result().T, sum_up.result()
         left, right = sum_left.result(), sum_right.result()
         grad_out = left[:part, :width]
-        grad_qkv = jnp.concatenate([left[:part, width:], right[:part]], axis=1)
-        vector = jnp.concatenate([left[part, width:], right[part]])
+        joined = [left[:, width:], right[:, :width], right[:, width:]]
         own_vectors = [left[part, i * TILE : i * TILE + part] for i in range(6)]
         own_vectors.append(left[part + 1, : sizes[-1]])
     else:
@@ -1595,15 +1602,19 @@
         grad_out = own_rows(left[:, :part])
         own_vectors = [own_values(left[:, part, i * TILE : i * TILE + part]) for i in range(6)]
         own_vectors.append(own_values(left[:, part + 1, : sizes[-1]]))
-        wide = jnp.concatenate([scatter(back[3], back[4]) for back in backs], axis=2)
-        grad_qkv = own_rows(wide[:, :part])
-        vector = lax.psum(jnp.sum(wide[:, part], axis=0), "fsdp")
-
-    depth = grad_qkv.shape[0]
-    grad_qkv = grad_qkv.reshape(depth, pairs, 3, lanes).transpose(0, 2, 1, 3)
-    grad_qkv = grad_qkv.reshape(depth, 3 * width)
-    vector = vector.reshape(pairs, 3, lanes)
-    vector = jnp.concatenate([vector[:, 0].reshape(-1), vector[:, 2].reshape(-1)])
+        whole_grads = [scatter(back[3], back[4]) for back in backs]
+        joined = []
+        for grads in whole_grads:
+            line = lax.psum(jnp.sum(grads[:, part], axis=0), "fsdp")
+            joined.append(jnp.concatenate([own_rows(grads[:, :part]), line[None]], axis=0))
+
+    span = width // cuts
+    ordered = [
+        group[:, kind * span : (kind + 1) * span] for kind in range(3) for group in joined
+    ]
+    depth = joined[0].shape[0] - 1 if not paired else part
+    grad_qkv = jnp.concatenate([group[:depth] for group in ordered], axis=1)
+    vector = jnp.concatenate([group[depth] for group in ordered[:cuts] + ordered[2 * cuts :]])
     shard = vector.shape[0] // ring
     grad_bqv = lax.dynamic_slice(vector, (fsdp * shard,), (shard,))
     grad_bout, grad_g1, grad_s1, grad_bdown, grad_g2, grad_s2, grad_bup = own_vectors

time: 316 us -> 309 us (0.978)
  starting transfers between devices: 59.9 us -> 54.4 us
    ppermute x56, waiting for transfers between devices: 41.7 us -> 53.4 us  [swap(): return lax.ppermute(value, axis, [(i, i ^ bit) for i in range(size)])]
    ppermute x11 -> x10, waiting for transfers between devices: 24 us -> 14.9 us  [along_z(): return lax.ppermute(value, 'batch', pairs)]
    ppermute x11 -> x10, starting transfers between devices: 19.4 us -> 12.5 us  [along_z(): return lax.ppermute(value, 'batch', pairs)]
    unnamed x107 -> x118, local copies, waits for them, and re-layouts: 13.6 us -> 13.6 us
  transfers between devices with their start and end apart: 67 -> 66, of which waited for: 22 -> 23; matrix products, arithmetic and copies ran while one was open for 7% -> 7% of each run, Pallas kernels for 35% -> 36%
where the time goes in v4:
time: 309 us; the launch traced here: 304 us
  Pallas kernels  143 us (46%)
  waiting for transfers between devices  68.3 us (22%)
  starting transfers between devices  54.4 us (18%)
  local copies, waits for them, and re-layouts  23.2 us (8%)
  other arithmetic  13.5 us (4%)
    pallas_call x21, Pallas kernels, apply(): return run(index, *placed, *after)  143 us
    ppermute x56, waiting for transfers between devices, swap(): return lax.ppermute(value, axis, [(i, i ^ bit) for i in range(size)])  53.4 us
    ppermute x56, starting transfers between devices, swap(): return lax.ppermute(value, axis, [(i, i ^ bit) for i in range(size)])  41.8 us
    ppermute x10, waiting for transfers between devices, along_z(): return lax.ppermute(value, 'batch', pairs)  14.9 us
    unnamed x118, local copies, waits for them, and re-layouts  13.6 us
    ppermute x10, starting transfers between devices, along_z(): return lax.ppermute(value, 'batch', pairs)  12.5 us
  transfers between devices with their start and end apart: 66, of which 23 were waited for; matrix products, arithmetic and copies ran while one was open for 7% of the time, Pallas kernels for 36%

profile of v4, /device:TPU:0, one launch (start us, length us, event | category | flops | bytes accessed | tf_op | source)
XLA Modules:
  0.0 304.3 jit_solution(15086946474885514433)
XLA Ops:
  2.4 3.0 collective-permute-start
  21.1 7.1 %collective-permute-done.5.refs_8_.refs_17_ = bf16[48,2304]{1,0:T(8,128)(2,1)S(1)} collective-permute-done((bf16[48,2304]{1,0:T(8,128)(2,1)S(1)}, bf16[48,2304]{1,0:T(8,128)(2,1)S(1)}, u32[]{:S(2)}, u32[]{:S(2)}) %collective-permute-start.5) | collective-permute-done | bytes 221216 | tf_op jit(solution)/shard_map/ppermute | solution.py:103
  31.6 9.4 %shard_map.271 = (bf16[1024,2304]{1,0:T(8,128)(2,1)S(1)}, f32[8,128]{1,0:T(8,128)}) custom-call(s32[1]{0:T(128)} %bitcast.refs_0_, bf16[1024,768]{1,0:T(8,128)(2,1)} %bitcast.31, bf16[112,2304]{1,0:T(8,128)(2,1)} %copy-done.32, bf16[112,2304]{1,0:T(8,128)(2,1)} %copy-done.33, bf16[112,2304]{1,0:T(8,128)(2,1)} %copy-done.34, ...), custom_call_target="tpu_custom_call" | custom-call | flops 3623878656 | bytes 9830400 | tf_op jit(solution)/shard_map/pallas_call | solution.py:93
  41.0 5.0 %shard_map.272 = (bf16[1024,768]{1,0:T(8,128)(2,1)S(1)}, f32[2,6,2,512]{3,2,1,0:T(2,128)S(1)}, f32[8,128]{1,0:T(8,128)S(1)}) custom-call(s32[1]{0:T(128)} %bitcast.refs_0_, bf16[1024,2304]{1,0:T(8,128)(2,1)S(1)} %get-tuple-element.283.refs_1_.refs_2_.refs_3_, s32[2,1,512]{2,1,0:T(1,128)} %reshape.243.refs_2_.refs_4_.refs_6_), custom_call_target="tpu_custom_call" | custom-call | flops 805306368 | bytes 3145728 | tf_op jit(solution)/shard_map/pallas_call | solution.py:93
  46.0 3.1 %collective-permute-done.9.refs_5_.refs_4_.refs_10_ = bf16[112,3840]{1,0:T(8,128)(2,1)S(1)} collective-permute-done((bf16[112,3840]{1,0:T(8,128)(2,1)}, bf16[112,3840]{1,0:T(8,128)(2,1)S(1)}, u32[]{:S(2)}, u32[]{:S(2)}) %collective-permute-start.9) | collective-permute-done | bytes 860192 | tf_op jit(solution)/shard_map/ppermute | solution.py:103
  51.6 5.0 %shard_map.273 = (bf16[1024,768]{1,0:T(8,128)(2,1)S(1)}, f32[2,6,2,512]{3,2,1,0:T(2,128)S(1)}, f32[8,128]{1,0:T(8,128)S(1)}) custom-call(s32[1]{0:T(128)} %bitcast.refs_0_, bf16[1024,2304]{1,0:T(8,128)(2,1)S(1)} %get-tuple-element.283.refs_1_.refs_2_.refs_3_, ...), custom_call_target="tpu_custom_call", output_to_operand_aliasing={{0}: (3, {}), {1}: (4, {})} | custom-call | flops 805306368 | bytes 3145728 | tf_op jit(solution)/shard_map/pallas_call | solution.py:93
  56.6 4.1 %collective-permute-done.14.refs_9_.refs_15_ = bf16[48,3840]{1,0:T(8,128)(2,1)S(1)} collective-permute-done((bf16[48,3840]{1,0:T(8,128)(2,1)S(1)}, bf16[48,3840]{1,0:T(8,128)(2,1)S(1)}, u32[]{:S(2)}, u32[]{:S(2)}) %collective-permute-start.14) | collective-permute-done | bytes 368672 | tf_op jit(solution)/shard_map/ppermute | solution.py:103
  60.6 2.5 collective-permute-done.15.refs_10_.refs_16_
  67.7 6.9 %shard_map.274 = (f32[1024,768]{1,0:T(8,128)}, f32[1024,1]{1,0:T(8,128)}, bf16[1024,768]{1,0:T(8,128)(2,1)S(1)}, f32[8,768]{1,0:T(8,128)S(1)}, f32[1,3072]{1,0:T(1,128)S(1)}, /*index=5*/f32[8,128]{1,0:T(8,128)S(1)}) custom-call(s32[1]{0:T(128)} %bitcast.refs_0_, bf16[1024,768]{1,0:T(8,128)(2,1)S(1)} %get-tuple-element.291.refs_1_.refs_6_, ...), custom_call_target="tpu_custom_call" | custom-call | flops 1207959552 | bytes 9043968 | tf_op jit(solution)/shard_map/pallas_call | solution.py:93
  74.6 4.5 %collective-permute-done.18.refs_13_.refs_7_.refs_2_ = bf16[384,768]{1,0:T(8,128)(2,1)} collective-permute-done((bf16[384,768]{1,0:T(8,128)(2,1)}, bf16[384,768]{1,0:T(8,128)(2,1)}, u32[]{:S(2)}, u32[]{:S(2)}) %collective-permute-start.18) | collective-permute-done | bytes 589856 | tf_op jit(solution)/shard_map/ppermute | solution.py:103
  81.4 12.9 %shard_map.275 = (bf16[1024,3072]{1,0:T(8,128)(2,1)}, bf16[1024,3072]{1,0:T(8,128)(2,1)}, f32[8,128]{1,0:T(8,128)S(1)}) custom-call(s32[1]{0:T(128)} %bitcast.refs_0_, bf16[1024,768]{1,0:T(8,128)(2,1)S(1)} %get-tuple-element.296.refs_1_, f32[1,3072]{1,0:T(1,128)S(1)} %get-tuple-element.297.refs_2_, bf16[112,3840]{1,0:T(8,128)(2,1)} %fusion.2.refs_3_.refs_9_, ...), custom_call_target="tpu_custom_call" | custom-call | flops 4831838208 | bytes 18874368 | tf_op jit(solution)/shard_map/pallas_call | solution.py:93
  97.4 15.6 %shard_map.276 = (bf16[1024,768]{1,0:T(8,128)(2,1)}, f32[1024,768]{1,0:T(8,128)}, f32[1024,1]{1,0:T(8,128)}, bf16[16,896]{1,0:T(8,128)(2,1)S(1)}, f32[16,768]{1,...) custom-call(s32[1]{0:T(128)} %bitcast.refs_0_, bf16[1024,3072]{1,0:T(8,128)(2,1)} %get-tuple-element.303.refs_1_.refs_7_, ...), custom_call_target="tpu_custom_call" | custom-call | flops 4831838208 | bytes 18874368 | tf_op jit(solution)/shard_map/pallas_call | solution.py:93
  114.6 2.6 collective-permute-start.26
  117.4 3.0 shard_map.277
  126.5 3.8 %shard_map.278 = (bf16[3072,768]{1,0:T(8,128)(2,1)S(1)}, bf16[768,3072]{1,0:T(8,128)(2,1)S(1)}, f32[8,128]{1,0:T(8,128)S(1)}) custom-call(s32[1]{0:T(128)} %bitcast.refs_0_, bf16[384,768]{1,0:T(8,128)(2,1)} %refs_1_.1, bf16[384,768]{1,0:T(8,128)(2,1)} %collective-permute-done.18.refs_13_.refs_7_.refs_2_, ...), custom_call_target="tpu_custom_call" | custom-call | bytes 18874368 | tf_op jit(solution)/shard_map/pallas_call | solution.py:93
  139.4 3.5 %shard_map.279 = (f32[16,1]{1,0:T(8,128)S(1)}, f32[16,768]{1,0:T(8,128)S(1)}, f32[8,128]{1,0:T(8,128)}) custom-call(s32[2]{0:T(128)S(1)} %pad_add_fusion.refs_0_, bf16[16,896]{1,0:T(8,128)(2,1)S(1)} %get-tuple-element.314.refs_3_.refs_1_, s32[16,1]{1,0:T(8,128)S(1)} %copy.40.refs_5_.refs_2_, f32[16,768]{1,0:T(8,128)S(1)} %get-tuple-element.311.refs_3_, ...), custom_call_target="tpu_custom_call" | custom-call | flops 402653184 | bytes 786432 | tf_op jit(solution)/shard_map/pallas_call | solution.py:93
  143.0 12.3 %shard_map.280 = (f32[1024,768]{1,0:T(8,128)S(1)}, bf16[1024,768]{1,0:T(8,128)(2,1)S(1)}, f32[8,768]{1,0:T(8,128)S(1)}, bf16[4,768,384]{2,1,0:T(8,128)(2,1)S(1)}...) custom-call(s32[1]{0:T(128)} %bitcast.refs_0_, bf16[1024,768]{1,0:T(8,128)(2,1)} %bitcast.42, ...), custom_call_target="tpu_custom_call" | custom-call | flops 4831838208 | bytes 20447232 | tf_op jit(solution)/shard_map/pallas_call | solution.py:93
  155.4 10.9 %shard_map.281 = (f32[1024,768]{1,0:T(8,128)S(1)}, f32[1,3072]{1,0:T(1,128)S(1)}, bf16[4,96,3072]{2,1,0:T(8,128)(2,1)S(1)}, bf16[4,96,3072]{2,1,0:T(8,128)(2,1)S(1)}, f32[8,128]{1,0:T(8,128)}) custom-call(s32[1]{0:T(128)} %bitcast.refs_0_, bf16[1024,768]{1,0:T(8,128)(2,1)S(1)} %get-tuple-element.329.refs_1_, bf16[1024,3072]{1,0:T(8,128)(2,1)} %get-tuple-element.330.refs_2_, ...), custom_call_target="tpu_custom_call" | custom-call | flops 7247757312 | bytes 23592960 | tf_op jit(solution)/shard_map/pallas_call | solution.py:93
  168.4 10.9 %shard_map.283 = (f32[1024,768]{1,0:T(8,128)S(1)}, f32[1,3072]{1,0:T(1,128)S(1)}, bf16[4,96,3072]{2,1,0:T(8,128)(2,1)S(1)}, bf16[4,96,3072]{2,1,0:T(8,128)(2,1)S(1)}, f32[8,128]{1,0:T(8,128)}) custom-call(s32[1]{0:T(128)} %bitcast.refs_0_, ...), custom_call_target="tpu_custom_call", output_to_operand_aliasing={{0}: (6, {}), {1}: (7, {}), {2}: (8, {}), {3}: (9, {})} | custom-call | flops 7247757312 | bytes 23592960 | tf_op jit(solution)/shard_map/pallas_call | solution.py:93
  182.6 8.7 %shard_map.284 = (f32[1024,768]{1,0:T(8,128)S(1)}, bf16[1024,768]{1,0:T(8,128)(2,1)S(1)}, bf16[4,112,768]{2,1,0:T(8,128)(2,1)S(1)}, bf16[4,112,768]{2,1,0:T(8,128)(2,1)}, f32[8,128]{1,0:T(8,128)}) custom-call(s32[1]{0:T(128)} %bitcast.refs_0_, f32[1024,768]{1,0:T(8,128)S(1)} %get-tuple-element.355.refs_1_, f32[1024,768]{1,0:T(8,128)S(1)} %get-tuple-element.356.refs_2_, ...), custom_call_target="tpu_custom_call" | custom-call | flops 2415919104 | bytes 18087936 | tf_op jit(solution)/shard_map/pallas_call | solution.py:93
  196.2 7.5 %shard_map.286 = (bf16[1024,256]{1,0:T(8,128)(2,1)S(1)}, bf16[1024,256]{1,0:T(8,128)(2,1)S(1)}, bf16[1024,256]{1,0:T(8,128)(2,1)S(1)}, bf16[4,112,768]{2,1,0:T(8...) custom-call(s32[1]{0:T(128)} %bitcast.refs_0_, bf16[1024,2304]{1,0:T(8,128)(2,1)} %copy-done, ...), custom_call_target="tpu_custom_call" | custom-call | flops 2013265920 | bytes 5242880 | tf_op jit(solution)/shard_map/pallas_call | solution.py:93
  209.0 2.4 collective-permute-start.42
  214.7 6.7 %shard_map.287 = (bf16[1024,256]{1,0:T(8,128)(2,1)S(1)}, bf16[1024,256]{1,0:T(8,128)(2,1)S(1)}, bf16[1024,256]{1,0:T(8,128)(2,1)S(1)}, bf16[4,112,768]{2,1,0:T(8...) custom-call(s32[1]{0:T(128)} %bitcast.refs_0_, bf16[1024,2304]{1,0:T(8,128)(2,1)} %copy-done, ...), custom_call_target="tpu_custom_call" | custom-call | flops 2013265920 | bytes 5242880 | tf_op jit(solution)/shard_map/pallas_call | solution.py:93
  224.7 6.7 %shard_map.289 = (bf16[1024,256]{1,0:T(8,128)(2,1)S(1)}, bf16[1024,256]{1,0:T(8,128)(2,1)S(1)}, bf16[1024,256]{1,0:T(8,128)(2,1)S(1)}, bf16[4,112,768]{2,1,0:T(8...) custom-call(s32[1]{0:T(128)} %bitcast.refs_0_, bf16[1024,2304]{1,0:T(8,128)(2,1)} %copy-done, ...), custom_call_target="tpu_custom_call" | custom-call | flops 2013265920 | bytes 5242880 | tf_op jit(solution)/shard_map/pallas_call | solution.py:93
  240.7 9.0 %shard_map.291 = (f32[1024,768]{1,0:T(8,128)}, f32[8,128]{1,0:T(8,128)}) custom-call(s32[1]{0:T(128)} %bitcast.refs_0_, f32[1024,768]{1,0:T(8,128)S(1)} %copy-done.8, bf16[1024,256]{1,0:T(8,128)(2,1)S(1)} %copy-done.19, bf16[1024,256]{1,0:T(8,128)(2,1)S(1)} %get-tuple-element.399.refs_3_, bf16[1024,256]{1,0:T(8,128)(2,1)S(1)} %get-tuple-element.419.refs_4_, ...), custom_call_target="tpu_custom_call" | custom-call | flops 3623878656 | bytes 14548992 | tf_op jit(solution)/shard_map/pallas_call | solution.py:93
  256.5 4.3 %collective-permute-done.54 = bf16[112,1536]{1,0:T(8,128)(2,1)S(1)} collective-permute-done((bf16[112,1536]{1,0:T(8,128)(2,1)S(1)}, bf16[112,1536]{1,0:T(8,128)(2,1)S(1)}, u32[]{:S(2)}, u32[]{:S(2)}) %collective-permute-start.54) | collective-permute-done | bytes 344096 | tf_op jit(solution)/shard_map/ppermute | solution.py:103
  260.9 3.3 %collective-permute-start.55 = (bf16[112,1536]{1,0:T(8,128)(2,1)S(1)}, bf16[112,1536]{1,0:T(8,128)(2,1)S(1)}, u32[]{:S(2)}, u32[]{:S(2)}) collective-permute-start(bf16[112,1536]{1,0:T(8,128)(2,1)S(1)} %add_convert_fusion.7), channel_id=1, source_target_pairs={{0,8},{24,16},{1,9},{25,17},{2,10},{26,18},{3,11},{27,19},{4,12},{... | collective-permute-start | bytes 1032200 | tf_op jit(solution)/shard_map/ppermute | solution.py:1292
  264.2 2.5 collective-permute-done.58
  271.5 11.7 %collective-permute-done.60 = bf16[56,1536]{1,0:T(8,128)(2,1)S(1)} collective-permute-done((bf16[56,1536]{1,0:T(8,128)(2,1)S(1)}, bf16[56,1536]{1,0:T(8,128)(2,1)S(1)}, u32[]{:S(2)}, u32[]{:S(2)}) %collective-permute-start.60) | collective-permute-done | bytes 172064 | tf_op jit(solution)/shard_map/ppermute | solution.py:103
  284.8 2.6 collective-permute-done.64
  291.9 5.2 %collective-permute-done.63 = bf16[56,1536]{1,0:T(8,128)(2,1)S(1)} collective-permute-done((bf16[56,1536]{1,0:T(8,128)(2,1)S(1)}, bf16[56,1536]{1,0:T(8,128)(2,1)S(1)}, u32[]{:S(2)}, u32[]{:S(2)}) %collective-permute-start.63) | collective-permute-done | bytes 172064 | tf_op jit(solution)/shard_map/ppermute | solution.py:1292
  297.3 3.6 %collective-permute-done.61 = bf16[112,1536]{1,0:T(8,128)(2,1)S(1)} collective-permute-done((bf16[112,1536]{1,0:T(8,128)(2,1)S(1)}, bf16[112,1536]{1,0:T(8,128)(2,1)S(1)}, u32[]{:S(2)}, u32[]{:S(2)}) %collective-permute-start.61) | collective-permute-done | bytes 344096 | tf_op jit(solution)/shard_map/ppermute | solution.py:1292
  (301 shorter events, 102.1 us)
Async XLA Ops:
  2.4 14.8 %collective-permute-start = (bf16[112,2304]{1,0:T(8,128)(2,1)S(1)}, bf16[112,2304]{1,0:T(8,128)(2,1)S(1)}, u32[]{:S(2)}, u32[]{:S(2)}) collective-permute-start(bf16[112,2304]{1,0:T(8,128)(2,1)S(1)} %fusion.3.refs_2_.refs_11_), channel_id=1, source_target_pairs={{0,2},{1,3},{2,0},{3,1},{4,6},{5,7},{6,4},{7,5},{8,10},{9,11},{10,... | collective-permute-start | bytes 1548296 | tf_op jit(solution)/shard_map/ppermute | solution.py:103
  5.4 13.2 %collective-permute-start.1 = (bf16[112,2304]{1,0:T(8,128)(2,1)S(1)}, bf16[112,2304]{1,0:T(8,128)(2,1)S(1)}, u32[]{:S(2)}, u32[]{:S(2)}) collective-permute-start(bf16[112,2304]{1,0:T(8,128)(2,1)S(1)} %fusion.3.refs_2_.refs_11_), channel_id=1, source_target_pairs={{0,4},{1,5},{2,6},{3,7},{4,0},{5,1},{6,2},{7,3},{8,12},{9,13},{10,... | collective-permute-start | bytes 1548296 | tf_op jit(solution)/shard_map/ppermute | solution.py:103
  6.9 22.1 %collective-permute-start.2 = (bf16[112,2304]{1,0:T(8,128)(2,1)S(1)}, bf16[112,2304]{1,0:T(8,128)(2,1)}, u32[]{:S(2)}, u32[]{:S(2)}) collective-permute-start(bf16[112,2304]{1,0:T(8,128)(2,1)S(1)} %fusion.3.refs_2_.refs_11_), channel_id=1, source_target_pairs={{0,1},{1,0},{2,3},{3,2},{4,5},{5,4},{6,7},{7,6},{8,9},{9,8},{10,11... | collective-permute-start | bytes 1548296 | tf_op jit(solution)/shard_map/ppermute | solution.py:103
  28.1 21.0 %collective-permute-start.9 = (bf16[112,3840]{1,0:T(8,128)(2,1)}, bf16[112,3840]{1,0:T(8,128)(2,1)S(1)}, u32[]{:S(2)}, u32[]{:S(2)}) collective-permute-start(bf16[112,3840]{1,0:T(8,128)(2,1)} %fusion.2.refs_3_.refs_9_), channel_id=1, source_target_pairs={{0,2},{1,3},{2,0},{3,1},{4,6},{5,7},{6,4},{7,5},{8,10},{9,11},{10,... | collective-permute-start | bytes 2580488 | tf_op jit(solution)/shard_map/ppermute | solution.py:103
  28.7 20.7 %collective-permute-start.10 = (bf16[112,3840]{1,0:T(8,128)(2,1)}, bf16[112,3840]{1,0:T(8,128)(2,1)S(1)}, u32[]{:S(2)}, u32[]{:S(2)}) collective-permute-start(bf16[112,3840]{1,0:T(8,128)(2,1)} %fusion.2.refs_3_.refs_9_), channel_id=1, source_target_pairs={{0,4},{1,5},{2,6},{3,7},{4,0},{5,1},{6,2},{7,3},{8,12},{9,13},{10,... | collective-permute-start | bytes 2580488 | tf_op jit(solution)/shard_map/ppermute | solution.py:103
  30.9 33.7 %collective-permute-start.11 = (bf16[112,3840]{1,0:T(8,128)(2,1)}, bf16[112,3840]{1,0:T(8,128)(2,1)S(1)}, u32[]{:S(2)}, u32[]{:S(2)}) collective-permute-start(bf16[112,3840]{1,0:T(8,128)(2,1)} %fusion.2.refs_3_.refs_9_), channel_id=1, source_target_pairs={{0,1},{1,0},{2,3},{3,2},{4,5},{5,4},{6,7},{7,6},{8,9},{9,8},{10,11... | collective-permute-start | bytes 2580488 | tf_op jit(solution)/shard_map/ppermute | solution.py:103
  49.4 15.8 %collective-permute-start.12 = (bf16[112,3840]{1,0:T(8,128)(2,1)S(1)}, bf16[112,3840]{1,0:T(8,128)(2,1)S(1)}, u32[]{:S(2)}, u32[]{:S(2)}) collective-permute-start(bf16[112,3840]{1,0:T(8,128)(2,1)S(1)} %collective-permute-done.9.refs_5_.refs_4_.refs_10_), channel_id=1, source_target_pairs={{0,1},{1,0},{2,3},{3,2},{4,5},{5,4},{6,7},{7,6},{8,9},{9,8},{10,11... | collective-permute-start | bytes 2580488 | tf_op jit(solution)/shard_map/ppermute | solution.py:103
  49.4 13.7 %collective-permute-start.15 = (bf16[64,3840]{1,0:T(8,128)(2,1)S(1)}, bf16[64,3840]{1,0:T(8,128)(2,1)S(1)}, u32[]{:S(2)}, u32[]{:S(2)}) collective-permute-start(bf16[64,3840]{1,0:T(8,128)(2,1)S(1)} %slice.296), channel_id=1, source_target_pairs={{0,4},{1,5},{2,6},{3,7},{4,0},{5,1},{6,2},{7,3},{8,12},{9,13},{10,... | collective-permute-start | bytes 1474568 | tf_op jit(solution)/shard_map/ppermute | solution.py:103
  51.6 13.6 %collective-permute-start.13 = (bf16[112,3840]{1,0:T(8,128)(2,1)S(1)}, bf16[112,3840]{1,0:T(8,128)(2,1)S(1)}, u32[]{:S(2)}, u32[]{:S(2)}) collective-permute-start(bf16[112,3840]{1,0:T(8,128)(2,1)S(1)} %collective-permute-done.10.refs_6_.refs_5_.refs_11_), channel_id=1, source_target_pairs={{0,1},{1,0},{2,3},{3,2},{4,5},{5,4},{6,7},{7,6},{8,9},{9,8},{10,11... | collective-permute-start | bytes 2580488 | tf_op jit(solution)/shard_map/ppermute | solution.py:103
  63.1 16.1 %collective-permute-start.18 = (bf16[384,768]{1,0:T(8,128)(2,1)}, bf16[384,768]{1,0:T(8,128)(2,1)}, u32[]{:S(2)}, u32[]{:S(2)}) collective-permute-start(bf16[384,768]{1,0:T(8,128)(2,1)} %refs_1_.1), channel_id=1, source_target_pairs={{0,2},{1,3},{2,0},{3,1},{4,6},{5,7},{6,4},{7,5},{8,10},{9,11},{10,... | collective-permute-start | bytes 1769480 | tf_op jit(solution)/shard_map/ppermute | solution.py:103
  64.6 15.8 %collective-permute-start.19 = (bf16[384,768]{1,0:T(8,128)(2,1)}, bf16[384,768]{1,0:T(8,128)(2,1)}, u32[]{:S(2)}, u32[]{:S(2)}) collective-permute-start(bf16[384,768]{1,0:T(8,128)(2,1)} %refs_1_.1), channel_id=1, source_target_pairs={{0,4},{1,5},{2,6},{3,7},{4,0},{5,1},{6,2},{7,3},{8,12},{9,13},{10,... | collective-permute-start | bytes 1769480 | tf_op jit(solution)/shard_map/ppermute | solution.py:103
  80.4 14.9 %collective-permute-start.23 = (bf16[384,768]{1,0:T(8,128)(2,1)}, bf16[384,768]{1,0:T(8,128)(2,1)S(1)}, u32[]{:S(2)}, u32[]{:S(2)}) collective-permute-start(bf16[384,768]{1,0:T(8,128)(2,1)} %collective-permute-done.18.refs_13_.refs_7_.refs_2_), channel_id=1, source_target_pairs={{0,4},{1,5},{2,6},{3,7},{4,0},{5,1},{6,2},{7,3},{8,12},{9,13},{10,... | collective-permute-start | bytes 1769480 | tf_op jit(solution)/shard_map/ppermute | solution.py:103
  80.9 14.4 %collective-permute-start.20 = (bf16[384,768]{1,0:T(8,128)(2,1)}, bf16[384,768]{1,0:T(8,128)(2,1)S(1)}, u32[]{:S(2)}, u32[]{:S(2)}) collective-permute-start(bf16[384,768]{1,0:T(8,128)(2,1)} %refs_1_.1), channel_id=1, source_target_pairs={{0,1},{1,0},{2,3},{3,2},{4,5},{5,4},{6,7},{7,6},{8,9},{9,8},{10,11... | collective-permute-start | bytes 1769480 | tf_op jit(solution)/shard_map/ppermute | solution.py:103
  80.9 14.4 %collective-permute-start.21 = (bf16[384,768]{1,0:T(8,128)(2,1)}, bf16[384,768]{1,0:T(8,128)(2,1)}, u32[]{:S(2)}, u32[]{:S(2)}) collective-permute-start(bf16[384,768]{1,0:T(8,128)(2,1)} %collective-permute-done.18.refs_13_.refs_7_.refs_2_), channel_id=1, source_target_pairs={{0,1},{1,0},{2,3},{3,2},{4,5},{5,4},{6,7},{7,6},{8,9},{9,8},{10,11... | collective-permute-start | bytes 1769480 | tf_op jit(solution)/shard_map/ppermute | solution.py:103
  81.4 13.9 %collective-permute-start.22 = (bf16[384,768]{1,0:T(8,128)(2,1)}, bf16[384,768]{1,0:T(8,128)(2,1)}, u32[]{:S(2)}, u32[]{:S(2)}) collective-permute-start(bf16[384,768]{1,0:T(8,128)(2,1)} %collective-permute-done.19.refs_14_.refs_8_.refs_3_), channel_id=1, source_target_pairs={{0,1},{1,0},{2,3},{3,2},{4,5},{5,4},{6,7},{7,6},{8,9},{9,8},{10,11... | collective-permute-start | bytes 1769480 | tf_op jit(solution)/shard_map/ppermute | solution.py:103
  179.8 13.1 %collective-permute-start.35 = (bf16[4,96,3072]{2,1,0:T(8,128)(2,1)S(1)}, bf16[4,96,3072]{2,1,0:T(8,128)(2,1)S(1)}, u32[]{:S(2)}, u32[]{:S(2)}) collective-permute-start(bf16[4,96,3072]{2,1,0:T(8,128)(2,1)S(1)} %get-tuple-element.365), channel_id=1, source_target_pairs={{0,1},{1,0},{2,3},{3,2},{4,5},{5,4},{6,7},{7,6},{8,9},{9,8},{10,11... | collective-permute-start | bytes 7077896 | tf_op jit(solution)/shard_map/ppermute | solution.py:103
  179.9 23.9 %collective-permute-start.36 = (bf16[768,384]{1,0:T(8,128)(2,1)S(1)}, bf16[768,384]{1,0:T(8,128)(2,1)S(1)}, u32[]{:S(2)}, u32[]{:S(2)}) collective-permute-start(bf16[768,384]{1,0:T(8,128)(2,1)S(1)} %fusion.4.refs_19_), channel_id=1, source_target_pairs={{0,2},{1,3},{2,0},{3,1},{4,6},{5,7},{6,4},{7,5},{8,10},{9,11},{10,... | collective-permute-start | bytes 1769480 | tf_op jit(solution)/shard_map/ppermute | solution.py:103
  181.5 22.3 %collective-permute-start.37 = (bf16[768,384]{1,0:T(8,128)(2,1)S(1)}, bf16[768,384]{1,0:T(8,128)(2,1)S(1)}, u32[]{:S(2)}, u32[]{:S(2)}) collective-permute-start(bf16[768,384]{1,0:T(8,128)(2,1)S(1)} %fusion.5.refs_20_), channel_id=1, source_target_pairs={{0,4},{1,5},{2,6},{3,7},{4,0},{5,1},{6,2},{7,3},{8,12},{9,13},{10,... | collective-permute-start | bytes 1769480 | tf_op jit(solution)/shard_map/ppermute | solution.py:103
  204.9 16.5 %collective-permute-start.40 = (bf16[4,112,768]{2,1,0:T(8,128)(2,1)}, bf16[4,112,768]{2,1,0:T(8,128)(2,1)}, u32[]{:S(2)}, u32[]{:S(2)}) collective-permute-start(bf16[4,112,768]{2,1,0:T(8,128)(2,1)} %get-tuple-element.393), channel_id=1, source_target_pairs={{0,1},{1,0},{2,3},{3,2},{4,5},{5,4},{6,7},{7,6},{8,9},{9,8},{10,11... | collective-permute-start | bytes 2064392 | tf_op jit(solution)/shard_map/ppermute | solution.py:103
  209.0 22.5 %collective-permute-start.42 = (bf16[768,384]{1,0:T(8,128)(2,1)}, bf16[768,384]{1,0:T(8,128)(2,1)}, u32[]{:S(2)}, u32[]{:S(2)}) collective-permute-start(bf16[768,384]{1,0:T(8,128)(2,1)} %add_convert_fusion.3.refs_8_), channel_id=1, source_target_pairs={{0,8},{24,16},{1,9},{25,17},{2,10},{26,18},{3,11},{27,19},{4,12},{... | collective-permute-start | bytes 1769480 | tf_op jit(solution)/shard_map/ppermute | solution.py:1292
  212.0 21.9 %collective-permute-start.43 = (bf16[96,3072]{1,0:T(8,128)(2,1)}, bf16[96,3072]{1,0:T(8,128)(2,1)S(1)}, u32[]{:S(2)}, u32[]{:S(2)}) collective-permute-start(bf16[96,3072]{1,0:T(8,128)(2,1)} %fusion.6.refs_9_), channel_id=1, source_target_pairs={{0,2},{1,3},{2,0},{3,1},{4,6},{5,7},{6,4},{7,5},{8,10},{9,11},{10,... | collective-permute-start | bytes 1769480 | tf_op jit(solution)/shard_map/ppermute | solution.py:103
  213.5 20.4 %collective-permute-start.44 = (bf16[96,3072]{1,0:T(8,128)(2,1)}, bf16[96,3072]{1,0:T(8,128)(2,1)S(1)}, u32[]{:S(2)}, u32[]{:S(2)}) collective-permute-start(bf16[96,3072]{1,0:T(8,128)(2,1)} %fusion.7.refs_10_), channel_id=1, source_target_pairs={{0,4},{1,5},{2,6},{3,7},{4,0},{5,1},{6,2},{7,3},{8,12},{9,13},{10,... | collective-permute-start | bytes 1769480 | tf_op jit(solution)/shard_map/ppermute | solution.py:103
  232.9 19.2 %collective-permute-start.51 = (bf16[768,384]{1,0:T(8,128)(2,1)S(1)}, bf16[768,384]{1,0:T(8,128)(2,1)S(1)}, u32[]{:S(2)}, u32[]{:S(2)}) collective-permute-start(bf16[768,384]{1,0:T(8,128)(2,1)S(1)} %add_convert_fusion.2.refs_21_), channel_id=1, source_target_pairs={{8,16},{16,8},{9,17},{17,9},{10,18},{18,10},{11,19},{19,11},{12,20... | collective-permute-start | bytes 1769480 | tf_op jit(solution)/shard_map/ppermute | solution.py:1292
  234.8 17.5 %collective-permute-start.52 = (bf16[48,3072]{1,0:T(8,128)(2,1)S(1)}, bf16[48,3072]{1,0:T(8,128)(2,1)S(1)}, u32[]{:S(2)}, u32[]{:S(2)}) collective-permute-start(bf16[48,3072]{1,0:T(8,128)(2,1)S(1)} %broadcast_select_fusion.2.refs_22_), channel_id=1, source_target_pairs={{0,8},{8,0},{16,24},{24,16},{1,9},{9,1},{17,25},{25,17},{2,10},{10... | collective-permute-start | bytes 884744 | tf_op jit(solution)/shard_map/ppermute | solution.py:103
  236.3 18.9 %collective-permute-start.53 = (bf16[112,1536]{1,0:T(8,128)(2,1)S(1)}, bf16[112,1536]{1,0:T(8,128)(2,1)S(1)}, u32[]{:S(2)}, u32[]{:S(2)}) collective-permute-start(bf16[112,1536]{1,0:T(8,128)(2,1)S(1)} %fusion.8.refs_23_), channel_id=1, source_target_pairs={{0,2},{1,3},{2,0},{3,1},{4,6},{5,7},{6,4},{7,5},{8,10},{9,11},{10,... | collective-permute-start | bytes 1032200 | tf_op jit(solution)/shard_map/ppermute | solution.py:103
  250.8 13.4 %collective-permute-start.57 = (bf16[112,1536]{1,0:T(8,128)(2,1)S(1)}, bf16[112,1536]{1,0:T(8,128)(2,1)S(1)}, u32[]{:S(2)}, u32[]{:S(2)}) collective-permute-start(bf16[112,1536]{1,0:T(8,128)(2,1)S(1)} %fusion.9), channel_id=1, source_target_pairs={{0,2},{1,3},{2,0},{3,1},{4,6},{5,7},{6,4},{7,5},{8,10},{9,11},{10,... | collective-permute-start | bytes 1032200 | tf_op jit(solution)/shard_map/ppermute | solution.py:103
  252.4 15.9 %collective-permute-start.56 = (bf16[48,3072]{1,0:T(8,128)(2,1)S(1)}, bf16[48,3072]{1,0:T(8,128)(2,1)S(1)}, u32[]{:S(2)}, u32[]{:S(2)}) collective-permute-start(bf16[48,3072]{1,0:T(8,128)(2,1)S(1)} %add_convert_fusion.9), channel_id=1, source_target_pairs={{0,16},{16,0},{8,24},{24,8},{1,17},{17,1},{9,25},{25,9},{2,18},{18... | collective-permute-start | bytes 884744 | tf_op jit(solution)/shard_map/ppermute | solution.py:1292
  254.1 12.6 %collective-permute-start.58 = (bf16[112,1536]{1,0:T(8,128)(2,1)S(1)}, bf16[112,1536]{1,0:T(8,128)(2,1)S(1)}, u32[]{:S(2)}, u32[]{:S(2)}) collective-permute-start(bf16[112,1536]{1,0:T(8,128)(2,1)S(1)} %fusion.11), channel_id=1, source_target_pairs={{0,4},{1,5},{2,6},{3,7},{4,0},{5,1},{6,2},{7,3},{8,12},{9,13},{10,... | collective-permute-start | bytes 1032200 | tf_op jit(solution)/shard_map/ppermute | solution.py:103
  255.2 28.1 %collective-permute-start.65 = (bf16[768,384]{1,0:T(8,128)(2,1)S(1)}, bf16[768,384]{1,0:T(8,128)(2,1)S(1)}, u32[]{:S(2)}, u32[]{:S(2)}) collective-permute-start(bf16[768,384]{1,0:T(8,128)(2,1)S(1)} %add_convert_fusion), channel_id=1, source_target_pairs={{8,0},{16,24},{9,1},{17,25},{10,2},{18,26},{11,3},{19,27},{12,4},{... | collective-permute-start | bytes 1769480 | tf_op jit(solution)/shard_map/ppermute | solution.py:1292
  266.8 16.3 %collective-permute-start.60 = (bf16[56,1536]{1,0:T(8,128)(2,1)S(1)}, bf16[56,1536]{1,0:T(8,128)(2,1)S(1)}, u32[]{:S(2)}, u32[]{:S(2)}) collective-permute-start(bf16[56,1536]{1,0:T(8,128)(2,1)S(1)} %broadcast_select_fusion.5), channel_id=1, source_target_pairs={{0,8},{8,0},{16,24},{24,16},{1,9},{9,1},{17,25},{25,17},{2,10},{10... | collective-permute-start | bytes 516104 | tf_op jit(solution)/shard_map/ppermute | solution.py:103
  268.4 19.1 %collective-permute-start.64 = (bf16[48,3072]{1,0:T(8,128)(2,1)S(1)}, bf16[48,3072]{1,0:T(8,128)(2,1)S(1)}, u32[]{:S(2)}, u32[]{:S(2)}) collective-permute-start(bf16[48,3072]{1,0:T(8,128)(2,1)S(1)} %add_convert_fusion.8), channel_id=1, source_target_pairs={{0,8},{8,0},{16,24},{24,16},{1,9},{9,1},{17,25},{25,17},{2,10},{10... | collective-permute-start | bytes 884744 | tf_op jit(solution)/shard_map/ppermute | solution.py:1292
  270.8 17.8 %collective-permute-start.59 = (bf16[112,1536]{1,0:T(8,128)(2,1)S(1)}, bf16[112,1536]{1,0:T(8,128)(2,1)S(1)}, u32[]{:S(2)}, u32[]{:S(2)}) collective-permute-start(bf16[112,1536]{1,0:T(8,128)(2,1)S(1)} %add_convert_fusion.5), channel_id=1, source_target_pairs={{8,16},{16,8},{9,17},{17,9},{10,18},{18,10},{11,19},{19,11},{12,20... | collective-permute-start | bytes 1032200 | tf_op jit(solution)/shard_map/ppermute | solution.py:1292
  (80 other events, 675.1 us)

commit v5 on v4

--- a/solution.py
+++ b/solution.py
@@ -26,7 +26,7 @@
 f32 = jnp.float32
 ANY = pl.BlockSpec(memory_space=pl.ANY)
 HELD = pl.BlockSpec(memory_space=pltpu.VMEM)
-VMEM_BYTES = 24 * 1024 * 1024
+VMEM_BYTES = 16 * 1024 * 1024
 
 
 def dot(left, right):
@@ -654,6 +654,7 @@
         count * (width * 10 + inner * 2) + width * inner * 2,
         after=after,
         near=(3, 5, -4, -5, -6),
+        room=24 * 1024 * 1024,
     )(index, activated, normed, vectors, seg_rows, positive, *arrays_of(pieces))
 
 
@@ -842,35 +843,30 @@
         target_ref[place * rows : (place + 1) * rows] = turn_ref[pl.ds(start, rows)]
 
 
-def weights_kernel(down_meta, up_meta, index_ref, *refs):
-    pieces, (wd_ref, wu_ref, sems, up_sems) = refs[:-4], refs[-4:]
-    low, high = pieces[: len(down_meta)], pieces[len(down_meta) :]
-    width, inner = wu_ref.shape
-    here = slice(width, width + inner)
-    copies = copies_of(down_meta, inner // BLOCKS, low, wd_ref, sems, index_ref[0])
-    copies += copies_of(up_meta, width // BLOCKS, high, wu_ref, up_sems, index_ref[0], here)
+def weights_kernel(meta, base, index_ref, *refs):
+    pieces, (out_ref, sems) = refs[:-2], refs[-2:]
+    height, width = out_ref.shape
+    here = slice(base, base + width)
+    copies = copies_of(meta, height // BLOCKS, pieces, out_ref, sems, index_ref[0], here)
     start_all(copies)
     wait_all(copies)
 
 
-def hold_weights(index, down_pieces, up_pieces, width, inner, after=()):
-    down_meta, up_meta = meta_of(down_pieces), meta_of(up_pieces)
+def hold_weights(index, pieces, shape, base, after=()):
+    meta = meta_of(pieces)
     return call(
-        functools.partial(weights_kernel, down_meta, up_meta),
+        functools.partial(weights_kernel, meta, base),
         (1,),
-        [ANY] * (len(down_meta) + len(up_meta)),
-        [HELD, HELD],
-        [shaped((inner, width), bf16), shaped((width, inner), bf16)],
-        [
-            pltpu.SemaphoreType.DMA((len(down_meta),)),
-            pltpu.SemaphoreType.DMA((len(up_meta),)),
-        ],
+        [ANY] * len(meta),
+        [HELD],
+        [shaped(shape, bf16)],
+        [pltpu.SemaphoreType.DMA((len(meta),))],
         0,
-        width * inner * 8,
+        shape[0] * shape[1] * 4,
         0,
         after,
-        near=(-1, -2),
-    )(index, *arrays_of(down_pieces), *arrays_of(up_pieces))
+        near=(-1,),
+    )(index, *arrays_of(pieces))
 
 
 def turned_kernel(index_ref, one_ref, two_ref, out_one_ref, out_two_ref, turn_ref):
@@ -1294,8 +1290,7 @@
 
 def core_kernel(parts, index_ref, *refs):
     keeps, others = refs[:parts], refs[parts : 2 * parts]
-    mine_ref, x_ref, y_ref, top_ref, low_ref = refs[2 * parts :]
-    half = top_ref.shape[0]
+    mine_ref, x_ref, y_ref, *far_refs = refs[2 * parts :]
     at = 0
     for keep, other in zip(keeps, others):
         cols = slice(at, at + keep.shape[2])
@@ -1303,32 +1298,35 @@
         for place, target in enumerate((mine_ref, x_ref, y_ref)):
             target[:, cols] = add(keep[place], other[place]).astype(bf16)
         far = add(keep[3], other[3]).astype(bf16)
-        top_ref[:, cols] = far[:half]
-        low_ref[:, cols] = far[half:]
-
-
-def add_cores(index, keeps, others):
+        row = 0
+        for far_ref in far_refs:
+            far_ref[:, cols] = far[row : row + far_ref.shape[0]]
+            row += far_ref.shape[0]
+
+
+def add_cores(index, keeps, others, whole_far):
     rows = keeps[0].shape[1]
     width = sum(keep.shape[2] for keep in keeps)
     half = rows // 32 * 16
-    heights = (rows, rows, rows, half, rows - half)
+    heights = (rows, rows, rows) + ((rows,) if whole_far else (half, rows - half))
     count = 2 * len(keeps)
     return call(
         functools.partial(core_kernel, len(keeps)),
         (1,),
         [HELD] * count,
-        [HELD] * 5,
+        [HELD] * len(heights),
         [shaped((height, width), bf16) for height in heights],
         [],
         rows * width * 4,
         rows * width * 24,
-        near=tuple(range(1, 1 + count)) + (-1, -2, -3, -4, -5),
+        near=tuple(range(1, 1 + count)) + (-1, -2, -3, -4, -5)[: len(heights)],
     )(index, *keeps, *others)
 
 
 class Sum:
-    def __init__(self, index, planes, keeps, sends, line):
+    def __init__(self, index, planes, keeps, sends, line, axis=None):
         self.index, self.planes, self.keeps, self.line = index, planes, keeps, line
+        self.axis = axis
         self.arrived = [fsdp_swap(send, 1) for send in sends]
         self.stages = [self.over_core, self.over_far, self.over_chips, self.over_z, self.over_middle]
 
@@ -1337,16 +1335,23 @@
         return list(self.stages.pop(0)(*self.arrived))
 
     def over_core(self, *others):
-        *self.blocks, _ = add_cores(self.index, self.keeps, others)
-        self.half = self.blocks[3].shape[0]
-        self.arrived = [fsdp_swap(self.blocks[3], 2), fsdp_swap(self.blocks[4], 4)]
-        return self.blocks[3:]
-
-    def over_far(self, top, low):
-        _, over_x, over_y, _, _ = self.blocks
-        half = self.half
-        over_x = over_x.at[half:].set(add(over_x[half:], low).astype(bf16))
-        over_y = over_y.at[:half].set(add(over_y[:half], top).astype(bf16))
+        *self.blocks, _ = add_cores(self.index, self.keeps, others, self.axis is not None)
+        far = self.blocks[3:]
+        axes = (2, 4) if self.axis is None else (self.axis,)
+        self.arrived = [fsdp_swap(block, axis) for block, axis in zip(far, axes)]
+        return far
+
+    def over_far(self, *arrived):
+        over_x, over_y = self.blocks[1:3]
+        if self.axis is None:
+            top, low = arrived
+            half = top.shape[0]
+            over_x = over_x.at[half:].set(add(over_x[half:], low).astype(bf16))
+            over_y = over_y.at[:half].set(add(over_y[:half], top).astype(bf16))
+        elif self.axis == 2:
+            over_y = rounded(add(over_y, arrived[0]))
+        else:
+            over_x = rounded(add(over_x, arrived[0]))
         self.arrived = [fsdp_swap(over_x, 2), fsdp_swap(over_y, 4)]
         return [over_x, over_y]
 
@@ -1455,7 +1460,8 @@
     normed1, root1, hidden, rows, bias_up, clock = project(
         index, context, token_rows, mid_pieces, sizes, (clock,)
     )
-    late = ()
+    hidden_turned, tokens_turned, clock = hold_turned(index, hidden, token_rows, (clock,))
+    late = (clock,)
     if paired:
         *third_xy, clock = tie((*third_xy, clock))
         third_far = fsdp_swap(third_xy[0], 4)
@@ -1469,22 +1475,20 @@
         index, activated, normed1, rows, seg_rows, pos_col, down_pieces, (clock,)
     )
 
-    hidden_turned, tokens_turned, clock = hold_turned(index, hidden, token_rows, (payload,))
+    wd_full, clock = hold_weights(index, down_pieces, (inner, width), 0, (payload,))
     if paired:
         line = [payload] + [swap(payload, "batch", planes, bit) for bit in (1, 2, 3)]
         *line, clock = tie((*line, clock))
         line = jnp.concatenate(line, axis=0)
         plane = [line] + [fsdp_swap(line, bit) for bit in (2, 4, 6)]
-        wd_full, wu_full, clock = hold_weights(
-            index, down_pieces, mid_pieces, width, inner, (line, clock)
-        )
+        wu_full, clock = hold_weights(index, mid_pieces, (width, inner), width, (line, clock))
         *plane, clock = tie((*plane, clock))
         plane = jnp.concatenate(plane, axis=0)
         everyone = [plane, fsdp_swap(plane, 1)]
         layout = (2, ring // 2, planes)
         flip = me * own
     else:
-        wd_full, wu_full, clock = hold_weights(index, down_pieces, mid_pieces, width, inner)
+        wu_full, clock = hold_weights(index, mid_pieces, (width, inner), width)
         everyone = [lax.all_gather(payload, ("batch", "fsdp"), axis=0, tiled=True)]
         layout = (1, planes * ring, 1)
         flip = jnp.zeros_like(me)
@@ -1493,8 +1497,8 @@
         place, layout, everyone, payload, pos_col, pooled, stats, (clock,)
     )
 
-    def start(keeps, sends, line):
-        return Sum(index, planes, keeps, sends, line) if paired else None
+    def start(keeps, sends, line, axis=None):
+        return Sum(index, planes, keeps, sends, line, axis) if paired else None
 
     def go(results, *sums):
         sent, clock = [], results[0]
@@ -1557,11 +1561,11 @@
         )
         if cut == 0:
             back, sent = go(back, sum_down, sum_up)
-            sum_left = start([keep_out, back[3]], [send_out, back[4]], True)
+            sum_left = start([keep_out, back[3]], [send_out, back[4]], True, 2)
         if cut == 1:
             back, sent = go(back, sum_left)
         if cut == 2:
-            sum_right = start([backs[1][3], back[3]], [backs[1][4], back[4]], False)
+            sum_right = start([backs[1][3], back[3]], [backs[1][4], back[4]], False, 4)
             back, sent = go(back, sum_down, sum_up, sum_left, sum_right)
         backs.append(back)
     grads = [backs[cut][kind] for kind in range(3) for cut in range(cuts)]

time: 309 us -> 306 us (level)
  waiting for transfers between devices: 68.3 us -> 64.9 us
    ppermute x56 -> x54, waiting for transfers between devices: 53.4 us -> 48.1 us  [swap(): return lax.ppermute(value, axis, [(i, i ^ bit) for i in range(size)])]
    ppermute x56 -> x54, starting transfers between devices: 41.8 us -> 40.3 us  [swap(): return lax.ppermute(value, axis, [(i, i ^ bit) for i in range(size)])]
    unnamed x118 -> x116, local copies, waits for them, and re-layouts: 13.6 us -> 14.8 us
    pallas_call x21 -> x22, Pallas kernels: 143 us -> 144 us  [apply(): return run(index, *placed, *after)]
  transfers between devices with their start and end apart: 66 -> 64, of which waited for: 23 -> 23; matrix products, arithmetic and copies ran while one was open for 7% -> 7% of each run, Pallas kernels for 36% -> 37%
where the time goes in v5:
time: 306 us; the launch traced here: 301 us
  Pallas kernels  144 us (47%)
  waiting for transfers between devices  64.9 us (21%)
  starting transfers between devices  52.5 us (17%)
  local copies, waits for them, and re-layouts  24.3 us (8%)
  other arithmetic  13.4 us (4%)
    pallas_call x22, Pallas kernels, apply(): return run(index, *placed, *after)  144 us
    ppermute x54, waiting for transfers between devices, swap(): return lax.ppermute(value, axis, [(i, i ^ bit) for i in range(size)])  48.1 us
    ppermute x54, starting transfers between devices, swap(): return lax.ppermute(value, axis, [(i, i ^ bit) for i in range(size)])  40.3 us
    ppermute x10, waiting for transfers between devices, along_z(): return lax.ppermute(value, 'batch', pairs)  16.8 us
    unnamed x116, local copies, waits for them, and re-layouts  14.8 us
    ppermute x10, starting transfers between devices, along_z(): return lax.ppermute(value, 'batch', pairs)  12.2 us
  transfers between devices with their start and end apart: 64, of which 23 were waited for; matrix products, arithmetic and copies ran while one was open for 7% of the time, Pallas kernels for 37%

profile of v5, /device:TPU:0, one launch (start us, length us, event | category | flops | bytes accessed | tf_op | source)
XLA Modules:
  0.0 300.9 jit_solution(10954771984612448837)
XLA Ops:
  2.4 3.0 collective-permute-start
  21.1 7.1 %collective-permute-done.5.refs_8_.refs_17_ = bf16[48,2304]{1,0:T(8,128)(2,1)S(1)} collective-permute-done((bf16[48,2304]{1,0:T(8,128)(2,1)S(1)}, bf16[48,2304]{1,0:T(8,128)(2,1)S(1)}, u32[]{:S(2)}, u32[]{:S(2)}) %collective-permute-start.5) | collective-permute-done | bytes 221216 | tf_op jit(solution)/shard_map/ppermute | solution.py:103
  31.6 9.4 %shard_map.271 = (bf16[1024,2304]{1,0:T(8,128)(2,1)S(1)}, f32[8,128]{1,0:T(8,128)}) custom-call(s32[1]{0:T(128)} %bitcast.refs_0_, bf16[1024,768]{1,0:T(8,128)(2,1)} %bitcast.31, bf16[112,2304]{1,0:T(8,128)(2,1)} %copy-done.33, bf16[112,2304]{1,0:T(8,128)(2,1)} %copy-done.34, bf16[112,2304]{1,0:T(8,128)(2,1)} %copy-done.35, ...), custom_call_target="tpu_custom_call" | custom-call | flops 3623878656 | bytes 9830400 | tf_op jit(solution)/shard_map/pallas_call | solution.py:93
  41.0 5.0 %shard_map.272 = (bf16[1024,768]{1,0:T(8,128)(2,1)S(1)}, f32[2,6,2,512]{3,2,1,0:T(2,128)S(1)}, f32[8,128]{1,0:T(8,128)S(1)}) custom-call(s32[1]{0:T(128)} %bitcast.refs_0_, bf16[1024,2304]{1,0:T(8,128)(2,1)S(1)} %get-tuple-element.232.refs_1_.refs_2_.refs_3_, s32[2,1,512]{2,1,0:T(1,128)} %reshape.151.refs_2_.refs_4_.refs_6_), custom_call_target="tpu_custom_call" | custom-call | flops 805306368 | bytes 3145728 | tf_op jit(solution)/shard_map/pallas_call | solution.py:93
  46.0 3.1 %collective-permute-done.9.refs_5_.refs_4_.refs_2_.refs_10_ = bf16[112,3840]{1,0:T(8,128)(2,1)S(1)} collective-permute-done((bf16[112,3840]{1,0:T(8,128)(2,1)}, bf16[112,3840]{1,0:T(8,128)(2,1)S(1)}, u32[]{:S(2)}, u32[]{:S(2)}) %collective-permute-start.9) | collective-permute-done | bytes 860192 | tf_op jit(solution)/shard_map/ppermute | solution.py:103
  51.6 5.0 %shard_map.273 = (bf16[1024,768]{1,0:T(8,128)(2,1)S(1)}, f32[2,6,2,512]{3,2,1,0:T(2,128)S(1)}, f32[8,128]{1,0:T(8,128)S(1)}) custom-call(s32[1]{0:T(128)} %bitcast.refs_0_, bf16[1024,2304]{1,0:T(8,128)(2,1)S(1)} %get-tuple-element.232.refs_1_.refs_2_.refs_3_, ...), custom_call_target="tpu_custom_call", output_to_operand_aliasing={{0}: (3, {}), {1}: (4, {})} | custom-call | flops 805306368 | bytes 3145728 | tf_op jit(solution)/shard_map/pallas_call | solution.py:93
  56.6 4.1 %collective-permute-done.14.refs_9_.refs_7_.refs_15_ = bf16[48,3840]{1,0:T(8,128)(2,1)S(1)} collective-permute-done((bf16[48,3840]{1,0:T(8,128)(2,1)S(1)}, bf16[48,3840]{1,0:T(8,128)(2,1)S(1)}, u32[]{:S(2)}, u32[]{:S(2)}) %collective-permute-start.14) | collective-permute-done | bytes 368672 | tf_op jit(solution)/shard_map/ppermute | solution.py:103
  60.6 2.5 collective-permute-done.15.refs_10_.refs_8_.refs_16_
  67.7 6.9 %shard_map.274 = (f32[1024,768]{1,0:T(8,128)}, f32[1024,1]{1,0:T(8,128)}, bf16[1024,768]{1,0:T(8,128)(2,1)S(1)}, f32[8,768]{1,0:T(8,128)S(1)}, f32[1,3072]{1,0:T(1,128)S(1)}, /*index=5*/f32[8,128]{1,0:T(8,128)S(1)}) custom-call(s32[1]{0:T(128)} %bitcast.refs_0_, bf16[1024,768]{1,0:T(8,128)(2,1)S(1)} %get-tuple-element.240.refs_1_.refs_6_, ...), custom_call_target="tpu_custom_call" | custom-call | flops 1207959552 | bytes 9043968 | tf_op jit(solution)/shard_map/pallas_call | solution.py:93
  75.8 3.1 %shard_map.275 = (bf16[768,1024]{1,0:T(8,128)(2,1)S(1)}, bf16[768,1024]{1,0:T(8,128)(2,1)S(1)}, f32[8,128]{1,0:T(8,128)S(1)}) custom-call(s32[1]{0:T(128)} %bitcast.refs_0_, bf16[1024,768]{1,0:T(8,128)(2,1)} %copy-done.11, bf16[1024,768]{1,0:T(8,128)(2,1)} %bitcast.33, f32[8,128]{1,0:T(8,128)S(1)} %get-tuple-element.248.refs_3_), custom_call_target="tpu_custom_call" | custom-call | bytes 6291456 | tf_op jit(solution)/shard_map/pallas_call | solution.py:93
  82.1 12.7 %shard_map.276 = (bf16[1024,3072]{1,0:T(8,128)(2,1)}, bf16[1024,3072]{1,0:T(8,128)(2,1)}, f32[8,128]{1,0:T(8,128)S(1)}) custom-call(s32[1]{0:T(128)} %bitcast.refs_0_, bf16[1024,768]{1,0:T(8,128)(2,1)S(1)} %copy-done.12, f32[1,3072]{1,0:T(1,128)S(1)} %get-tuple-element.246.refs_2_, bf16[112,3840]{1,0:T(8,128)(2,1)} %fusion.2.refs_3_.refs_1_.refs_9_, ...), custom_call_target="tpu_custom_call" | custom-call | flops 4831838208 | bytes 18874368 | tf_op jit(solution)/shard_map/pallas_call | solution.py:93
  95.8 2.2 collective-permute-done.24.refs_13_.refs_8_
  98.1 15.6 %shard_map.277 = (bf16[1024,768]{1,0:T(8,128)(2,1)}, f32[1024,768]{1,0:T(8,128)}, f32[1024,1]{1,0:T(8,128)}, bf16[16,896]{1,0:T(8,128)(2,1)S(1)}, f32[16,768]{1,...) custom-call(s32[1]{0:T(128)} %bitcast.refs_0_, bf16[1024,3072]{1,0:T(8,128)(2,1)} %get-tuple-element.253.refs_1_.refs_7_, ...), custom_call_target="tpu_custom_call" | custom-call | flops 4831838208 | bytes 18874368 | tf_op jit(solution)/shard_map/pallas_call | solution.py:93
  115.3 2.6 collective-permute-start.26
  118.2 2.4 shard_map.278
  127.2 2.4 shard_map.279
  136.6 3.5 %shard_map.280 = (f32[16,1]{1,0:T(8,128)S(1)}, f32[16,768]{1,0:T(8,128)S(1)}, f32[8,128]{1,0:T(8,128)}) custom-call(s32[2]{0:T(128)S(1)} %pad_add_fusion.refs_0_, bf16[16,896]{1,0:T(8,128)(2,1)S(1)} %get-tuple-element.264.refs_9_.refs_1_, s32[16,1]{1,0:T(8,128)S(1)} %copy.40.refs_5_.refs_2_, f32[16,768]{1,0:T(8,128)S(1)} %get-tuple-element.261.refs_3_, ...), custom_call_target="tpu_custom_call" | custom-call | flops 402653184 | bytes 786432 | tf_op jit(solution)/shard_map/pallas_call | solution.py:93
  140.1 12.3 %shard_map.281 = (f32[1024,768]{1,0:T(8,128)S(1)}, bf16[1024,768]{1,0:T(8,128)(2,1)S(1)}, f32[8,768]{1,0:T(8,128)S(1)}, bf16[4,768,384]{2,1,0:T(8,128)(2,1)S(1)}...) custom-call(s32[1]{0:T(128)} %bitcast.refs_0_, bf16[1024,768]{1,0:T(8,128)(2,1)} %bitcast.42, ...), custom_call_target="tpu_custom_call" | custom-call | flops 4831838208 | bytes 20447232 | tf_op jit(solution)/shard_map/pallas_call | solution.py:93
  152.6 10.9 %shard_map.282 = (f32[1024,768]{1,0:T(8,128)S(1)}, f32[1,3072]{1,0:T(1,128)S(1)}, bf16[4,96,3072]{2,1,0:T(8,128)(2,1)S(1)}, bf16[4,96,3072]{2,1,0:T(8,128)(2,1)S(1)}, f32[8,128]{1,0:T(8,128)}) custom-call(s32[1]{0:T(128)} %bitcast.refs_0_, bf16[1024,768]{1,0:T(8,128)(2,1)S(1)} %get-tuple-element.279.refs_1_, bf16[1024,3072]{1,0:T(8,128)(2,1)} %get-tuple-element.280.refs_2_, ...), custom_call_target="tpu_custom_call" | custom-call | flops 7247757312 | bytes 23592960 | tf_op jit(solution)/shard_map/pallas_call | solution.py:93
  166.2 10.9 %shard_map.284 = (f32[1024,768]{1,0:T(8,128)S(1)}, f32[1,3072]{1,0:T(1,128)S(1)}, bf16[4,96,3072]{2,1,0:T(8,128)(2,1)S(1)}, bf16[4,96,3072]{2,1,0:T(8,128)(2,1)S(1)}, f32[8,128]{1,0:T(8,128)}) custom-call(s32[1]{0:T(128)} %bitcast.refs_0_, ...), custom_call_target="tpu_custom_call", output_to_operand_aliasing={{0}: (6, {}), {1}: (7, {}), {2}: (8, {}), {3}: (9, {})} | custom-call | flops 7247757312 | bytes 23592960 | tf_op jit(solution)/shard_map/pallas_call | solution.py:93
  179.8 8.7 %shard_map.285 = (f32[1024,768]{1,0:T(8,128)S(1)}, bf16[1024,768]{1,0:T(8,128)(2,1)S(1)}, bf16[4,112,768]{2,1,0:T(8,128)(2,1)S(1)}, bf16[4,112,768]{2,1,0:T(8,128)(2,1)}, f32[8,128]{1,0:T(8,128)}) custom-call(s32[1]{0:T(128)} %bitcast.refs_0_, f32[1024,768]{1,0:T(8,128)S(1)} %get-tuple-element.305.refs_1_, f32[1024,768]{1,0:T(8,128)S(1)} %get-tuple-element.306.refs_2_, ...), custom_call_target="tpu_custom_call" | custom-call | flops 2415919104 | bytes 18087936 | tf_op jit(solution)/shard_map/pallas_call | solution.py:93
  194.0 7.5 %shard_map.287 = (bf16[1024,256]{1,0:T(8,128)(2,1)S(1)}, bf16[1024,256]{1,0:T(8,128)(2,1)S(1)}, bf16[1024,256]{1,0:T(8,128)(2,1)S(1)}, bf16[4,112,768]{2,1,0:T(8...) custom-call(s32[1]{0:T(128)} %bitcast.refs_0_, bf16[1024,2304]{1,0:T(8,128)(2,1)} %copy-done, ...), custom_call_target="tpu_custom_call" | custom-call | flops 2013265920 | bytes 5242880 | tf_op jit(solution)/shard_map/pallas_call | solution.py:93
  206.7 3.0 %collective-permute-start.42 = (bf16[768,384]{1,0:T(8,128)(2,1)}, bf16[768,384]{1,0:T(8,128)(2,1)}, u32[]{:S(2)}, u32[]{:S(2)}) collective-permute-start(bf16[768,384]{1,0:T(8,128)(2,1)} %add_convert_fusion.3.refs_8_), channel_id=1, source_target_pairs={{0,8},{24,16},{1,9},{25,17},{2,10},{26,18},{3,11},{27,19},{4,12},{... | collective-permute-start | bytes 1769480 | tf_op jit(solution)/shard_map/ppermute | solution.py:1288
  212.2 6.7 %shard_map.288 = (bf16[1024,256]{1,0:T(8,128)(2,1)S(1)}, bf16[1024,256]{1,0:T(8,128)(2,1)S(1)}, bf16[1024,256]{1,0:T(8,128)(2,1)S(1)}, bf16[4,112,768]{2,1,0:T(8...) custom-call(s32[1]{0:T(128)} %bitcast.refs_0_, bf16[1024,2304]{1,0:T(8,128)(2,1)} %copy-done, ...), custom_call_target="tpu_custom_call" | custom-call | flops 2013265920 | bytes 5242880 | tf_op jit(solution)/shard_map/pallas_call | solution.py:93
  222.0 6.7 %shard_map.290 = (bf16[1024,256]{1,0:T(8,128)(2,1)S(1)}, bf16[1024,256]{1,0:T(8,128)(2,1)S(1)}, bf16[1024,256]{1,0:T(8,128)(2,1)S(1)}, bf16[4,112,768]{2,1,0:T(8...) custom-call(s32[1]{0:T(128)} %bitcast.refs_0_, bf16[1024,2304]{1,0:T(8,128)(2,1)} %copy-done, ...), custom_call_target="tpu_custom_call" | custom-call | flops 2013265920 | bytes 5242880 | tf_op jit(solution)/shard_map/pallas_call | solution.py:93
  237.6 9.0 %shard_map.292 = (f32[1024,768]{1,0:T(8,128)}, f32[8,128]{1,0:T(8,128)}) custom-call(s32[1]{0:T(128)} %bitcast.refs_0_, f32[1024,768]{1,0:T(8,128)S(1)} %copy-done.8, bf16[1024,256]{1,0:T(8,128)(2,1)S(1)} %copy-done.20, bf16[1024,256]{1,0:T(8,128)(2,1)S(1)} %get-tuple-element.348.refs_3_, bf16[1024,256]{1,0:T(8,128)(2,1)S(1)} %get-tuple-element.366.refs_4_, ...), custom_call_target="tpu_custom_call" | custom-call | flops 3623878656 | bytes 14548992 | tf_op jit(solution)/shard_map/pallas_call | solution.py:93
  253.8 3.0 collective-permute-start.53
  256.8 3.2 %collective-permute-done.56 = bf16[112,1536]{1,0:T(8,128)(2,1)S(1)} collective-permute-done((bf16[112,1536]{1,0:T(8,128)(2,1)S(1)}, bf16[112,1536]{1,0:T(8,128)(2,1)S(1)}, u32[]{:S(2)}, u32[]{:S(2)}) %collective-permute-start.56) | collective-permute-done | bytes 344096 | tf_op jit(solution)/shard_map/ppermute | solution.py:103
  265.2 13.8 %collective-permute-done.58 = bf16[56,1536]{1,0:T(8,128)(2,1)S(1)} collective-permute-done((bf16[56,1536]{1,0:T(8,128)(2,1)S(1)}, bf16[56,1536]{1,0:T(8,128)(2,1)S(1)}, u32[]{:S(2)}, u32[]{:S(2)}) %collective-permute-start.58) | collective-permute-done | bytes 172064 | tf_op jit(solution)/shard_map/ppermute | solution.py:103
  280.7 2.9 collective-permute-done.62
  288.0 5.7 %collective-permute-done.61 = bf16[56,1536]{1,0:T(8,128)(2,1)S(1)} collective-permute-done((bf16[56,1536]{1,0:T(8,128)(2,1)S(1)}, bf16[56,1536]{1,0:T(8,128)(2,1)S(1)}, u32[]{:S(2)}, u32[]{:S(2)}) %collective-permute-start.61) | collective-permute-done | bytes 172064 | tf_op jit(solution)/shard_map/ppermute | solution.py:1288
  293.9 3.6 %collective-permute-done.59 = bf16[112,1536]{1,0:T(8,128)(2,1)S(1)} collective-permute-done((bf16[112,1536]{1,0:T(8,128)(2,1)S(1)}, bf16[112,1536]{1,0:T(8,128)(2,1)S(1)}, u32[]{:S(2)}, u32[]{:S(2)}) %collective-permute-start.59) | collective-permute-done | bytes 344096 | tf_op jit(solution)/shard_map/ppermute | solution.py:1288
  (294 shorter events, 100.5 us)
Async XLA Ops:
  2.4 14.8 %collective-permute-start = (bf16[112,2304]{1,0:T(8,128)(2,1)S(1)}, bf16[112,2304]{1,0:T(8,128)(2,1)S(1)}, u32[]{:S(2)}, u32[]{:S(2)}) collective-permute-start(bf16[112,2304]{1,0:T(8,128)(2,1)S(1)} %fusion.3.refs_2_.refs_11_), channel_id=1, source_target_pairs={{0,2},{1,3},{2,0},{3,1},{4,6},{5,7},{6,4},{7,5},{8,10},{9,11},{10,... | collective-permute-start | bytes 1548296 | tf_op jit(solution)/shard_map/ppermute | solution.py:103
  5.4 13.2 %collective-permute-start.1 = (bf16[112,2304]{1,0:T(8,128)(2,1)S(1)}, bf16[112,2304]{1,0:T(8,128)(2,1)S(1)}, u32[]{:S(2)}, u32[]{:S(2)}) collective-permute-start(bf16[112,2304]{1,0:T(8,128)(2,1)S(1)} %fusion.3.refs_2_.refs_11_), channel_id=1, source_target_pairs={{0,4},{1,5},{2,6},{3,7},{4,0},{5,1},{6,2},{7,3},{8,12},{9,13},{10,... | collective-permute-start | bytes 1548296 | tf_op jit(solution)/shard_map/ppermute | solution.py:103
  6.9 22.1 %collective-permute-start.2 = (bf16[112,2304]{1,0:T(8,128)(2,1)S(1)}, bf16[112,2304]{1,0:T(8,128)(2,1)}, u32[]{:S(2)}, u32[]{:S(2)}) collective-permute-start(bf16[112,2304]{1,0:T(8,128)(2,1)S(1)} %fusion.3.refs_2_.refs_11_), channel_id=1, source_target_pairs={{0,1},{1,0},{2,3},{3,2},{4,5},{5,4},{6,7},{7,6},{8,9},{9,8},{10,11... | collective-permute-start | bytes 1548296 | tf_op jit(solution)/shard_map/ppermute | solution.py:103
  28.1 21.0 %collective-permute-start.9 = (bf16[112,3840]{1,0:T(8,128)(2,1)}, bf16[112,3840]{1,0:T(8,128)(2,1)S(1)}, u32[]{:S(2)}, u32[]{:S(2)}) collective-permute-start(bf16[112,3840]{1,0:T(8,128)(2,1)} %fusion.2.refs_3_.refs_1_.refs_9_), channel_id=1, source_target_pairs={{0,2},{1,3},{2,0},{3,1},{4,6},{5,7},{6,4},{7,5},{8,10},{9,11},{10,... | collective-permute-start | bytes 2580488 | tf_op jit(solution)/shard_map/ppermute | solution.py:103
  28.7 20.7 %collective-permute-start.10 = (bf16[112,3840]{1,0:T(8,128)(2,1)}, bf16[112,3840]{1,0:T(8,128)(2,1)S(1)}, u32[]{:S(2)}, u32[]{:S(2)}) collective-permute-start(bf16[112,3840]{1,0:T(8,128)(2,1)} %fusion.2.refs_3_.refs_1_.refs_9_), channel_id=1, source_target_pairs={{0,4},{1,5},{2,6},{3,7},{4,0},{5,1},{6,2},{7,3},{8,12},{9,13},{10,... | collective-permute-start | bytes 2580488 | tf_op jit(solution)/shard_map/ppermute | solution.py:103
  30.9 33.7 %collective-permute-start.11 = (bf16[112,3840]{1,0:T(8,128)(2,1)}, bf16[112,3840]{1,0:T(8,128)(2,1)S(1)}, u32[]{:S(2)}, u32[]{:S(2)}) collective-permute-start(bf16[112,3840]{1,0:T(8,128)(2,1)} %fusion.2.refs_3_.refs_1_.refs_9_), channel_id=1, source_target_pairs={{0,1},{1,0},{2,3},{3,2},{4,5},{5,4},{6,7},{7,6},{8,9},{9,8},{10,11... | collective-permute-start | bytes 2580488 | tf_op jit(solution)/shard_map/ppermute | solution.py:103
  49.4 15.8 %collective-permute-start.12 = (bf16[112,3840]{1,0:T(8,128)(2,1)S(1)}, bf16[112,3840]{1,0:T(8,128)(2,1)S(1)}, u32[]{:S(2)}, u32[]{:S(2)}) collective-permute-start(bf16[112,3840]{1,0:T(8,128)(2,1)S(1)} %collective-permute-done.9.refs_5_.refs_4_.refs_2_.refs_10_), channel_id=1, source_target_pairs={{0,1},{1,0},{2,3},{3,2},{4,5},{5,4},{6,7},{7,6},{8,9},{9,8},{10,11... | collective-permute-start | bytes 2580488 | tf_op jit(solution)/shard_map/ppermute | solution.py:103
  49.4 13.7 %collective-permute-start.15 = (bf16[64,3840]{1,0:T(8,128)(2,1)S(1)}, bf16[64,3840]{1,0:T(8,128)(2,1)S(1)}, u32[]{:S(2)}, u32[]{:S(2)}) collective-permute-start(bf16[64,3840]{1,0:T(8,128)(2,1)S(1)} %slice.216), channel_id=1, source_target_pairs={{0,4},{1,5},{2,6},{3,7},{4,0},{5,1},{6,2},{7,3},{8,12},{9,13},{10,... | collective-permute-start | bytes 1474568 | tf_op jit(solution)/shard_map/ppermute | solution.py:103
  51.6 13.6 %collective-permute-start.13 = (bf16[112,3840]{1,0:T(8,128)(2,1)S(1)}, bf16[112,3840]{1,0:T(8,128)(2,1)S(1)}, u32[]{:S(2)}, u32[]{:S(2)}) collective-permute-start(bf16[112,3840]{1,0:T(8,128)(2,1)S(1)} %collective-permute-done.10.refs_6_.refs_5_.refs_3_.refs_11_), channel_id=1, source_target_pairs={{0,1},{1,0},{2,3},{3,2},{4,5},{5,4},{6,7},{7,6},{8,9},{9,8},{10,11... | collective-permute-start | bytes 2580488 | tf_op jit(solution)/shard_map/ppermute | solution.py:103
  63.1 16.9 %collective-permute-start.18 = (bf16[384,768]{1,0:T(8,128)(2,1)}, bf16[384,768]{1,0:T(8,128)(2,1)}, u32[]{:S(2)}, u32[]{:S(2)}) collective-permute-start(bf16[384,768]{1,0:T(8,128)(2,1)} %refs_1_.1), channel_id=1, source_target_pairs={{0,2},{1,3},{2,0},{3,1},{4,6},{5,7},{6,4},{7,5},{8,10},{9,11},{10,... | collective-permute-start | bytes 1769480 | tf_op jit(solution)/shard_map/ppermute | solution.py:103
  64.6 15.8 %collective-permute-start.19 = (bf16[384,768]{1,0:T(8,128)(2,1)}, bf16[384,768]{1,0:T(8,128)(2,1)}, u32[]{:S(2)}, u32[]{:S(2)}) collective-permute-start(bf16[384,768]{1,0:T(8,128)(2,1)} %refs_1_.1), channel_id=1, source_target_pairs={{0,4},{1,5},{2,6},{3,7},{4,0},{5,1},{6,2},{7,3},{8,12},{9,13},{10,... | collective-permute-start | bytes 1769480 | tf_op jit(solution)/shard_map/ppermute | solution.py:103
  80.4 15.4 %collective-permute-start.23 = (bf16[384,768]{1,0:T(8,128)(2,1)}, bf16[384,768]{1,0:T(8,128)(2,1)}, u32[]{:S(2)}, u32[]{:S(2)}) collective-permute-start(bf16[384,768]{1,0:T(8,128)(2,1)} %collective-permute-done.18.refs_13_.refs_7_.refs_2_), channel_id=1, source_target_pairs={{0,4},{1,5},{2,6},{3,7},{4,0},{5,1},{6,2},{7,3},{8,12},{9,13},{10,... | collective-permute-start | bytes 1769480 | tf_op jit(solution)/shard_map/ppermute | solution.py:103
  81.6 14.3 %collective-permute-start.20 = (bf16[384,768]{1,0:T(8,128)(2,1)}, bf16[384,768]{1,0:T(8,128)(2,1)}, u32[]{:S(2)}, u32[]{:S(2)}) collective-permute-start(bf16[384,768]{1,0:T(8,128)(2,1)} %refs_1_.1), channel_id=1, source_target_pairs={{0,1},{1,0},{2,3},{3,2},{4,5},{5,4},{6,7},{7,6},{8,9},{9,8},{10,11... | collective-permute-start | bytes 1769480 | tf_op jit(solution)/shard_map/ppermute | solution.py:103
  81.6 14.3 %collective-permute-start.21 = (bf16[384,768]{1,0:T(8,128)(2,1)}, bf16[384,768]{1,0:T(8,128)(2,1)}, u32[]{:S(2)}, u32[]{:S(2)}) collective-permute-start(bf16[384,768]{1,0:T(8,128)(2,1)} %collective-permute-done.18.refs_13_.refs_7_.refs_2_), channel_id=1, source_target_pairs={{0,1},{1,0},{2,3},{3,2},{4,5},{5,4},{6,7},{7,6},{8,9},{9,8},{10,11... | collective-permute-start | bytes 1769480 | tf_op jit(solution)/shard_map/ppermute | solution.py:103
  82.1 13.8 %collective-permute-start.22 = (bf16[384,768]{1,0:T(8,128)(2,1)}, bf16[384,768]{1,0:T(8,128)(2,1)}, u32[]{:S(2)}, u32[]{:S(2)}) collective-permute-start(bf16[384,768]{1,0:T(8,128)(2,1)} %collective-permute-done.19.refs_14_.refs_8_.refs_3_), channel_id=1, source_target_pairs={{0,1},{1,0},{2,3},{3,2},{4,5},{5,4},{6,7},{7,6},{8,9},{9,8},{10,11... | collective-permute-start | bytes 1769480 | tf_op jit(solution)/shard_map/ppermute | solution.py:103
  164.1 13.1 %collective-permute-start.33 = (bf16[384,384]{1,0:T(8,128)(2,1)S(1)}, bf16[384,384]{1,0:T(8,128)(2,1)S(1)}, u32[]{:S(2)}, u32[]{:S(2)}) collective-permute-start(bf16[384,384]{1,0:T(8,128)(2,1)S(1)} %get-tuple-element.291.refs_10_), channel_id=1, source_target_pairs={{0,2},{1,3},{2,0},{3,1},{4,6},{5,7},{6,4},{7,5},{8,10},{9,11},{10,... | collective-permute-start | bytes 884744 | tf_op jit(solution)/shard_map/ppermute | solution.py:103
  177.7 23.9 %collective-permute-start.36 = (bf16[768,384]{1,0:T(8,128)(2,1)S(1)}, bf16[768,384]{1,0:T(8,128)(2,1)S(1)}, u32[]{:S(2)}, u32[]{:S(2)}) collective-permute-start(bf16[768,384]{1,0:T(8,128)(2,1)S(1)} %fusion.4.refs_19_), channel_id=1, source_target_pairs={{0,2},{1,3},{2,0},{3,1},{4,6},{5,7},{6,4},{7,5},{8,10},{9,11},{10,... | collective-permute-start | bytes 1769480 | tf_op jit(solution)/shard_map/ppermute | solution.py:103
  179.3 22.3 %collective-permute-start.37 = (bf16[768,384]{1,0:T(8,128)(2,1)S(1)}, bf16[768,384]{1,0:T(8,128)(2,1)S(1)}, u32[]{:S(2)}, u32[]{:S(2)}) collective-permute-start(bf16[768,384]{1,0:T(8,128)(2,1)S(1)} %fusion.5.refs_20_), channel_id=1, source_target_pairs={{0,4},{1,5},{2,6},{3,7},{4,0},{5,1},{6,2},{7,3},{8,12},{9,13},{10,... | collective-permute-start | bytes 1769480 | tf_op jit(solution)/shard_map/ppermute | solution.py:103
  202.6 16.2 %collective-permute-start.40 = (bf16[4,112,768]{2,1,0:T(8,128)(2,1)}, bf16[4,112,768]{2,1,0:T(8,128)(2,1)}, u32[]{:S(2)}, u32[]{:S(2)}) collective-permute-start(bf16[4,112,768]{2,1,0:T(8,128)(2,1)} %get-tuple-element.343), channel_id=1, source_target_pairs={{0,1},{1,0},{2,3},{3,2},{4,5},{5,4},{6,7},{7,6},{8,9},{9,8},{10,11... | collective-permute-start | bytes 2064392 | tf_op jit(solution)/shard_map/ppermute | solution.py:103
  206.7 22.0 %collective-permute-start.42 = (bf16[768,384]{1,0:T(8,128)(2,1)}, bf16[768,384]{1,0:T(8,128)(2,1)}, u32[]{:S(2)}, u32[]{:S(2)}) collective-permute-start(bf16[768,384]{1,0:T(8,128)(2,1)} %add_convert_fusion.3.refs_8_), channel_id=1, source_target_pairs={{0,8},{24,16},{1,9},{25,17},{2,10},{26,18},{3,11},{27,19},{4,12},{... | collective-permute-start | bytes 1769480 | tf_op jit(solution)/shard_map/ppermute | solution.py:1288
  210.4 20.8 %collective-permute-start.43 = (bf16[96,3072]{1,0:T(8,128)(2,1)}, bf16[96,3072]{1,0:T(8,128)(2,1)S(1)}, u32[]{:S(2)}, u32[]{:S(2)}) collective-permute-start(bf16[96,3072]{1,0:T(8,128)(2,1)} %fusion.6.refs_9_), channel_id=1, source_target_pairs={{0,2},{1,3},{2,0},{3,1},{4,6},{5,7},{6,4},{7,5},{8,10},{9,11},{10,... | collective-permute-start | bytes 1769480 | tf_op jit(solution)/shard_map/ppermute | solution.py:103
  211.6 19.5 %collective-permute-start.44 = (bf16[96,3072]{1,0:T(8,128)(2,1)}, bf16[96,3072]{1,0:T(8,128)(2,1)S(1)}, u32[]{:S(2)}, u32[]{:S(2)}) collective-permute-start(bf16[96,3072]{1,0:T(8,128)(2,1)} %fusion.7.refs_10_), channel_id=1, source_target_pairs={{0,4},{1,5},{2,6},{3,7},{4,0},{5,1},{6,2},{7,3},{8,12},{9,13},{10,... | collective-permute-start | bytes 1769480 | tf_op jit(solution)/shard_map/ppermute | solution.py:103
  230.2 17.7 %collective-permute-start.49 = (bf16[768,384]{1,0:T(8,128)(2,1)S(1)}, bf16[768,384]{1,0:T(8,128)(2,1)S(1)}, u32[]{:S(2)}, u32[]{:S(2)}) collective-permute-start(bf16[768,384]{1,0:T(8,128)(2,1)S(1)} %add_convert_fusion.2.refs_21_), channel_id=1, source_target_pairs={{8,16},{16,8},{9,17},{17,9},{10,18},{18,10},{11,19},{19,11},{12,20... | collective-permute-start | bytes 1769480 | tf_op jit(solution)/shard_map/ppermute | solution.py:1288
  232.0 16.0 %collective-permute-start.50 = (bf16[48,3072]{1,0:T(8,128)(2,1)S(1)}, bf16[48,3072]{1,0:T(8,128)(2,1)S(1)}, u32[]{:S(2)}, u32[]{:S(2)}) collective-permute-start(bf16[48,3072]{1,0:T(8,128)(2,1)S(1)} %broadcast_select_fusion.2.refs_22_), channel_id=1, source_target_pairs={{0,8},{8,0},{16,24},{24,16},{1,9},{9,1},{17,25},{25,17},{2,10},{10... | collective-permute-start | bytes 884744 | tf_op jit(solution)/shard_map/ppermute | solution.py:103
  233.4 17.3 %collective-permute-start.51 = (bf16[112,1536]{1,0:T(8,128)(2,1)S(1)}, bf16[112,1536]{1,0:T(8,128)(2,1)S(1)}, u32[]{:S(2)}, u32[]{:S(2)}) collective-permute-start(bf16[112,1536]{1,0:T(8,128)(2,1)S(1)} %get-tuple-element.358.refs_23_), channel_id=1, source_target_pairs={{0,2},{1,3},{2,0},{3,1},{4,6},{5,7},{6,4},{7,5},{8,10},{9,11},{10,... | collective-permute-start | bytes 1032200 | tf_op jit(solution)/shard_map/ppermute | solution.py:103
  236.6 17.1 %collective-permute-start.52 = (bf16[112,1536]{1,0:T(8,128)(2,1)S(1)}, bf16[112,1536]{1,0:T(8,128)(2,1)S(1)}, u32[]{:S(2)}, u32[]{:S(2)}) collective-permute-start(bf16[112,1536]{1,0:T(8,128)(2,1)S(1)} %add_convert_fusion.9.refs_24_), channel_id=1, source_target_pairs={{0,4},{1,5},{2,6},{3,7},{4,0},{5,1},{6,2},{7,3},{8,12},{9,13},{10,... | collective-permute-start | bytes 1032200 | tf_op jit(solution)/shard_map/ppermute | solution.py:103
  246.6 13.4 %collective-permute-start.56 = (bf16[112,1536]{1,0:T(8,128)(2,1)S(1)}, bf16[112,1536]{1,0:T(8,128)(2,1)S(1)}, u32[]{:S(2)}, u32[]{:S(2)}) collective-permute-start(bf16[112,1536]{1,0:T(8,128)(2,1)S(1)} %get-tuple-element.376), channel_id=1, source_target_pairs={{0,4},{1,5},{2,6},{3,7},{4,0},{5,1},{6,2},{7,3},{8,12},{9,13},{10,... | collective-permute-start | bytes 1032200 | tf_op jit(solution)/shard_map/ppermute | solution.py:103
  248.2 15.3 %collective-permute-start.54 = (bf16[48,3072]{1,0:T(8,128)(2,1)S(1)}, bf16[48,3072]{1,0:T(8,128)(2,1)S(1)}, u32[]{:S(2)}, u32[]{:S(2)}) collective-permute-start(bf16[48,3072]{1,0:T(8,128)(2,1)S(1)} %add_convert_fusion.11), channel_id=1, source_target_pairs={{0,16},{16,0},{8,24},{24,8},{1,17},{17,1},{9,25},{25,9},{2,18},{18... | collective-permute-start | bytes 884744 | tf_op jit(solution)/shard_map/ppermute | solution.py:1288
  250.7 28.5 %collective-permute-start.63 = (bf16[768,384]{1,0:T(8,128)(2,1)S(1)}, bf16[768,384]{1,0:T(8,128)(2,1)S(1)}, u32[]{:S(2)}, u32[]{:S(2)}) collective-permute-start(bf16[768,384]{1,0:T(8,128)(2,1)S(1)} %add_convert_fusion), channel_id=1, source_target_pairs={{8,0},{16,24},{9,1},{17,25},{10,2},{18,26},{11,3},{19,27},{12,4},{... | collective-permute-start | bytes 1769480 | tf_op jit(solution)/shard_map/ppermute | solution.py:1288
  260.1 18.9 %collective-permute-start.58 = (bf16[56,1536]{1,0:T(8,128)(2,1)S(1)}, bf16[56,1536]{1,0:T(8,128)(2,1)S(1)}, u32[]{:S(2)}, u32[]{:S(2)}) collective-permute-start(bf16[56,1536]{1,0:T(8,128)(2,1)S(1)} %broadcast_select_fusion.5), channel_id=1, source_target_pairs={{0,8},{8,0},{16,24},{24,16},{1,9},{9,1},{17,25},{25,17},{2,10},{10... | collective-permute-start | bytes 516104 | tf_op jit(solution)/shard_map/ppermute | solution.py:103
  263.5 20.0 %collective-permute-start.62 = (bf16[48,3072]{1,0:T(8,128)(2,1)S(1)}, bf16[48,3072]{1,0:T(8,128)(2,1)S(1)}, u32[]{:S(2)}, u32[]{:S(2)}) collective-permute-start(bf16[48,3072]{1,0:T(8,128)(2,1)S(1)} %add_convert_fusion.10), channel_id=1, source_target_pairs={{0,8},{8,0},{16,24},{24,16},{1,9},{9,1},{17,25},{25,17},{2,10},{10... | collective-permute-start | bytes 884744 | tf_op jit(solution)/shard_map/ppermute | solution.py:1288
  264.6 20.1 %collective-permute-start.57 = (bf16[112,1536]{1,0:T(8,128)(2,1)S(1)}, bf16[112,1536]{1,0:T(8,128)(2,1)S(1)}, u32[]{:S(2)}, u32[]{:S(2)}) collective-permute-start(bf16[112,1536]{1,0:T(8,128)(2,1)S(1)} %add_convert_fusion.5), channel_id=1, source_target_pairs={{8,16},{16,8},{9,17},{17,9},{10,18},{18,10},{11,19},{19,11},{12,20... | collective-permute-start | bytes 1032200 | tf_op jit(solution)/shard_map/ppermute | solution.py:1288
  (77 other events, 619.8 us)

commit v6 on v5

--- a/solution.py
+++ b/solution.py
@@ -730,7 +730,7 @@
         total * width * 2,
         total * total,
         after=after,
-        near=(1, 2, 3, 4, -1, -2),
+        near=tuple(range(1, 5 + len(everyone))) + (-1, -2),
     )(place, payload, positive, pooled, stats, *everyone)
 
 
@@ -1483,8 +1483,7 @@
         plane = [line] + [fsdp_swap(line, bit) for bit in (2, 4, 6)]
         wu_full, clock = hold_weights(index, mid_pieces, (width, inner), width, (line, clock))
         *plane, clock = tie((*plane, clock))
-        plane = jnp.concatenate(plane, axis=0)
-        everyone = [plane, fsdp_swap(plane, 1)]
+        everyone = list(plane) + [fsdp_swap(value, 1) for value in plane]
         layout = (2, ring // 2, planes)
         flip = me * own
     else:

time: 306 us -> 305 us (level)
    ppermute x54 -> x57, starting transfers between devices: 40.3 us -> 41.7 us  [swap(): return lax.ppermute(value, axis, [(i, i ^ bit) for i in range(size)])]
    unnamed x116 -> x117, local copies, waits for them, and re-layouts: 14.8 us -> 13.5 us
    ppermute x54 -> x57, waiting for transfers between devices: 48.1 us -> 46.9 us  [swap(): return lax.ppermute(value, axis, [(i, i ^ bit) for i in range(size)])]
  transfers between devices with their start and end apart: 64 -> 67, of which waited for: 23 -> 26; matrix products, arithmetic and copies ran while one was open for 7% -> 7% of each run, Pallas kernels for 37% -> 37%
where the time goes in v6:
time: 305 us; the launch traced here: 300 us
  Pallas kernels  144 us (47%)
  waiting for transfers between devices  63.7 us (21%)
  starting transfers between devices  54 us (18%)
  local copies, waits for them, and re-layouts  22.4 us (7%)
  other arithmetic  13.4 us (4%)
    pallas_call x22, Pallas kernels, apply(): return run(index, *placed, *after)  144 us
    ppermute x57, waiting for transfers between devices, swap(): return lax.ppermute(value, axis, [(i, i ^ bit) for i in range(size)])  46.9 us
    ppermute x57, starting transfers between devices, swap(): return lax.ppermute(value, axis, [(i, i ^ bit) for i in range(size)])  41.7 us
    ppermute x10, waiting for transfers between devices, along_z(): return lax.ppermute(value, 'batch', pairs)  16.7 us
    unnamed x117, local copies, waits for them, and re-layouts  13.5 us
    ppermute x10, starting transfers between devices, along_z(): return lax.ppermute(value, 'batch', pairs)  12.3 us
  transfers between devices with their start and end apart: 67, of which 26 were waited for; matrix products, arithmetic and copies ran while one was open for 7% of the time, Pallas kernels for 37%

profile of v6, /device:TPU:0, one launch (start us, length us, event | category | flops | bytes accessed | tf_op | source)
XLA Modules:
  0.0 299.9 jit_solution(4762894315993480339)
XLA Ops:
  2.4 3.0 %collective-permute-start = (bf16[112,2304]{1,0:T(8,128)(2,1)S(1)}, bf16[112,2304]{1,0:T(8,128)(2,1)S(1)}, u32[]{:S(2)}, u32[]{:S(2)}) collective-permute-start(bf16[112,2304]{1,0:T(8,128)(2,1)S(1)} %fusion.3.refs_2_.refs_11_), channel_id=1, source_target_pairs={{0,2},{1,3},{2,0},{3,1},{4,6},{5,7},{6,4},{7,5},{8,10},{9,11},{10,... | collective-permute-start | bytes 1548296 | tf_op jit(solution)/shard_map/ppermute | solution.py:103
  21.1 7.1 %collective-permute-done.5.refs_8_.refs_17_ = bf16[48,2304]{1,0:T(8,128)(2,1)S(1)} collective-permute-done((bf16[48,2304]{1,0:T(8,128)(2,1)S(1)}, bf16[48,2304]{1,0:T(8,128)(2,1)S(1)}, u32[]{:S(2)}, u32[]{:S(2)}) %collective-permute-start.5) | collective-permute-done | bytes 221216 | tf_op jit(solution)/shard_map/ppermute | solution.py:103
  31.6 9.4 %shard_map.271 = (bf16[1024,2304]{1,0:T(8,128)(2,1)S(1)}, f32[8,128]{1,0:T(8,128)}) custom-call(s32[1]{0:T(128)} %bitcast.refs_0_, bf16[1024,768]{1,0:T(8,128)(2,1)} %bitcast.31, bf16[112,2304]{1,0:T(8,128)(2,1)} %copy-done.35, bf16[112,2304]{1,0:T(8,128)(2,1)} %copy-done.36, bf16[112,2304]{1,0:T(8,128)(2,1)} %copy-done.37, ...), custom_call_target="tpu_custom_call" | custom-call | flops 3623878656 | bytes 9830400 | tf_op jit(solution)/shard_map/pallas_call | solution.py:93
  41.0 5.0 %shard_map.272 = (bf16[1024,768]{1,0:T(8,128)(2,1)S(1)}, f32[2,6,2,512]{3,2,1,0:T(2,128)S(1)}, f32[8,128]{1,0:T(8,128)S(1)}) custom-call(s32[1]{0:T(128)} %bitcast.refs_0_, bf16[1024,2304]{1,0:T(8,128)(2,1)S(1)} %get-tuple-element.232.refs_1_.refs_2_.refs_3_, s32[2,1,512]{2,1,0:T(1,128)} %reshape.151.refs_2_.refs_4_.refs_6_), custom_call_target="tpu_custom_call" | custom-call | flops 805306368 | bytes 3145728 | tf_op jit(solution)/shard_map/pallas_call | solution.py:93
  46.0 3.1 %collective-permute-done.9.refs_5_.refs_4_.refs_2_.refs_10_ = bf16[112,3840]{1,0:T(8,128)(2,1)S(1)} collective-permute-done((bf16[112,3840]{1,0:T(8,128)(2,1)}, bf16[112,3840]{1,0:T(8,128)(2,1)S(1)}, u32[]{:S(2)}, u32[]{:S(2)}) %collective-permute-start.9) | collective-permute-done | bytes 860192 | tf_op jit(solution)/shard_map/ppermute | solution.py:103
  51.6 5.0 %shard_map.273 = (bf16[1024,768]{1,0:T(8,128)(2,1)S(1)}, f32[2,6,2,512]{3,2,1,0:T(2,128)S(1)}, f32[8,128]{1,0:T(8,128)S(1)}) custom-call(s32[1]{0:T(128)} %bitcast.refs_0_, bf16[1024,2304]{1,0:T(8,128)(2,1)S(1)} %get-tuple-element.232.refs_1_.refs_2_.refs_3_, ...), custom_call_target="tpu_custom_call", output_to_operand_aliasing={{0}: (3, {}), {1}: (4, {})} | custom-call | flops 805306368 | bytes 3145728 | tf_op jit(solution)/shard_map/pallas_call | solution.py:93
  56.6 4.0 %collective-permute-done.14.refs_9_.refs_7_.refs_15_ = bf16[48,3840]{1,0:T(8,128)(2,1)S(1)} collective-permute-done((bf16[48,3840]{1,0:T(8,128)(2,1)S(1)}, bf16[48,3840]{1,0:T(8,128)(2,1)S(1)}, u32[]{:S(2)}, u32[]{:S(2)}) %collective-permute-start.14) | collective-permute-done | bytes 368672 | tf_op jit(solution)/shard_map/ppermute | solution.py:103
  60.6 2.5 collective-permute-done.15.refs_10_.refs_8_.refs_16_
  67.7 6.9 %shard_map.274 = (f32[1024,768]{1,0:T(8,128)}, f32[1024,1]{1,0:T(8,128)}, bf16[1024,768]{1,0:T(8,128)(2,1)S(1)}, f32[8,768]{1,0:T(8,128)S(1)}, f32[1,3072]{1,0:T(1,128)S(1)}, /*index=5*/f32[8,128]{1,0:T(8,128)S(1)}) custom-call(s32[1]{0:T(128)} %bitcast.refs_0_, bf16[1024,768]{1,0:T(8,128)(2,1)S(1)} %get-tuple-element.240.refs_1_.refs_6_, ...), custom_call_target="tpu_custom_call" | custom-call | flops 1207959552 | bytes 9043968 | tf_op jit(solution)/shard_map/pallas_call | solution.py:93
  75.8 3.1 %shard_map.275 = (bf16[768,1024]{1,0:T(8,128)(2,1)S(1)}, bf16[768,1024]{1,0:T(8,128)(2,1)S(1)}, f32[8,128]{1,0:T(8,128)S(1)}) custom-call(s32[1]{0:T(128)} %bitcast.refs_0_, bf16[1024,768]{1,0:T(8,128)(2,1)} %copy-done.11, bf16[1024,768]{1,0:T(8,128)(2,1)} %bitcast.33, f32[8,128]{1,0:T(8,128)S(1)} %get-tuple-element.248.refs_3_), custom_call_target="tpu_custom_call" | custom-call | bytes 6291456 | tf_op jit(solution)/shard_map/pallas_call | solution.py:93
  82.1 12.9 %shard_map.276 = (bf16[1024,3072]{1,0:T(8,128)(2,1)}, bf16[1024,3072]{1,0:T(8,128)(2,1)}, f32[8,128]{1,0:T(8,128)S(1)}) custom-call(s32[1]{0:T(128)} %bitcast.refs_0_, bf16[1024,768]{1,0:T(8,128)(2,1)S(1)} %copy-done.12, f32[1,3072]{1,0:T(1,128)S(1)} %get-tuple-element.246.refs_2_, bf16[112,3840]{1,0:T(8,128)(2,1)} %fusion.2.refs_3_.refs_1_.refs_9_, ...), custom_call_target="tpu_custom_call" | custom-call | flops 4831838208 | bytes 18874368 | tf_op jit(solution)/shard_map/pallas_call | solution.py:93
  95.8 2.2 collective-permute-done.24.refs_13_.refs_8_
  98.1 15.6 %shard_map.277 = (bf16[1024,768]{1,0:T(8,128)(2,1)}, f32[1024,768]{1,0:T(8,128)}, f32[1024,1]{1,0:T(8,128)}, bf16[16,896]{1,0:T(8,128)(2,1)S(1)}, f32[16,768]{1,...) custom-call(s32[1]{0:T(128)} %bitcast.refs_0_, bf16[1024,3072]{1,0:T(8,128)(2,1)} %get-tuple-element.253.refs_1_.refs_7_, ...), custom_call_target="tpu_custom_call" | custom-call | flops 4831838208 | bytes 18874368 | tf_op jit(solution)/shard_map/pallas_call | solution.py:93
  115.3 2.6 collective-permute-start.26
  118.1 2.4 shard_map.278
  127.2 2.4 shard_map.279
  134.9 4.0 %shard_map.280 = (f32[16,1]{1,0:T(8,128)S(1)}, f32[16,768]{1,0:T(8,128)S(1)}, f32[8,128]{1,0:T(8,128)}) custom-call(s32[2]{0:T(128)S(1)} %pad_add_fusion.refs_0_, bf16[16,896]{1,0:T(8,128)(2,1)S(1)} %get-tuple-element.264.refs_9_.refs_1_, s32[16,1]{1,0:T(8,128)S(1)} %copy.40.refs_5_.refs_2_, f32[16,768]{1,0:T(8,128)S(1)} %get-tuple-element.261.refs_3_, ...), custom_call_target="tpu_custom_call" | custom-call | flops 402653184 | bytes 786432 | tf_op jit(solution)/shard_map/pallas_call | solution.py:93
  138.9 12.3 %shard_map.281 = (f32[1024,768]{1,0:T(8,128)S(1)}, bf16[1024,768]{1,0:T(8,128)(2,1)S(1)}, f32[8,768]{1,0:T(8,128)S(1)}, bf16[4,768,384]{2,1,0:T(8,128)(2,1)S(1)}...) custom-call(s32[1]{0:T(128)} %bitcast.refs_0_, bf16[1024,768]{1,0:T(8,128)(2,1)} %bitcast.42, ...), custom_call_target="tpu_custom_call" | custom-call | flops 4831838208 | bytes 20447232 | tf_op jit(solution)/shard_map/pallas_call | solution.py:93
  151.6 10.9 %shard_map.282 = (f32[1024,768]{1,0:T(8,128)S(1)}, f32[1,3072]{1,0:T(1,128)S(1)}, bf16[4,96,3072]{2,1,0:T(8,128)(2,1)S(1)}, bf16[4,96,3072]{2,1,0:T(8,128)(2,1)S(1)}, f32[8,128]{1,0:T(8,128)}) custom-call(s32[1]{0:T(128)} %bitcast.refs_0_, bf16[1024,768]{1,0:T(8,128)(2,1)S(1)} %get-tuple-element.279.refs_1_, bf16[1024,3072]{1,0:T(8,128)(2,1)} %get-tuple-element.280.refs_2_, ...), custom_call_target="tpu_custom_call" | custom-call | flops 7247757312 | bytes 23592960 | tf_op jit(solution)/shard_map/pallas_call | solution.py:93
  165.2 10.9 %shard_map.284 = (f32[1024,768]{1,0:T(8,128)S(1)}, f32[1,3072]{1,0:T(1,128)S(1)}, bf16[4,96,3072]{2,1,0:T(8,128)(2,1)S(1)}, bf16[4,96,3072]{2,1,0:T(8,128)(2,1)S(1)}, f32[8,128]{1,0:T(8,128)}) custom-call(s32[1]{0:T(128)} %bitcast.refs_0_, ...), custom_call_target="tpu_custom_call", output_to_operand_aliasing={{0}: (6, {}), {1}: (7, {}), {2}: (8, {}), {3}: (9, {})} | custom-call | flops 7247757312 | bytes 23592960 | tf_op jit(solution)/shard_map/pallas_call | solution.py:93
  178.7 8.7 %shard_map.285 = (f32[1024,768]{1,0:T(8,128)S(1)}, bf16[1024,768]{1,0:T(8,128)(2,1)S(1)}, bf16[4,112,768]{2,1,0:T(8,128)(2,1)S(1)}, bf16[4,112,768]{2,1,0:T(8,128)(2,1)}, f32[8,128]{1,0:T(8,128)}) custom-call(s32[1]{0:T(128)} %bitcast.refs_0_, f32[1024,768]{1,0:T(8,128)S(1)} %get-tuple-element.305.refs_1_, f32[1024,768]{1,0:T(8,128)S(1)} %get-tuple-element.306.refs_2_, ...), custom_call_target="tpu_custom_call" | custom-call | flops 2415919104 | bytes 18087936 | tf_op jit(solution)/shard_map/pallas_call | solution.py:93
  193.0 7.5 %shard_map.287 = (bf16[1024,256]{1,0:T(8,128)(2,1)S(1)}, bf16[1024,256]{1,0:T(8,128)(2,1)S(1)}, bf16[1024,256]{1,0:T(8,128)(2,1)S(1)}, bf16[4,112,768]{2,1,0:T(8...) custom-call(s32[1]{0:T(128)} %bitcast.refs_0_, bf16[1024,2304]{1,0:T(8,128)(2,1)} %copy-done, ...), custom_call_target="tpu_custom_call" | custom-call | flops 2013265920 | bytes 5242880 | tf_op jit(solution)/shard_map/pallas_call | solution.py:93
  205.7 3.1 %collective-permute-start.45 = (bf16[768,384]{1,0:T(8,128)(2,1)}, bf16[768,384]{1,0:T(8,128)(2,1)}, u32[]{:S(2)}, u32[]{:S(2)}) collective-permute-start(bf16[768,384]{1,0:T(8,128)(2,1)} %add_convert_fusion.3.refs_8_), channel_id=1, source_target_pairs={{0,8},{24,16},{1,9},{25,17},{2,10},{26,18},{3,11},{27,19},{4,12},{... | collective-permute-start | bytes 1769480 | tf_op jit(solution)/shard_map/ppermute | solution.py:1288
  211.1 6.7 %shard_map.288 = (bf16[1024,256]{1,0:T(8,128)(2,1)S(1)}, bf16[1024,256]{1,0:T(8,128)(2,1)S(1)}, bf16[1024,256]{1,0:T(8,128)(2,1)S(1)}, bf16[4,112,768]{2,1,0:T(8...) custom-call(s32[1]{0:T(128)} %bitcast.refs_0_, bf16[1024,2304]{1,0:T(8,128)(2,1)} %copy-done, ...), custom_call_target="tpu_custom_call" | custom-call | flops 2013265920 | bytes 5242880 | tf_op jit(solution)/shard_map/pallas_call | solution.py:93
  221.0 6.7 %shard_map.290 = (bf16[1024,256]{1,0:T(8,128)(2,1)S(1)}, bf16[1024,256]{1,0:T(8,128)(2,1)S(1)}, bf16[1024,256]{1,0:T(8,128)(2,1)S(1)}, bf16[4,112,768]{2,1,0:T(8...) custom-call(s32[1]{0:T(128)} %bitcast.refs_0_, bf16[1024,2304]{1,0:T(8,128)(2,1)} %copy-done, ...), custom_call_target="tpu_custom_call" | custom-call | flops 2013265920 | bytes 5242880 | tf_op jit(solution)/shard_map/pallas_call | solution.py:93
  236.6 9.0 %shard_map.292 = (f32[1024,768]{1,0:T(8,128)}, f32[8,128]{1,0:T(8,128)}) custom-call(s32[1]{0:T(128)} %bitcast.refs_0_, f32[1024,768]{1,0:T(8,128)S(1)} %copy-done.8, bf16[1024,256]{1,0:T(8,128)(2,1)S(1)} %copy-done.20, bf16[1024,256]{1,0:T(8,128)(2,1)S(1)} %get-tuple-element.348.refs_3_, bf16[1024,256]{1,0:T(8,128)(2,1)S(1)} %get-tuple-element.366.refs_4_, ...), custom_call_target="tpu_custom_call" | custom-call | flops 3623878656 | bytes 14548992 | tf_op jit(solution)/shard_map/pallas_call | solution.py:93
  252.8 3.0 %collective-permute-start.56 = (bf16[112,1536]{1,0:T(8,128)(2,1)S(1)}, bf16[112,1536]{1,0:T(8,128)(2,1)S(1)}, u32[]{:S(2)}, u32[]{:S(2)}) collective-permute-start(bf16[112,1536]{1,0:T(8,128)(2,1)S(1)} %add_convert_fusion.7), channel_id=1, source_target_pairs={{0,8},{24,16},{1,9},{25,17},{2,10},{26,18},{3,11},{27,19},{4,12},{... | collective-permute-start | bytes 1032200 | tf_op jit(solution)/shard_map/ppermute | solution.py:1288
  255.8 3.1 %collective-permute-done.59 = bf16[112,1536]{1,0:T(8,128)(2,1)S(1)} collective-permute-done((bf16[112,1536]{1,0:T(8,128)(2,1)S(1)}, bf16[112,1536]{1,0:T(8,128)(2,1)S(1)}, u32[]{:S(2)}, u32[]{:S(2)}) %collective-permute-start.59) | collective-permute-done | bytes 344096 | tf_op jit(solution)/shard_map/ppermute | solution.py:103
  264.3 13.8 %collective-permute-done.61 = bf16[56,1536]{1,0:T(8,128)(2,1)S(1)} collective-permute-done((bf16[56,1536]{1,0:T(8,128)(2,1)S(1)}, bf16[56,1536]{1,0:T(8,128)(2,1)S(1)}, u32[]{:S(2)}, u32[]{:S(2)}) %collective-permute-start.61) | collective-permute-done | bytes 172064 | tf_op jit(solution)/shard_map/ppermute | solution.py:103
  279.7 2.8 collective-permute-done.65
  287.0 5.7 %collective-permute-done.64 = bf16[56,1536]{1,0:T(8,128)(2,1)S(1)} collective-permute-done((bf16[56,1536]{1,0:T(8,128)(2,1)S(1)}, bf16[56,1536]{1,0:T(8,128)(2,1)S(1)}, u32[]{:S(2)}, u32[]{:S(2)}) %collective-permute-start.64) | collective-permute-done | bytes 172064 | tf_op jit(solution)/shard_map/ppermute | solution.py:1288
  292.9 3.6 %collective-permute-done.62 = bf16[112,1536]{1,0:T(8,128)(2,1)S(1)} collective-permute-done((bf16[112,1536]{1,0:T(8,128)(2,1)S(1)}, bf16[112,1536]{1,0:T(8,128)(2,1)S(1)}, u32[]{:S(2)}, u32[]{:S(2)}) %collective-permute-start.62) | collective-permute-done | bytes 344096 | tf_op jit(solution)/shard_map/ppermute | solution.py:1288
  (300 shorter events, 98.8 us)
Async XLA Ops:
  2.4 14.8 %collective-permute-start = (bf16[112,2304]{1,0:T(8,128)(2,1)S(1)}, bf16[112,2304]{1,0:T(8,128)(2,1)S(1)}, u32[]{:S(2)}, u32[]{:S(2)}) collective-permute-start(bf16[112,2304]{1,0:T(8,128)(2,1)S(1)} %fusion.3.refs_2_.refs_11_), channel_id=1, source_target_pairs={{0,2},{1,3},{2,0},{3,1},{4,6},{5,7},{6,4},{7,5},{8,10},{9,11},{10,... | collective-permute-start | bytes 1548296 | tf_op jit(solution)/shard_map/ppermute | solution.py:103
  5.4 13.2 %collective-permute-start.1 = (bf16[112,2304]{1,0:T(8,128)(2,1)S(1)}, bf16[112,2304]{1,0:T(8,128)(2,1)S(1)}, u32[]{:S(2)}, u32[]{:S(2)}) collective-permute-start(bf16[112,2304]{1,0:T(8,128)(2,1)S(1)} %fusion.3.refs_2_.refs_11_), channel_id=1, source_target_pairs={{0,4},{1,5},{2,6},{3,7},{4,0},{5,1},{6,2},{7,3},{8,12},{9,13},{10,... | collective-permute-start | bytes 1548296 | tf_op jit(solution)/shard_map/ppermute | solution.py:103
  6.9 22.1 %collective-permute-start.2 = (bf16[112,2304]{1,0:T(8,128)(2,1)S(1)}, bf16[112,2304]{1,0:T(8,128)(2,1)}, u32[]{:S(2)}, u32[]{:S(2)}) collective-permute-start(bf16[112,2304]{1,0:T(8,128)(2,1)S(1)} %fusion.3.refs_2_.refs_11_), channel_id=1, source_target_pairs={{0,1},{1,0},{2,3},{3,2},{4,5},{5,4},{6,7},{7,6},{8,9},{9,8},{10,11... | collective-permute-start | bytes 1548296 | tf_op jit(solution)/shard_map/ppermute | solution.py:103
  28.1 21.0 %collective-permute-start.9 = (bf16[112,3840]{1,0:T(8,128)(2,1)}, bf16[112,3840]{1,0:T(8,128)(2,1)S(1)}, u32[]{:S(2)}, u32[]{:S(2)}) collective-permute-start(bf16[112,3840]{1,0:T(8,128)(2,1)} %fusion.2.refs_3_.refs_1_.refs_9_), channel_id=1, source_target_pairs={{0,2},{1,3},{2,0},{3,1},{4,6},{5,7},{6,4},{7,5},{8,10},{9,11},{10,... | collective-permute-start | bytes 2580488 | tf_op jit(solution)/shard_map/ppermute | solution.py:103
  28.7 20.7 %collective-permute-start.10 = (bf16[112,3840]{1,0:T(8,128)(2,1)}, bf16[112,3840]{1,0:T(8,128)(2,1)S(1)}, u32[]{:S(2)}, u32[]{:S(2)}) collective-permute-start(bf16[112,3840]{1,0:T(8,128)(2,1)} %fusion.2.refs_3_.refs_1_.refs_9_), channel_id=1, source_target_pairs={{0,4},{1,5},{2,6},{3,7},{4,0},{5,1},{6,2},{7,3},{8,12},{9,13},{10,... | collective-permute-start | bytes 2580488 | tf_op jit(solution)/shard_map/ppermute | solution.py:103
  30.9 33.7 %collective-permute-start.11 = (bf16[112,3840]{1,0:T(8,128)(2,1)}, bf16[112,3840]{1,0:T(8,128)(2,1)S(1)}, u32[]{:S(2)}, u32[]{:S(2)}) collective-permute-start(bf16[112,3840]{1,0:T(8,128)(2,1)} %fusion.2.refs_3_.refs_1_.refs_9_), channel_id=1, source_target_pairs={{0,1},{1,0},{2,3},{3,2},{4,5},{5,4},{6,7},{7,6},{8,9},{9,8},{10,11... | collective-permute-start | bytes 2580488 | tf_op jit(solution)/shard_map/ppermute | solution.py:103
  49.4 15.8 %collective-permute-start.12 = (bf16[112,3840]{1,0:T(8,128)(2,1)S(1)}, bf16[112,3840]{1,0:T(8,128)(2,1)S(1)}, u32[]{:S(2)}, u32[]{:S(2)}) collective-permute-start(bf16[112,3840]{1,0:T(8,128)(2,1)S(1)} %collective-permute-done.9.refs_5_.refs_4_.refs_2_.refs_10_), channel_id=1, source_target_pairs={{0,1},{1,0},{2,3},{3,2},{4,5},{5,4},{6,7},{7,6},{8,9},{9,8},{10,11... | collective-permute-start | bytes 2580488 | tf_op jit(solution)/shard_map/ppermute | solution.py:103
  49.4 13.7 %collective-permute-start.15 = (bf16[64,3840]{1,0:T(8,128)(2,1)S(1)}, bf16[64,3840]{1,0:T(8,128)(2,1)S(1)}, u32[]{:S(2)}, u32[]{:S(2)}) collective-permute-start(bf16[64,3840]{1,0:T(8,128)(2,1)S(1)} %slice.216), channel_id=1, source_target_pairs={{0,4},{1,5},{2,6},{3,7},{4,0},{5,1},{6,2},{7,3},{8,12},{9,13},{10,... | collective-permute-start | bytes 1474568 | tf_op jit(solution)/shard_map/ppermute | solution.py:103
  51.6 13.6 %collective-permute-start.13 = (bf16[112,3840]{1,0:T(8,128)(2,1)S(1)}, bf16[112,3840]{1,0:T(8,128)(2,1)S(1)}, u32[]{:S(2)}, u32[]{:S(2)}) collective-permute-start(bf16[112,3840]{1,0:T(8,128)(2,1)S(1)} %collective-permute-done.10.refs_6_.refs_5_.refs_3_.refs_11_), channel_id=1, source_target_pairs={{0,1},{1,0},{2,3},{3,2},{4,5},{5,4},{6,7},{7,6},{8,9},{9,8},{10,11... | collective-permute-start | bytes 2580488 | tf_op jit(solution)/shard_map/ppermute | solution.py:103
  63.1 16.9 %collective-permute-start.18 = (bf16[384,768]{1,0:T(8,128)(2,1)}, bf16[384,768]{1,0:T(8,128)(2,1)}, u32[]{:S(2)}, u32[]{:S(2)}) collective-permute-start(bf16[384,768]{1,0:T(8,128)(2,1)} %refs_1_.1), channel_id=1, source_target_pairs={{0,2},{1,3},{2,0},{3,1},{4,6},{5,7},{6,4},{7,5},{8,10},{9,11},{10,... | collective-permute-start | bytes 1769480 | tf_op jit(solution)/shard_map/ppermute | solution.py:103
  64.6 15.8 %collective-permute-start.19 = (bf16[384,768]{1,0:T(8,128)(2,1)}, bf16[384,768]{1,0:T(8,128)(2,1)}, u32[]{:S(2)}, u32[]{:S(2)}) collective-permute-start(bf16[384,768]{1,0:T(8,128)(2,1)} %refs_1_.1), channel_id=1, source_target_pairs={{0,4},{1,5},{2,6},{3,7},{4,0},{5,1},{6,2},{7,3},{8,12},{9,13},{10,... | collective-permute-start | bytes 1769480 | tf_op jit(solution)/shard_map/ppermute | solution.py:103
  80.4 15.4 %collective-permute-start.23 = (bf16[384,768]{1,0:T(8,128)(2,1)}, bf16[384,768]{1,0:T(8,128)(2,1)}, u32[]{:S(2)}, u32[]{:S(2)}) collective-permute-start(bf16[384,768]{1,0:T(8,128)(2,1)} %collective-permute-done.18.refs_13_.refs_7_.refs_2_), channel_id=1, source_target_pairs={{0,4},{1,5},{2,6},{3,7},{4,0},{5,1},{6,2},{7,3},{8,12},{9,13},{10,... | collective-permute-start | bytes 1769480 | tf_op jit(solution)/shard_map/ppermute | solution.py:103
  81.6 14.3 %collective-permute-start.20 = (bf16[384,768]{1,0:T(8,128)(2,1)}, bf16[384,768]{1,0:T(8,128)(2,1)}, u32[]{:S(2)}, u32[]{:S(2)}) collective-permute-start(bf16[384,768]{1,0:T(8,128)(2,1)} %refs_1_.1), channel_id=1, source_target_pairs={{0,1},{1,0},{2,3},{3,2},{4,5},{5,4},{6,7},{7,6},{8,9},{9,8},{10,11... | collective-permute-start | bytes 1769480 | tf_op jit(solution)/shard_map/ppermute | solution.py:103
  81.6 14.3 %collective-permute-start.21 = (bf16[384,768]{1,0:T(8,128)(2,1)}, bf16[384,768]{1,0:T(8,128)(2,1)}, u32[]{:S(2)}, u32[]{:S(2)}) collective-permute-start(bf16[384,768]{1,0:T(8,128)(2,1)} %collective-permute-done.18.refs_13_.refs_7_.refs_2_), channel_id=1, source_target_pairs={{0,1},{1,0},{2,3},{3,2},{4,5},{5,4},{6,7},{7,6},{8,9},{9,8},{10,11... | collective-permute-start | bytes 1769480 | tf_op jit(solution)/shard_map/ppermute | solution.py:103
  82.1 13.8 %collective-permute-start.22 = (bf16[384,768]{1,0:T(8,128)(2,1)}, bf16[384,768]{1,0:T(8,128)(2,1)}, u32[]{:S(2)}, u32[]{:S(2)}) collective-permute-start(bf16[384,768]{1,0:T(8,128)(2,1)} %collective-permute-done.19.refs_14_.refs_8_.refs_3_), channel_id=1, source_target_pairs={{0,1},{1,0},{2,3},{3,2},{4,5},{5,4},{6,7},{7,6},{8,9},{9,8},{10,11... | collective-permute-start | bytes 1769480 | tf_op jit(solution)/shard_map/ppermute | solution.py:103
  163.1 13.1 %collective-permute-start.36 = (bf16[384,384]{1,0:T(8,128)(2,1)S(1)}, bf16[384,384]{1,0:T(8,128)(2,1)S(1)}, u32[]{:S(2)}, u32[]{:S(2)}) collective-permute-start(bf16[384,384]{1,0:T(8,128)(2,1)S(1)} %get-tuple-element.291.refs_10_), channel_id=1, source_target_pairs={{0,2},{1,3},{2,0},{3,1},{4,6},{5,7},{6,4},{7,5},{8,10},{9,11},{10,... | collective-permute-start | bytes 884744 | tf_op jit(solution)/shard_map/ppermute | solution.py:103
  176.7 23.9 %collective-permute-start.39 = (bf16[768,384]{1,0:T(8,128)(2,1)S(1)}, bf16[768,384]{1,0:T(8,128)(2,1)S(1)}, u32[]{:S(2)}, u32[]{:S(2)}) collective-permute-start(bf16[768,384]{1,0:T(8,128)(2,1)S(1)} %fusion.4.refs_19_), channel_id=1, source_target_pairs={{0,2},{1,3},{2,0},{3,1},{4,6},{5,7},{6,4},{7,5},{8,10},{9,11},{10,... | collective-permute-start | bytes 1769480 | tf_op jit(solution)/shard_map/ppermute | solution.py:103
  178.2 22.3 %collective-permute-start.40 = (bf16[768,384]{1,0:T(8,128)(2,1)S(1)}, bf16[768,384]{1,0:T(8,128)(2,1)S(1)}, u32[]{:S(2)}, u32[]{:S(2)}) collective-permute-start(bf16[768,384]{1,0:T(8,128)(2,1)S(1)} %fusion.5.refs_20_), channel_id=1, source_target_pairs={{0,4},{1,5},{2,6},{3,7},{4,0},{5,1},{6,2},{7,3},{8,12},{9,13},{10,... | collective-permute-start | bytes 1769480 | tf_op jit(solution)/shard_map/ppermute | solution.py:103
  201.6 16.2 %collective-permute-start.43 = (bf16[4,112,768]{2,1,0:T(8,128)(2,1)}, bf16[4,112,768]{2,1,0:T(8,128)(2,1)}, u32[]{:S(2)}, u32[]{:S(2)}) collective-permute-start(bf16[4,112,768]{2,1,0:T(8,128)(2,1)} %get-tuple-element.343), channel_id=1, source_target_pairs={{0,1},{1,0},{2,3},{3,2},{4,5},{5,4},{6,7},{7,6},{8,9},{9,8},{10,11... | collective-permute-start | bytes 2064392 | tf_op jit(solution)/shard_map/ppermute | solution.py:103
  205.7 22.0 %collective-permute-start.45 = (bf16[768,384]{1,0:T(8,128)(2,1)}, bf16[768,384]{1,0:T(8,128)(2,1)}, u32[]{:S(2)}, u32[]{:S(2)}) collective-permute-start(bf16[768,384]{1,0:T(8,128)(2,1)} %add_convert_fusion.3.refs_8_), channel_id=1, source_target_pairs={{0,8},{24,16},{1,9},{25,17},{2,10},{26,18},{3,11},{27,19},{4,12},{... | collective-permute-start | bytes 1769480 | tf_op jit(solution)/shard_map/ppermute | solution.py:1288
  209.4 20.7 %collective-permute-start.46 = (bf16[96,3072]{1,0:T(8,128)(2,1)}, bf16[96,3072]{1,0:T(8,128)(2,1)S(1)}, u32[]{:S(2)}, u32[]{:S(2)}) collective-permute-start(bf16[96,3072]{1,0:T(8,128)(2,1)} %fusion.6.refs_9_), channel_id=1, source_target_pairs={{0,2},{1,3},{2,0},{3,1},{4,6},{5,7},{6,4},{7,5},{8,10},{9,11},{10,... | collective-permute-start | bytes 1769480 | tf_op jit(solution)/shard_map/ppermute | solution.py:103
  210.6 19.5 %collective-permute-start.47 = (bf16[96,3072]{1,0:T(8,128)(2,1)}, bf16[96,3072]{1,0:T(8,128)(2,1)S(1)}, u32[]{:S(2)}, u32[]{:S(2)}) collective-permute-start(bf16[96,3072]{1,0:T(8,128)(2,1)} %fusion.7.refs_10_), channel_id=1, source_target_pairs={{0,4},{1,5},{2,6},{3,7},{4,0},{5,1},{6,2},{7,3},{8,12},{9,13},{10,... | collective-permute-start | bytes 1769480 | tf_op jit(solution)/shard_map/ppermute | solution.py:103
  229.2 17.7 %collective-permute-start.52 = (bf16[768,384]{1,0:T(8,128)(2,1)S(1)}, bf16[768,384]{1,0:T(8,128)(2,1)S(1)}, u32[]{:S(2)}, u32[]{:S(2)}) collective-permute-start(bf16[768,384]{1,0:T(8,128)(2,1)S(1)} %add_convert_fusion.2.refs_21_), channel_id=1, source_target_pairs={{8,16},{16,8},{9,17},{17,9},{10,18},{18,10},{11,19},{19,11},{12,20... | collective-permute-start | bytes 1769480 | tf_op jit(solution)/shard_map/ppermute | solution.py:1288
  231.0 16.0 %collective-permute-start.53 = (bf16[48,3072]{1,0:T(8,128)(2,1)S(1)}, bf16[48,3072]{1,0:T(8,128)(2,1)S(1)}, u32[]{:S(2)}, u32[]{:S(2)}) collective-permute-start(bf16[48,3072]{1,0:T(8,128)(2,1)S(1)} %broadcast_select_fusion.2.refs_22_), channel_id=1, source_target_pairs={{0,8},{8,0},{16,24},{24,16},{1,9},{9,1},{17,25},{25,17},{2,10},{10... | collective-permute-start | bytes 884744 | tf_op jit(solution)/shard_map/ppermute | solution.py:103
  232.5 17.3 %collective-permute-start.54 = (bf16[112,1536]{1,0:T(8,128)(2,1)S(1)}, bf16[112,1536]{1,0:T(8,128)(2,1)S(1)}, u32[]{:S(2)}, u32[]{:S(2)}) collective-permute-start(bf16[112,1536]{1,0:T(8,128)(2,1)S(1)} %get-tuple-element.358.refs_23_), channel_id=1, source_target_pairs={{0,2},{1,3},{2,0},{3,1},{4,6},{5,7},{6,4},{7,5},{8,10},{9,11},{10,... | collective-permute-start | bytes 1032200 | tf_op jit(solution)/shard_map/ppermute | solution.py:103
  235.7 17.0 %collective-permute-start.55 = (bf16[112,1536]{1,0:T(8,128)(2,1)S(1)}, bf16[112,1536]{1,0:T(8,128)(2,1)S(1)}, u32[]{:S(2)}, u32[]{:S(2)}) collective-permute-start(bf16[112,1536]{1,0:T(8,128)(2,1)S(1)} %add_convert_fusion.9.refs_24_), channel_id=1, source_target_pairs={{0,4},{1,5},{2,6},{3,7},{4,0},{5,1},{6,2},{7,3},{8,12},{9,13},{10,... | collective-permute-start | bytes 1032200 | tf_op jit(solution)/shard_map/ppermute | solution.py:103
  245.5 13.4 %collective-permute-start.59 = (bf16[112,1536]{1,0:T(8,128)(2,1)S(1)}, bf16[112,1536]{1,0:T(8,128)(2,1)S(1)}, u32[]{:S(2)}, u32[]{:S(2)}) collective-permute-start(bf16[112,1536]{1,0:T(8,128)(2,1)S(1)} %get-tuple-element.376), channel_id=1, source_target_pairs={{0,4},{1,5},{2,6},{3,7},{4,0},{5,1},{6,2},{7,3},{8,12},{9,13},{10,... | collective-permute-start | bytes 1032200 | tf_op jit(solution)/shard_map/ppermute | solution.py:103
  247.2 15.3 %collective-permute-start.57 = (bf16[48,3072]{1,0:T(8,128)(2,1)S(1)}, bf16[48,3072]{1,0:T(8,128)(2,1)S(1)}, u32[]{:S(2)}, u32[]{:S(2)}) collective-permute-start(bf16[48,3072]{1,0:T(8,128)(2,1)S(1)} %add_convert_fusion.11), channel_id=1, source_target_pairs={{0,16},{16,0},{8,24},{24,8},{1,17},{17,1},{9,25},{25,9},{2,18},{18... | collective-permute-start | bytes 884744 | tf_op jit(solution)/shard_map/ppermute | solution.py:1288
  249.7 28.5 %collective-permute-start.66 = (bf16[768,384]{1,0:T(8,128)(2,1)S(1)}, bf16[768,384]{1,0:T(8,128)(2,1)S(1)}, u32[]{:S(2)}, u32[]{:S(2)}) collective-permute-start(bf16[768,384]{1,0:T(8,128)(2,1)S(1)} %add_convert_fusion), channel_id=1, source_target_pairs={{8,0},{16,24},{9,1},{17,25},{10,2},{18,26},{11,3},{19,27},{12,4},{... | collective-permute-start | bytes 1769480 | tf_op jit(solution)/shard_map/ppermute | solution.py:1288
  259.1 18.9 %collective-permute-start.61 = (bf16[56,1536]{1,0:T(8,128)(2,1)S(1)}, bf16[56,1536]{1,0:T(8,128)(2,1)S(1)}, u32[]{:S(2)}, u32[]{:S(2)}) collective-permute-start(bf16[56,1536]{1,0:T(8,128)(2,1)S(1)} %broadcast_select_fusion.5), channel_id=1, source_target_pairs={{0,8},{8,0},{16,24},{24,16},{1,9},{9,1},{17,25},{25,17},{2,10},{10... | collective-permute-start | bytes 516104 | tf_op jit(solution)/shard_map/ppermute | solution.py:103
  262.6 20.0 %collective-permute-start.65 = (bf16[48,3072]{1,0:T(8,128)(2,1)S(1)}, bf16[48,3072]{1,0:T(8,128)(2,1)S(1)}, u32[]{:S(2)}, u32[]{:S(2)}) collective-permute-start(bf16[48,3072]{1,0:T(8,128)(2,1)S(1)} %add_convert_fusion.10), channel_id=1, source_target_pairs={{0,8},{8,0},{16,24},{24,16},{1,9},{9,1},{17,25},{25,17},{2,10},{10... | collective-permute-start | bytes 884744 | tf_op jit(solution)/shard_map/ppermute | solution.py:1288
  263.6 20.1 %collective-permute-start.60 = (bf16[112,1536]{1,0:T(8,128)(2,1)S(1)}, bf16[112,1536]{1,0:T(8,128)(2,1)S(1)}, u32[]{:S(2)}, u32[]{:S(2)}) collective-permute-start(bf16[112,1536]{1,0:T(8,128)(2,1)S(1)} %add_convert_fusion.5), channel_id=1, source_target_pairs={{8,16},{16,8},{9,17},{17,9},{10,18},{18,10},{11,19},{19,11},{12,20... | collective-permute-start | bytes 1032200 | tf_op jit(solution)/shard_map/ppermute | solution.py:1288
  (82 other events, 632.4 us)
